TPU v7x, 32 devices: a whole 2x2x4 slice. The times are simulated.
32 devices in a mesh: groups: 2 (over y), seq: 4 (over z), tensor: 2 (over x), dp: 2 (over core).
Axes of the slice: x: 2, y: 2, z: 4, core: 2. Of those that a mesh axis runs over, the one named last changes fastest.
Arguments:
- hidden_in: bfloat16 [1024, 14336], P(('groups', 'seq'), ('tensor', 'dp')), parts along dimension 0, may hold values from -6 to 6
- cotangent: bfloat16 [1024, 8192], P(('groups', 'tensor', 'dp'), 'seq'), parts along dimension 0, may hold values from -6 to 6
- down_weight: bfloat16 [14336, 8192], P(('tensor', 'dp'), 'seq'), may hold values from -0.0625 to 0.0625
- tile_ids: int32 [8, 4, 4], P(('groups', 'seq'), ('tensor', 'dp')), parts along dimension 0, may hold values from 0 to 447, as said below
- tile_live: int32 [8, 4, 4], P(('groups', 'seq'), ('tensor', 'dp')), parts along dimension 0, may hold values from 0 to 1, as said below
- values: float32 [8, 4, 4, 128, 128], P(('groups', 'seq'), ('tensor', 'dp')), parts along dimension 0, may hold values from -0.5 to 0.5
- moment_one: float32 [8, 4, 4, 128, 128], P(('groups', 'seq'), ('tensor', 'dp')), parts along dimension 0, may hold values from -12 to 12
- moment_two: float32 [8, 4, 4, 128, 128], P(('groups', 'seq'), ('tensor', 'dp')), parts along dimension 0, may hold values from 0.01 to 4
Outputs:
- hidden_grad: bfloat16 [1024, 14336], P(('groups', 'seq'), ('tensor', 'dp')), parts along dimension 0
- values_new: float32 [8, 4, 4, 128, 128], P(('groups', 'seq'), ('tensor', 'dp')), parts along dimension 0
- moment_one_new: float32 [8, 4, 4, 128, 128], P(('groups', 'seq'), ('tensor', 'dp')), parts along dimension 0
- moment_two_new: float32 [8, 4, 4, 128, 128], P(('groups', 'seq'), ('tensor', 'dp')), parts along dimension 0
There are 2 independent parts, one for each index of `groups`. A program takes and returns all parts, laid end to end along the dimension named above; an argument that names none is the same for every part. Nothing has to cross between parts.
Inputs may be any that keep to these rules, and one draw needn't show every extreme that they name: `tile_live`: in every region the live slots come first, every region has at least one, and some region has all 4 live. `tile_ids`: the 4 entries of a region are distinct tile numbers t = f * 16 + d of its 28 x 16 blocks.
All inputs are finite; a program needn't handle non-finite values.
Results may differ from a plain program's by a relative error of at most 0.009.
Values may be sent and summed in bfloat16 or wider, within the bound.
No kernel may reach another device: no remote copies, remote signals or barrier semaphores. Data moves between devices by JAX's collectives and lax.ppermute only.
A program may use at most 128 MiB of HBM per device.

v0:
```python
import jax
import jax.numpy as jnp
from jax import lax
from jax.sharding import PartitionSpec as P

STEP = 100


BETA_ONE = 0.9
BETA_TWO = 0.999
RATE = 0.01
EPSILON = 1e-08


def pick_blocks(wide_rows, chooser, block_size):
    row_count = wide_rows.shape[0]
    grouped = wide_rows.reshape(row_count, chooser.shape[-1], block_size)
    picked = jnp.einsum("tkc,jk->jtc", grouped, chooser, preferred_element_type=jnp.float32)
    return picked.astype(jnp.bfloat16)


def per_device(
    hidden_in, cotangent, down_weight, tile_ids, tile_live, values, moment_one, moment_two
):
    span_count = lax.axis_size("seq")
    seq_here = lax.axis_index("seq")
    slot_count = values.shape[2]
    block_size = values.shape[3]
    f_width = down_weight.shape[0]
    d_width = down_weight.shape[1]
    f_blocks = f_width // block_size
    d_blocks = d_width // block_size
    rows_here = hidden_in.shape[0]
    peer_ids, peer_live = (
        lax.all_gather(tile_ids, "seq", axis=0, tiled=True),
        lax.all_gather(tile_live, "seq", axis=0, tiled=True),
    )
    peer_ids = peer_ids[:, 0, :]
    peer_live = peer_live[:, 0, :]
    counts = jnp.sum(peer_live, axis=1)
    prefix = jnp.cumsum(counts) - counts
    line_total = jnp.sum(counts)
    slot_index = jnp.arange(slot_count, dtype=jnp.int32)
    my_ids = tile_ids[0, 0]
    my_live = tile_live[0, 0] > 0
    my_rank = prefix[seq_here] + slot_index
    dest_owner = my_rank % span_count
    dest_slot = jnp.minimum(my_rank // span_count, slot_count - 1)
    held_rank = slot_index * span_count + seq_here
    held_live = held_rank < line_total
    below = (prefix[None, :] <= held_rank[:, None]).astype(jnp.int32)
    source = jnp.clip(jnp.sum(below, axis=1) - 1, 0, span_count - 1)
    source_slot = jnp.clip(held_rank - prefix[source], 0, slot_count - 1)
    stored = values[0, 0]
    stored_half = stored.astype(jnp.bfloat16)
    all_values = lax.all_gather(stored_half[None], "seq", axis=0, tiled=True)
    held_tiles = all_values[dest_owner, dest_slot]
    held_tiles = jnp.where(my_live[:, None, None], held_tiles, jnp.zeros_like(held_tiles))
    rows_all = lax.all_gather(cotangent, ("tensor", "dp"), axis=0, tiled=True)
    f_pick = jax.nn.one_hot(my_ids // d_blocks, f_blocks, dtype=jnp.bfloat16)
    d_pick = jax.nn.one_hot(my_ids % d_blocks, d_blocks, dtype=jnp.bfloat16)
    d_columns = pick_blocks(rows_all, d_pick, block_size)
    f_place = f_pick.astype(jnp.float32)
    dense_part = lax.dot_general(
        rows_all, down_weight, (((1,), (1,)), ((), ())), preferred_element_type=jnp.float32
    )
    col_block = d_columns
    tile_part = jnp.einsum(
        "jtd,jfd->jtf", col_block, held_tiles, preferred_element_type=jnp.float32
    )
    placed = jnp.einsum("jtf,jk->tkf", tile_part, f_place, precision=lax.Precision.HIGHEST)
    hidden_grad = lax.psum_scatter(
        (dense_part + placed.reshape(rows_here * lax.axis_size("seq"), f_width)).astype(
            jnp.bfloat16
        ),
        "seq",
        scatter_dimension=0,
        tiled=True,
    )
    h_columns = pick_blocks(
        lax.all_gather(hidden_in, "seq", axis=0, tiled=True), f_pick, block_size
    )
    col_block = d_columns
    tile_grads = jnp.einsum(
        "jtf,jtd->jfd", h_columns, col_block, preferred_element_type=jnp.float32
    )
    tile_grads = jnp.where(my_live[:, None, None], tile_grads, jnp.zeros_like(tile_grads))
    every_grad = lax.all_gather(
        tile_grads[None].astype(jnp.bfloat16), "seq", axis=0, tiled=True
    ).astype(jnp.float32)
    owned_grad = every_grad[source, source_slot]
    keep_mask = held_live[:, None, None]
    moment_new = BETA_ONE * moment_one[0, 0] + (1.0 - BETA_ONE) * owned_grad
    square_new = BETA_TWO * moment_two[0, 0] + (1.0 - BETA_TWO) * owned_grad * owned_grad
    stepped = (
        moment_new
        / (1.0 - BETA_ONE**STEP)
        / (jnp.sqrt(square_new / (1.0 - BETA_TWO**STEP)) + EPSILON)
    )
    updated = stored - RATE * stepped
    values_new = jnp.where(keep_mask, updated, stored)[None, None]
    moment_one_new = jnp.where(keep_mask, moment_new, moment_one[0, 0])[None, None]
    moment_two_new = jnp.where(keep_mask, square_new, moment_two[0, 0])[None, None]
    return (hidden_grad, values_new, moment_one_new, moment_two_new)


def solution(mesh):
    return jax.shard_map(
        per_device,
        mesh=mesh,
        in_specs=(
            P(("groups", "seq"), ("tensor", "dp")),
            P(("groups", "tensor", "dp"), "seq"),
            P(("tensor", "dp"), "seq"),
            P(("groups", "seq"), ("tensor", "dp"), None),
            P(("groups", "seq"), ("tensor", "dp"), None),
            P(("groups", "seq"), ("tensor", "dp"), None, None, None),
            P(("groups", "seq"), ("tensor", "dp"), None, None, None),
            P(("groups", "seq"), ("tensor", "dp"), None, None, None),
        ),
        out_specs=(
            P(("groups", "seq"), ("tensor", "dp")),
            P(("groups", "seq"), ("tensor", "dp"), None, None, None),
            P(("groups", "seq"), ("tensor", "dp"), None, None, None),
            P(("groups", "seq"), ("tensor", "dp"), None, None, None),
        ),
        check_vma=False,
    )
```

profile of v0, /device:TPU:0, one launch (start us, length us, event | category | flops | bytes accessed | tf_op | source)
XLA Modules:
  0.0 279.8 jit_solution(18066065488321881078)
XLA Ops:
  7.2 0.7 all-gather.5.cloned.1.call-update
  7.9 2.2 copy.29
  10.2 12.7 %all_gather.17 = s32[4,1,4]{2,1,0:T(1,128)S(1)} all-gather(s32[1,1,4]{2,1,0:T(1,128)} %param.12), channel_id=1, replica_groups=mesh['groups'=2,'seq'=4,'tensor'=2,'dp'=2] {'seq'}, dimensions={0}, use_global_device_ids=true | all-gather | bytes 80 | tf_op jit(solution)/shard_map/all_gather | solution.py:36
  22.9 0.7 fusion.34
  23.8 0.6 dynamic_slice.3
  24.6 0.6 gather_fusion.1
  25.3 0.7 fusion.30
  25.9 0.7 broadcast_compare_fusion
  26.6 0.7 compare_bitcast_fusion
  27.3 0.7 and_select_fusion.3
  27.9 6.9 %all-gather.5.cloned.1.call-done = bf16[512,2048]{1,0:T(8,128)(2,1)} async-done(((bf16[128,2048]{1,0:T(8,128)(2,1)}), bf16[512,2048]{1,0:T(8,128)(2,1)}) %all-gather.5.cloned.1.call-update) | async-done | bytes 2097168 | tf_op jit(solution)/shard_map/all_gather | solution.py:59
  34.9 2.2 copy.33
  37.6 71.5 %all-gather.7.cloned.1.call-done = bf16[512,3584]{0,1:T(8,128)(2,1)} async-done(((bf16[128,3584]{0,1:T(8,128)(2,1)}), bf16[512,3584]{0,1:T(8,128)(2,1)}) %all-gather.7.cloned.1.call-update) | async-done | bytes 3670032 | tf_op jit(solution)/shard_map/all_gather | solution.py:81
  109.0 7.8 %copy.30 = bf16[512,28,128]{2,1,0:T(8,128)(2,1)} copy(bf16[512,28,128]{0,2,1:T(8,128)(2,1)} %bitcast.76) | data formatting | bytes 7340032 | tf_op jit(solution)/shard_map/reshape | solution.py:17
  116.9 3.0 %convolution_convert_fusion = bf16[4,512,128]{2,0,1:T(4,128)(2,1)S(1)} fusion(bf16[512,28,128]{2,1,0:T(8,128)(2,1)} %copy.30, s32[4]{0:T(128)S(1)} %get-tuple-element.10), kind=kOutput, calls=%fused_computation.5 | convolution fusion | flops 14942320 | bytes 4194320 | tf_op jit(solution)/shard_map/tkc,jk->jtc/dot_general | solution.py:18
  120.3 16.2 %all-gather.1 = bf16[16,128,128]{2,1,0:T(8,128)(2,1)S(1)} all-gather(bf16[4,128,128]{2,1,0:T(8,128)(2,1)S(1)} %fusion), channel_id=3, replica_groups=mesh['groups'=2,'seq'=4,'tensor'=2,'dp'=2] {'seq'}, dimensions={0}, use_global_device_ids=true | all-gather | bytes 655360 | tf_op jit(solution)/shard_map/all_gather | solution.py:88
  137.2 1.1 fusion.9
  138.3 15.0 %all-gather = bf16[4,1,4,128,128]{4,3,2,1,0:T(8,128)(2,1)S(1)} all-gather(bf16[1,1,4,128,128]{4,3,2,1,0:T(8,128)(2,1)S(1)} %get-tuple-element.9), channel_id=2, replica_groups=mesh['groups'=2,'seq'=4,'tensor'=2,'dp'=2] {'seq'}, dimensions={0}, use_global_device_ids=true | all-gather | bytes 655360 | tf_op jit(solution)/shard_map/all_gather | solution.py:56
  153.3 0.6 gather_fusion
  154.3 6.9 %convolution_bitcast_fusion = f32[512,28,128]{2,1,0:T(8,128)} fusion(f32[4,512,128]{2,1,0:T(8,128)S(1)} %fusion.4, s32[4]{0:T(128)S(1)} %get-tuple-element.10), kind=kOutput, calls=%fused_computation.4 | convolution fusion | flops 88080496 | bytes 8388624 | tf_op jit(solution)/shard_map/jtf,jk->tkf/dot_general | solution.py:71
  161.2 9.8 %copy.27 = f32[512,28,128]{0,2,1:T(8,128)} copy(f32[512,28,128]{2,1,0:T(8,128)} %convolution_bitcast_fusion) | data formatting | bytes 14680064 | tf_op jit(solution)/shard_map/jtf,jk->tkf/transpose | solution.py:71
  171.0 8.5 %copy.28 = f32[512,3584]{1,0:T(8,128)} copy(f32[512,3584]{0,1:T(8,128)} %bitcast.74) | data formatting | bytes 14680064 | tf_op jit(solution)/shard_map/reshape | solution.py:73
  179.5 26.5 %add_convert_fusion = bf16[512,3584]{1,0:T(8,128)(2,1)} fusion(f32[512,3584]{1,0:T(8,128)} %copy.28, bf16[512,2048]{1,0:T(8,128)(2,1)S(1)} %copy-done, bf16[3584,2048]{1,0:T(8,128)(2,1)} %param.10), kind=kOutput, calls=%fused_computation.3 | convolution fusion | flops 7519862784 | bytes 27787264 | tf_op jit(solution)/shard_map/dot_general | solution.py:64
  206.1 67.2 %reduce-scatter.2.cloned.1.call-done = bf16[128,3584]{1,0:T(8,128)(2,1)} async-done(((bf16[512,3584]{1,0:T(8,128)(2,1)}), bf16[128,3584]{1,0:T(8,128)(2,1)}) %reduce-scatter.2.cloned.1.call-update) | async-done | bytes 917520 | tf_op jit(solution)/shard_map/reduce_scatter | solution.py:72
  (24 shorter events, 2.5 us)
Async XLA Ops:
  7.2 27.7 %all-gather.5.cloned.1.call-start = ((), (), s32[]{:S(2)}) async-start(), calls=%async_computation.1 | async-start | bytes 2621440 | tf_op jit(solution)/shard_map/all_gather | solution.py:59
  7.9 101.1 %all-gather.7.cloned.1.call-start = ((), (), s32[]{:S(2)}) async-start(), calls=%async_computation.3 | async-start | bytes 4587520 | tf_op jit(solution)/shard_map/all_gather | solution.py:81
  10.2 263.1 %reduce-scatter.2.cloned.1.call-start = ((), (), s32[]{:S(2)}) async-start(), calls=%async_computation.2 | async-start | bytes 4587520 | tf_op jit(solution)/shard_map/reduce_scatter | solution.py:72
  116.9 20.3 %copy-start.1 = (f32[1,1,4,128,128]{4,3,2,1,0:T(8,128)S(1)}, f32[1,1,4,128,128]{4,3,2,1,0:T(8,128)}, u32[]{:S(2)}) copy-start(f32[1,1,4,128,128]{4,3,2,1,0:T(8,128)} %param.15) | copy-start | bytes 786436
  116.9 20.3 %copy-start.2 = (f32[1,1,4,128,128]{4,3,2,1,0:T(8,128)S(1)}, f32[1,1,4,128,128]{4,3,2,1,0:T(8,128)}, u32[]{:S(2)}) copy-start(f32[1,1,4,128,128]{4,3,2,1,0:T(8,128)} %param.13) | copy-start | bytes 786436
  116.9 20.3 %copy-start.3 = (f32[1,1,4,128,128]{4,3,2,1,0:T(8,128)S(1)}, f32[1,1,4,128,128]{4,3,2,1,0:T(8,128)}, u32[]{:S(2)}) copy-start(f32[1,1,4,128,128]{4,3,2,1,0:T(8,128)} %param.14) | copy-start | bytes 786436
  171.0 8.5 %copy-start = (bf16[512,2048]{1,0:T(8,128)(2,1)S(1)}, bf16[512,2048]{1,0:T(8,128)(2,1)}, u32[]{:S(2)}) copy-start(bf16[512,2048]{1,0:T(8,128)(2,1)} %all-gather.5.cloned.1.call-done) | copy-start | bytes 6291460
Sparse Core Ops, SparseCore 0:
  9.6 25.2 all-gather.4
  37.0 71.9 all-gather.6
  206.2 67.0 reduce-scatter.1
where the time goes:
time: 281 us; the launch traced here: 280 us
  waiting for transfers between devices  146 us (52%)
  blocking collectives  43.9 us (16%)
  matrix products  37.7 us (13%)
  local copies, waits for them, and re-layouts  32.9 us (12%)
  between operations  13.8 us (5%)
  other arithmetic  4.98 us (2%)
    all_gather x1, waiting for transfers between devices, per_device(): lax.all_gather(hidden_in, 'seq', axis=0, tiled=True)  71.5 us
    reduce_scatter x1, waiting for transfers between devices, per_device(): lax.psum_scatter((dense_part + placed.reshape(rows_here * lax.axis_size('...  67.2 us
    dot_general x1, matrix products, per_device(): lax.dot_general(rows_all, down_weight, (((1,), (1,)), ((), ())), preferre...  26.5 us
    all_gather x1, blocking collectives, per_device(): lax.all_gather(tile_grads[None].astype(jnp.bfloat16), 'seq', axis=0, tile...  16.2 us
    all_gather x1, blocking collectives, per_device(): all_values = lax.all_gather(stored_half[None], 'seq', axis=0, tiled=True)  15 us
    all_gather x1, blocking collectives, per_device(): lax.all_gather(tile_live, 'seq', axis=0, tiled=True)  12.7 us
    transpose x1, local copies, waits for them, and re-layouts, per_device(): jnp.einsum('jtf,jk->tkf', tile_part, f_place, precision=lax.Precision.HIG...  9.81 us
    reshape x1, local copies, waits for them, and re-layouts, per_device(): placed.reshape(rows_here * lax.axis_size('seq'), f_width)  8.52 us
  transfers between devices with their start and end apart: 3, of which 3 were waited for; matrix products, arithmetic and copies ran while one was open for 4% of the time, Pallas kernels for 0%

commit v1 on v0

v1 whole, which is shorter than its diff:
```python
import functools

import jax
import jax.numpy as jnp
from jax import lax
from jax.experimental import pallas as pl
from jax.experimental.pallas import tpu as pltpu
from jax.sharding import PartitionSpec as P

STEP = 100
BETA_ONE = 0.9
BETA_TWO = 0.999
RATE = 0.01
EPSILON = 1e-08
VMEM_LIMIT = 48 * 1024 * 1024


def vmem():
    return pl.BlockSpec(memory_space=pltpu.VMEM)


def smem():
    return pl.BlockSpec(memory_space=pltpu.SMEM)


def params():
    return pltpu.CompilerParams(vmem_limit_bytes=VMEM_LIMIT)


def region_count(meta, region, slots):
    count = meta[region, slots]
    for slot in range(1, slots):
        count = count + meta[region, slots + slot]
    return count


def region_counts(meta, spans, slots):
    counts = [region_count(meta, region, slots) for region in range(spans)]
    prefix, total = [], jnp.int32(0)
    for count in counts:
        prefix.append(total)
        total = total + count
    return counts, prefix, total


def pick_kernel(spans, slots, block, d_blocks, meta, here, values, hidden, value_out, hidden_out):
    counts, prefix, _ = region_counts(meta, spans, slots)
    me = here[0]
    for region in range(spans):
        slot = lax.rem(me - lax.rem(prefix[region], spans) + spans, spans)
        live = slot < counts[region]
        owned = jnp.minimum(lax.div(prefix[region] + slot, spans), slots - 1)
        tile = values[owned]
        value_out[region] = jnp.where(live, tile, jnp.zeros_like(tile)).astype(jnp.bfloat16)
        for j in range(slots):
            start = pl.multiple_of(lax.div(meta[region, j], d_blocks) * block, block)
            hidden_out[region, j] = hidden[:, pl.ds(start, block)]


def grad_kernel(spans, slots, block, d_blocks, meta, here, hidden, rows, out):
    me = here[0]
    count = region_count(meta, me, slots)
    before = jnp.int32(0)
    for region in range(spans):
        before = before + jnp.where(region < me, region_count(meta, region, slots), 0)
    out[...] = jnp.zeros_like(out)
    chunk = hidden.shape[2]
    for j in range(slots):

        @pl.when(j < count)
        def _():
            d_start = pl.multiple_of(lax.rem(meta[me, j], d_blocks) * block, block)
            total = jnp.zeros((block, block), jnp.float32)
            for part in range(spans):
                total = total + lax.dot_general(
                    hidden[part, j],
                    rows[pl.ds(part * chunk, chunk), pl.ds(d_start, block)],
                    (((0,), (0,)), ((), ())),
                    preferred_element_type=jnp.float32,
                )
            out[lax.rem(before + j, spans)] = total.astype(out.dtype)


def adam_kernel(spans, slots, meta, here, grads, values, one, two, values_new, one_new, two_new):
    counts, prefix, total = region_counts(meta, spans, slots)
    me = here[0]
    for owned in range(slots):
        rank = owned * spans + me
        source = jnp.int32(0)
        for region in range(1, spans):
            source = jnp.where(prefix[region] <= rank, region, source)
        live = rank < total
        grad = grads[source].astype(jnp.float32)
        stored, old_one, old_two = values[owned], one[owned], two[owned]
        new_one = BETA_ONE * old_one + (1.0 - BETA_ONE) * grad
        new_two = BETA_TWO * old_two + (1.0 - BETA_TWO) * grad * grad
        stepped = (
            new_one
            / (1.0 - BETA_ONE**STEP)
            / (jnp.sqrt(new_two / (1.0 - BETA_TWO**STEP)) + EPSILON)
        )
        values_new[owned] = jnp.where(live, stored - RATE * stepped, stored)
        one_new[owned] = jnp.where(live, new_one, old_one)
        two_new[owned] = jnp.where(live, new_two, old_two)


def exchange(array):
    return lax.all_to_all(array, "seq", 0, 0, tiled=True)


def per_device(
    hidden_in, cotangent, down_weight, tile_ids, tile_live, values, moment_one, moment_two
):
    spans = lax.axis_size("seq")
    slots, block = values.shape[2], values.shape[3]
    f_width, d_width = down_weight.shape
    d_blocks, f_blocks = d_width // block, f_width // block
    chunk = hidden_in.shape[0]
    tokens = chunk * spans
    here = lax.axis_index("seq").astype(jnp.int32)[None]
    sizes = (spans, slots, block, d_blocks)

    meta = jnp.concatenate([tile_ids[0], tile_live[0]], axis=1)
    meta = lax.all_gather(meta, "seq", axis=0, tiled=True)
    rows = lax.all_gather(cotangent, ("tensor", "dp"), axis=0, tiled=True)

    value_send, hidden_send = pl.pallas_call(
        functools.partial(pick_kernel, *sizes),
        out_shape=(
            jax.ShapeDtypeStruct((spans, block, block), jnp.bfloat16),
            jax.ShapeDtypeStruct((spans, slots, chunk, block), jnp.bfloat16),
        ),
        in_specs=[smem(), smem(), vmem(), vmem()],
        out_specs=(vmem(), vmem()),
        compiler_params=params(),
        name="pick",
    )(meta, here, values[0, 0], hidden_in)
    held = exchange(value_send)
    hidden_cols = exchange(hidden_send)

    group = max(size for size in range(1, 5) if f_blocks % size == 0)
    width = group * block
    parts = 2 if (f_blocks // group) > 1 else 1
    steps_all = f_width // width
    cuts = [steps_all * part // parts for part in range(parts + 1)]
    pieces = []
    for low, high in zip(cuts[:-1], cuts[1:]):
        piece = pl.pallas_call(
            functools.partial(offset_kernel, low, *sizes),
            grid=(high - low,),
            out_shape=jax.ShapeDtypeStruct((tokens, (high - low) * width), jnp.bfloat16),
            in_specs=[
                smem(),
                smem(),
                pl.BlockSpec((tokens, d_width), lambda i: (0, 0)),
                pl.BlockSpec((width, d_width), lambda i, low=low: (i + low, 0)),
                pl.BlockSpec((spans, block, block), lambda i: (0, 0, 0)),
            ],
            out_specs=pl.BlockSpec((tokens, width), lambda i: (0, i)),
            scratch_shapes=[pltpu.VMEM((tokens, width), jnp.float32)],
            compiler_params=params(),
            cost_estimate=pl.CostEstimate(
                flops=2 * tokens * d_width * (high - low) * width,
                bytes_accessed=2 * d_width * (high - low) * width,
                transcendentals=0,
            ),
            name="partial",
        )(meta, here, rows, down_weight, held)
        pieces.append(lax.psum_scatter(piece, "seq", scatter_dimension=0, tiled=True))
    hidden_grad = jnp.concatenate(pieces, axis=1)

    grad_send = pl.pallas_call(
        functools.partial(grad_kernel, *sizes),
        out_shape=jax.ShapeDtypeStruct((spans, block, block), jnp.bfloat16),
        in_specs=[smem(), smem(), vmem(), vmem()],
        out_specs=vmem(),
        compiler_params=params(),
        name="tile_grad",
    )(meta, here, hidden_cols, rows)
    grads = exchange(grad_send)
    tile = jax.ShapeDtypeStruct((slots, block, block), jnp.float32)
    new = pl.pallas_call(
        functools.partial(adam_kernel, spans, slots),
        out_shape=(tile, tile, tile),
        in_specs=[smem(), smem()] + [vmem()] * 4,
        out_specs=(vmem(), vmem(), vmem()),
        compiler_params=params(),
        name="adam",
    )(meta, here, grads, values[0, 0], moment_one[0, 0], moment_two[0, 0])
    return (hidden_grad,) + tuple(array[None, None] for array in new)


def offset_kernel(low, spans, slots, block, d_blocks, meta, here, rows, weight, held, out, total):
    step = pl.program_id(0) + low
    partial_step(step, spans, slots, block, d_blocks, meta, here, rows, weight, held, out, total)


def partial_step(
    step, spans, slots, block, d_blocks, meta, here, rows, weight, held, out, total
):
    width = weight.shape[0]
    total[...] = lax.dot_general(
        rows[...], weight[...], (((1,), (1,)), ((), ())), preferred_element_type=jnp.float32
    )
    me = here[0]
    count = region_count(meta, me, slots)
    before = jnp.int32(0)
    for region in range(spans):
        before = before + jnp.where(region < me, region_count(meta, region, slots), 0)
    for j in range(slots):
        tile = meta[me, j]
        f_start = lax.div(tile, d_blocks) * block - step * width

        @pl.when((j < count) & (f_start >= 0) & (f_start < width))
        def _():
            d_start = pl.multiple_of(lax.rem(tile, d_blocks) * block, block)
            place = pl.ds(pl.multiple_of(f_start, block), block)
            total[:, place] += lax.dot_general(
                rows[:, pl.ds(d_start, block)],
                held[lax.rem(before + j, spans)],
                (((1,), (1,)), ((), ())),
                preferred_element_type=jnp.float32,
            )

    out[...] = total[...].astype(out.dtype)


def solution(mesh):
    shards = P(("groups", "seq"), ("tensor", "dp"))
    tiles = P(("groups", "seq"), ("tensor", "dp"), None, None, None)
    lists = P(("groups", "seq"), ("tensor", "dp"), None)
    return jax.shard_map(
        per_device,
        mesh=mesh,
        in_specs=(
            shards,
            P(("groups", "tensor", "dp"), "seq"),
            P(("tensor", "dp"), "seq"),
            lists,
            lists,
            tiles,
            tiles,
            tiles,
        ),
        out_specs=(shards, tiles, tiles, tiles),
        check_vma=False,
    )
```

time: 281 us -> 144 us (0.51)
  waiting for transfers between devices: 146 us -> 40 us
  matrix products: 37.7 us -> 0 us
  local copies, waits for them, and re-layouts: 32.9 us -> 6.23 us
  blocking collectives: 43.9 us -> 63.2 us
  Pallas kernels: 0 us -> 17.6 us
    all_gather x2 -> x1, waiting for transfers between devices: 78.4 us -> 2.47 us  [per_device(): rows = lax.all_gather(cotangent, ('tensor', 'dp'), axis=0, tiled=True)]
    all_to_all x0 -> x3, blocking collectives: none -> 50.7 us  [exchange(): return lax.all_to_all(array, 'seq', 0, 0, tiled=True)]
    dot_general x6 -> x0, matrix products: 37.7 us -> none  [the longest x1 26.5 us: per_device(): lax.dot_general(rows_all, down_weight, (((1,), (1,)), ((), ())), preferre...]
    all_gather x3 -> x1, blocking collectives: 43.9 us -> 12.5 us  [per_device(): meta = lax.all_gather(meta, 'seq', axis=0, tiled=True)]
    reduce_scatter x1 -> x2, waiting for transfers between devices: 67.2 us -> 36.8 us  [per_device(): lax.psum_scatter(piece, 'seq', scatter_dimension=0, tiled=True)]
    pallas_call x0 -> x5, Pallas kernels: none -> 17.6 us  [the longest x2 14.2 us: per_device(): pl.pallas_call(functools.partial(offset_kernel, low, *sizes), grid=(high...]
    reshape x2 -> x0, local copies, waits for them, and re-layouts: 16.3 us -> none  [the longest x1 8.52 us: per_device(): placed.reshape(rows_here * lax.axis_size('seq'), f_width)]
    transpose x1 -> x0, local copies, waits for them, and re-layouts: 9.81 us -> none  [per_device(): jnp.einsum('jtf,jk->tkf', tile_part, f_place, precision=lax.Precision.HIG...]
  transfers between devices with their start and end apart: 3 -> 3, of which waited for: 3 -> 2; matrix products, arithmetic and copies ran while one was open for 4% -> 1% of each run, Pallas kernels for 0% -> 8%
where the time goes in v1:
time: 144 us
  blocking collectives  63.2 us (44%)
  waiting for transfers between devices  40 us (28%)
  Pallas kernels  17.6 us (12%)
  between operations  13.8 us (10%)
  local copies, waits for them, and re-layouts  6.23 us (4%)
  other arithmetic  2.88 us (2%)
    all_to_all x3, blocking collectives, exchange(): return lax.all_to_all(array, 'seq', 0, 0, tiled=True)  50.7 us
    reduce_scatter x2, waiting for transfers between devices, per_device(): lax.psum_scatter(piece, 'seq', scatter_dimension=0, tiled=True)  36.8 us
    pallas_call x2, Pallas kernels, per_device(): pl.pallas_call(functools.partial(offset_kernel, low, *sizes), grid=(high...  14.2 us
    all_gather x1, blocking collectives, per_device(): meta = lax.all_gather(meta, 'seq', axis=0, tiled=True)  12.5 us
    unnamed x18, local copies, waits for them, and re-layouts  6.23 us
  transfers between devices with their start and end apart: 3, of which 2 were waited for; matrix products, arithmetic and copies ran while one was open for 1% of the time, Pallas kernels for 8%

profile of v1, /device:TPU:0, one launch (start us, length us, event | category | flops | bytes accessed | tf_op | source)
XLA Modules:
  0.0 143.9 jit_solution(6914891777087792241)
XLA Ops:
  7.2 0.0 all-gather.3.cloned.1.call-start
  7.2 0.7 all-gather.3.cloned.1.call-update
  7.9 0.0 reduce-scatter.3.cloned.1.call-start
  7.9 0.7 add_bitcast_fusion
  8.7 12.5 %all-gather = s32[4,1,8]{2,1,0:T(1,128)S(1)} all-gather(s32[1,1,8]{2,1,0:T(1,128)S(1)} %add_bitcast_fusion), channel_id=1, replica_groups=mesh['groups'=2,'seq'=4,'tensor'=2,'dp'=2] {'seq'}, dimensions={0}, use_global_device_ids=true | all-gather | bytes 160 | tf_op jit(solution)/shard_map/all_gather | solution.py:124
  21.2 0.9 copy-done.4
  22.2 1.2 copy-done.6
  23.4 0.7 pick.1
  24.1 8.3 %all_to_all.15.held = bf16[4,128,128]{2,1,0:T(8,128)(2,1)S(1)} all-to-all(bf16[4,128,128]{2,1,0:T(8,128)(2,1)S(1)} %get-tuple-element.9), channel_id=1, replica_groups=mesh['groups'=2,'seq'=4,'tensor'=2,'dp'=2] {'seq'}, dimensions={0} | all-to-all | bytes 262144 | tf_op jit(solution)/shard_map/all_to_all | solution.py:108
  32.4 2.5 %all-gather.3.cloned.1.call-done.rows = bf16[512,2048]{1,0:T(8,128)(2,1)} async-done(((bf16[128,2048]{1,0:T(8,128)(2,1)}), bf16[512,2048]{1,0:T(8,128)(2,1)}) %all-gather.3.cloned.1.call-update) | async-done | bytes 2097168 | tf_op jit(solution)/shard_map/all_gather | solution.py:125
  34.9 1.6 %copy-done = bf16[512,2048]{1,0:T(8,128)(2,1)S(1)} copy-done((bf16[512,2048]{1,0:T(8,128)(2,1)S(1)}, bf16[512,2048]{1,0:T(8,128)(2,1)}, u32[]{:S(2)}) %copy-start) | copy-done | bytes 2097176
  36.5 6.4 %partial.2 = bf16[512,1536]{1,0:T(8,128)(2,1)S(1)} custom-call(s32[4,8]{1,0:T(4,128)S(1)} %bitcast.17, s32[1]{0:T(128)} %bitcast.4.here, bf16[512,2048]{1,0:T(8,128)(2,1)S(1)} %copy-done, bf16[3584,2048]{1,0:T(8,128)(2,1)} %weight.3, bf16[4,128,128]{2,1,0:T(8,128)(2,1)S(1)} %all_to_all.15.held), custom_call_target="tpu_custom_call" | custom-call | flops 3221225472 | bytes 6291456 | tf_op jit(solution)/shard_map/partial/pallas_call | solution.py:148
  42.9 1.2 copy-done.3
  44.0 0.0 reduce-scatter.3.cloned.1.call-update
  44.1 0.0 reduce-scatter.5.cloned.1.call-start
  44.1 7.8 %partial.3 = bf16[512,2048]{1,0:T(8,128)(2,1)S(1)} custom-call(s32[4,8]{1,0:T(4,128)S(1)} %bitcast.18, s32[1]{0:T(128)} %bitcast.4.here, bf16[512,2048]{1,0:T(8,128)(2,1)S(1)} %copy-done.1, bf16[3584,2048]{1,0:T(8,128)(2,1)} %weight.3, bf16[4,128,128]{2,1,0:T(8,128)(2,1)S(1)} %all_to_all.15.held), custom_call_target="tpu_custom_call" | custom-call | flops 4294967296 | bytes 8388608 | tf_op jit(solution)/shard_map/partial/pallas_call | solution.py:148
  51.9 1.3 copy-done.2
  53.3 0.0 reduce-scatter.5.cloned.1.call-update
  53.3 34.1 %all_to_all.16.hidden = bf16[4,4,128,128]{3,2,1,0:T(8,128)(2,1)S(1)} all-to-all(bf16[4,4,128,128]{3,2,1,0:T(8,128)(2,1)S(1)} %get-tuple-element.10), channel_id=1, replica_groups=mesh['groups'=2,'seq'=4,'tensor'=2,'dp'=2] {'seq'}, dimensions={0} | all-to-all | bytes 1048576 | tf_op jit(solution)/shard_map/all_to_all | solution.py:108
  87.4 1.0 tile_grad.1
  88.4 8.3 %all_to_all.17.grads = bf16[4,128,128]{2,1,0:T(8,128)(2,1)S(1)} all-to-all(bf16[4,128,128]{2,1,0:T(8,128)(2,1)S(1)} %tile_grad.1), channel_id=1, replica_groups=mesh['groups'=2,'seq'=4,'tensor'=2,'dp'=2] {'seq'}, dimensions={0} | all-to-all | bytes 262144 | tf_op jit(solution)/shard_map/all_to_all | solution.py:108
  96.7 1.6 %adam.1 = (f32[4,128,128]{2,1,0:T(8,128)}, f32[4,128,128]{2,1,0:T(8,128)}, f32[4,128,128]{2,1,0:T(8,128)}) custom-call(s32[4,8]{1,0:T(4,128)S(1)} %bitcast.20, s32[1]{0:T(128)} %bitcast.4.here, bf16[4,128,128]{2,1,0:T(8,128)(2,1)S(1)} %all_to_all.17.grads, f32[4,128,128]{2,1,0:T(8,128)S(1)} %bitcast.13, f32[4,128,128]{2,1,0:T(8,128)S(1)} %bitcast.14, ...), custom_call_target="tpu_custom_call" | custom-call | tf_op jit(solution)/shard_map/adam/pallas_call | solution.py:182
  98.4 36.8 %reduce-scatter.5.cloned.1.call-done = bf16[128,2048]{1,0:T(8,128)(2,1)} async-done(((bf16[512,2048]{1,0:T(8,128)(2,1)}), bf16[128,2048]{1,0:T(8,128)(2,1)}) %reduce-scatter.5.cloned.1.call-update) | async-done | bytes 524304 | tf_op jit(solution)/shard_map/reduce_scatter | solution.py:169
  135.2 2.1 %pad_maximum_fusion = bf16[128,3584]{1,0:T(8,128)(2,1)} fusion(bf16[128,2048]{1,0:T(8,128)(2,1)} %reduce-scatter.5.cloned.1.call-done, bf16[128,1536]{1,0:T(8,128)(2,1)} %reduce-scatter.3.cloned.1.call-done), kind=kLoop, calls=%fused_computation | loop fusion | flops 1835008 | bytes 1835008 | tf_op jit(solution)/shard_map/concatenate | solution.py:170
  (14 shorter events, 0.0 us)
Async XLA Ops:
  7.2 27.7 %all-gather.3.cloned.1.call-start = ((), (), s32[]{:S(2)}) async-start(), calls=%async_computation.5 | async-start | bytes 2621440 | tf_op jit(solution)/shard_map/all_gather | solution.py:125
  7.9 90.5 %reduce-scatter.3.cloned.1.call-start = ((), (), s32[]{:S(2)}) async-start(), calls=%async_computation.6 | async-start | bytes 1966080 | tf_op jit(solution)/shard_map/reduce_scatter | solution.py:169
  21.2 1.0 copy-start.4
  22.2 1.2 copy-start.6
  34.9 1.6 %copy-start = (bf16[512,2048]{1,0:T(8,128)(2,1)S(1)}, bf16[512,2048]{1,0:T(8,128)(2,1)}, u32[]{:S(2)}) copy-start(bf16[512,2048]{1,0:T(8,128)(2,1)} %all-gather.3.cloned.1.call-done.rows) | copy-start | bytes 6291460
  36.5 7.6 %copy-start.1 = (bf16[512,2048]{1,0:T(8,128)(2,1)S(1)}, bf16[512,2048]{1,0:T(8,128)(2,1)}, u32[]{:S(2)}) copy-start(bf16[512,2048]{1,0:T(8,128)(2,1)} %all-gather.3.cloned.1.call-done.rows) | copy-start | bytes 6291460
  42.9 1.2 copy-start.3
  44.1 91.1 %reduce-scatter.5.cloned.1.call-start = ((), (), s32[]{:S(2)}) async-start(), calls=%async_computation.7 | async-start | bytes 2621440 | tf_op jit(solution)/shard_map/reduce_scatter | solution.py:169
  51.9 1.3 copy-start.2
  53.3 43.4 %copy-start.5 = (f32[1,1,4,128,128]{4,3,2,1,0:T(8,128)S(1)}, f32[1,1,4,128,128]{4,3,2,1,0:T(8,128)}, u32[]{:S(2)}) copy-start(f32[1,1,4,128,128]{4,3,2,1,0:T(8,128)} %param.13) | copy-start | bytes 786436
  53.3 43.4 %copy-start.7 = (f32[1,1,4,128,128]{4,3,2,1,0:T(8,128)S(1)}, f32[1,1,4,128,128]{4,3,2,1,0:T(8,128)}, u32[]{:S(2)}) copy-start(f32[1,1,4,128,128]{4,3,2,1,0:T(8,128)} %param.14) | copy-start | bytes 786436
  53.3 43.4 %copy-start.8 = (f32[1,1,4,128,128]{4,3,2,1,0:T(8,128)S(1)}, f32[1,1,4,128,128]{4,3,2,1,0:T(8,128)}, u32[]{:S(2)}) copy-start(f32[1,1,4,128,128]{4,3,2,1,0:T(8,128)} %param.15) | copy-start | bytes 786436
Sparse Core Ops, SparseCore 0:
  9.6 25.2 all-gather.2
  44.2 43.9 reduce-scatter.2
  90.4 44.7 reduce-scatter.4

commit v2 on v1

v2 whole, which is shorter than its diff:
```python
import functools

import jax
import jax.numpy as jnp
from jax import lax
from jax.experimental import pallas as pl
from jax.experimental.pallas import tpu as pltpu
from jax.sharding import PartitionSpec as P

STEP = 100
BETA_ONE = 0.9
BETA_TWO = 0.999
RATE = 0.01
EPSILON = 1e-08
VMEM_LIMIT = 48 * 1024 * 1024
NT = (((1,), (1,)), ((), ()))
TN = (((0,), (0,)), ((), ()))


def vmem():
    return pl.BlockSpec(memory_space=pltpu.VMEM)


def smem():
    return pl.BlockSpec(memory_space=pltpu.SMEM)


def anywhere():
    return pl.BlockSpec(memory_space=pl.ANY)


def params():
    return pltpu.CompilerParams(vmem_limit_bytes=VMEM_LIMIT)


def wrap(index, size):
    return lax.rem(index + size, size)


def live_count(meta, region, slots):
    count = meta[region, slots]
    for slot in range(1, slots):
        count = count + meta[region, slots + slot]
    return count


def rank_before(meta, region, spans, slots):
    before = jnp.int32(0)
    for other in range(spans):
        before = before + jnp.where(other < region, live_count(meta, other, slots), 0)
    return before


def pick_kernel(spans, slots, block, d_blocks, meta, values, hidden, *outs):
    me = lax.axis_index("seq")
    for s in range(spans):
        region = lax.rem(me + s, spans)
        before = rank_before(meta, region, spans, slots)
        slot = wrap(me - lax.rem(before, spans), spans)
        live = slot < live_count(meta, region, slots)
        tile = values[jnp.minimum(lax.div(before + slot, spans), slots - 1)]
        outs[s][...] = jnp.where(live, tile, jnp.zeros_like(tile)).astype(jnp.bfloat16)
        for j in range(slots):
            start = pl.multiple_of(lax.div(meta[region, j], d_blocks) * block, block)
            outs[spans + s][j] = hidden[:, pl.ds(start, block)]


def chunk_place(chunk):
    tensors, cores = lax.axis_size("tensor"), lax.axis_size("dp")
    t_place = wrap(lax.div(chunk, cores) - lax.axis_index("tensor"), tensors)
    d_place = wrap(lax.rem(chunk, cores) - lax.axis_index("dp"), cores)
    return t_place * cores + d_place


def step_kernel(sizes, low, chunks_of, arrivals, meta, held, weight, *refs):
    spans, slots, block, d_blocks = sizes
    places = lax.axis_size("tensor") * lax.axis_size("dp")
    gathered, refs = refs[:places], refs[places:]
    arrived, refs = refs[: sum(arrivals)], refs[sum(arrivals) :]
    outs, (rows, total, sem) = refs[: len(chunks_of)], refs[len(chunks_of) :]
    step = pl.program_id(0)
    me = lax.axis_index("seq")
    chunk = gathered[0].shape[0]

    @pl.when(step == 0)
    def _():
        for k, chunk_of in enumerate(chunks_of):
            place = chunk_place(jnp.clip(chunk_of(me), 0, spans - 1))
            for p in range(places):

                @pl.when(place == p)
                def _():
                    copy = pltpu.make_async_copy(
                        gathered[p], rows.at[pl.ds(k * chunk, chunk)], sem
                    )
                    copy.start()
                    copy.wait()

    total[...] = lax.dot_general(rows[...], weight[...], NT, preferred_element_type=jnp.float32)
    width = weight.shape[0]
    count = live_count(meta, me, slots)
    before = rank_before(meta, me, spans, slots)
    for j in range(slots):
        tile = meta[me, j]
        f_start = lax.div(tile, d_blocks) * block - (step + low) * width

        @pl.when((j < count) & (f_start >= 0) & (f_start < width))
        def _():
            d_start = pl.multiple_of(lax.rem(tile, d_blocks) * block, block)
            place = pl.ds(pl.multiple_of(f_start, block), block)
            owner = lax.rem(before + j, spans)
            total[:, place] += lax.dot_general(
                rows[:, pl.ds(d_start, block)],
                held[wrap(me - owner, spans)],
                NT,
                preferred_element_type=jnp.float32,
            )

    at = 0
    for k, out in enumerate(outs):
        result = total[k * chunk : (k + 1) * chunk]
        for _ in range(arrivals[k]):
            result = result + arrived[at][...].astype(jnp.float32)
            at += 1
        out[...] = result.astype(out.dtype)


def step_call(sizes, low, high, width, chunks_of, arrived, meta, held, weight, gathered, dtype):
    chunk, d_width = gathered[0].shape
    many = len(chunks_of)
    columns = pl.BlockSpec((chunk, width), lambda i: (0, i))
    given = [array for group in arrived for array in group]
    return pl.pallas_call(
        functools.partial(step_kernel, sizes, low, chunks_of, [len(group) for group in arrived]),
        grid=(high - low,),
        out_shape=[jax.ShapeDtypeStruct((chunk, (high - low) * width), dtype)] * many,
        in_specs=[
            smem(),
            pl.BlockSpec(held.shape, lambda i: (0, 0, 0)),
            pl.BlockSpec((width, d_width), lambda i: (i + low, 0)),
        ]
        + [anywhere()] * len(gathered)
        + [columns] * len(given),
        out_specs=[columns] * many,
        scratch_shapes=[
            pltpu.VMEM((many * chunk, d_width), gathered[0].dtype),
            pltpu.VMEM((many * chunk, width), jnp.float32),
            pltpu.SemaphoreType.DMA,
        ],
        compiler_params=params(),
        cost_estimate=pl.CostEstimate(
            flops=2 * many * chunk * d_width * (high - low) * width,
            bytes_accessed=2 * d_width * (high - low) * width,
            transcendentals=0,
        ),
        name="partial",
    )(meta, held, weight, *gathered, *given)


def last_kernel(with_out, own, right, left, *refs):
    out = refs[-1]
    total = own[...] + right[...].astype(jnp.float32) + left[...].astype(jnp.float32)
    out[...] = total.astype(out.dtype)


def last_call(low, high, width, own, right, left, out, shape):
    chunk = own.shape[0]
    columns = pl.BlockSpec((chunk, width), lambda i: (0, i))
    return pl.pallas_call(
        functools.partial(last_kernel, out is not None),
        grid=(high - low,),
        out_shape=shape,
        in_specs=[columns] * 3 + ([] if out is None else [anywhere()]),
        out_specs=pl.BlockSpec((chunk, width), lambda i: (0, i + low)),
        input_output_aliases={} if out is None else {3: 0},
        compiler_params=params(),
        name="last_sum",
    )(own, right, left, *([] if out is None else [out]))


def grad_kernel(spans, slots, block, d_blocks, meta, *refs):
    places = lax.axis_size("tensor") * lax.axis_size("dp")
    hidden, refs = refs[:spans], refs[spans:]
    gathered, refs = refs[:places], refs[places:]
    outs, (cols,) = refs[:spans], refs[spans:]
    me = lax.axis_index("seq")
    tensors, cores = lax.axis_size("tensor"), lax.axis_size("dp")
    count = live_count(meta, me, slots)
    before = rank_before(meta, me, spans, slots)
    for s in range(spans):
        cols[s] = hidden[s][...]
    for s in range(spans):
        slot = wrap(lax.rem(me + s, spans) - lax.rem(before, spans), spans)
        outs[s][...] = jnp.zeros_like(outs[s])

        @pl.when(slot < count)
        def _():
            d_start = pl.multiple_of(lax.rem(meta[me, slot], d_blocks) * block, block)
            total = jnp.zeros((block, block), jnp.float32)
            for p in range(places):
                t_place = lax.rem(lax.axis_index("tensor") + p // cores, tensors)
                d_place = lax.rem(lax.axis_index("dp") + p % cores, cores)
                chunk = t_place * cores + d_place
                total = total + lax.dot_general(
                    cols[wrap(me - chunk, spans), slot],
                    gathered[p][:, pl.ds(d_start, block)],
                    TN,
                    preferred_element_type=jnp.float32,
                )
            outs[s][...] = total.astype(outs[s].dtype)


def adam_kernel(spans, slots, meta, *refs):
    arrived, refs = refs[:spans], refs[spans:]
    values, one, two, values_new, one_new, two_new, grads = refs
    me = lax.axis_index("seq")
    for s in range(spans):
        grads[s] = arrived[s][...]
    befores = [rank_before(meta, region, spans, slots) for region in range(spans)]
    total = befores[-1] + live_count(meta, spans - 1, slots)
    for owned in range(slots):
        rank = owned * spans + me
        source = jnp.int32(0)
        for region in range(1, spans):
            source = jnp.where(befores[region] <= rank, region, source)
        live = rank < total
        grad = grads[wrap(me - source, spans)].astype(jnp.float32)
        stored, old_one, old_two = values[owned], one[owned], two[owned]
        new_one = BETA_ONE * old_one + (1.0 - BETA_ONE) * grad
        new_two = BETA_TWO * old_two + (1.0 - BETA_TWO) * grad * grad
        stepped = (
            new_one
            / (1.0 - BETA_ONE**STEP)
            / (jnp.sqrt(new_two / (1.0 - BETA_TWO**STEP)) + EPSILON)
        )
        values_new[owned] = jnp.where(live, stored - RATE * stepped, stored)
        one_new[owned] = jnp.where(live, new_one, old_one)
        two_new[owned] = jnp.where(live, new_two, old_two)


def take_from(array, axis, places):
    size = lax.axis_size(axis)
    return lax.ppermute(array, axis, [((i + places) % size, i) for i in range(size)])


def exchange(pieces):
    return [pieces[0]] + [take_from(pieces[s], "seq", -s) for s in range(1, len(pieces))]


def gather_rows(own):
    gathered = []
    for t_place in range(lax.axis_size("tensor")):
        first = take_from(own, "tensor", t_place) if t_place else own
        gathered.append(first)
        for d_place in range(1, lax.axis_size("dp")):
            gathered.append(take_from(first, "dp", d_place))
    return gathered


def per_device(
    hidden_in, cotangent, down_weight, tile_ids, tile_live, values, moment_one, moment_two
):
    spans = lax.axis_size("seq")
    slots, block = values.shape[2], values.shape[3]
    f_width, d_width = down_weight.shape
    d_blocks, f_blocks = d_width // block, f_width // block
    chunk = hidden_in.shape[0]
    sizes = (spans, slots, block, d_blocks)

    gathered = gather_rows(cotangent)
    meta = jnp.concatenate([tile_ids[0], tile_live[0]], axis=1)
    meta = lax.all_gather(meta, "seq", axis=0, tiled=True)

    value_tile = jax.ShapeDtypeStruct((block, block), jnp.bfloat16)
    hidden_tiles = jax.ShapeDtypeStruct((slots, chunk, block), jnp.bfloat16)
    picked = pl.pallas_call(
        functools.partial(pick_kernel, *sizes),
        out_shape=[value_tile] * spans + [hidden_tiles] * spans,
        in_specs=[smem(), vmem(), vmem()],
        out_specs=[vmem()] * (2 * spans),
        compiler_params=params(),
        name="pick",
    )(meta, values[0, 0], hidden_in)
    held = jnp.stack(exchange(picked[:spans]))
    hidden_cols = exchange(picked[spans:])

    group = max(size for size in range(1, 3) if f_blocks % size == 0)
    width = group * block
    steps = f_blocks // group
    parts = max(count for count in (1, 2) if steps % count == 0)
    cuts = [steps * part // parts for part in range(parts + 1)]
    ranges = list(zip(cuts[:-1], cuts[1:]))
    half = spans // 2
    up, down = [[] for _ in ranges], [[] for _ in ranges]
    for t in range(1, spans):
        ups = lambda me, t=t: spans - t + me
        downs = lambda me, t=t: me + t - spans
        for part, (low, high) in enumerate(ranges):
            if t <= half:
                either = lambda me, ups=ups, downs=downs: jnp.where(me < half, ups(me), downs(me))
                chunks_of, arrived = [either], [up[part] + down[part]]
            else:
                chunks_of, arrived = [ups, downs], [up[part], down[part]]
            sums = step_call(
                sizes, low, high, width, chunks_of, arrived, meta, held, down_weight, gathered,
                jnp.bfloat16,
            )
            up[part] = [lax.ppermute(sums[0], "seq", [(z, z + 1) for z in range(t)])]
            down[part] = [
                lax.ppermute(sums[-1], "seq", [(spans - 1 - z, spans - 2 - z) for z in range(t)])
            ]

    send = pl.pallas_call(
        functools.partial(grad_kernel, *sizes),
        out_shape=[value_tile] * spans,
        in_specs=[smem()] + [vmem()] * (spans + len(gathered)),
        out_specs=[vmem()] * spans,
        scratch_shapes=[pltpu.VMEM((spans, slots, chunk, block), jnp.bfloat16)],
        compiler_params=params(),
        name="tile_grad",
    )(meta, *hidden_cols, *gathered)
    grads = exchange(send)
    tile = jax.ShapeDtypeStruct((slots, block, block), jnp.float32)
    new = pl.pallas_call(
        functools.partial(adam_kernel, spans, slots),
        out_shape=(tile, tile, tile),
        in_specs=[smem()] + [vmem()] * (spans + 3),
        out_specs=(vmem(), vmem(), vmem()),
        scratch_shapes=[pltpu.VMEM((spans, block, block), jnp.bfloat16)],
        compiler_params=params(),
        name="adam",
    )(meta, *grads, values[0, 0], moment_one[0, 0], moment_two[0, 0])

    hidden_grad = None
    shape = jax.ShapeDtypeStruct((chunk, f_width), jnp.bfloat16)
    for part, (low, high) in enumerate(ranges):
        (own,) = step_call(
            sizes, low, high, width, [lambda me: me], [[]], meta, held, down_weight, gathered,
            jnp.float32,
        )
        hidden_grad = last_call(
            low, high, width, own, up[part][0], down[part][0], hidden_grad, shape
        )
    return (hidden_grad,) + tuple(array[None, None] for array in new)


def solution(mesh):
    shards = P(("groups", "seq"), ("tensor", "dp"))
    tiles = P(("groups", "seq"), ("tensor", "dp"), None, None, None)
    lists = P(("groups", "seq"), ("tensor", "dp"), None)
    return jax.shard_map(
        per_device,
        mesh=mesh,
        in_specs=(
            shards,
            P(("groups", "tensor", "dp"), "seq"),
            P(("tensor", "dp"), "seq"),
            lists,
            lists,
            tiles,
            tiles,
            tiles,
        ),
        out_specs=(shards, tiles, tiles, tiles),
        check_vma=False,
    )
```

time: 144 us -> 155 us (1.076); the launches traced: 144 us -> 153 us
  blocking collectives: 63.2 us -> 11.3 us
  Pallas kernels: 17.6 us -> 68.4 us
  starting transfers between devices: 0.12 us -> 41 us
  between operations: 13.8 us -> 0.97 us
  waiting for transfers between devices: 40 us -> 27.4 us
  local copies, waits for them, and re-layouts: 6.23 us -> 3.18 us
  other arithmetic: 2.88 us -> 0.77 us
    pallas_call x4 -> x12, Pallas kernels: 15.9 us -> 66.8 us  [the longest x8 59.7 us: step_call(): pl.pallas_call(functools.partial(step_kernel, sizes, low, chunks_of, [len...]
    all_to_all x3 -> x0, blocking collectives: 50.7 us -> none  [exchange(): return lax.all_to_all(array, 'seq', 0, 0, tiled=True)]
    ppermute x0 -> x24, starting transfers between devices: none -> 41 us  [the longest x6 18.5 us: per_device(): up[part] = [lax.ppermute(sums[0], 'seq', [(z, z + 1) for z in range(t)])]]
    reduce_scatter x2 -> x0, waiting for transfers between devices: 36.8 us -> none  [per_device(): lax.psum_scatter(piece, 'seq', scatter_dimension=0, tiled=True)]
    ppermute x0 -> x24, waiting for transfers between devices: none -> 27.4 us  [the longest x12 27.3 us: take_from(): lax.ppermute(array, axis, [((i + places) % size, i) for i in range(size)])]
    unnamed x18 -> x12, local copies, waits for them, and re-layouts: 6.23 us -> 3.18 us
    all_gather x1 -> x0, waiting for transfers between devices: 2.47 us -> none  [per_device(): rows = lax.all_gather(cotangent, ('tensor', 'dp'), axis=0, tiled=True)]
    concatenate x1 -> x0, other arithmetic: 2.14 us -> none  [per_device(): hidden_grad = jnp.concatenate(pieces, axis=1)]
  transfers between devices with their start and end apart: 3 -> 24, of which waited for: 2 -> 5; matrix products, arithmetic and copies ran while one was open for 1% -> 0% of each run, Pallas kernels for 8% -> 38%
where the time goes in v2:
time: 155 us; the launch traced here: 153 us
  Pallas kernels  68.4 us (44%)
  starting transfers between devices  41 us (26%)
  waiting for transfers between devices  27.4 us (18%)
  blocking collectives  11.3 us (7%)
  local copies, waits for them, and re-layouts  3.18 us (2%)
    pallas_call x8, Pallas kernels, step_call(): pl.pallas_call(functools.partial(step_kernel, sizes, low, chunks_of, [len...  59.7 us
    ppermute x12, waiting for transfers between devices, take_from(): lax.ppermute(array, axis, [((i + places) % size, i) for i in range(size)])  27.3 us
    ppermute x6, starting transfers between devices, per_device(): up[part] = [lax.ppermute(sums[0], 'seq', [(z, z + 1) for z in range(t)])]  18.5 us
    ppermute x12, starting transfers between devices, take_from(): lax.ppermute(array, axis, [((i + places) % size, i) for i in range(size)])  17.2 us
    all_gather x1, blocking collectives, per_device(): meta = lax.all_gather(meta, 'seq', axis=0, tiled=True)  11.3 us
    pallas_call x2, Pallas kernels, last_call(): pl.pallas_call(functools.partial(last_kernel, out is not None), grid=(hig...  5.44 us
    ppermute x6, starting transfers between devices, per_device(): lax.ppermute(sums[-1], 'seq', [(spans - 1 - z, spans - 2 - z) for z in ra...  5.34 us
    unnamed x12, local copies, waits for them, and re-layouts  3.18 us
  transfers between devices with their start and end apart: 24, of which 5 were waited for; matrix products, arithmetic and copies ran while one was open for 0% of the time, Pallas kernels for 38%

profile of v2, /device:TPU:0, one launch (start us, length us, event | category | flops | bytes accessed | tf_op | source)
XLA Modules:
  0.0 153.1 jit_solution(1885168696234529146)
XLA Ops:
  0.6 3.0 %collective-permute-start.4 = (bf16[128,2048]{1,0:T(8,128)(2,1)}, bf16[128,2048]{1,0:T(8,128)(2,1)S(1)}, u32[]{:S(2)}, u32[]{:S(2)}) collective-permute-start(bf16[128,2048]{1,0:T(8,128)(2,1)} %refs_4_.1), channel_id=1, source_target_pairs={{2,0},{0,2},{3,1},{1,3},{6,4},{4,6},{7,5},{5,7},{10,8},{8,10},{11,... | collective-permute-start | bytes 1572872 | tf_op jit(solution)/shard_map/ppermute | solution.py:243
  3.6 12.1 %collective-permute-done.4.refs_2_.refs_6_ = bf16[128,2048]{1,0:T(8,128)(2,1)S(1)} collective-permute-done((bf16[128,2048]{1,0:T(8,128)(2,1)}, bf16[128,2048]{1,0:T(8,128)(2,1)S(1)}, u32[]{:S(2)}, u32[]{:S(2)}) %collective-permute-start.4) | collective-permute-done | bytes 524320 | tf_op jit(solution)/shard_map/ppermute | solution.py:243
  16.5 11.3 %all-gather = s32[4,1,8]{2,1,0:T(1,128)S(1)} all-gather(s32[1,1,8]{2,1,0:T(1,128)S(1)} %add_bitcast_fusion), channel_id=1, replica_groups=mesh['groups'=2,'seq'=4,'tensor'=2,'dp'=2] {'seq'}, dimensions={0}, use_global_device_ids=true | all-gather | bytes 160 | tf_op jit(solution)/shard_map/all_gather | solution.py:272
  31.2 3.5 %collective-permute-start.2 = (bf16[128,128]{1,0:T(8,128)(2,1)S(1)}, bf16[128,128]{1,0:T(8,128)(2,1)S(1)}, u32[]{:S(2)}, u32[]{:S(2)}) collective-permute-start(bf16[128,128]{1,0:T(8,128)(2,1)S(1)} %get-tuple-element.26), channel_id=1, source_target_pairs={{4,0},{8,4},{12,8},{0,12},{5,1},{9,5},{13,9},{1,13},{6,2},{10,6},{... | collective-permute-start | bytes 98312 | tf_op jit(solution)/shard_map/ppermute | solution.py:243
  34.6 1.9 %collective-permute-done = bf16[128,128]{1,0:T(8,128)(2,1)S(1)} collective-permute-done((bf16[128,128]{1,0:T(8,128)(2,1)S(1)}, bf16[128,128]{1,0:T(8,128)(2,1)S(1)}, u32[]{:S(2)}, u32[]{:S(2)}) %collective-permute-start) | collective-permute-done | bytes 32800 | tf_op jit(solution)/shard_map/ppermute | solution.py:243
  38.2 7.3 %partial.13 = bf16[128,1792]{1,0:T(8,128)(2,1)S(1)} custom-call(s32[4,8]{1,0:T(4,128)S(1)} %bitcast.18, bf16[4,128,128]{2,1,0:T(8,128)(2,1)S(1)} %pad_maximum_fusion.held, bf16[3584,2048]{1,0:T(8,128)(2,1)} %weight.15, bf16[128,2048]{1,0:T(8,128)(2,1)S(1)} %copy-done, bf16[128,2048]{1,0:T(8,128)(2,1)S(1)} %collective-permute-done.3.refs_1_.refs_5_, ...), custom_call_target="tpu_custom_call" | custom-call | flops 939524096 | bytes 7340032 | tf_op jit(solution)/shard_map/partial/pallas_call | solution.py:133
  45.5 4.0 %collective-permute-start.12 = (bf16[128,1792]{1,0:T(8,128)(2,1)S(1)}, bf16[128,1792]{1,0:T(8,128)(2,1)S(1)}, u32[]{:S(2)}, u32[]{:S(2)}) collective-permute-start(bf16[128,1792]{1,0:T(8,128)(2,1)S(1)} %partial.13), channel_id=1, source_target_pairs={{0,4},{1,5},{2,6},{3,7},{16,20},{17,21},{18,22},{19,23}} | collective-permute-start | bytes 1376264 | tf_op jit(solution)/shard_map/ppermute | solution.py:308
  50.2 7.5 %partial.9 = bf16[128,1792]{1,0:T(8,128)(2,1)S(1)} custom-call(s32[4,8]{1,0:T(4,128)S(1)} %bitcast.19, bf16[4,128,128]{2,1,0:T(8,128)(2,1)S(1)} %pad_maximum_fusion.held, bf16[3584,2048]{1,0:T(8,128)(2,1)} %weight.15, bf16[128,2048]{1,0:T(8,128)(2,1)S(1)} %copy-done, bf16[128,2048]{1,0:T(8,128)(2,1)S(1)} %collective-permute-done.3.refs_1_.refs_5_, ...), custom_call_target="tpu_custom_call" | custom-call | flops 939524096 | bytes 7340032 | tf_op jit(solution)/shard_map/partial/pallas_call | solution.py:133
  59.7 7.4 %partial.14 = bf16[128,1792]{1,0:T(8,128)(2,1)S(1)} custom-call(s32[4,8]{1,0:T(4,128)S(1)} %bitcast.20, bf16[4,128,128]{2,1,0:T(8,128)(2,1)S(1)} %pad_maximum_fusion.held, bf16[3584,2048]{1,0:T(8,128)(2,1)} %weight.15, bf16[128,2048]{1,0:T(8,128)(2,1)S(1)} %copy-done, bf16[128,2048]{1,0:T(8,128)(2,1)S(1)} %collective-permute-done.3.refs_1_.refs_5_, ...), custom_call_target="tpu_custom_call" | custom-call | flops 939524096 | bytes 7340032 | tf_op jit(solution)/shard_map/partial/pallas_call | solution.py:133
  69.2 7.5 %partial.10 = bf16[128,1792]{1,0:T(8,128)(2,1)S(1)} custom-call(s32[4,8]{1,0:T(4,128)S(1)} %bitcast.21, bf16[4,128,128]{2,1,0:T(8,128)(2,1)S(1)} %pad_maximum_fusion.held, bf16[3584,2048]{1,0:T(8,128)(2,1)} %weight.15, bf16[128,2048]{1,0:T(8,128)(2,1)S(1)} %copy-done, bf16[128,2048]{1,0:T(8,128)(2,1)S(1)} %collective-permute-done.3.refs_1_.refs_5_, ...), custom_call_target="tpu_custom_call" | custom-call | flops 939524096 | bytes 7340032 | tf_op jit(solution)/shard_map/partial/pallas_call | solution.py:133
  76.7 3.2 %collective-permute-start.8 = (bf16[128,1792]{1,0:T(8,128)(2,1)S(1)}, bf16[128,1792]{1,0:T(8,128)(2,1)S(1)}, u32[]{:S(2)}, u32[]{:S(2)}) collective-permute-start(bf16[128,1792]{1,0:T(8,128)(2,1)S(1)} %partial.10), channel_id=1, source_target_pairs={{0,4},{4,8},{1,5},{5,9},{2,6},{6,10},{3,7},{7,11},{16,20},{20,24},... | collective-permute-start | bytes 1376264 | tf_op jit(solution)/shard_map/ppermute | solution.py:308
  80.7 3.2 %collective-permute-start.18 = (bf16[4,128,128]{2,1,0:T(8,128)(2,1)S(1)}, bf16[4,128,128]{2,1,0:T(8,128)(2,1)S(1)}, u32[]{:S(2)}, u32[]{:S(2)}) collective-permute-start(bf16[4,128,128]{2,1,0:T(8,128)(2,1)S(1)} %get-tuple-element.32), channel_id=1, source_target_pairs={{12,0},{0,4},{4,8},{8,12},{13,1},{1,5},{5,9},{9,13},{14,2},{2,6},{... | collective-permute-start | bytes 393224 | tf_op jit(solution)/shard_map/ppermute | solution.py:243
  83.9 2.2 %collective-permute-start.19 = (bf16[4,128,128]{2,1,0:T(8,128)(2,1)S(1)}, bf16[4,128,128]{2,1,0:T(8,128)(2,1)S(1)}, u32[]{:S(2)}, u32[]{:S(2)}) collective-permute-start(bf16[4,128,128]{2,1,0:T(8,128)(2,1)S(1)} %get-tuple-element.33), channel_id=1, source_target_pairs={{8,0},{12,4},{0,8},{4,12},{9,1},{13,5},{1,9},{5,13},{10,2},{14,6},... | collective-permute-start | bytes 393224 | tf_op jit(solution)/shard_map/ppermute | solution.py:243
  86.0 7.4 %partial.15 = (bf16[128,1792]{1,0:T(8,128)(2,1)S(1)}, bf16[128,1792]{1,0:T(8,128)(2,1)S(1)}) custom-call(s32[4,8]{1,0:T(4,128)S(1)} %bitcast.22, bf16[4,128,128]{2,1,0:T(8,128)(2,1)S(1)} %pad_maximum_fusion.held, bf16[3584,2048]{1,0:T(8,128)(2,1)} %weight.15, bf16[128,2048]{1,0:T(8,128)(2,1)S(1)} %copy-done, ...), custom_call_target="tpu_custom_call" | custom-call | flops 1879048192 | bytes 7340032 | tf_op jit(solution)/shard_map/partial/pallas_call | solution.py:133
  93.5 2.4 %collective-permute-start.16 = (bf16[128,1792]{1,0:T(8,128)(2,1)S(1)}, bf16[128,1792]{1,0:T(8,128)(2,1)S(1)}, u32[]{:S(2)}, u32[]{:S(2)}) collective-permute-start(bf16[128,1792]{1,0:T(8,128)(2,1)S(1)} %get-tuple-element.29), channel_id=1, source_target_pairs={{0,4},{4,8},{8,12},{1,5},{5,9},{9,13},{2,6},{6,10},{10,14},{3,7},{... | collective-permute-start | bytes 1376264 | tf_op jit(solution)/shard_map/ppermute | solution.py:308
  97.3 7.6 %partial.11 = (bf16[128,1792]{1,0:T(8,128)(2,1)S(1)}, bf16[128,1792]{1,0:T(8,128)(2,1)S(1)}) custom-call(s32[4,8]{1,0:T(4,128)S(1)} %bitcast.23, bf16[4,128,128]{2,1,0:T(8,128)(2,1)S(1)} %pad_maximum_fusion.held, bf16[3584,2048]{1,0:T(8,128)(2,1)} %weight.15, bf16[128,2048]{1,0:T(8,128)(2,1)S(1)} %copy-done, ...), custom_call_target="tpu_custom_call" | custom-call | flops 1879048192 | bytes 7340032 | tf_op jit(solution)/shard_map/partial/pallas_call | solution.py:133
  104.9 6.2 %collective-permute-start.10 = (bf16[128,1792]{1,0:T(8,128)(2,1)S(1)}, bf16[128,1792]{1,0:T(8,128)(2,1)S(1)}, u32[]{:S(2)}, u32[]{:S(2)}) collective-permute-start(bf16[128,1792]{1,0:T(8,128)(2,1)S(1)} %get-tuple-element.27), channel_id=1, source_target_pairs={{0,4},{4,8},{8,12},{1,5},{5,9},{9,13},{2,6},{6,10},{10,14},{3,7},{... | collective-permute-start | bytes 1376264 | tf_op jit(solution)/shard_map/ppermute | solution.py:308
  112.4 3.3 %collective-permute-start.20 = (bf16[4,128,128]{2,1,0:T(8,128)(2,1)S(1)}, bf16[4,128,128]{2,1,0:T(8,128)(2,1)S(1)}, u32[]{:S(2)}, u32[]{:S(2)}) collective-permute-start(bf16[4,128,128]{2,1,0:T(8,128)(2,1)S(1)} %get-tuple-element.34), channel_id=1, source_target_pairs={{4,0},{8,4},{12,8},{0,12},{5,1},{9,5},{13,9},{1,13},{6,2},{10,6},{... | collective-permute-start | bytes 393224 | tf_op jit(solution)/shard_map/ppermute | solution.py:243
  115.7 7.6 %collective-permute-done.20.refs_3_ = bf16[4,128,128]{2,1,0:T(8,128)(2,1)S(1)} collective-permute-done((bf16[4,128,128]{2,1,0:T(8,128)(2,1)S(1)}, bf16[4,128,128]{2,1,0:T(8,128)(2,1)S(1)}, u32[]{:S(2)}, u32[]{:S(2)}) %collective-permute-start.20) | collective-permute-done | bytes 131104 | tf_op jit(solution)/shard_map/ppermute | solution.py:243
  124.7 5.2 %collective-permute-done.21.refs_1_ = bf16[128,128]{1,0:T(8,128)(2,1)S(1)} collective-permute-done((bf16[128,128]{1,0:T(8,128)(2,1)S(1)}, bf16[128,128]{1,0:T(8,128)(2,1)S(1)}, u32[]{:S(2)}, u32[]{:S(2)}) %collective-permute-start.21) | collective-permute-done | bytes 32800 | tf_op jit(solution)/shard_map/ppermute | solution.py:243
  129.9 7.4 %partial.12.own = f32[128,1792]{1,0:T(8,128)S(1)} custom-call(s32[4,8]{1,0:T(4,128)S(1)} %bitcast.25, bf16[4,128,128]{2,1,0:T(8,128)(2,1)S(1)} %pad_maximum_fusion.held, bf16[3584,2048]{1,0:T(8,128)(2,1)} %weight.15, bf16[128,2048]{1,0:T(8,128)(2,1)S(1)} %copy-done, bf16[128,2048]{1,0:T(8,128)(2,1)S(1)} %collective-permute-done.3.refs_1_.refs_5_, ...), custom_call_target="tpu_custom_call" | custom-call | flops 939524096 | bytes 7340032 | tf_op jit(solution)/shard_map/partial/pallas_call | solution.py:133
  138.5 7.5 %partial.8.own = f32[128,1792]{1,0:T(8,128)S(1)} custom-call(s32[4,8]{1,0:T(4,128)S(1)} %bitcast.26, bf16[4,128,128]{2,1,0:T(8,128)(2,1)S(1)} %pad_maximum_fusion.held, bf16[3584,2048]{1,0:T(8,128)(2,1)} %weight.15, bf16[128,2048]{1,0:T(8,128)(2,1)S(1)} %copy-done, bf16[128,2048]{1,0:T(8,128)(2,1)S(1)} %collective-permute-done.3.refs_1_.refs_5_, ...), custom_call_target="tpu_custom_call" | custom-call | flops 939524096 | bytes 7340032 | tf_op jit(solution)/shard_map/partial/pallas_call | solution.py:133
  147.6 2.7 %last_sum.2.refs_0_ = bf16[128,3584]{1,0:T(8,128)(2,1)} custom-call(f32[128,1792]{1,0:T(8,128)S(1)} %partial.12.own, bf16[128,1792]{1,0:T(8,128)(2,1)S(1)} %collective-permute-done.16.right, bf16[128,1792]{1,0:T(8,128)(2,1)S(1)} %collective-permute-done.17.left), custom_call_target="tpu_custom_call" | custom-call | tf_op jit(solution)/shard_map/last_sum/pallas_call | solution.py:169
  150.4 2.7 %last_sum.3 = bf16[128,3584]{1,0:T(8,128)(2,1)} custom-call(f32[128,1792]{1,0:T(8,128)S(1)} %partial.8.own, bf16[128,1792]{1,0:T(8,128)(2,1)S(1)} %collective-permute-done.10.right, bf16[128,1792]{1,0:T(8,128)(2,1)S(1)} %collective-permute-done.11.left, bf16[128,3584]{1,0:T(8,128)(2,1)} %last_sum.2.refs_0_), custom_call_target="tpu_custom_call", output_to_operand_aliasing={{}: (3, {})} | custom-call | tf_op jit(solution)/shard_map/last_sum/pallas_call | solution.py:169
  (52 shorter events, 17.9 us)
Async XLA Ops:
  0.6 15.1 %collective-permute-start.4 = (bf16[128,2048]{1,0:T(8,128)(2,1)}, bf16[128,2048]{1,0:T(8,128)(2,1)S(1)}, u32[]{:S(2)}, u32[]{:S(2)}) collective-permute-start(bf16[128,2048]{1,0:T(8,128)(2,1)} %refs_4_.1), channel_id=1, source_target_pairs={{2,0},{0,2},{3,1},{1,3},{6,4},{4,6},{7,5},{5,7},{10,8},{8,10},{11,... | collective-permute-start | bytes 1572872 | tf_op jit(solution)/shard_map/ppermute | solution.py:243
  3.6 33.5 %collective-permute-start.3 = (bf16[128,2048]{1,0:T(8,128)(2,1)}, bf16[128,2048]{1,0:T(8,128)(2,1)S(1)}, u32[]{:S(2)}, u32[]{:S(2)}) collective-permute-start(bf16[128,2048]{1,0:T(8,128)(2,1)} %refs_4_.1), channel_id=1, source_target_pairs={{1,0},{0,1},{3,2},{2,3},{5,4},{4,5},{7,6},{6,7},{9,8},{8,9},{11,10... | collective-permute-start | bytes 1572872 | tf_op jit(solution)/shard_map/ppermute | solution.py:243
  15.8 21.4 %collective-permute-start.5 = (bf16[128,2048]{1,0:T(8,128)(2,1)S(1)}, bf16[128,2048]{1,0:T(8,128)(2,1)S(1)}, u32[]{:S(2)}, u32[]{:S(2)}) collective-permute-start(bf16[128,2048]{1,0:T(8,128)(2,1)S(1)} %collective-permute-done.4.refs_2_.refs_6_), channel_id=1, source_target_pairs={{1,0},{0,1},{3,2},{2,3},{5,4},{4,5},{7,6},{6,7},{9,8},{8,9},{11,10... | collective-permute-start | bytes 1572872 | tf_op jit(solution)/shard_map/ppermute | solution.py:243
  30.8 5.8 %collective-permute-start = (bf16[128,128]{1,0:T(8,128)(2,1)S(1)}, bf16[128,128]{1,0:T(8,128)(2,1)S(1)}, u32[]{:S(2)}, u32[]{:S(2)}) collective-permute-start(bf16[128,128]{1,0:T(8,128)(2,1)S(1)} %get-tuple-element.24), channel_id=1, source_target_pairs={{12,0},{0,4},{4,8},{8,12},{13,1},{1,5},{5,9},{9,13},{14,2},{2,6},{... | collective-permute-start | bytes 98312 | tf_op jit(solution)/shard_map/ppermute | solution.py:243
  30.8 5.7 %collective-permute-start.1 = (bf16[128,128]{1,0:T(8,128)(2,1)S(1)}, bf16[128,128]{1,0:T(8,128)(2,1)S(1)}, u32[]{:S(2)}, u32[]{:S(2)}) collective-permute-start(bf16[128,128]{1,0:T(8,128)(2,1)S(1)} %get-tuple-element.25), channel_id=1, source_target_pairs={{8,0},{12,4},{0,8},{4,12},{9,1},{13,5},{1,9},{5,13},{10,2},{14,6},... | collective-permute-start | bytes 98312 | tf_op jit(solution)/shard_map/ppermute | solution.py:243
  31.2 5.9 %collective-permute-start.2 = (bf16[128,128]{1,0:T(8,128)(2,1)S(1)}, bf16[128,128]{1,0:T(8,128)(2,1)S(1)}, u32[]{:S(2)}, u32[]{:S(2)}) collective-permute-start(bf16[128,128]{1,0:T(8,128)(2,1)S(1)} %get-tuple-element.26), channel_id=1, source_target_pairs={{4,0},{8,4},{12,8},{0,12},{5,1},{9,5},{13,9},{1,13},{6,2},{10,6},{... | collective-permute-start | bytes 98312 | tf_op jit(solution)/shard_map/ppermute | solution.py:243
  45.5 14.2 %collective-permute-start.12 = (bf16[128,1792]{1,0:T(8,128)(2,1)S(1)}, bf16[128,1792]{1,0:T(8,128)(2,1)S(1)}, u32[]{:S(2)}, u32[]{:S(2)}) collective-permute-start(bf16[128,1792]{1,0:T(8,128)(2,1)S(1)} %partial.13), channel_id=1, source_target_pairs={{0,4},{1,5},{2,6},{3,7},{16,20},{17,21},{18,22},{19,23}} | collective-permute-start | bytes 1376264 | tf_op jit(solution)/shard_map/ppermute | solution.py:308
  49.5 10.3 %collective-permute-start.13 = (bf16[128,1792]{1,0:T(8,128)(2,1)S(1)}, bf16[128,1792]{1,0:T(8,128)(2,1)S(1)}, u32[]{:S(2)}, u32[]{:S(2)}) collective-permute-start(bf16[128,1792]{1,0:T(8,128)(2,1)S(1)} %partial.13), channel_id=1, source_target_pairs={{12,8},{13,9},{14,10},{15,11},{28,24},{29,25},{30,26},{31,27}} | collective-permute-start | bytes 1376264 | tf_op jit(solution)/shard_map/ppermute | solution.py:310
  57.7 11.5 %collective-permute-start.6 = (bf16[128,1792]{1,0:T(8,128)(2,1)S(1)}, bf16[128,1792]{1,0:T(8,128)(2,1)S(1)}, u32[]{:S(2)}, u32[]{:S(2)}) collective-permute-start(bf16[128,1792]{1,0:T(8,128)(2,1)S(1)} %partial.9), channel_id=1, source_target_pairs={{0,4},{1,5},{2,6},{3,7},{16,20},{17,21},{18,22},{19,23}} | collective-permute-start | bytes 1376264 | tf_op jit(solution)/shard_map/ppermute | solution.py:308
  59.0 10.2 %collective-permute-start.7 = (bf16[128,1792]{1,0:T(8,128)(2,1)S(1)}, bf16[128,1792]{1,0:T(8,128)(2,1)S(1)}, u32[]{:S(2)}, u32[]{:S(2)}) collective-permute-start(bf16[128,1792]{1,0:T(8,128)(2,1)S(1)} %partial.9), channel_id=1, source_target_pairs={{12,8},{13,9},{14,10},{15,11},{28,24},{29,25},{30,26},{31,27}} | collective-permute-start | bytes 1376264 | tf_op jit(solution)/shard_map/ppermute | solution.py:310
  67.2 16.7 %collective-permute-start.14 = (bf16[128,1792]{1,0:T(8,128)(2,1)S(1)}, bf16[128,1792]{1,0:T(8,128)(2,1)S(1)}, u32[]{:S(2)}, u32[]{:S(2)}) collective-permute-start(bf16[128,1792]{1,0:T(8,128)(2,1)S(1)} %partial.14), channel_id=1, source_target_pairs={{0,4},{4,8},{1,5},{5,9},{2,6},{6,10},{3,7},{7,11},{16,20},{20,24},... | collective-permute-start | bytes 1376264 | tf_op jit(solution)/shard_map/ppermute | solution.py:308
  68.5 17.6 %collective-permute-start.15 = (bf16[128,1792]{1,0:T(8,128)(2,1)S(1)}, bf16[128,1792]{1,0:T(8,128)(2,1)S(1)}, u32[]{:S(2)}, u32[]{:S(2)}) collective-permute-start(bf16[128,1792]{1,0:T(8,128)(2,1)S(1)} %partial.14), channel_id=1, source_target_pairs={{12,8},{8,4},{13,9},{9,5},{14,10},{10,6},{15,11},{11,7},{28,24},{2... | collective-permute-start | bytes 1376264 | tf_op jit(solution)/shard_map/ppermute | solution.py:310
  76.7 19.2 %collective-permute-start.8 = (bf16[128,1792]{1,0:T(8,128)(2,1)S(1)}, bf16[128,1792]{1,0:T(8,128)(2,1)S(1)}, u32[]{:S(2)}, u32[]{:S(2)}) collective-permute-start(bf16[128,1792]{1,0:T(8,128)(2,1)S(1)} %partial.10), channel_id=1, source_target_pairs={{0,4},{4,8},{1,5},{5,9},{2,6},{6,10},{3,7},{7,11},{16,20},{20,24},... | collective-permute-start | bytes 1376264 | tf_op jit(solution)/shard_map/ppermute | solution.py:308
  80.0 17.2 %collective-permute-start.9 = (bf16[128,1792]{1,0:T(8,128)(2,1)S(1)}, bf16[128,1792]{1,0:T(8,128)(2,1)S(1)}, u32[]{:S(2)}, u32[]{:S(2)}) collective-permute-start(bf16[128,1792]{1,0:T(8,128)(2,1)S(1)} %partial.10), channel_id=1, source_target_pairs={{12,8},{8,4},{13,9},{9,5},{14,10},{10,6},{15,11},{11,7},{28,24},{2... | collective-permute-start | bytes 1376264 | tf_op jit(solution)/shard_map/ppermute | solution.py:310
  80.7 30.4 %collective-permute-start.18 = (bf16[4,128,128]{2,1,0:T(8,128)(2,1)S(1)}, bf16[4,128,128]{2,1,0:T(8,128)(2,1)S(1)}, u32[]{:S(2)}, u32[]{:S(2)}) collective-permute-start(bf16[4,128,128]{2,1,0:T(8,128)(2,1)S(1)} %get-tuple-element.32), channel_id=1, source_target_pairs={{12,0},{0,4},{4,8},{8,12},{13,1},{1,5},{5,9},{9,13},{14,2},{2,6},{... | collective-permute-start | bytes 393224 | tf_op jit(solution)/shard_map/ppermute | solution.py:243
  83.9 28.6 %collective-permute-start.19 = (bf16[4,128,128]{2,1,0:T(8,128)(2,1)S(1)}, bf16[4,128,128]{2,1,0:T(8,128)(2,1)S(1)}, u32[]{:S(2)}, u32[]{:S(2)}) collective-permute-start(bf16[4,128,128]{2,1,0:T(8,128)(2,1)S(1)} %get-tuple-element.33), channel_id=1, source_target_pairs={{8,0},{12,4},{0,8},{4,12},{9,1},{13,5},{1,9},{5,13},{10,2},{14,6},... | collective-permute-start | bytes 393224 | tf_op jit(solution)/shard_map/ppermute | solution.py:243
  93.5 54.1 %collective-permute-start.16 = (bf16[128,1792]{1,0:T(8,128)(2,1)S(1)}, bf16[128,1792]{1,0:T(8,128)(2,1)S(1)}, u32[]{:S(2)}, u32[]{:S(2)}) collective-permute-start(bf16[128,1792]{1,0:T(8,128)(2,1)S(1)} %get-tuple-element.29), channel_id=1, source_target_pairs={{0,4},{4,8},{8,12},{1,5},{5,9},{9,13},{2,6},{6,10},{10,14},{3,7},{... | collective-permute-start | bytes 1376264 | tf_op jit(solution)/shard_map/ppermute | solution.py:308
  95.9 51.7 %collective-permute-start.17 = (bf16[128,1792]{1,0:T(8,128)(2,1)S(1)}, bf16[128,1792]{1,0:T(8,128)(2,1)S(1)}, u32[]{:S(2)}, u32[]{:S(2)}) collective-permute-start(bf16[128,1792]{1,0:T(8,128)(2,1)S(1)} %get-tuple-element.30), channel_id=1, source_target_pairs={{12,8},{8,4},{4,0},{13,9},{9,5},{5,1},{14,10},{10,6},{6,2},{15,11}... | collective-permute-start | bytes 1376264 | tf_op jit(solution)/shard_map/ppermute | solution.py:310
  104.9 45.5 %collective-permute-start.10 = (bf16[128,1792]{1,0:T(8,128)(2,1)S(1)}, bf16[128,1792]{1,0:T(8,128)(2,1)S(1)}, u32[]{:S(2)}, u32[]{:S(2)}) collective-permute-start(bf16[128,1792]{1,0:T(8,128)(2,1)S(1)} %get-tuple-element.27), channel_id=1, source_target_pairs={{0,4},{4,8},{8,12},{1,5},{5,9},{9,13},{2,6},{6,10},{10,14},{3,7},{... | collective-permute-start | bytes 1376264 | tf_op jit(solution)/shard_map/ppermute | solution.py:308
  111.1 39.2 %collective-permute-start.11 = (bf16[128,1792]{1,0:T(8,128)(2,1)S(1)}, bf16[128,1792]{1,0:T(8,128)(2,1)S(1)}, u32[]{:S(2)}, u32[]{:S(2)}) collective-permute-start(bf16[128,1792]{1,0:T(8,128)(2,1)S(1)} %get-tuple-element.28), channel_id=1, source_target_pairs={{12,8},{8,4},{4,0},{13,9},{9,5},{5,1},{14,10},{10,6},{6,2},{15,11}... | collective-permute-start | bytes 1376264 | tf_op jit(solution)/shard_map/ppermute | solution.py:310
  112.4 10.8 %collective-permute-start.20 = (bf16[4,128,128]{2,1,0:T(8,128)(2,1)S(1)}, bf16[4,128,128]{2,1,0:T(8,128)(2,1)S(1)}, u32[]{:S(2)}, u32[]{:S(2)}) collective-permute-start(bf16[4,128,128]{2,1,0:T(8,128)(2,1)S(1)} %get-tuple-element.34), channel_id=1, source_target_pairs={{4,0},{8,4},{12,8},{0,12},{5,1},{9,5},{13,9},{1,13},{6,2},{10,6},{... | collective-permute-start | bytes 393224 | tf_op jit(solution)/shard_map/ppermute | solution.py:243
  124.1 5.8 %collective-permute-start.21 = (bf16[128,128]{1,0:T(8,128)(2,1)S(1)}, bf16[128,128]{1,0:T(8,128)(2,1)S(1)}, u32[]{:S(2)}, u32[]{:S(2)}) collective-permute-start(bf16[128,128]{1,0:T(8,128)(2,1)S(1)} %get-tuple-element.36), channel_id=1, source_target_pairs={{12,0},{0,4},{4,8},{8,12},{13,1},{1,5},{5,9},{9,13},{14,2},{2,6},{... | collective-permute-start | bytes 98312 | tf_op jit(solution)/shard_map/ppermute | solution.py:243
  129.9 7.5 %collective-permute-start.22 = (bf16[128,128]{1,0:T(8,128)(2,1)S(1)}, bf16[128,128]{1,0:T(8,128)(2,1)S(1)}, u32[]{:S(2)}, u32[]{:S(2)}) collective-permute-start(bf16[128,128]{1,0:T(8,128)(2,1)S(1)} %get-tuple-element.37), channel_id=1, source_target_pairs={{8,0},{12,4},{0,8},{4,12},{9,1},{13,5},{1,9},{5,13},{10,2},{14,6},... | collective-permute-start | bytes 98312 | tf_op jit(solution)/shard_map/ppermute | solution.py:243
  137.4 8.6 %collective-permute-start.23 = (bf16[128,128]{1,0:T(8,128)(2,1)S(1)}, bf16[128,128]{1,0:T(8,128)(2,1)S(1)}, u32[]{:S(2)}, u32[]{:S(2)}) collective-permute-start(bf16[128,128]{1,0:T(8,128)(2,1)S(1)} %get-tuple-element.38), channel_id=1, source_target_pairs={{4,0},{8,4},{12,8},{0,12},{5,1},{9,5},{13,9},{1,13},{6,2},{10,6},{... | collective-permute-start | bytes 98312 | tf_op jit(solution)/shard_map/ppermute | solution.py:243
  (6 other events, 51.4 us)

commit v3 on v2

v3 whole, which is shorter than its diff:
```python
import functools

import jax
import jax.numpy as jnp
from jax import lax
from jax.experimental import pallas as pl
from jax.experimental.pallas import tpu as pltpu
from jax.sharding import PartitionSpec as P

STEP = 100
BETA_ONE = 0.9
BETA_TWO = 0.999
RATE = 0.01
EPSILON = 1e-08
VMEM_LIMIT = 24 * 1024 * 1024
PARTS = 3
NT = (((1,), (1,)), ((), ()))
TN = (((0,), (0,)), ((), ()))


def vmem():
    return pl.BlockSpec(memory_space=pltpu.VMEM)


def smem():
    return pl.BlockSpec(memory_space=pltpu.SMEM)


def hbm():
    return pl.BlockSpec(memory_space=pltpu.HBM)


def stay(array):
    return pltpu.with_memory_space_constraint(array, pltpu.HBM)


def params():
    return pltpu.CompilerParams(vmem_limit_bytes=VMEM_LIMIT)


def wrap(index, size):
    return lax.rem(index + size, size)


def live_count(meta, region, slots):
    count = meta[region, slots]
    for slot in range(1, slots):
        count = count + meta[region, slots + slot]
    return count


def rank_before(meta, region, spans, slots):
    before = jnp.int32(0)
    for other in range(spans):
        before = before + jnp.where(other < region, live_count(meta, other, slots), 0)
    return before


def pick_kernel(spans, slots, block, d_blocks, meta, values, hidden, *refs):
    value_outs, hidden_outs = refs[:spans], refs[spans : 2 * spans]
    tiles, value_sems, hidden_sems = refs[2 * spans :]
    me = lax.axis_index("seq")
    lives, value_copies, hidden_copies = [], [], []
    for s in range(spans):
        region = lax.rem(me + s, spans)
        before = rank_before(meta, region, spans, slots)
        slot = wrap(me - lax.rem(before, spans), spans)
        lives.append(slot < live_count(meta, region, slots))
        owned = jnp.minimum(lax.div(before + slot, spans), slots - 1)
        copy = pltpu.make_async_copy(values.at[owned], tiles.at[s], value_sems.at[s])
        copy.start()
        value_copies.append(copy)
    for s in range(spans):
        region = lax.rem(me + s, spans)
        for j in range(slots):
            start = pl.multiple_of(lax.div(meta[region, j], d_blocks) * block, block)
            copy = pltpu.make_async_copy(
                hidden.at[:, pl.ds(start, block)], hidden_outs[s].at[j], hidden_sems.at[s, j]
            )
            copy.start()
            hidden_copies.append(copy)
    for s in range(spans):
        value_copies[s].wait()
        tile = tiles[s]
        value_outs[s][...] = jnp.where(lives[s], tile, jnp.zeros_like(tile)).astype(jnp.bfloat16)
    for copy in hidden_copies:
        copy.wait()


def chunk_at(place):
    tensors, cores = lax.axis_size("tensor"), lax.axis_size("dp")
    t_place = lax.rem(lax.axis_index("tensor") + place // cores, tensors)
    d_place = lax.rem(lax.axis_index("dp") + place % cores, cores)
    return t_place * cores + d_place


def matmul_kernel(sizes, low, first_part, meta, held, weight, *refs):
    spans, slots, block, d_blocks = sizes
    step = pl.program_id(0)
    if first_part:
        gathered, (out, first, rows, total, sem) = refs[:spans], refs[spans:]
        chunk = gathered[0].shape[0]

        @pl.when(step == 0)
        def _():
            copy = pltpu.make_async_copy(gathered[0], rows.at[pl.ds(0, chunk)], sem)
            copy.start()
            for p in range(1, spans):
                rows[p * chunk : (p + 1) * chunk] = gathered[p][...]
            copy.wait()

    else:
        rows, out, first, total = refs
        chunk = rows.shape[0] // spans
    me = lax.axis_index("seq")
    width = weight.shape[0]
    here = pl.ds(pl.multiple_of(step * width, width), width)
    total[...] = lax.dot_general(rows[...], weight[...], NT, preferred_element_type=jnp.float32)
    count = live_count(meta, me, slots)
    before = rank_before(meta, me, spans, slots)
    for j in range(slots):
        tile = meta[me, j]
        f_start = lax.div(tile, d_blocks) * block - (low + step) * width

        @pl.when((j < count) & (f_start >= 0) & (f_start < width))
        def _():
            d_start = pl.multiple_of(lax.rem(tile, d_blocks) * block, block)
            place = pl.ds(pl.multiple_of(f_start, block), block)
            owner = lax.rem(before + j, spans)
            total[:, place] += lax.dot_general(
                rows[:, pl.ds(d_start, block)],
                held[wrap(me - owner, spans)],
                NT,
                preferred_element_type=jnp.float32,
            )

    first_chunk = wrap(me - 1, spans)
    for p in range(spans):
        result = total[p * chunk : (p + 1) * chunk].astype(out.dtype)
        out[chunk_at(p), :, here] = result

        @pl.when(chunk_at(p) == first_chunk)
        def _():
            first[:, here] = result


def matmul_call(sizes, low, high, width, meta, held, weight, gathered, rows):
    spans = sizes[0]
    chunk, d_width = gathered[0].shape
    columns = (high - low) * width
    first_part = rows is None
    shapes = [
        jax.ShapeDtypeStruct((spans, chunk, columns), jnp.bfloat16),
        jax.ShapeDtypeStruct((chunk, columns), jnp.bfloat16),
    ]
    scratch = [pltpu.VMEM((spans * chunk, width), jnp.float32)]
    if first_part:
        shapes.append(jax.ShapeDtypeStruct((spans * chunk, d_width), gathered[0].dtype))
        scratch.append(pltpu.SemaphoreType.DMA)
    return pl.pallas_call(
        functools.partial(matmul_kernel, sizes, low, first_part),
        grid=(high - low,),
        out_shape=shapes,
        in_specs=[smem(), vmem(), pl.BlockSpec((width, d_width), lambda i: (i + low, 0))]
        + ([hbm()] + [vmem()] * (spans - 1) if first_part else [vmem()]),
        out_specs=[vmem()] * len(shapes),
        scratch_shapes=scratch,
        compiler_params=params(),
        cost_estimate=pl.CostEstimate(
            flops=2 * spans * chunk * d_width * columns,
            bytes_accessed=2 * d_width * columns,
            transcendentals=0,
        ),
        name="partial",
    )(
        meta,
        held,
        stay(weight),
        *([stay(gathered[0]), *gathered[1:]] if first_part else [rows]),
    )


def add_kernel(t, partials, arrived, out):
    spans = partials.shape[0]
    chunk = wrap(lax.axis_index("seq") - t, spans)
    result = partials[chunk].astype(jnp.float32) + arrived[...].astype(jnp.float32)
    out[...] = result.astype(out.dtype)


def add_call(t, partials, arrived):
    return pl.pallas_call(
        functools.partial(add_kernel, t),
        out_shape=jax.ShapeDtypeStruct(arrived.shape, arrived.dtype),
        in_specs=[vmem(), vmem()],
        out_specs=vmem(),
        compiler_params=params(),
        name="add",
    )(partials, arrived)


def last_kernel(low, partials, arrived, *refs):
    out, total, sem = refs[-3:]
    columns = partials.shape[2]
    result = partials[lax.axis_index("seq")].astype(jnp.float32) + arrived[...].astype(jnp.float32)
    total[...] = result.astype(out.dtype)
    copy = pltpu.make_async_copy(total, out.at[:, pl.ds(low, columns)], sem)
    copy.start()
    copy.wait()


def last_call(low, partials, arrived, out, shape):
    _, chunk, columns = partials.shape
    given = [] if out is None else [out]
    return pl.pallas_call(
        functools.partial(last_kernel, low),
        out_shape=shape,
        in_specs=[vmem()] * 2 + [hbm()] * len(given),
        out_specs=hbm(),
        scratch_shapes=[pltpu.VMEM((chunk, columns), shape.dtype), pltpu.SemaphoreType.DMA],
        input_output_aliases={2: 0} if given else {},
        compiler_params=params(),
        name="last_sum",
    )(partials, arrived, *given)


def grad_kernel(spans, slots, block, d_blocks, meta, *refs):
    places = lax.axis_size("tensor") * lax.axis_size("dp")
    hidden, refs = refs[:spans], refs[spans:]
    gathered, refs = refs[:places], refs[places:]
    outs, (cols,) = refs[:spans], refs[spans:]
    me = lax.axis_index("seq")
    count = live_count(meta, me, slots)
    before = rank_before(meta, me, spans, slots)
    for s in range(spans):
        cols[s] = hidden[s][...]
    for s in range(spans):
        slot = wrap(lax.rem(me + s, spans) - lax.rem(before, spans), spans)
        outs[s][...] = jnp.zeros_like(outs[s])

        @pl.when(slot < count)
        def _():
            d_start = pl.multiple_of(lax.rem(meta[me, slot], d_blocks) * block, block)
            total = jnp.zeros((block, block), jnp.float32)
            for p in range(places):
                chunk = chunk_at(p)
                total = total + lax.dot_general(
                    cols[wrap(me - chunk, spans), slot],
                    gathered[p][:, pl.ds(d_start, block)],
                    TN,
                    preferred_element_type=jnp.float32,
                )
            outs[s][...] = total.astype(outs[s].dtype)


def adam_kernel(spans, slots, meta, *refs):
    arrived, refs = refs[:spans], refs[spans:]
    values, one, two, values_new, one_new, two_new, grads = refs
    me = lax.axis_index("seq")
    for s in range(spans):
        grads[s] = arrived[s][...]
    befores = [rank_before(meta, region, spans, slots) for region in range(spans)]
    total = befores[-1] + live_count(meta, spans - 1, slots)
    for owned in range(slots):
        rank = owned * spans + me
        source = jnp.int32(0)
        for region in range(1, spans):
            source = jnp.where(befores[region] <= rank, region, source)
        live = rank < total
        grad = grads[wrap(me - source, spans)].astype(jnp.float32)
        stored, old_one, old_two = values[owned], one[owned], two[owned]
        new_one = BETA_ONE * old_one + (1.0 - BETA_ONE) * grad
        new_two = BETA_TWO * old_two + (1.0 - BETA_TWO) * grad * grad
        stepped = (
            new_one
            / (1.0 - BETA_ONE**STEP)
            / (jnp.sqrt(new_two / (1.0 - BETA_TWO**STEP)) + EPSILON)
        )
        values_new[owned] = jnp.where(live, stored - RATE * stepped, stored)
        one_new[owned] = jnp.where(live, new_one, old_one)
        two_new[owned] = jnp.where(live, new_two, old_two)


def take_from(array, axis, places):
    size = lax.axis_size(axis)
    return lax.ppermute(array, axis, [((i + places) % size, i) for i in range(size)])


def exchange(pieces):
    return [pieces[0]] + [take_from(pieces[s], "seq", -s) for s in range(1, len(pieces))]


def gather_rows(own, after):
    gathered = []
    for t_place in range(lax.axis_size("tensor")):
        first = take_from(own, "tensor", t_place) if t_place else own
        gathered.append(first)
        if t_place:
            first, _ = lax.optimization_barrier((first, after))
        for d_place in range(1, lax.axis_size("dp")):
            gathered.append(take_from(first, "dp", d_place))
    return gathered


def per_device(
    hidden_in, cotangent, down_weight, tile_ids, tile_live, values, moment_one, moment_two
):
    spans = lax.axis_size("seq")
    slots, block = values.shape[2], values.shape[3]
    f_width, d_width = down_weight.shape
    d_blocks, f_blocks = d_width // block, f_width // block
    chunk = hidden_in.shape[0]
    sizes = (spans, slots, block, d_blocks)

    meta = jnp.concatenate([tile_ids[0], tile_live[0]], axis=1)
    meta = lax.all_gather(meta, "seq", axis=0, tiled=True)

    value_tile = jax.ShapeDtypeStruct((block, block), jnp.bfloat16)
    hidden_tiles = jax.ShapeDtypeStruct((slots, chunk, block), jnp.bfloat16)
    picked = pl.pallas_call(
        functools.partial(pick_kernel, *sizes),
        out_shape=[value_tile] * spans + [hidden_tiles] * spans,
        in_specs=[smem(), hbm(), hbm()],
        out_specs=[vmem()] * (2 * spans),
        scratch_shapes=[
            pltpu.VMEM((spans, block, block), jnp.float32),
            pltpu.SemaphoreType.DMA((spans,)),
            pltpu.SemaphoreType.DMA((spans, slots)),
        ],
        compiler_params=params(),
        name="pick",
    )(meta, stay(values[0, 0]), stay(hidden_in))
    held = jnp.stack(exchange(picked[:spans]))
    hidden_cols = exchange(picked[spans:])
    gathered = gather_rows(cotangent, (held, hidden_cols[1]))

    group = max(size for size in range(1, 5) if f_blocks % size == 0)
    width = group * block
    steps = f_blocks // group
    cuts = [(steps * part + 1) // PARTS for part in range(PARTS + 1)]
    ranges = list(zip(cuts[:-1], cuts[1:]))
    partials, moving, rows = [], [], None
    for low, high in ranges:
        if len(partials) == 1:
            rows, hidden_cols = lax.optimization_barrier((rows, hidden_cols))
        if len(partials) == 2:
            moving[0] = add_call(2, partials[0], moving[0])
            rows, moving[0] = lax.optimization_barrier((rows, moving[0]))
        partial, first, *more = matmul_call(
            sizes, low, high, width, meta, held, down_weight, gathered, rows
        )
        rows = more[0] if more else rows
        partials.append(partial)
        moving.append(take_from(first, "seq", -1))
    for t in range(2, spans):
        for part in range(len(ranges)):
            if (t, part) != (2, 0):
                moving[part] = add_call(t, partials[part], moving[part])
            moving[part] = take_from(moving[part], "seq", -1)

    send = pl.pallas_call(
        functools.partial(grad_kernel, *sizes),
        out_shape=[value_tile] * spans,
        in_specs=[smem()] + [vmem()] * (spans + len(gathered)),
        out_specs=[vmem()] * spans,
        scratch_shapes=[pltpu.VMEM((spans, slots, chunk, block), jnp.bfloat16)],
        compiler_params=params(),
        name="tile_grad",
    )(meta, *hidden_cols, *gathered)
    grads = exchange(send)
    tile = jax.ShapeDtypeStruct((slots, block, block), jnp.float32)
    new = pl.pallas_call(
        functools.partial(adam_kernel, spans, slots),
        out_shape=(tile, tile, tile),
        in_specs=[smem()] + [vmem()] * (spans + 3),
        out_specs=(vmem(), vmem(), vmem()),
        scratch_shapes=[pltpu.VMEM((spans, block, block), jnp.bfloat16)],
        compiler_params=params(),
        name="adam",
    )(meta, *grads, values[0, 0], moment_one[0, 0], moment_two[0, 0])

    hidden_grad = None
    shape = jax.ShapeDtypeStruct((chunk, f_width), jnp.bfloat16)
    for part, (low, _) in enumerate(ranges):
        hidden_grad = last_call(
            low * width, partials[part], moving[part], hidden_grad, shape
        )
    return (hidden_grad,) + tuple(array[None, None] for array in new)


def solution(mesh):
    shards = P(("groups", "seq"), ("tensor", "dp"))
    tiles = P(("groups", "seq"), ("tensor", "dp"), None, None, None)
    lists = P(("groups", "seq"), ("tensor", "dp"), None)
    return jax.shard_map(
        per_device,
        mesh=mesh,
        in_specs=(
            shards,
            P(("groups", "tensor", "dp"), "seq"),
            P(("tensor", "dp"), "seq"),
            lists,
            lists,
            tiles,
            tiles,
            tiles,
        ),
        out_specs=(shards, tiles, tiles, tiles),
        check_vma=False,
    )
```

time: 155 us -> 113 us (0.73)
  Pallas kernels: 68.4 us -> 23.9 us
  waiting for transfers between devices: 27.4 us -> 57.3 us
  starting transfers between devices: 41 us -> 18.7 us
  local copies, waits for them, and re-layouts: 3.18 us -> 0.03 us
    pallas_call x10 -> x12, Pallas kernels: 65.2 us -> 19.4 us  [the longest x3 16.4 us: matmul_call(): pl.pallas_call(functools.partial(matmul_kernel, sizes, low, first_part),...]
    ppermute x12 -> x21, waiting for transfers between devices: 27.3 us -> 57.3 us  [take_from(): lax.ppermute(array, axis, [((i + places) % size, i) for i in range(size)])]
    ppermute x12 -> x0, starting transfers between devices: 23.9 us -> none  [the longest x6 18.5 us: per_device(): up[part] = [lax.ppermute(sums[0], 'seq', [(z, z + 1) for z in range(t)])]]
    unnamed x12 -> x8, local copies, waits for them, and re-layouts: 3.18 us -> 0.03 us
    ppermute x12 -> x21, starting transfers between devices: 17.2 us -> 18.7 us  [take_from(): lax.ppermute(array, axis, [((i + places) % size, i) for i in range(size)])]
  transfers between devices with their start and end apart: 24 -> 21, of which waited for: 5 -> 15; matrix products, arithmetic and copies ran while one was open for 0% -> 1% of each run, Pallas kernels for 38% -> 21%
where the time goes in v3:
time: 113 us; the launch traced here: 112 us
  waiting for transfers between devices  57.3 us (51%)
  Pallas kernels  23.9 us (21%)
  starting transfers between devices  18.7 us (17%)
  blocking collectives  11.1 us (10%)
    ppermute x21, waiting for transfers between devices, take_from(): lax.ppermute(array, axis, [((i + places) % size, i) for i in range(size)])  57.3 us
    ppermute x21, starting transfers between devices, take_from(): lax.ppermute(array, axis, [((i + places) % size, i) for i in range(size)])  18.7 us
    pallas_call x3, Pallas kernels, matmul_call(): pl.pallas_call(functools.partial(matmul_kernel, sizes, low, first_part),...  16.4 us
    all_gather x1, blocking collectives, per_device(): meta = lax.all_gather(meta, 'seq', axis=0, tiled=True)  11.1 us
    pallas_call x3, Pallas kernels, last_call(): pl.pallas_call(functools.partial(last_kernel, low), out_shape=shape, in_s...  2.43 us
  transfers between devices with their start and end apart: 21, of which 15 were waited for; matrix products, arithmetic and copies ran while one was open for 1% of the time, Pallas kernels for 21%

profile of v3, /device:TPU:0, one launch (start us, length us, event | category | flops | bytes accessed | tf_op | source)
XLA Modules:
  0.0 112.5 jit_solution(17975717276372358415)
XLA Ops:
  0.6 3.0 %collective-permute-start.4 = (bf16[128,2048]{1,0:T(8,128)(2,1)}, bf16[128,2048]{1,0:T(8,128)(2,1)S(1)}, u32[]{:S(2)}, u32[]{:S(2)}) collective-permute-start(bf16[128,2048]{1,0:T(8,128)(2,1)} %refs_4_.1), channel_id=1, source_target_pairs={{2,0},{0,2},{3,1},{1,3},{6,4},{4,6},{7,5},{5,7},{10,8},{8,10},{11,... | collective-permute-start | bytes 1572872 | tf_op jit(solution)/shard_map/ppermute | solution.py:285
  4.4 11.1 %all-gather = s32[4,1,8]{2,1,0:T(1,128)S(1)} all-gather(s32[1,1,8]{2,1,0:T(1,128)S(1)} %add_bitcast_fusion), channel_id=1, replica_groups=mesh['groups'=2,'seq'=4,'tensor'=2,'dp'=2] {'seq'}, dimensions={0}, use_global_device_ids=true | all-gather | bytes 160 | tf_op jit(solution)/shard_map/all_gather | solution.py:315
  15.5 2.0 %pick.1 = (bf16[128,128]{1,0:T(8,128)(2,1)S(1)}, bf16[128,128]{1,0:T(8,128)(2,1)S(1)}, bf16[128,128]{1,0:T(8,128)(2,1)S(1)}, bf16[128,128]{1,0:T(8,128)(2,1)S(1)...) custom-call(s32[4,8]{1,0:T(4,128)S(1)} %bitcast.19, ...), custom_call_target="tpu_custom_call" | custom-call | tf_op jit(solution)/shard_map/pick/pallas_call | solution.py:319
  17.9 3.5 %collective-permute-start.2 = (bf16[128,128]{1,0:T(8,128)(2,1)S(1)}, bf16[128,128]{1,0:T(8,128)(2,1)S(1)}, u32[]{:S(2)}, u32[]{:S(2)}) collective-permute-start(bf16[128,128]{1,0:T(8,128)(2,1)S(1)} %get-tuple-element.37), channel_id=1, source_target_pairs={{4,0},{8,4},{12,8},{0,12},{5,1},{9,5},{13,9},{1,13},{6,2},{10,6},{... | collective-permute-start | bytes 98312 | tf_op jit(solution)/shard_map/ppermute | solution.py:285
  21.9 1.7 %collective-permute-done = bf16[128,128]{1,0:T(8,128)(2,1)S(1)} collective-permute-done((bf16[128,128]{1,0:T(8,128)(2,1)S(1)}, bf16[128,128]{1,0:T(8,128)(2,1)S(1)}, u32[]{:S(2)}, u32[]{:S(2)}) %collective-permute-start) | collective-permute-done | bytes 32800 | tf_op jit(solution)/shard_map/ppermute | solution.py:285
  24.3 3.8 %collective-permute-done.5.refs_1_ = bf16[4,128,128]{2,1,0:T(8,128)(2,1)S(1)} collective-permute-done((bf16[4,128,128]{2,1,0:T(8,128)(2,1)S(1)}, bf16[4,128,128]{2,1,0:T(8,128)(2,1)S(1)}, u32[]{:S(2)}, u32[]{:S(2)}) %collective-permute-start.5) | collective-permute-done | bytes 131104 | tf_op jit(solution)/shard_map/ppermute | solution.py:285
  28.3 0.9 collective-permute-start.8
  30.0 5.7 %partial.3 = (bf16[4,128,1024]{2,1,0:T(8,128)(2,1)S(1)}, bf16[128,1024]{1,0:T(8,128)(2,1)S(1)}, bf16[512,2048]{1,0:T(8,128)(2,1)S(1)}) custom-call(s32[4,8]{1,0:T(4,128)S(1)} %bitcast.20, bf16[4,128,128]{2,1,0:T(8,128)(2,1)S(1)} %pad_maximum_fusion.held, bf16[3584,2048]{1,0:T(8,128)(2,1)} %weight.5, bf16[128,2048]{1,0:T(8,128)(2,1)} %refs_4_.1, ...), custom_call_target="tpu_custom_call" | custom-call | flops 2147483648 | bytes 4194304 | tf_op jit(solution)/shard_map/partial/pallas_call | solution.py:160
  36.8 2.5 %collective-permute-start.9 = (bf16[128,1024]{1,0:T(8,128)(2,1)S(1)}, bf16[128,1024]{1,0:T(8,128)(2,1)S(1)}, u32[]{:S(2)}, u32[]{:S(2)}) collective-permute-start(bf16[128,1024]{1,0:T(8,128)(2,1)S(1)} %get-tuple-element.46), channel_id=1, source_target_pairs={{12,0},{0,4},{4,8},{8,12},{13,1},{1,5},{5,9},{9,13},{14,2},{2,6},{... | collective-permute-start | bytes 786440 | tf_op jit(solution)/shard_map/ppermute | solution.py:285
  39.4 6.1 %partial.5 = (bf16[4,128,1536]{2,1,0:T(8,128)(2,1)S(1)}, bf16[128,1536]{1,0:T(8,128)(2,1)S(1)}) custom-call(s32[4,8]{1,0:T(4,128)S(1)} %bitcast.21, bf16[4,128,128]{2,1,0:T(8,128)(2,1)S(1)} %pad_maximum_fusion.held, bf16[3584,2048]{1,0:T(8,128)(2,1)} %weight.5, bf16[512,2048]{1,0:T(8,128)(2,1)S(1)} %get-tuple-element.47.refs_0_), custom_call_target="tpu_custom_call" | custom-call | flops 3221225472 | bytes 6291456 | tf_op jit(solution)/shard_map/partial/pallas_call | solution.py:160
  45.5 1.3 %collective-permute-done.9.arrived = bf16[128,1024]{1,0:T(8,128)(2,1)S(1)} collective-permute-done((bf16[128,1024]{1,0:T(8,128)(2,1)S(1)}, bf16[128,1024]{1,0:T(8,128)(2,1)S(1)}, u32[]{:S(2)}, u32[]{:S(2)}) %collective-permute-start.9) | collective-permute-done | bytes 262176 | tf_op jit(solution)/shard_map/ppermute | solution.py:285
  46.8 4.7 %partial.4 = (bf16[4,128,1024]{2,1,0:T(8,128)(2,1)S(1)}, bf16[128,1024]{1,0:T(8,128)(2,1)S(1)}) custom-call(s32[4,8]{1,0:T(4,128)S(1)} %bitcast.22, bf16[4,128,128]{2,1,0:T(8,128)(2,1)S(1)} %pad_maximum_fusion.held, bf16[3584,2048]{1,0:T(8,128)(2,1)} %weight.5, bf16[512,2048]{1,0:T(8,128)(2,1)S(1)} %get-tuple-element.47.refs_0_), custom_call_target="tpu_custom_call" | custom-call | flops 2147483648 | bytes 4194304 | tf_op jit(solution)/shard_map/partial/pallas_call | solution.py:160
  51.5 1.3 %collective-permute-start.10 = (bf16[128,1024]{1,0:T(8,128)(2,1)S(1)}, bf16[128,1024]{1,0:T(8,128)(2,1)S(1)}, u32[]{:S(2)}, u32[]{:S(2)}) collective-permute-start(bf16[128,1024]{1,0:T(8,128)(2,1)S(1)} %get-tuple-element.49), channel_id=1, source_target_pairs={{12,0},{0,4},{4,8},{8,12},{13,1},{1,5},{5,9},{9,13},{14,2},{2,6},{... | collective-permute-start | bytes 786440 | tf_op jit(solution)/shard_map/ppermute | solution.py:285
  52.9 6.4 %collective-permute-done.13.arrived = bf16[128,1536]{1,0:T(8,128)(2,1)S(1)} collective-permute-done((bf16[128,1536]{1,0:T(8,128)(2,1)S(1)}, bf16[128,1536]{1,0:T(8,128)(2,1)S(1)}, u32[]{:S(2)}, u32[]{:S(2)}) %collective-permute-start.13) | collective-permute-done | bytes 393248 | tf_op jit(solution)/shard_map/ppermute | solution.py:285
  60.2 4.6 %collective-permute-done.10.arrived = bf16[128,1024]{1,0:T(8,128)(2,1)S(1)} collective-permute-done((bf16[128,1024]{1,0:T(8,128)(2,1)S(1)}, bf16[128,1024]{1,0:T(8,128)(2,1)S(1)}, u32[]{:S(2)}, u32[]{:S(2)}) %collective-permute-start.10) | collective-permute-done | bytes 262176 | tf_op jit(solution)/shard_map/ppermute | solution.py:285
  65.0 8.3 %collective-permute-done.14.arrived = bf16[128,1536]{1,0:T(8,128)(2,1)S(1)} collective-permute-done((bf16[128,1536]{1,0:T(8,128)(2,1)S(1)}, bf16[128,1536]{1,0:T(8,128)(2,1)S(1)}, u32[]{:S(2)}, u32[]{:S(2)}) %collective-permute-start.14) | collective-permute-done | bytes 393248 | tf_op jit(solution)/shard_map/ppermute | solution.py:285
  73.5 5.4 %collective-permute-done.16.arrived = bf16[128,1024]{1,0:T(8,128)(2,1)S(1)} collective-permute-done((bf16[128,1024]{1,0:T(8,128)(2,1)S(1)}, bf16[128,1024]{1,0:T(8,128)(2,1)S(1)}, u32[]{:S(2)}, u32[]{:S(2)}) %collective-permute-start.16) | collective-permute-done | bytes 262176 | tf_op jit(solution)/shard_map/ppermute | solution.py:285
  79.1 5.4 %collective-permute-done.11.arrived = bf16[128,1024]{1,0:T(8,128)(2,1)S(1)} collective-permute-done((bf16[128,1024]{1,0:T(8,128)(2,1)S(1)}, bf16[128,1024]{1,0:T(8,128)(2,1)S(1)}, u32[]{:S(2)}, u32[]{:S(2)}) %collective-permute-start.11) | collective-permute-done | bytes 262176 | tf_op jit(solution)/shard_map/ppermute | solution.py:285
  85.6 1.1 collective-permute-start.18
  86.6 4.0 %collective-permute-start.19 = (bf16[128,128]{1,0:T(8,128)(2,1)S(1)}, bf16[128,128]{1,0:T(8,128)(2,1)S(1)}, u32[]{:S(2)}, u32[]{:S(2)}) collective-permute-start(bf16[128,128]{1,0:T(8,128)(2,1)S(1)} %get-tuple-element.59), channel_id=1, source_target_pairs={{8,0},{12,4},{0,8},{4,12},{9,1},{13,5},{1,9},{5,13},{10,2},{14,6},... | collective-permute-start | bytes 98312 | tf_op jit(solution)/shard_map/ppermute | solution.py:285
  90.7 13.8 %collective-permute-done.18.refs_1_ = bf16[128,128]{1,0:T(8,128)(2,1)S(1)} collective-permute-done((bf16[128,128]{1,0:T(8,128)(2,1)S(1)}, bf16[128,128]{1,0:T(8,128)(2,1)S(1)}, u32[]{:S(2)}, u32[]{:S(2)}) %collective-permute-start.18) | collective-permute-done | bytes 32800 | tf_op jit(solution)/shard_map/ppermute | solution.py:285
  104.5 1.0 collective-permute-done.19.refs_2_
  105.4 3.0 %collective-permute-done.20.refs_3_ = bf16[128,128]{1,0:T(8,128)(2,1)S(1)} collective-permute-done((bf16[128,128]{1,0:T(8,128)(2,1)S(1)}, bf16[128,128]{1,0:T(8,128)(2,1)S(1)}, u32[]{:S(2)}, u32[]{:S(2)}) %collective-permute-start.20) | collective-permute-done | bytes 32800 | tf_op jit(solution)/shard_map/ppermute | solution.py:285
  108.4 1.6 %adam.1 = (f32[4,128,128]{2,1,0:T(8,128)}, f32[4,128,128]{2,1,0:T(8,128)}, f32[4,128,128]{2,1,0:T(8,128)}) custom-call(s32[4,8]{1,0:T(4,128)S(1)} %bitcast.24, bf16[128,128]{1,0:T(8,128)(2,1)S(1)} %get-tuple-element.57.refs_0_, bf16[128,128]{1,0:T(8,128)(2,1)S(1)} %collective-permute-done.18.refs_1_, bf16[128,128]{1,0:T(8,128)(2,1)S(1)} %collective-permute-done.19.refs_2_, ...), custom_call_target="tpu_custom_call" | custom-call | tf_op jit(solution)/shard_map/adam/pallas_call | solution.py:371
  (44 shorter events, 9.5 us)
Async XLA Ops:
  0.6 27.5 %collective-permute-start.4 = (bf16[128,2048]{1,0:T(8,128)(2,1)}, bf16[128,2048]{1,0:T(8,128)(2,1)S(1)}, u32[]{:S(2)}, u32[]{:S(2)}) collective-permute-start(bf16[128,2048]{1,0:T(8,128)(2,1)} %refs_4_.1), channel_id=1, source_target_pairs={{2,0},{0,2},{3,1},{1,3},{6,4},{4,6},{7,5},{5,7},{10,8},{8,10},{11,... | collective-permute-start | bytes 1572872 | tf_op jit(solution)/shard_map/ppermute | solution.py:285
  17.5 6.1 %collective-permute-start = (bf16[128,128]{1,0:T(8,128)(2,1)S(1)}, bf16[128,128]{1,0:T(8,128)(2,1)S(1)}, u32[]{:S(2)}, u32[]{:S(2)}) collective-permute-start(bf16[128,128]{1,0:T(8,128)(2,1)S(1)} %get-tuple-element.35), channel_id=1, source_target_pairs={{12,0},{0,4},{4,8},{8,12},{13,1},{1,5},{5,9},{9,13},{14,2},{2,6},{... | collective-permute-start | bytes 98312 | tf_op jit(solution)/shard_map/ppermute | solution.py:285
  17.5 6.1 %collective-permute-start.1 = (bf16[128,128]{1,0:T(8,128)(2,1)S(1)}, bf16[128,128]{1,0:T(8,128)(2,1)S(1)}, u32[]{:S(2)}, u32[]{:S(2)}) collective-permute-start(bf16[128,128]{1,0:T(8,128)(2,1)S(1)} %get-tuple-element.36), channel_id=1, source_target_pairs={{8,0},{12,4},{0,8},{4,12},{9,1},{13,5},{1,9},{5,13},{10,2},{14,6},... | collective-permute-start | bytes 98312 | tf_op jit(solution)/shard_map/ppermute | solution.py:285
  17.9 6.4 %collective-permute-start.2 = (bf16[128,128]{1,0:T(8,128)(2,1)S(1)}, bf16[128,128]{1,0:T(8,128)(2,1)S(1)}, u32[]{:S(2)}, u32[]{:S(2)}) collective-permute-start(bf16[128,128]{1,0:T(8,128)(2,1)S(1)} %get-tuple-element.37), channel_id=1, source_target_pairs={{4,0},{8,4},{12,8},{0,12},{5,1},{9,5},{13,9},{1,13},{6,2},{10,6},{... | collective-permute-start | bytes 98312 | tf_op jit(solution)/shard_map/ppermute | solution.py:285
  21.3 6.8 %collective-permute-start.5 = (bf16[4,128,128]{2,1,0:T(8,128)(2,1)S(1)}, bf16[4,128,128]{2,1,0:T(8,128)(2,1)S(1)}, u32[]{:S(2)}, u32[]{:S(2)}) collective-permute-start(bf16[4,128,128]{2,1,0:T(8,128)(2,1)S(1)} %get-tuple-element.38), channel_id=1, source_target_pairs={{12,0},{0,4},{4,8},{8,12},{13,1},{1,5},{5,9},{9,13},{14,2},{2,6},{... | collective-permute-start | bytes 393224 | tf_op jit(solution)/shard_map/ppermute | solution.py:285
  23.6 5.7 %collective-permute-start.3 = (bf16[128,2048]{1,0:T(8,128)(2,1)}, bf16[128,2048]{1,0:T(8,128)(2,1)S(1)}, u32[]{:S(2)}, u32[]{:S(2)}) collective-permute-start(bf16[128,2048]{1,0:T(8,128)(2,1)} %refs_4_.1), channel_id=1, source_target_pairs={{1,0},{0,1},{3,2},{2,3},{5,4},{4,5},{7,6},{6,7},{9,8},{8,9},{11,10... | collective-permute-start | bytes 1572872 | tf_op jit(solution)/shard_map/ppermute | solution.py:285
  28.1 1.9 %collective-permute-start.6 = (bf16[128,2048]{1,0:T(8,128)(2,1)S(1)}, bf16[128,2048]{1,0:T(8,128)(2,1)S(1)}, u32[]{:S(2)}, u32[]{:S(2)}) collective-permute-start(bf16[128,2048]{1,0:T(8,128)(2,1)S(1)} %collective-permute-done.4.refs_2_.refs_6_), channel_id=1, source_target_pairs={{1,0},{0,1},{3,2},{2,3},{5,4},{4,5},{7,6},{6,7},{9,8},{8,9},{11,10... | collective-permute-start | bytes 1572872 | tf_op jit(solution)/shard_map/ppermute | solution.py:285
  28.1 7.9 %collective-permute-start.7 = (bf16[4,128,128]{2,1,0:T(8,128)(2,1)S(1)}, bf16[4,128,128]{2,1,0:T(8,128)(2,1)S(1)}, u32[]{:S(2)}, u32[]{:S(2)}) collective-permute-start(bf16[4,128,128]{2,1,0:T(8,128)(2,1)S(1)} %get-tuple-element.42), channel_id=1, source_target_pairs={{8,0},{12,4},{0,8},{4,12},{9,1},{13,5},{1,9},{5,13},{10,2},{14,6},... | collective-permute-start | bytes 393224 | tf_op jit(solution)/shard_map/ppermute | solution.py:285
  28.3 8.5 %collective-permute-start.8 = (bf16[4,128,128]{2,1,0:T(8,128)(2,1)S(1)}, bf16[4,128,128]{2,1,0:T(8,128)(2,1)S(1)}, u32[]{:S(2)}, u32[]{:S(2)}) collective-permute-start(bf16[4,128,128]{2,1,0:T(8,128)(2,1)S(1)} %get-tuple-element.43), channel_id=1, source_target_pairs={{4,0},{8,4},{12,8},{0,12},{5,1},{9,5},{13,9},{1,13},{6,2},{10,6},{... | collective-permute-start | bytes 393224 | tf_op jit(solution)/shard_map/ppermute | solution.py:285
  36.8 9.9 %collective-permute-start.9 = (bf16[128,1024]{1,0:T(8,128)(2,1)S(1)}, bf16[128,1024]{1,0:T(8,128)(2,1)S(1)}, u32[]{:S(2)}, u32[]{:S(2)}) collective-permute-start(bf16[128,1024]{1,0:T(8,128)(2,1)S(1)} %get-tuple-element.46), channel_id=1, source_target_pairs={{12,0},{0,4},{4,8},{8,12},{13,1},{1,5},{5,9},{9,13},{14,2},{2,6},{... | collective-permute-start | bytes 786440 | tf_op jit(solution)/shard_map/ppermute | solution.py:285
  45.4 13.8 %collective-permute-start.13 = (bf16[128,1536]{1,0:T(8,128)(2,1)S(1)}, bf16[128,1536]{1,0:T(8,128)(2,1)S(1)}, u32[]{:S(2)}, u32[]{:S(2)}) collective-permute-start(bf16[128,1536]{1,0:T(8,128)(2,1)S(1)} %get-tuple-element.51), channel_id=1, source_target_pairs={{12,0},{0,4},{4,8},{8,12},{13,1},{1,5},{5,9},{9,13},{14,2},{2,6},{... | collective-permute-start | bytes 1179656 | tf_op jit(solution)/shard_map/ppermute | solution.py:285
  51.5 13.3 %collective-permute-start.10 = (bf16[128,1024]{1,0:T(8,128)(2,1)S(1)}, bf16[128,1024]{1,0:T(8,128)(2,1)S(1)}, u32[]{:S(2)}, u32[]{:S(2)}) collective-permute-start(bf16[128,1024]{1,0:T(8,128)(2,1)S(1)} %get-tuple-element.49), channel_id=1, source_target_pairs={{12,0},{0,4},{4,8},{8,12},{13,1},{1,5},{5,9},{9,13},{14,2},{2,6},{... | collective-permute-start | bytes 786440 | tf_op jit(solution)/shard_map/ppermute | solution.py:285
  59.4 13.9 %collective-permute-start.14 = (bf16[128,1536]{1,0:T(8,128)(2,1)S(1)}, bf16[128,1536]{1,0:T(8,128)(2,1)S(1)}, u32[]{:S(2)}, u32[]{:S(2)}) collective-permute-start(bf16[128,1536]{1,0:T(8,128)(2,1)S(1)} %add.11), channel_id=1, source_target_pairs={{12,0},{0,4},{4,8},{8,12},{13,1},{1,5},{5,9},{9,13},{14,2},{2,6},{... | collective-permute-start | bytes 1179656 | tf_op jit(solution)/shard_map/ppermute | solution.py:285
  59.4 19.5 %collective-permute-start.16 = (bf16[128,1024]{1,0:T(8,128)(2,1)S(1)}, bf16[128,1024]{1,0:T(8,128)(2,1)S(1)}, u32[]{:S(2)}, u32[]{:S(2)}) collective-permute-start(bf16[128,1024]{1,0:T(8,128)(2,1)S(1)} %add.8), channel_id=1, source_target_pairs={{12,0},{0,4},{4,8},{8,12},{13,1},{1,5},{5,9},{9,13},{14,2},{2,6},{... | collective-permute-start | bytes 786440 | tf_op jit(solution)/shard_map/ppermute | solution.py:285
  65.0 19.6 %collective-permute-start.11 = (bf16[128,1024]{1,0:T(8,128)(2,1)S(1)}, bf16[128,1024]{1,0:T(8,128)(2,1)S(1)}, u32[]{:S(2)}, u32[]{:S(2)}) collective-permute-start(bf16[128,1024]{1,0:T(8,128)(2,1)S(1)} %add.9), channel_id=1, source_target_pairs={{12,0},{0,4},{4,8},{8,12},{13,1},{1,5},{5,9},{9,13},{14,2},{2,6},{... | collective-permute-start | bytes 786440 | tf_op jit(solution)/shard_map/ppermute | solution.py:285
  73.4 37.4 %collective-permute-start.15 = (bf16[128,1536]{1,0:T(8,128)(2,1)S(1)}, bf16[128,1536]{1,0:T(8,128)(2,1)S(1)}, u32[]{:S(2)}, u32[]{:S(2)}) collective-permute-start(bf16[128,1536]{1,0:T(8,128)(2,1)S(1)} %add.12), channel_id=1, source_target_pairs={{12,0},{0,4},{4,8},{8,12},{13,1},{1,5},{5,9},{9,13},{14,2},{2,6},{... | collective-permute-start | bytes 1179656 | tf_op jit(solution)/shard_map/ppermute | solution.py:285
  79.0 29.4 %copy-start.1 = (f32[1,1,4,128,128]{4,3,2,1,0:T(8,128)S(1)}, f32[1,1,4,128,128]{4,3,2,1,0:T(8,128)}, u32[]{:S(2)}) copy-start(f32[1,1,4,128,128]{4,3,2,1,0:T(8,128)} %param.13) | copy-start | bytes 786436
  79.0 29.4 %copy-start.2 = (f32[1,1,4,128,128]{4,3,2,1,0:T(8,128)S(1)}, f32[1,1,4,128,128]{4,3,2,1,0:T(8,128)}, u32[]{:S(2)}) copy-start(f32[1,1,4,128,128]{4,3,2,1,0:T(8,128)} %param.14) | copy-start | bytes 786436
  79.0 29.4 %copy-start.3 = (f32[1,1,4,128,128]{4,3,2,1,0:T(8,128)S(1)}, f32[1,1,4,128,128]{4,3,2,1,0:T(8,128)}, u32[]{:S(2)}) copy-start(f32[1,1,4,128,128]{4,3,2,1,0:T(8,128)} %param.15) | copy-start | bytes 786436
  79.0 31.0 %collective-permute-start.17 = (bf16[128,1024]{1,0:T(8,128)(2,1)S(1)}, bf16[128,1024]{1,0:T(8,128)(2,1)S(1)}, u32[]{:S(2)}, u32[]{:S(2)}) collective-permute-start(bf16[128,1024]{1,0:T(8,128)(2,1)S(1)} %add.13), channel_id=1, source_target_pairs={{12,0},{0,4},{4,8},{8,12},{13,1},{1,5},{5,9},{9,13},{14,2},{2,6},{... | collective-permute-start | bytes 786440 | tf_op jit(solution)/shard_map/ppermute | solution.py:285
  84.6 27.1 %collective-permute-start.12 = (bf16[128,1024]{1,0:T(8,128)(2,1)S(1)}, bf16[128,1024]{1,0:T(8,128)(2,1)S(1)}, u32[]{:S(2)}, u32[]{:S(2)}) collective-permute-start(bf16[128,1024]{1,0:T(8,128)(2,1)S(1)} %add.10), channel_id=1, source_target_pairs={{12,0},{0,4},{4,8},{8,12},{13,1},{1,5},{5,9},{9,13},{14,2},{2,6},{... | collective-permute-start | bytes 786440 | tf_op jit(solution)/shard_map/ppermute | solution.py:285
  85.6 18.9 %collective-permute-start.18 = (bf16[128,128]{1,0:T(8,128)(2,1)S(1)}, bf16[128,128]{1,0:T(8,128)(2,1)S(1)}, u32[]{:S(2)}, u32[]{:S(2)}) collective-permute-start(bf16[128,128]{1,0:T(8,128)(2,1)S(1)} %get-tuple-element.58), channel_id=1, source_target_pairs={{12,0},{0,4},{4,8},{8,12},{13,1},{1,5},{5,9},{9,13},{14,2},{2,6},{... | collective-permute-start | bytes 98312 | tf_op jit(solution)/shard_map/ppermute | solution.py:285
  86.6 18.8 %collective-permute-start.19 = (bf16[128,128]{1,0:T(8,128)(2,1)S(1)}, bf16[128,128]{1,0:T(8,128)(2,1)S(1)}, u32[]{:S(2)}, u32[]{:S(2)}) collective-permute-start(bf16[128,128]{1,0:T(8,128)(2,1)S(1)} %get-tuple-element.59), channel_id=1, source_target_pairs={{8,0},{12,4},{0,8},{4,12},{9,1},{13,5},{1,9},{5,13},{10,2},{14,6},... | collective-permute-start | bytes 98312 | tf_op jit(solution)/shard_map/ppermute | solution.py:285
  104.5 3.9 %collective-permute-start.20 = (bf16[128,128]{1,0:T(8,128)(2,1)S(1)}, bf16[128,128]{1,0:T(8,128)(2,1)S(1)}, u32[]{:S(2)}, u32[]{:S(2)}) collective-permute-start(bf16[128,128]{1,0:T(8,128)(2,1)S(1)} %get-tuple-element.60), channel_id=1, source_target_pairs={{4,0},{8,4},{12,8},{0,12},{5,1},{9,5},{13,9},{1,13},{6,2},{10,6},{... | collective-permute-start | bytes 98312 | tf_op jit(solution)/shard_map/ppermute | solution.py:285
  (1 other events, 11.3 us)

commit v4 on v3

v4 whole, which is shorter than its diff:
```python
import functools

import jax
import jax.numpy as jnp
from jax import lax
from jax.experimental import pallas as pl
from jax.experimental.pallas import tpu as pltpu
from jax.sharding import PartitionSpec as P

STEP = 100
BETA_ONE = 0.9
BETA_TWO = 0.999
RATE = 0.01
EPSILON = 1e-08
VMEM_LIMIT = 24 * 1024 * 1024
PARTS = 3
NT = (((1,), (1,)), ((), ()))
TN = (((0,), (0,)), ((), ()))


def vmem():
    return pl.BlockSpec(memory_space=pltpu.VMEM)


def smem():
    return pl.BlockSpec(memory_space=pltpu.SMEM)


def hbm():
    return pl.BlockSpec(memory_space=pltpu.HBM)


def stay(array):
    return pltpu.with_memory_space_constraint(array, pltpu.HBM)


def params():
    return pltpu.CompilerParams(vmem_limit_bytes=VMEM_LIMIT)


def wrap(index, size):
    return lax.rem(index + size, size)


class Lists:
    def __init__(self, rows, spans, slots):
        self.rows, self.spans, self.slots = rows, spans, slots
        self.me = lax.axis_index("seq")
        self.counts = []
        for s in range(spans):
            count = self.live(s, 0)
            for slot in range(1, slots):
                count = count + self.live(s, slot)
            self.counts.append(count)

    def tile(self, s, slot):
        ref, row = self.rows[s]
        return ref[row, slot]

    def live(self, s, slot):
        ref, row = self.rows[s]
        return ref[row, self.slots + slot]

    def region(self, s):
        return lax.rem(self.me + s, self.spans)

    def before(self, s):
        region, before = self.region(s), jnp.int32(0)
        for other in range(self.spans):
            before = before + jnp.where(self.region(other) < region, self.counts[other], 0)
        return before


def table_lists(table, spans, slots):
    return Lists([(table, s) for s in range(spans)], spans, slots)


def pick_kernel(spans, slots, block, d_blocks, *refs):
    metas, (values, hidden, table), refs = refs[:spans], refs[spans : spans + 3], refs[spans + 3 :]
    value_outs, hidden_outs = refs[:spans], refs[spans : 2 * spans]
    tiles, value_sems, hidden_sems = refs[2 * spans :]
    lists = Lists([(meta, 0) for meta in metas], spans, slots)
    lives, value_copies, hidden_copies = [], [], []
    for s in range(spans):
        before = lists.before(s)
        slot = wrap(lists.me - lax.rem(before, spans), spans)
        lives.append(slot < lists.counts[s])
        owned = jnp.minimum(lax.div(before + slot, spans), slots - 1)
        copy = pltpu.make_async_copy(values.at[owned], tiles.at[s], value_sems.at[s])
        copy.start()
        value_copies.append(copy)
    for s in range(spans):
        for j in range(slots):
            start = pl.multiple_of(lax.div(lists.tile(s, j), d_blocks) * block, block)
            copy = pltpu.make_async_copy(
                hidden.at[:, pl.ds(start, block)], hidden_outs[s].at[j], hidden_sems.at[s, j]
            )
            copy.start()
            hidden_copies.append(copy)
        for j in range(2 * slots):
            table[s, j] = metas[s][0, j]
    for s in range(spans):
        value_copies[s].wait()
        tile = tiles[s]
        value_outs[s][...] = jnp.where(lives[s], tile, jnp.zeros_like(tile)).astype(jnp.bfloat16)
    for copy in hidden_copies:
        copy.wait()


def lay_kernel(own, weight, *refs):
    others, (rows, first_weight, sems) = refs[:-3], refs[-3:]
    chunk = own.shape[0]
    weight_copy = pltpu.make_async_copy(
        weight.at[pl.ds(0, first_weight.shape[0])], first_weight, sems.at[0]
    )
    weight_copy.start()
    own_copy = pltpu.make_async_copy(own, rows.at[pl.ds(0, chunk)], sems.at[1])
    own_copy.start()
    for p, other in enumerate(others):
        rows[(p + 1) * chunk : (p + 2) * chunk] = other[...]
    own_copy.wait()
    weight_copy.wait()


def chunk_at(place):
    tensors, cores = lax.axis_size("tensor"), lax.axis_size("dp")
    t_place = lax.rem(lax.axis_index("tensor") + place // cores, tensors)
    d_place = lax.rem(lax.axis_index("dp") + place % cores, cores)
    return t_place * cores + d_place


def matmul_kernel(sizes, low, width, pieces, table, held, weight, *refs):
    spans, slots, block, d_blocks = sizes
    step = pl.program_id(0)
    if pieces > 1:
        given, (out, first, rows, total) = refs[:pieces], refs[pieces:]

        @pl.when(step == 0)
        def _():
            at = 0
            for piece in given:
                rows[at : at + piece.shape[0]] = piece[...]
                at += piece.shape[0]

    else:
        rows, out, first, total = refs
    chunk = rows.shape[0] // spans
    here = pl.ds(pl.multiple_of(step * width, width), width)
    weights = weight[here] if weight.shape[0] > width else weight[...]
    total[...] = lax.dot_general(rows[...], weights, NT, preferred_element_type=jnp.float32)
    lists = table_lists(table, spans, slots)
    before = lists.before(0)
    for j in range(slots):
        tile = lists.tile(0, j)
        f_start = lax.div(tile, d_blocks) * block - (low + step) * width

        @pl.when((j < lists.counts[0]) & (f_start >= 0) & (f_start < width))
        def _():
            d_start = pl.multiple_of(lax.rem(tile, d_blocks) * block, block)
            place = pl.ds(pl.multiple_of(f_start, block), block)
            owner = lax.rem(before + j, spans)
            total[:, place] += lax.dot_general(
                rows[:, pl.ds(d_start, block)],
                held[wrap(lists.me - owner, spans)],
                NT,
                preferred_element_type=jnp.float32,
            )

    first_chunk = wrap(lists.me - 1, spans)
    for p in range(spans):
        result = total[p * chunk : (p + 1) * chunk].astype(out.dtype)
        out[chunk_at(p), :, here] = result

        @pl.when(chunk_at(p) == first_chunk)
        def _():
            first[:, here] = result


def matmul_call(sizes, low, high, width, table, held, weight, pieces):
    spans = sizes[0]
    tokens, d_width = sum(piece.shape[0] for piece in pieces), weight.shape[1]
    columns = (high - low) * width
    shapes = [
        jax.ShapeDtypeStruct((spans, tokens // spans, columns), jnp.bfloat16),
        jax.ShapeDtypeStruct((tokens // spans, columns), jnp.bfloat16),
    ]
    if len(pieces) > 1:
        shapes.append(jax.ShapeDtypeStruct((tokens, d_width), pieces[0].dtype))
    if weight.shape[0] == columns:
        weight_spec = vmem()
    else:
        weight, weight_spec = stay(weight), pl.BlockSpec((width, d_width), lambda i: (i + low, 0))
    return pl.pallas_call(
        functools.partial(matmul_kernel, sizes, low, width, len(pieces)),
        grid=(high - low,),
        out_shape=shapes,
        in_specs=[smem(), vmem(), weight_spec] + [vmem()] * len(pieces),
        out_specs=[vmem()] * len(shapes),
        scratch_shapes=[pltpu.VMEM((tokens, width), jnp.float32)],
        compiler_params=params(),
        cost_estimate=pl.CostEstimate(
            flops=2 * tokens * d_width * columns,
            bytes_accessed=2 * d_width * columns,
            transcendentals=0,
        ),
        name="partial",
    )(table, held, weight, *pieces)


def add_kernel(t, partials, arrived, out):
    spans = partials.shape[0]
    chunk = wrap(lax.axis_index("seq") - t, spans)
    result = partials[chunk].astype(jnp.float32) + arrived[...].astype(jnp.float32)
    out[...] = result.astype(out.dtype)


def add_call(t, partials, arrived):
    return pl.pallas_call(
        functools.partial(add_kernel, t),
        out_shape=jax.ShapeDtypeStruct(arrived.shape, arrived.dtype),
        in_specs=[vmem(), vmem()],
        out_specs=vmem(),
        compiler_params=params(),
        name="add",
    )(partials, arrived)


def last_kernel(low, partials, arrived, *refs):
    out, total, sem = refs[-3:]
    columns = partials.shape[2]
    result = partials[lax.axis_index("seq")].astype(jnp.float32) + arrived[...].astype(jnp.float32)
    total[...] = result.astype(out.dtype)
    copy = pltpu.make_async_copy(total, out.at[:, pl.ds(low, columns)], sem)
    copy.start()
    copy.wait()


def last_call(low, partials, arrived, out, shape):
    _, chunk, columns = partials.shape
    given = [] if out is None else [out]
    return pl.pallas_call(
        functools.partial(last_kernel, low),
        out_shape=shape,
        in_specs=[vmem()] * 2 + [hbm()] * len(given),
        out_specs=hbm(),
        scratch_shapes=[pltpu.VMEM((chunk, columns), shape.dtype), pltpu.SemaphoreType.DMA],
        input_output_aliases={2: 0} if given else {},
        compiler_params=params(),
        name="last_sum",
    )(partials, arrived, *given)


def grad_kernel(spans, slots, block, d_blocks, table, rows, *refs):
    hidden, outs, (cols,) = refs[:spans], refs[spans : 2 * spans], refs[2 * spans :]
    lists = table_lists(table, spans, slots)
    before = lists.before(0)
    chunk = rows.shape[0] // spans
    for s in range(spans):
        cols[s] = hidden[s][...]
    for s in range(spans):
        slot = wrap(lists.region(s) - lax.rem(before, spans), spans)
        outs[s][...] = jnp.zeros_like(outs[s])

        @pl.when(slot < lists.counts[0])
        def _():
            d_start = pl.multiple_of(lax.rem(table[0, slot], d_blocks) * block, block)
            total = jnp.zeros((block, block), jnp.float32)
            for p in range(spans):
                total = total + lax.dot_general(
                    cols[wrap(lists.me - chunk_at(p), spans), slot],
                    rows[p * chunk : (p + 1) * chunk, pl.ds(d_start, block)],
                    TN,
                    preferred_element_type=jnp.float32,
                )
            outs[s][...] = total.astype(outs[s].dtype)


def grad_call(sizes, table, rows, hidden_cols):
    spans = sizes[0]
    slots, chunk, block = hidden_cols[0].shape
    return pl.pallas_call(
        functools.partial(grad_kernel, *sizes),
        out_shape=[jax.ShapeDtypeStruct((block, block), jnp.bfloat16)] * spans,
        in_specs=[smem()] + [vmem()] * (spans + 1),
        out_specs=[vmem()] * spans,
        scratch_shapes=[pltpu.VMEM((spans, slots, chunk, block), jnp.bfloat16)],
        compiler_params=params(),
        name="tile_grad",
    )(table, rows, *hidden_cols)


def adam_kernel(spans, slots, table, *refs):
    arrived, refs = refs[:spans], refs[spans:]
    values, one, two, values_new, one_new, two_new, grads = refs
    lists = table_lists(table, spans, slots)
    for s in range(spans):
        grads[s] = arrived[s][...]
    befores = [lists.before(s) for s in range(spans)]
    for owned in range(slots):
        rank = owned * spans + lists.me
        live, source = jnp.bool_(False), jnp.int32(0)
        for s in range(spans):
            holds = (befores[s] <= rank) & (rank < befores[s] + lists.counts[s])
            live, source = live | holds, jnp.where(holds, (spans - s) % spans, source)
        grad = grads[source].astype(jnp.float32)
        stored, old_one, old_two = values[owned], one[owned], two[owned]
        new_one = BETA_ONE * old_one + (1.0 - BETA_ONE) * grad
        new_two = BETA_TWO * old_two + (1.0 - BETA_TWO) * grad * grad
        stepped = (
            new_one
            / (1.0 - BETA_ONE**STEP)
            / (jnp.sqrt(new_two / (1.0 - BETA_TWO**STEP)) + EPSILON)
        )
        values_new[owned] = jnp.where(live, stored - RATE * stepped, stored)
        one_new[owned] = jnp.where(live, new_one, old_one)
        two_new[owned] = jnp.where(live, new_two, old_two)


def adam_call(sizes, table, grads, *states):
    spans, slots, block, _ = sizes
    tile = jax.ShapeDtypeStruct((slots, block, block), jnp.float32)
    return pl.pallas_call(
        functools.partial(adam_kernel, spans, slots),
        out_shape=(tile, tile, tile),
        in_specs=[smem()] + [vmem()] * (spans + 3),
        out_specs=(vmem(), vmem(), vmem()),
        scratch_shapes=[pltpu.VMEM((spans, block, block), jnp.bfloat16)],
        compiler_params=params(),
        name="adam",
    )(table, *grads, *[state[0, 0] for state in states])


def take_from(array, axis, places):
    size = lax.axis_size(axis)
    return lax.ppermute(array, axis, [((i + places) % size, i) for i in range(size)])


def exchange(pieces):
    return [pieces[0]] + [take_from(pieces[s], "seq", -s) for s in range(1, len(pieces))]


def per_device(
    hidden_in, cotangent, down_weight, tile_ids, tile_live, values, moment_one, moment_two
):
    spans, cores = lax.axis_size("seq"), lax.axis_size("dp")
    slots, block = values.shape[2], values.shape[3]
    f_width, d_width = down_weight.shape
    d_blocks, f_blocks = d_width // block, f_width // block
    chunk = hidden_in.shape[0]
    sizes = (spans, slots, block, d_blocks)
    group = max(size for size in range(1, 5) if f_blocks % size == 0)
    width = group * block
    steps = f_blocks // group
    cuts = [(steps * part + 1) // PARTS for part in range(PARTS + 1)]
    ranges = list(zip(cuts[:-1], cuts[1:]))

    firsts = [take_from(cotangent, "tensor", t) for t in range(1, lax.axis_size("tensor"))]
    local = [take_from(cotangent, "dp", d) for d in range(1, cores)]
    meta = jnp.concatenate([tile_ids[0], tile_live[0]], axis=1)
    metas = [meta] + [take_from(meta, "seq", s) for s in range(1, spans)]

    value_tile = jax.ShapeDtypeStruct((block, block), jnp.bfloat16)
    hidden_tiles = jax.ShapeDtypeStruct((slots, chunk, block), jnp.bfloat16)
    table, *picked = pl.pallas_call(
        functools.partial(pick_kernel, *sizes),
        out_shape=[jax.ShapeDtypeStruct((spans, 2 * slots), jnp.int32)]
        + [value_tile] * spans
        + [hidden_tiles] * spans,
        in_specs=[smem()] * spans + [hbm(), hbm()],
        out_specs=[smem()] + [vmem()] * (2 * spans),
        scratch_shapes=[
            pltpu.VMEM((spans, block, block), jnp.float32),
            pltpu.SemaphoreType.DMA((spans,)),
            pltpu.SemaphoreType.DMA((spans, slots)),
        ],
        compiler_params=params(),
        name="pick",
    )(*metas, stay(values[0, 0]), stay(hidden_in))
    held = jnp.stack(exchange(picked[:spans]))
    hidden_cols = exchange(picked[spans:])

    local_rows, first_weight = pl.pallas_call(
        lay_kernel,
        out_shape=[
            jax.ShapeDtypeStruct((cores * chunk, d_width), cotangent.dtype),
            jax.ShapeDtypeStruct((ranges[0][1] * width, d_width), down_weight.dtype),
        ],
        in_specs=[hbm(), hbm()] + [vmem()] * (cores - 1),
        out_specs=[vmem(), vmem()],
        scratch_shapes=[pltpu.SemaphoreType.DMA((2,))],
        compiler_params=params(),
        name="lay",
    )(stay(cotangent), stay(down_weight), *local)

    firsts, *_ = lax.optimization_barrier((firsts, held, hidden_cols[1], local_rows, first_weight))
    pieces = [local_rows]
    for first in firsts:
        pieces += [first] + [take_from(first, "dp", d) for d in range(1, cores)]

    partials, moving = [], []
    for part, (low, high) in enumerate(ranges):
        if part == 1:
            rows, hidden_cols = lax.optimization_barrier((rows, hidden_cols))
        if part == 2:
            moving[0] = add_call(2, partials[0], moving[0])
            send = grad_call(sizes, table, rows, hidden_cols)
            rows, moving[0], send = lax.optimization_barrier((rows, moving[0], send))
        weight = down_weight if part else first_weight
        partial, first, *more = matmul_call(
            sizes, low, high, width, table, held, weight, [rows] if part else pieces
        )
        rows = more[0] if more else rows
        partials.append(partial)
        moving.append(take_from(first, "seq", -1))

    grads = exchange(send)
    for t in range(2, spans):
        for part in range(len(ranges)):
            if (t, part) == (2, 1):
                moving[part], grads = lax.optimization_barrier((moving[part], grads))
                new = adam_call(sizes, table, grads, values, moment_one, moment_two)
            if (t, part) == (spans - 1, 0):
                moving[part], new = lax.optimization_barrier((moving[part], new))
            if (t, part) != (2, 0):
                moving[part] = add_call(t, partials[part], moving[part])
            moving[part] = take_from(moving[part], "seq", -1)

    hidden_grad = None
    shape = jax.ShapeDtypeStruct((chunk, f_width), jnp.bfloat16)
    for part, (low, _) in enumerate(ranges):
        hidden_grad = last_call(low * width, partials[part], moving[part], hidden_grad, shape)
    return (hidden_grad,) + tuple(array[None, None] for array in new)


def solution(mesh):
    shards = P(("groups", "seq"), ("tensor", "dp"))
    tiles = P(("groups", "seq"), ("tensor", "dp"), None, None, None)
    lists = P(("groups", "seq"), ("tensor", "dp"), None)
    return jax.shard_map(
        per_device,
        mesh=mesh,
        in_specs=(
            shards,
            P(("groups", "tensor", "dp"), "seq"),
            P(("tensor", "dp"), "seq"),
            lists,
            lists,
            tiles,
            tiles,
            tiles,
        ),
        out_specs=(shards, tiles, tiles, tiles),
        check_vma=False,
    )
```

time: 113 us -> 114 us (level)
  the two profiles are of different devices: /device:TPU:0 before, /device:TPU:12 now
where the time goes in v4:
time: 114 us
  waiting for transfers between devices  63.4 us (56%)
  Pallas kernels  25.9 us (23%)
  starting transfers between devices  23.1 us (20%)
    ppermute x24, waiting for transfers between devices, take_from(): lax.ppermute(array, axis, [((i + places) % size, i) for i in range(size)])  63.4 us
    ppermute x24, starting transfers between devices, take_from(): lax.ppermute(array, axis, [((i + places) % size, i) for i in range(size)])  23.1 us
    pallas_call x3, Pallas kernels, matmul_call(): pl.pallas_call(functools.partial(matmul_kernel, sizes, low, width, len(pi...  14.9 us
    pallas_call x1, Pallas kernels, per_device(): pl.pallas_call(functools.partial(pick_kernel, *sizes), out_shape=[jax.Sha...  2.6 us
    pallas_call x3, Pallas kernels, last_call(): pl.pallas_call(functools.partial(last_kernel, low), out_shape=shape, in_s...  2.42 us
    pallas_call x1, Pallas kernels, per_device(): pl.pallas_call(lay_kernel, out_shape=[jax.ShapeDtypeStruct((cores * chunk...  2.32 us
  transfers between devices with their start and end apart: 24, of which 15 were waited for; matrix products, arithmetic and copies ran while one was open for 1% of the time, Pallas kernels for 22%

profile of v4, /device:TPU:12, one launch (start us, length us, event | category | flops | bytes accessed | tf_op | source)
XLA Modules:
  0.0 114.1 jit_solution(10114350188658686074)
XLA Ops:
  0.7 1.6 %collective-permute-start.7 = (bf16[128,2048]{1,0:T(8,128)(2,1)}, bf16[128,2048]{1,0:T(8,128)(2,1)S(1)}, u32[]{:S(2)}, u32[]{:S(2)}) collective-permute-start(bf16[128,2048]{1,0:T(8,128)(2,1)} %own.1), channel_id=1, source_target_pairs={{2,0},{0,2},{3,1},{1,3},{6,4},{4,6},{7,5},{5,7},{10,8},{8,10},{11,... | collective-permute-start | bytes 1572872 | tf_op jit(solution)/shard_map/ppermute | solution.py:335
  3.0 1.6 %collective-permute-start.2 = (s32[1,8]{1,0:T(1,128)S(1)}, s32[1,8]{1,0:T(1,128)S(1)}, u32[]{:S(2)}, u32[]{:S(2)}) collective-permute-start(s32[1,8]{1,0:T(1,128)S(1)} %pad_add_fusion.refs_0_), channel_id=1, source_target_pairs={{12,0},{0,4},{4,8},{8,12},{13,1},{1,5},{5,9},{9,13},{14,2},{2,6},{... | collective-permute-start | bytes 104 | tf_op jit(solution)/shard_map/ppermute | solution.py:335
  5.8 1.8 %collective-permute-start = (s32[1,8]{1,0:T(1,128)S(1)}, s32[1,8]{1,0:T(1,128)S(1)}, u32[]{:S(2)}, u32[]{:S(2)}) collective-permute-start(s32[1,8]{1,0:T(1,128)S(1)} %pad_add_fusion.refs_0_), channel_id=1, source_target_pairs={{4,0},{8,4},{12,8},{0,12},{5,1},{9,5},{13,9},{1,13},{6,2},{10,6},{... | collective-permute-start | bytes 104 | tf_op jit(solution)/shard_map/ppermute | solution.py:335
  9.4 2.6 %pick.1 = (s32[4,8]{1,0:T(4,128)S(1)}, bf16[128,128]{1,0:T(8,128)(2,1)S(1)}, bf16[128,128]{1,0:T(8,128)(2,1)S(1)}, bf16[128,128]{1,0:T(8,128)(2,1)S(1)}, bf16[12...) custom-call(s32[1,8]{1,0:T(1,128)S(1)} %pad_add_fusion.refs_0_, ...), custom_call_target="tpu_custom_call" | custom-call | tf_op jit(solution)/shard_map/pick/pallas_call | solution.py:364
  13.3 2.9 %collective-permute-start.4 = (bf16[128,128]{1,0:T(8,128)(2,1)S(1)}, bf16[128,128]{1,0:T(8,128)(2,1)S(1)}, u32[]{:S(2)}, u32[]{:S(2)}) collective-permute-start(bf16[128,128]{1,0:T(8,128)(2,1)S(1)} %get-tuple-element.53), channel_id=1, source_target_pairs={{8,0},{12,4},{0,8},{4,12},{9,1},{13,5},{1,9},{5,13},{10,2},{14,6},... | collective-permute-start | bytes 98312 | tf_op jit(solution)/shard_map/ppermute | solution.py:335
  18.5 1.6 %collective-permute-done.5 = bf16[128,128]{1,0:T(8,128)(2,1)S(1)} collective-permute-done((bf16[128,128]{1,0:T(8,128)(2,1)S(1)}, bf16[128,128]{1,0:T(8,128)(2,1)S(1)}, u32[]{:S(2)}, u32[]{:S(2)}) %collective-permute-start.5) | collective-permute-done | bytes 32800 | tf_op jit(solution)/shard_map/ppermute | solution.py:335
  20.2 2.3 %lay.1 = (bf16[256,2048]{1,0:T(8,128)(2,1)S(1)}, bf16[1024,2048]{1,0:T(8,128)(2,1)S(1)}) custom-call(bf16[128,2048]{1,0:T(8,128)(2,1)} %own.1, bf16[3584,2048]{1,0:T(8,128)(2,1)} %weight.5, bf16[128,2048]{1,0:T(8,128)(2,1)S(1)} %collective-permute-done.6.refs_0_), custom_call_target="tpu_custom_call" | custom-call | tf_op jit(solution)/shard_map/lay/pallas_call | solution.py:382
  22.6 2.4 %collective-permute-start.10 = (bf16[4,128,128]{2,1,0:T(8,128)(2,1)S(1)}, bf16[4,128,128]{2,1,0:T(8,128)(2,1)S(1)}, u32[]{:S(2)}, u32[]{:S(2)}) collective-permute-start(bf16[4,128,128]{2,1,0:T(8,128)(2,1)S(1)} %get-tuple-element.61), channel_id=1, source_target_pairs={{8,0},{12,4},{0,8},{4,12},{9,1},{13,5},{1,9},{5,13},{10,2},{14,6},... | collective-permute-start | bytes 393224 | tf_op jit(solution)/shard_map/ppermute | solution.py:335
  25.0 1.5 %collective-permute-start.11 = (bf16[4,128,128]{2,1,0:T(8,128)(2,1)S(1)}, bf16[4,128,128]{2,1,0:T(8,128)(2,1)S(1)}, u32[]{:S(2)}, u32[]{:S(2)}) collective-permute-start(bf16[4,128,128]{2,1,0:T(8,128)(2,1)S(1)} %get-tuple-element.62), channel_id=1, source_target_pairs={{4,0},{8,4},{12,8},{0,12},{5,1},{9,5},{13,9},{1,13},{6,2},{10,6},{... | collective-permute-start | bytes 393224 | tf_op jit(solution)/shard_map/ppermute | solution.py:335
  26.5 3.7 %partial.3 = (bf16[4,128,1024]{2,1,0:T(8,128)(2,1)S(1)}, bf16[128,1024]{1,0:T(8,128)(2,1)S(1)}, bf16[512,2048]{1,0:T(8,128)(2,1)S(1)}) custom-call(s32[4,8]{1,0:T(4,128)S(1)} %get-tuple-element.50.table, bf16[4,128,128]{2,1,0:T(8,128)(2,1)S(1)} %pad_maximum_fusion.held, bf16[1024,2048]{1,0:T(8,128)(2,1)S(1)} %get-tuple-element.55.weight, ...), custom_call_target="tpu_custom_call" | custom-call | flops 2147483648 | bytes 4194304 | tf_op jit(solution)/shard_map/partial/pallas_call | solution.py:193
  30.2 3.7 %collective-permute-done.10.refs_2_ = bf16[4,128,128]{2,1,0:T(8,128)(2,1)S(1)} collective-permute-done((bf16[4,128,128]{2,1,0:T(8,128)(2,1)S(1)}, bf16[4,128,128]{2,1,0:T(8,128)(2,1)S(1)}, u32[]{:S(2)}, u32[]{:S(2)}) %collective-permute-start.10) | collective-permute-done | bytes 131104 | tf_op jit(solution)/shard_map/ppermute | solution.py:335
  35.1 6.1 %partial.5 = (bf16[4,128,1536]{2,1,0:T(8,128)(2,1)S(1)}, bf16[128,1536]{1,0:T(8,128)(2,1)S(1)}) custom-call(s32[4,8]{1,0:T(4,128)S(1)} %get-tuple-element.50.table, bf16[4,128,128]{2,1,0:T(8,128)(2,1)S(1)} %pad_maximum_fusion.held, bf16[3584,2048]{1,0:T(8,128)(2,1)} %weight.5, bf16[512,2048]{1,0:T(8,128)(2,1)S(1)} %get-tuple-element.74.rows.refs_0_), custom_call_target="tpu_custom_call" | custom-call | flops 3221225472 | bytes 6291456 | tf_op jit(solution)/shard_map/partial/pallas_call | solution.py:193
  41.1 2.9 %collective-permute-start.16 = (bf16[128,1536]{1,0:T(8,128)(2,1)S(1)}, bf16[128,1536]{1,0:T(8,128)(2,1)S(1)}, u32[]{:S(2)}, u32[]{:S(2)}) collective-permute-start(bf16[128,1536]{1,0:T(8,128)(2,1)S(1)} %get-tuple-element.78), channel_id=1, source_target_pairs={{12,0},{0,4},{4,8},{8,12},{13,1},{1,5},{5,9},{9,13},{14,2},{2,6},{... | collective-permute-start | bytes 1179656 | tf_op jit(solution)/shard_map/ppermute | solution.py:335
  44.0 1.6 %tile_grad.1 = (bf16[128,128]{1,0:T(8,128)(2,1)S(1)}, bf16[128,128]{1,0:T(8,128)(2,1)S(1)}, bf16[128,128]{1,0:T(8,128)(2,1)S(1)}, bf16[128,128]{1,0:T(8,128)(2,1)S(1)}) custom-call(s32[4,8]{1,0:T(4,128)S(1)} %get-tuple-element.50.table, bf16[512,2048]{1,0:T(8,128)(2,1)S(1)} %get-tuple-element.74.rows.refs_0_, ...), custom_call_target="tpu_custom_call" | custom-call | tf_op jit(solution)/shard_map/tile_grad/pallas_call | solution.py:281
  45.8 1.7 %collective-permute-start.18 = (bf16[128,128]{1,0:T(8,128)(2,1)S(1)}, bf16[128,128]{1,0:T(8,128)(2,1)S(1)}, u32[]{:S(2)}, u32[]{:S(2)}) collective-permute-start(bf16[128,128]{1,0:T(8,128)(2,1)S(1)} %get-tuple-element.81), channel_id=1, source_target_pairs={{8,0},{12,4},{0,8},{4,12},{9,1},{13,5},{1,9},{5,13},{10,2},{14,6},... | collective-permute-start | bytes 98312 | tf_op jit(solution)/shard_map/ppermute | solution.py:335
  47.5 1.5 %collective-permute-start.19 = (bf16[128,128]{1,0:T(8,128)(2,1)S(1)}, bf16[128,128]{1,0:T(8,128)(2,1)S(1)}, u32[]{:S(2)}, u32[]{:S(2)}) collective-permute-start(bf16[128,128]{1,0:T(8,128)(2,1)S(1)} %get-tuple-element.82), channel_id=1, source_target_pairs={{4,0},{8,4},{12,8},{0,12},{5,1},{9,5},{13,9},{1,13},{6,2},{10,6},{... | collective-permute-start | bytes 98312 | tf_op jit(solution)/shard_map/ppermute | solution.py:335
  49.1 5.1 %partial.4 = (bf16[4,128,1024]{2,1,0:T(8,128)(2,1)S(1)}, bf16[128,1024]{1,0:T(8,128)(2,1)S(1)}) custom-call(s32[4,8]{1,0:T(4,128)S(1)} %get-tuple-element.50.table, bf16[4,128,128]{2,1,0:T(8,128)(2,1)S(1)} %pad_maximum_fusion.held, bf16[3584,2048]{1,0:T(8,128)(2,1)} %weight.5, bf16[512,2048]{1,0:T(8,128)(2,1)S(1)} %get-tuple-element.74.rows.refs_0_), custom_call_target="tpu_custom_call" | custom-call | flops 2147483648 | bytes 4194304 | tf_op jit(solution)/shard_map/partial/pallas_call | solution.py:193
  56.2 15.1 %collective-permute-done.19.refs_3_ = bf16[128,128]{1,0:T(8,128)(2,1)S(1)} collective-permute-done((bf16[128,128]{1,0:T(8,128)(2,1)S(1)}, bf16[128,128]{1,0:T(8,128)(2,1)S(1)}, u32[]{:S(2)}, u32[]{:S(2)}) %collective-permute-start.19) | collective-permute-done | bytes 32800 | tf_op jit(solution)/shard_map/ppermute | solution.py:335
  71.7 11.7 %collective-permute-done.20.arrived = bf16[128,1536]{1,0:T(8,128)(2,1)S(1)} collective-permute-done((bf16[128,1536]{1,0:T(8,128)(2,1)S(1)}, bf16[128,1536]{1,0:T(8,128)(2,1)S(1)}, u32[]{:S(2)}, u32[]{:S(2)}) %collective-permute-start.20) | collective-permute-done | bytes 393248 | tf_op jit(solution)/shard_map/ppermute | solution.py:335
  83.6 1.6 %adam.1 = (f32[4,128,128]{2,1,0:T(8,128)}, f32[4,128,128]{2,1,0:T(8,128)}, f32[4,128,128]{2,1,0:T(8,128)}) custom-call(s32[4,8]{1,0:T(4,128)S(1)} %get-tuple-element.50.table, bf16[128,128]{1,0:T(8,128)(2,1)S(1)} %get-tuple-element.85.refs_0_, bf16[128,128]{1,0:T(8,128)(2,1)S(1)} %collective-permute-done.17.refs_1_, ...), custom_call_target="tpu_custom_call" | custom-call | tf_op jit(solution)/shard_map/adam/pallas_call | solution.py:322
  85.3 3.8 %collective-permute-done.22.arrived = bf16[128,1024]{1,0:T(8,128)(2,1)S(1)} collective-permute-done((bf16[128,1024]{1,0:T(8,128)(2,1)S(1)}, bf16[128,1024]{1,0:T(8,128)(2,1)S(1)}, u32[]{:S(2)}, u32[]{:S(2)}) %collective-permute-start.22) | collective-permute-done | bytes 262176 | tf_op jit(solution)/shard_map/ppermute | solution.py:335
  89.2 5.5 %collective-permute-done.14.arrived = bf16[128,1024]{1,0:T(8,128)(2,1)S(1)} collective-permute-done((bf16[128,1024]{1,0:T(8,128)(2,1)S(1)}, bf16[128,1024]{1,0:T(8,128)(2,1)S(1)}, u32[]{:S(2)}, u32[]{:S(2)}) %collective-permute-start.14) | collective-permute-done | bytes 262176 | tf_op jit(solution)/shard_map/ppermute | solution.py:335
  94.8 13.9 %collective-permute-done.23.arrived = bf16[128,1024]{1,0:T(8,128)(2,1)S(1)} collective-permute-done((bf16[128,1024]{1,0:T(8,128)(2,1)S(1)}, bf16[128,1024]{1,0:T(8,128)(2,1)S(1)}, u32[]{:S(2)}, u32[]{:S(2)}) %collective-permute-start.23) | collective-permute-done | bytes 262176 | tf_op jit(solution)/shard_map/ppermute | solution.py:335
  110.3 3.0 %collective-permute-done.15.arrived = bf16[128,1024]{1,0:T(8,128)(2,1)S(1)} collective-permute-done((bf16[128,1024]{1,0:T(8,128)(2,1)S(1)}, bf16[128,1024]{1,0:T(8,128)(2,1)S(1)}, u32[]{:S(2)}, u32[]{:S(2)}) %collective-permute-start.15) | collective-permute-done | bytes 262176 | tf_op jit(solution)/shard_map/ppermute | solution.py:335
  (48 shorter events, 14.1 us)
Async XLA Ops:
  0.6 19.5 %collective-permute-start.6 = (bf16[128,2048]{1,0:T(8,128)(2,1)}, bf16[128,2048]{1,0:T(8,128)(2,1)S(1)}, u32[]{:S(2)}, u32[]{:S(2)}) collective-permute-start(bf16[128,2048]{1,0:T(8,128)(2,1)} %own.1), channel_id=1, source_target_pairs={{1,0},{0,1},{3,2},{2,3},{5,4},{4,5},{7,6},{6,7},{9,8},{8,9},{11,10... | collective-permute-start | bytes 1572872 | tf_op jit(solution)/shard_map/ppermute | solution.py:335
  0.7 21.9 %collective-permute-start.7 = (bf16[128,2048]{1,0:T(8,128)(2,1)}, bf16[128,2048]{1,0:T(8,128)(2,1)S(1)}, u32[]{:S(2)}, u32[]{:S(2)}) collective-permute-start(bf16[128,2048]{1,0:T(8,128)(2,1)} %own.1), channel_id=1, source_target_pairs={{2,0},{0,2},{3,1},{1,3},{6,4},{4,6},{7,5},{5,7},{10,8},{8,10},{11,... | collective-permute-start | bytes 1572872 | tf_op jit(solution)/shard_map/ppermute | solution.py:335
  3.0 4.6 %collective-permute-start.2 = (s32[1,8]{1,0:T(1,128)S(1)}, s32[1,8]{1,0:T(1,128)S(1)}, u32[]{:S(2)}, u32[]{:S(2)}) collective-permute-start(s32[1,8]{1,0:T(1,128)S(1)} %pad_add_fusion.refs_0_), channel_id=1, source_target_pairs={{12,0},{0,4},{4,8},{8,12},{13,1},{1,5},{5,9},{9,13},{14,2},{2,6},{... | collective-permute-start | bytes 104 | tf_op jit(solution)/shard_map/ppermute | solution.py:335
  4.6 4.4 %collective-permute-start.1 = (s32[1,8]{1,0:T(1,128)S(1)}, s32[1,8]{1,0:T(1,128)S(1)}, u32[]{:S(2)}, u32[]{:S(2)}) collective-permute-start(s32[1,8]{1,0:T(1,128)S(1)} %pad_add_fusion.refs_0_), channel_id=1, source_target_pairs={{8,0},{12,4},{0,8},{4,12},{9,1},{13,5},{1,9},{5,13},{10,2},{14,6},... | collective-permute-start | bytes 104 | tf_op jit(solution)/shard_map/ppermute | solution.py:335
  5.8 3.5 %collective-permute-start = (s32[1,8]{1,0:T(1,128)S(1)}, s32[1,8]{1,0:T(1,128)S(1)}, u32[]{:S(2)}, u32[]{:S(2)}) collective-permute-start(s32[1,8]{1,0:T(1,128)S(1)} %pad_add_fusion.refs_0_), channel_id=1, source_target_pairs={{4,0},{8,4},{12,8},{0,12},{5,1},{9,5},{13,9},{1,13},{6,2},{10,6},{... | collective-permute-start | bytes 104 | tf_op jit(solution)/shard_map/ppermute | solution.py:335
  12.0 5.6 %collective-permute-start.3 = (bf16[128,128]{1,0:T(8,128)(2,1)S(1)}, bf16[128,128]{1,0:T(8,128)(2,1)S(1)}, u32[]{:S(2)}, u32[]{:S(2)}) collective-permute-start(bf16[128,128]{1,0:T(8,128)(2,1)S(1)} %get-tuple-element.52), channel_id=1, source_target_pairs={{12,0},{0,4},{4,8},{8,12},{13,1},{1,5},{5,9},{9,13},{14,2},{2,6},{... | collective-permute-start | bytes 98312 | tf_op jit(solution)/shard_map/ppermute | solution.py:335
  13.3 5.3 %collective-permute-start.4 = (bf16[128,128]{1,0:T(8,128)(2,1)S(1)}, bf16[128,128]{1,0:T(8,128)(2,1)S(1)}, u32[]{:S(2)}, u32[]{:S(2)}) collective-permute-start(bf16[128,128]{1,0:T(8,128)(2,1)S(1)} %get-tuple-element.53), channel_id=1, source_target_pairs={{8,0},{12,4},{0,8},{4,12},{9,1},{13,5},{1,9},{5,13},{10,2},{14,6},... | collective-permute-start | bytes 98312 | tf_op jit(solution)/shard_map/ppermute | solution.py:335
  16.2 3.9 %collective-permute-start.5 = (bf16[128,128]{1,0:T(8,128)(2,1)S(1)}, bf16[128,128]{1,0:T(8,128)(2,1)S(1)}, u32[]{:S(2)}, u32[]{:S(2)}) collective-permute-start(bf16[128,128]{1,0:T(8,128)(2,1)S(1)} %get-tuple-element.54), channel_id=1, source_target_pairs={{4,0},{8,4},{12,8},{0,12},{5,1},{9,5},{13,9},{1,13},{6,2},{10,6},{... | collective-permute-start | bytes 98312 | tf_op jit(solution)/shard_map/ppermute | solution.py:335
  17.6 5.0 %collective-permute-start.8 = (bf16[4,128,128]{2,1,0:T(8,128)(2,1)S(1)}, bf16[4,128,128]{2,1,0:T(8,128)(2,1)S(1)}, u32[]{:S(2)}, u32[]{:S(2)}) collective-permute-start(bf16[4,128,128]{2,1,0:T(8,128)(2,1)S(1)} %get-tuple-element.57), channel_id=1, source_target_pairs={{12,0},{0,4},{4,8},{8,12},{13,1},{1,5},{5,9},{9,13},{14,2},{2,6},{... | collective-permute-start | bytes 393224 | tf_op jit(solution)/shard_map/ppermute | solution.py:335
  22.6 3.9 %collective-permute-start.9 = (bf16[128,2048]{1,0:T(8,128)(2,1)S(1)}, bf16[128,2048]{1,0:T(8,128)(2,1)S(1)}, u32[]{:S(2)}, u32[]{:S(2)}) collective-permute-start(bf16[128,2048]{1,0:T(8,128)(2,1)S(1)} %collective-permute-done.7.refs_1_), channel_id=1, source_target_pairs={{1,0},{0,1},{3,2},{2,3},{5,4},{4,5},{7,6},{6,7},{9,8},{8,9},{11,10... | collective-permute-start | bytes 1572872 | tf_op jit(solution)/shard_map/ppermute | solution.py:335
  22.6 11.4 %collective-permute-start.10 = (bf16[4,128,128]{2,1,0:T(8,128)(2,1)S(1)}, bf16[4,128,128]{2,1,0:T(8,128)(2,1)S(1)}, u32[]{:S(2)}, u32[]{:S(2)}) collective-permute-start(bf16[4,128,128]{2,1,0:T(8,128)(2,1)S(1)} %get-tuple-element.61), channel_id=1, source_target_pairs={{8,0},{12,4},{0,8},{4,12},{9,1},{13,5},{1,9},{5,13},{10,2},{14,6},... | collective-permute-start | bytes 393224 | tf_op jit(solution)/shard_map/ppermute | solution.py:335
  25.0 10.1 %collective-permute-start.11 = (bf16[4,128,128]{2,1,0:T(8,128)(2,1)S(1)}, bf16[4,128,128]{2,1,0:T(8,128)(2,1)S(1)}, u32[]{:S(2)}, u32[]{:S(2)}) collective-permute-start(bf16[4,128,128]{2,1,0:T(8,128)(2,1)S(1)} %get-tuple-element.62), channel_id=1, source_target_pairs={{4,0},{8,4},{12,8},{0,12},{5,1},{9,5},{13,9},{1,13},{6,2},{10,6},{... | collective-permute-start | bytes 393224 | tf_op jit(solution)/shard_map/ppermute | solution.py:335
  35.1 10.5 %collective-permute-start.12 = (bf16[128,1024]{1,0:T(8,128)(2,1)S(1)}, bf16[128,1024]{1,0:T(8,128)(2,1)S(1)}, u32[]{:S(2)}, u32[]{:S(2)}) collective-permute-start(bf16[128,1024]{1,0:T(8,128)(2,1)S(1)} %get-tuple-element.65), channel_id=1, source_target_pairs={{12,0},{0,4},{4,8},{8,12},{13,1},{1,5},{5,9},{9,13},{14,2},{2,6},{... | collective-permute-start | bytes 786440 | tf_op jit(solution)/shard_map/ppermute | solution.py:335
  41.1 30.1 %collective-permute-start.16 = (bf16[128,1536]{1,0:T(8,128)(2,1)S(1)}, bf16[128,1536]{1,0:T(8,128)(2,1)S(1)}, u32[]{:S(2)}, u32[]{:S(2)}) collective-permute-start(bf16[128,1536]{1,0:T(8,128)(2,1)S(1)} %get-tuple-element.78), channel_id=1, source_target_pairs={{12,0},{0,4},{4,8},{8,12},{13,1},{1,5},{5,9},{9,13},{14,2},{2,6},{... | collective-permute-start | bytes 1179656 | tf_op jit(solution)/shard_map/ppermute | solution.py:335
  45.7 9.3 %collective-permute-start.17 = (bf16[128,128]{1,0:T(8,128)(2,1)S(1)}, bf16[128,128]{1,0:T(8,128)(2,1)S(1)}, u32[]{:S(2)}, u32[]{:S(2)}) collective-permute-start(bf16[128,128]{1,0:T(8,128)(2,1)S(1)} %get-tuple-element.80), channel_id=1, source_target_pairs={{12,0},{0,4},{4,8},{8,12},{13,1},{1,5},{5,9},{9,13},{14,2},{2,6},{... | collective-permute-start | bytes 98312 | tf_op jit(solution)/shard_map/ppermute | solution.py:335
  45.8 10.4 %collective-permute-start.18 = (bf16[128,128]{1,0:T(8,128)(2,1)S(1)}, bf16[128,128]{1,0:T(8,128)(2,1)S(1)}, u32[]{:S(2)}, u32[]{:S(2)}) collective-permute-start(bf16[128,128]{1,0:T(8,128)(2,1)S(1)} %get-tuple-element.81), channel_id=1, source_target_pairs={{8,0},{12,4},{0,8},{4,12},{9,1},{13,5},{1,9},{5,13},{10,2},{14,6},... | collective-permute-start | bytes 98312 | tf_op jit(solution)/shard_map/ppermute | solution.py:335
  47.5 23.7 %collective-permute-start.19 = (bf16[128,128]{1,0:T(8,128)(2,1)S(1)}, bf16[128,128]{1,0:T(8,128)(2,1)S(1)}, u32[]{:S(2)}, u32[]{:S(2)}) collective-permute-start(bf16[128,128]{1,0:T(8,128)(2,1)S(1)} %get-tuple-element.82), channel_id=1, source_target_pairs={{4,0},{8,4},{12,8},{0,12},{5,1},{9,5},{13,9},{1,13},{6,2},{10,6},{... | collective-permute-start | bytes 98312 | tf_op jit(solution)/shard_map/ppermute | solution.py:335
  54.2 17.3 %collective-permute-start.13 = (bf16[128,1024]{1,0:T(8,128)(2,1)S(1)}, bf16[128,1024]{1,0:T(8,128)(2,1)S(1)}, u32[]{:S(2)}, u32[]{:S(2)}) collective-permute-start(bf16[128,1024]{1,0:T(8,128)(2,1)S(1)} %get-tuple-element.76), channel_id=1, source_target_pairs={{12,0},{0,4},{4,8},{8,12},{13,1},{1,5},{5,9},{9,13},{14,2},{2,6},{... | collective-permute-start | bytes 786440 | tf_op jit(solution)/shard_map/ppermute | solution.py:335
  71.4 12.0 %collective-permute-start.20 = (bf16[128,1536]{1,0:T(8,128)(2,1)S(1)}, bf16[128,1536]{1,0:T(8,128)(2,1)S(1)}, u32[]{:S(2)}, u32[]{:S(2)}) collective-permute-start(bf16[128,1536]{1,0:T(8,128)(2,1)S(1)} %add.11), channel_id=1, source_target_pairs={{12,0},{0,4},{4,8},{8,12},{13,1},{1,5},{5,9},{9,13},{14,2},{2,6},{... | collective-permute-start | bytes 1179656 | tf_op jit(solution)/shard_map/ppermute | solution.py:335
  71.4 17.6 %collective-permute-start.22 = (bf16[128,1024]{1,0:T(8,128)(2,1)S(1)}, bf16[128,1024]{1,0:T(8,128)(2,1)S(1)}, u32[]{:S(2)}, u32[]{:S(2)}) collective-permute-start(bf16[128,1024]{1,0:T(8,128)(2,1)S(1)} %add.8), channel_id=1, source_target_pairs={{12,0},{0,4},{4,8},{8,12},{13,1},{1,5},{5,9},{9,13},{14,2},{2,6},{... | collective-permute-start | bytes 786440 | tf_op jit(solution)/shard_map/ppermute | solution.py:335
  71.6 23.0 %collective-permute-start.14 = (bf16[128,1024]{1,0:T(8,128)(2,1)S(1)}, bf16[128,1024]{1,0:T(8,128)(2,1)S(1)}, u32[]{:S(2)}, u32[]{:S(2)}) collective-permute-start(bf16[128,1024]{1,0:T(8,128)(2,1)S(1)} %add.9), channel_id=1, source_target_pairs={{12,0},{0,4},{4,8},{8,12},{13,1},{1,5},{5,9},{9,13},{14,2},{2,6},{... | collective-permute-start | bytes 786440 | tf_op jit(solution)/shard_map/ppermute | solution.py:335
  83.5 26.0 %collective-permute-start.21 = (bf16[128,1536]{1,0:T(8,128)(2,1)S(1)}, bf16[128,1536]{1,0:T(8,128)(2,1)S(1)}, u32[]{:S(2)}, u32[]{:S(2)}) collective-permute-start(bf16[128,1536]{1,0:T(8,128)(2,1)S(1)} %add.12), channel_id=1, source_target_pairs={{12,0},{0,4},{4,8},{8,12},{13,1},{1,5},{5,9},{9,13},{14,2},{2,6},{... | collective-permute-start | bytes 1179656 | tf_op jit(solution)/shard_map/ppermute | solution.py:335
  89.1 19.6 %collective-permute-start.23 = (bf16[128,1024]{1,0:T(8,128)(2,1)S(1)}, bf16[128,1024]{1,0:T(8,128)(2,1)S(1)}, u32[]{:S(2)}, u32[]{:S(2)}) collective-permute-start(bf16[128,1024]{1,0:T(8,128)(2,1)S(1)} %add.13), channel_id=1, source_target_pairs={{12,0},{0,4},{4,8},{8,12},{13,1},{1,5},{5,9},{9,13},{14,2},{2,6},{... | collective-permute-start | bytes 786440 | tf_op jit(solution)/shard_map/ppermute | solution.py:335
  94.7 18.6 %collective-permute-start.15 = (bf16[128,1024]{1,0:T(8,128)(2,1)S(1)}, bf16[128,1024]{1,0:T(8,128)(2,1)S(1)}, u32[]{:S(2)}, u32[]{:S(2)}) collective-permute-start(bf16[128,1024]{1,0:T(8,128)(2,1)S(1)} %add.10), channel_id=1, source_target_pairs={{12,0},{0,4},{4,8},{8,12},{13,1},{1,5},{5,9},{9,13},{14,2},{2,6},{... | collective-permute-start | bytes 786440 | tf_op jit(solution)/shard_map/ppermute | solution.py:335
  (3 other events, 88.3 us)

commit v5 on v4

--- a/solution.py
+++ b/solution.py
@@ -34,6 +34,10 @@
     return pltpu.with_memory_space_constraint(array, pltpu.HBM)
 
 
+def cost(count):
+    return pl.CostEstimate(flops=count, bytes_accessed=2 * count, transcendentals=0)
+
+
 def params():
     return pltpu.CompilerParams(vmem_limit_bytes=VMEM_LIMIT)
 
@@ -42,73 +46,46 @@
     return lax.rem(index + size, size)
 
 
-class Lists:
-    def __init__(self, rows, spans, slots):
-        self.rows, self.spans, self.slots = rows, spans, slots
-        self.me = lax.axis_index("seq")
-        self.counts = []
-        for s in range(spans):
-            count = self.live(s, 0)
-            for slot in range(1, slots):
-                count = count + self.live(s, slot)
-            self.counts.append(count)
-
-    def tile(self, s, slot):
-        ref, row = self.rows[s]
-        return ref[row, slot]
-
-    def live(self, s, slot):
-        ref, row = self.rows[s]
-        return ref[row, self.slots + slot]
-
-    def region(self, s):
-        return lax.rem(self.me + s, self.spans)
-
-    def before(self, s):
-        region, before = self.region(s), jnp.int32(0)
-        for other in range(self.spans):
-            before = before + jnp.where(self.region(other) < region, self.counts[other], 0)
-        return before
-
-
-def table_lists(table, spans, slots):
-    return Lists([(table, s) for s in range(spans)], spans, slots)
-
-
-def pick_kernel(spans, slots, block, d_blocks, *refs):
-    metas, (values, hidden, table), refs = refs[:spans], refs[spans : spans + 3], refs[spans + 3 :]
-    value_outs, hidden_outs = refs[:spans], refs[spans : 2 * spans]
-    tiles, value_sems, hidden_sems = refs[2 * spans :]
-    lists = Lists([(meta, 0) for meta in metas], spans, slots)
-    lives, value_copies, hidden_copies = [], [], []
-    for s in range(spans):
-        before = lists.before(s)
-        slot = wrap(lists.me - lax.rem(before, spans), spans)
-        lives.append(slot < lists.counts[s])
-        owned = jnp.minimum(lax.div(before + slot, spans), slots - 1)
-        copy = pltpu.make_async_copy(values.at[owned], tiles.at[s], value_sems.at[s])
-        copy.start()
-        value_copies.append(copy)
+def live_count(table, region, slots):
+    count = table[region, slots]
+    for slot in range(1, slots):
+        count = count + table[region, slots + slot]
+    return count
+
+
+def rank_before(table, region, spans, slots):
+    before = jnp.int32(0)
+    for other in range(spans):
+        before = before + jnp.where(other < region, live_count(table, other, slots), 0)
+    return before
+
+
+def early_kernel(values, hidden, values_half, hidden_here, stored, sems):
+    value_copy = pltpu.make_async_copy(values, stored, sems.at[0])
+    hidden_copy = pltpu.make_async_copy(hidden, hidden_here, sems.at[1])
+    value_copy.start()
+    hidden_copy.start()
+    value_copy.wait()
+    values_half[...] = stored[...].astype(values_half.dtype)
+    hidden_copy.wait()
+
+
+def pick_kernel(slots, block, d_blocks, table, hidden, *outs):
+    spans = len(outs)
+    me = lax.axis_index("seq")
     for s in range(spans):
         for j in range(slots):
-            start = pl.multiple_of(lax.div(lists.tile(s, j), d_blocks) * block, block)
-            copy = pltpu.make_async_copy(
-                hidden.at[:, pl.ds(start, block)], hidden_outs[s].at[j], hidden_sems.at[s, j]
-            )
-            copy.start()
-            hidden_copies.append(copy)
-        for j in range(2 * slots):
-            table[s, j] = metas[s][0, j]
-    for s in range(spans):
-        value_copies[s].wait()
-        tile = tiles[s]
-        value_outs[s][...] = jnp.where(lives[s], tile, jnp.zeros_like(tile)).astype(jnp.bfloat16)
-    for copy in hidden_copies:
-        copy.wait()
-
-
-def lay_kernel(own, weight, *refs):
-    others, (rows, first_weight, sems) = refs[:-3], refs[-3:]
+            tile = table[lax.rem(me + s, spans), j]
+            start = pl.multiple_of(lax.div(tile, d_blocks) * block, block)
+            outs[s][j] = hidden[:, pl.ds(start, block)]
+
+
+def lay_kernel(spans, slots, table, own, weight, *refs):
+    others, stored, (rows, first_weight, held, sems) = (
+        refs[: -4 - spans],
+        refs[-4 - spans : -4],
+        refs[-4:],
+    )
     chunk = own.shape[0]
     weight_copy = pltpu.make_async_copy(
         weight.at[pl.ds(0, first_weight.shape[0])], first_weight, sems.at[0]
@@ -118,6 +95,18 @@
     own_copy.start()
     for p, other in enumerate(others):
         rows[(p + 1) * chunk : (p + 2) * chunk] = other[...]
+    me = lax.axis_index("seq")
+    before = rank_before(table, me, spans, slots)
+    for j in range(slots):
+        rank = before + j
+        owned = jnp.minimum(lax.div(rank, spans), slots - 1)
+        place = wrap(lax.rem(rank, spans) - me, spans)
+        for s in range(spans):
+
+            @pl.when(place == s)
+            def _():
+                held[j] = stored[s][owned]
+
     own_copy.wait()
     weight_copy.wait()
 
@@ -148,25 +137,24 @@
     here = pl.ds(pl.multiple_of(step * width, width), width)
     weights = weight[here] if weight.shape[0] > width else weight[...]
     total[...] = lax.dot_general(rows[...], weights, NT, preferred_element_type=jnp.float32)
-    lists = table_lists(table, spans, slots)
-    before = lists.before(0)
+    me = lax.axis_index("seq")
+    count = live_count(table, me, slots)
     for j in range(slots):
-        tile = lists.tile(0, j)
+        tile = table[me, j]
         f_start = lax.div(tile, d_blocks) * block - (low + step) * width
 
-        @pl.when((j < lists.counts[0]) & (f_start >= 0) & (f_start < width))
+        @pl.when((j < count) & (f_start >= 0) & (f_start < width))
         def _():
             d_start = pl.multiple_of(lax.rem(tile, d_blocks) * block, block)
             place = pl.ds(pl.multiple_of(f_start, block), block)
-            owner = lax.rem(before + j, spans)
             total[:, place] += lax.dot_general(
                 rows[:, pl.ds(d_start, block)],
-                held[wrap(lists.me - owner, spans)],
+                held[j],
                 NT,
                 preferred_element_type=jnp.float32,
             )
 
-    first_chunk = wrap(lists.me - 1, spans)
+    first_chunk = wrap(me - 1, spans)
     for p in range(spans):
         result = total[p * chunk : (p + 1) * chunk].astype(out.dtype)
         out[chunk_at(p), :, here] = result
@@ -221,6 +209,7 @@
         in_specs=[vmem(), vmem()],
         out_specs=vmem(),
         compiler_params=params(),
+        cost_estimate=cost(arrived.size),
         name="add",
     )(partials, arrived)
 
@@ -246,28 +235,29 @@
         scratch_shapes=[pltpu.VMEM((chunk, columns), shape.dtype), pltpu.SemaphoreType.DMA],
         input_output_aliases={2: 0} if given else {},
         compiler_params=params(),
+        cost_estimate=cost(arrived.size),
         name="last_sum",
     )(partials, arrived, *given)
 
 
 def grad_kernel(spans, slots, block, d_blocks, table, rows, *refs):
     hidden, outs, (cols,) = refs[:spans], refs[spans : 2 * spans], refs[2 * spans :]
-    lists = table_lists(table, spans, slots)
-    before = lists.before(0)
+    me = lax.axis_index("seq")
+    count, before = live_count(table, me, slots), rank_before(table, me, spans, slots)
     chunk = rows.shape[0] // spans
     for s in range(spans):
         cols[s] = hidden[s][...]
     for s in range(spans):
-        slot = wrap(lists.region(s) - lax.rem(before, spans), spans)
+        slot = wrap(lax.rem(me + s, spans) - lax.rem(before, spans), spans)
         outs[s][...] = jnp.zeros_like(outs[s])
 
-        @pl.when(slot < lists.counts[0])
+        @pl.when(slot < count)
         def _():
-            d_start = pl.multiple_of(lax.rem(table[0, slot], d_blocks) * block, block)
+            d_start = pl.multiple_of(lax.rem(table[me, slot], d_blocks) * block, block)
             total = jnp.zeros((block, block), jnp.float32)
             for p in range(spans):
                 total = total + lax.dot_general(
-                    cols[wrap(lists.me - chunk_at(p), spans), slot],
+                    cols[wrap(me - chunk_at(p), spans), slot],
                     rows[p * chunk : (p + 1) * chunk, pl.ds(d_start, block)],
                     TN,
                     preferred_element_type=jnp.float32,
@@ -285,6 +275,7 @@
         out_specs=[vmem()] * spans,
         scratch_shapes=[pltpu.VMEM((spans, slots, chunk, block), jnp.bfloat16)],
         compiler_params=params(),
+        cost_estimate=cost(rows.size),
         name="tile_grad",
     )(table, rows, *hidden_cols)
 
@@ -292,17 +283,18 @@
 def adam_kernel(spans, slots, table, *refs):
     arrived, refs = refs[:spans], refs[spans:]
     values, one, two, values_new, one_new, two_new, grads = refs
-    lists = table_lists(table, spans, slots)
+    me = lax.axis_index("seq")
     for s in range(spans):
         grads[s] = arrived[s][...]
-    befores = [lists.before(s) for s in range(spans)]
+    befores = [rank_before(table, region, spans, slots) for region in range(spans)]
+    total = befores[-1] + live_count(table, spans - 1, slots)
     for owned in range(slots):
-        rank = owned * spans + lists.me
-        live, source = jnp.bool_(False), jnp.int32(0)
-        for s in range(spans):
-            holds = (befores[s] <= rank) & (rank < befores[s] + lists.counts[s])
-            live, source = live | holds, jnp.where(holds, (spans - s) % spans, source)
-        grad = grads[source].astype(jnp.float32)
+        rank = owned * spans + me
+        source = jnp.int32(0)
+        for region in range(1, spans):
+            source = jnp.where(befores[region] <= rank, region, source)
+        live = rank < total
+        grad = grads[wrap(me - source, spans)].astype(jnp.float32)
         stored, old_one, old_two = values[owned], one[owned], two[owned]
         new_one = BETA_ONE * old_one + (1.0 - BETA_ONE) * grad
         new_two = BETA_TWO * old_two + (1.0 - BETA_TWO) * grad * grad
@@ -326,6 +318,7 @@
         out_specs=(vmem(), vmem(), vmem()),
         scratch_shapes=[pltpu.VMEM((spans, block, block), jnp.bfloat16)],
         compiler_params=params(),
+        cost_estimate=cost(slots * block * block),
         name="adam",
     )(table, *grads, *[state[0, 0] for state in states])
 
@@ -356,55 +349,70 @@
 
     firsts = [take_from(cotangent, "tensor", t) for t in range(1, lax.axis_size("tensor"))]
     local = [take_from(cotangent, "dp", d) for d in range(1, cores)]
-    meta = jnp.concatenate([tile_ids[0], tile_live[0]], axis=1)
-    metas = [meta] + [take_from(meta, "seq", s) for s in range(1, spans)]
-
-    value_tile = jax.ShapeDtypeStruct((block, block), jnp.bfloat16)
-    hidden_tiles = jax.ShapeDtypeStruct((slots, chunk, block), jnp.bfloat16)
-    table, *picked = pl.pallas_call(
-        functools.partial(pick_kernel, *sizes),
-        out_shape=[jax.ShapeDtypeStruct((spans, 2 * slots), jnp.int32)]
-        + [value_tile] * spans
-        + [hidden_tiles] * spans,
-        in_specs=[smem()] * spans + [hbm(), hbm()],
-        out_specs=[smem()] + [vmem()] * (2 * spans),
+
+    values_half, hidden_here = pl.pallas_call(
+        early_kernel,
+        out_shape=[
+            jax.ShapeDtypeStruct((slots, block, block), jnp.bfloat16),
+            jax.ShapeDtypeStruct(hidden_in.shape, hidden_in.dtype),
+        ],
+        in_specs=[hbm(), hbm()],
+        out_specs=[vmem(), vmem()],
         scratch_shapes=[
-            pltpu.VMEM((spans, block, block), jnp.float32),
-            pltpu.SemaphoreType.DMA((spans,)),
-            pltpu.SemaphoreType.DMA((spans, slots)),
+            pltpu.VMEM((slots, block, block), jnp.float32),
+            pltpu.SemaphoreType.DMA((2,)),
         ],
         compiler_params=params(),
+        cost_estimate=cost(hidden_in.size),
+        name="early",
+    )(stay(values[0, 0]), stay(hidden_in))
+    stored = [values_half] + [take_from(values_half, "seq", s) for s in range(1, spans)]
+
+    ids, values_half = lax.optimization_barrier((tile_ids[0], values_half))
+    table = jnp.concatenate([ids, tile_live[0]], axis=1)
+    table = lax.all_gather(table, "seq", axis=0, tiled=True)
+    table, stored = lax.optimization_barrier((table, stored))
+    picked = pl.pallas_call(
+        functools.partial(pick_kernel, slots, block, d_blocks),
+        out_shape=[jax.ShapeDtypeStruct((slots, chunk, block), jnp.bfloat16)] * spans,
+        in_specs=[smem(), vmem()],
+        out_specs=[vmem()] * spans,
+        compiler_params=params(),
+        cost_estimate=cost(hidden_in.size),
         name="pick",
-    )(*metas, stay(values[0, 0]), stay(hidden_in))
-    held = jnp.stack(exchange(picked[:spans]))
-    hidden_cols = exchange(picked[spans:])
-
-    local_rows, first_weight = pl.pallas_call(
-        lay_kernel,
+    )(table, hidden_here)
+    hidden_cols = exchange(picked)
+
+    stored, hidden_cols[1] = lax.optimization_barrier((stored, hidden_cols[1]))
+    local_rows, first_weight, held = pl.pallas_call(
+        functools.partial(lay_kernel, spans, slots),
         out_shape=[
             jax.ShapeDtypeStruct((cores * chunk, d_width), cotangent.dtype),
             jax.ShapeDtypeStruct((ranges[0][1] * width, d_width), down_weight.dtype),
+            jax.ShapeDtypeStruct((slots, block, block), jnp.bfloat16),
         ],
-        in_specs=[hbm(), hbm()] + [vmem()] * (cores - 1),
-        out_specs=[vmem(), vmem()],
+        in_specs=[smem(), hbm(), hbm()] + [vmem()] * (cores - 1 + spans),
+        out_specs=[vmem()] * 3,
         scratch_shapes=[pltpu.SemaphoreType.DMA((2,))],
         compiler_params=params(),
+        cost_estimate=cost(cores * chunk * d_width),
         name="lay",
-    )(stay(cotangent), stay(down_weight), *local)
-
-    firsts, *_ = lax.optimization_barrier((firsts, held, hidden_cols[1], local_rows, first_weight))
+    )(table, stay(cotangent), stay(down_weight), *local, *stored)
+
+    firsts, picked = lax.optimization_barrier((firsts, picked))
     pieces = [local_rows]
     for first in firsts:
         pieces += [first] + [take_from(first, "dp", d) for d in range(1, cores)]
 
     partials, moving = [], []
     for part, (low, high) in enumerate(ranges):
+        if part == 0:
+            pieces, hidden_cols[-1] = lax.optimization_barrier((pieces, hidden_cols[-1]))
         if part == 1:
             rows, hidden_cols = lax.optimization_barrier((rows, hidden_cols))
         if part == 2:
             moving[0] = add_call(2, partials[0], moving[0])
-            send = grad_call(sizes, table, rows, hidden_cols)
-            rows, moving[0], send = lax.optimization_barrier((rows, moving[0], send))
+            rows, moving[0] = lax.optimization_barrier((rows, moving[0]))
         weight = down_weight if part else first_weight
         partial, first, *more = matmul_call(
             sizes, low, high, width, table, held, weight, [rows] if part else pieces
@@ -413,17 +421,16 @@
         partials.append(partial)
         moving.append(take_from(first, "seq", -1))
 
-    grads = exchange(send)
+    grads = exchange(grad_call(sizes, table, rows, hidden_cols))
     for t in range(2, spans):
         for part in range(len(ranges)):
-            if (t, part) == (2, 1):
+            if (t, part) == (spans - 1, len(ranges) - 1):
                 moving[part], grads = lax.optimization_barrier((moving[part], grads))
-                new = adam_call(sizes, table, grads, values, moment_one, moment_two)
-            if (t, part) == (spans - 1, 0):
-                moving[part], new = lax.optimization_barrier((moving[part], new))
             if (t, part) != (2, 0):
                 moving[part] = add_call(t, partials[part], moving[part])
             moving[part] = take_from(moving[part], "seq", -1)
+
+    new = adam_call(sizes, table, grads, values, moment_one, moment_two)
 
     hidden_grad = None
     shape = jax.ShapeDtypeStruct((chunk, f_width), jnp.bfloat16)

time: 114 us -> 108 us (0.947)
  the two profiles are of different devices: /device:TPU:12 before, /device:TPU:0 now
where the time goes in v5:
time: 108 us; the launch traced here: 107 us
  waiting for transfers between devices  37 us (34%)
  starting transfers between devices  35.1 us (32%)
  Pallas kernels  24.4 us (23%)
  blocking collectives  9.29 us (9%)
    ppermute x21, waiting for transfers between devices, take_from(): lax.ppermute(array, axis, [((i + places) % size, i) for i in range(size)])  37 us
    ppermute x21, starting transfers between devices, take_from(): lax.ppermute(array, axis, [((i + places) % size, i) for i in range(size)])  35.1 us
    pallas_call x3, Pallas kernels, matmul_call(): pl.pallas_call(functools.partial(matmul_kernel, sizes, low, width, len(pi...  14.1 us
    all_gather x1, blocking collectives, per_device(): table = lax.all_gather(table, 'seq', axis=0, tiled=True)  9.29 us
    pallas_call x1, Pallas kernels, per_device(): pl.pallas_call(functools.partial(lay_kernel, spans, slots), out_shape=[ja...  2.89 us
    pallas_call x3, Pallas kernels, last_call(): pl.pallas_call(functools.partial(last_kernel, low), out_shape=shape, in_s...  2.42 us
  transfers between devices with their start and end apart: 21, of which 9 were waited for; matrix products, arithmetic and copies ran while one was open for 1% of the time, Pallas kernels for 22%

profile of v5, /device:TPU:0, one launch (start us, length us, event | category | flops | bytes accessed | tf_op | source)
XLA Modules:
  0.0 107.3 jit_solution(6131839941284806087)
XLA Ops:
  0.6 3.0 %collective-permute-start.5 = (bf16[128,2048]{1,0:T(8,128)(2,1)}, bf16[128,2048]{1,0:T(8,128)(2,1)S(1)}, u32[]{:S(2)}, u32[]{:S(2)}) collective-permute-start(bf16[128,2048]{1,0:T(8,128)(2,1)} %own.1), channel_id=1, source_target_pairs={{2,0},{0,2},{3,1},{1,3},{6,4},{4,6},{7,5},{5,7},{10,8},{8,10},{11,... | collective-permute-start | bytes 1572872 | tf_op jit(solution)/shard_map/ppermute | solution.py:328
  4.9 1.6 %collective-permute-start.2 = (bf16[4,128,128]{2,1,0:T(8,128)(2,1)S(1)}, bf16[4,128,128]{2,1,0:T(8,128)(2,1)S(1)}, u32[]{:S(2)}, u32[]{:S(2)}) collective-permute-start(bf16[4,128,128]{2,1,0:T(8,128)(2,1)S(1)} %get-tuple-element.64.refs_1_), channel_id=1, source_target_pairs={{12,0},{0,4},{4,8},{8,12},{13,1},{1,5},{5,9},{9,13},{14,2},{2,6},{... | collective-permute-start | bytes 393224 | tf_op jit(solution)/shard_map/ppermute | solution.py:328
  6.6 2.6 %collective-permute-start.1 = (bf16[4,128,128]{2,1,0:T(8,128)(2,1)S(1)}, bf16[4,128,128]{2,1,0:T(8,128)(2,1)S(1)}, u32[]{:S(2)}, u32[]{:S(2)}) collective-permute-start(bf16[4,128,128]{2,1,0:T(8,128)(2,1)S(1)} %get-tuple-element.64.refs_1_), channel_id=1, source_target_pairs={{8,0},{12,4},{0,8},{4,12},{9,1},{13,5},{1,9},{5,13},{10,2},{14,6},... | collective-permute-start | bytes 393224 | tf_op jit(solution)/shard_map/ppermute | solution.py:328
  11.2 9.3 %all-gather = s32[4,1,8]{2,1,0:T(1,128)S(1)} all-gather(s32[1,1,8]{2,1,0:T(1,128)S(1)} %add_bitcast_fusion), channel_id=1, replica_groups=mesh['groups'=2,'seq'=4,'tensor'=2,'dp'=2] {'seq'}, dimensions={0}, use_global_device_ids=true | all-gather | bytes 160 | tf_op jit(solution)/shard_map/all_gather | solution.py:373
  21.4 1.7 %collective-permute-start.4 = (bf16[4,128,128]{2,1,0:T(8,128)(2,1)S(1)}, bf16[4,128,128]{2,1,0:T(8,128)(2,1)S(1)}, u32[]{:S(2)}, u32[]{:S(2)}) collective-permute-start(bf16[4,128,128]{2,1,0:T(8,128)(2,1)S(1)} %get-tuple-element.63), channel_id=1, source_target_pairs={{12,0},{0,4},{4,8},{8,12},{13,1},{1,5},{5,9},{9,13},{14,2},{2,6},{... | collective-permute-start | bytes 393224 | tf_op jit(solution)/shard_map/ppermute | solution.py:328
  23.1 2.1 %collective-permute-start.7 = (bf16[4,128,128]{2,1,0:T(8,128)(2,1)S(1)}, bf16[4,128,128]{2,1,0:T(8,128)(2,1)S(1)}, u32[]{:S(2)}, u32[]{:S(2)}) collective-permute-start(bf16[4,128,128]{2,1,0:T(8,128)(2,1)S(1)} %get-tuple-element.73), channel_id=1, source_target_pairs={{4,0},{8,4},{12,8},{0,12},{5,1},{9,5},{13,9},{1,13},{6,2},{10,6},{... | collective-permute-start | bytes 393224 | tf_op jit(solution)/shard_map/ppermute | solution.py:328
  25.2 1.6 %collective-permute-start.8 = (bf16[4,128,128]{2,1,0:T(8,128)(2,1)S(1)}, bf16[4,128,128]{2,1,0:T(8,128)(2,1)S(1)}, u32[]{:S(2)}, u32[]{:S(2)}) collective-permute-start(bf16[4,128,128]{2,1,0:T(8,128)(2,1)S(1)} %get-tuple-element.72), channel_id=1, source_target_pairs={{8,0},{12,4},{0,8},{4,12},{9,1},{13,5},{1,9},{5,13},{10,2},{14,6},... | collective-permute-start | bytes 393224 | tf_op jit(solution)/shard_map/ppermute | solution.py:328
  26.8 2.7 %collective-permute-done.4.refs_1_ = bf16[4,128,128]{2,1,0:T(8,128)(2,1)S(1)} collective-permute-done((bf16[4,128,128]{2,1,0:T(8,128)(2,1)S(1)}, bf16[4,128,128]{2,1,0:T(8,128)(2,1)S(1)}, u32[]{:S(2)}, u32[]{:S(2)}) %collective-permute-start.4) | collective-permute-done | bytes 131104 | tf_op jit(solution)/shard_map/ppermute | solution.py:328
  29.5 2.9 %lay.1 = (bf16[256,2048]{1,0:T(8,128)(2,1)S(1)}, bf16[1024,2048]{1,0:T(8,128)(2,1)S(1)}, bf16[4,128,128]{2,1,0:T(8,128)(2,1)S(1)}) custom-call(s32[4,8]{1,0:T(4,128)S(1)} %bitcast.16, bf16[128,2048]{1,0:T(8,128)(2,1)} %own.1, bf16[3584,2048]{1,0:T(8,128)(2,1)} %weight.5, bf16[128,2048]{1,0:T(8,128)(2,1)S(1)} %collective-permute-done.3.refs_0_, ...), custom_call_target="tpu_custom_call" | custom-call | flops 524288 | bytes 1048576 | tf_op jit(solution)/shard_map/lay/pallas_call | solution.py:387
  32.4 3.6 %partial.3 = (bf16[4,128,1024]{2,1,0:T(8,128)(2,1)S(1)}, bf16[128,1024]{1,0:T(8,128)(2,1)S(1)}, bf16[512,2048]{1,0:T(8,128)(2,1)S(1)}) custom-call(s32[4,8]{1,0:T(4,128)S(1)} %bitcast.17, bf16[4,128,128]{2,1,0:T(8,128)(2,1)S(1)} %get-tuple-element.68.held, bf16[1024,2048]{1,0:T(8,128)(2,1)S(1)} %get-tuple-element.69.weight, ...), custom_call_target="tpu_custom_call" | custom-call | flops 2147483648 | bytes 4194304 | tf_op jit(solution)/shard_map/partial/pallas_call | solution.py:181
  37.5 4.2 %collective-permute-start.9 = (bf16[128,1024]{1,0:T(8,128)(2,1)S(1)}, bf16[128,1024]{1,0:T(8,128)(2,1)S(1)}, u32[]{:S(2)}, u32[]{:S(2)}) collective-permute-start(bf16[128,1024]{1,0:T(8,128)(2,1)S(1)} %get-tuple-element.83), channel_id=1, source_target_pairs={{12,0},{0,4},{4,8},{8,12},{13,1},{1,5},{5,9},{9,13},{14,2},{2,6},{... | collective-permute-start | bytes 786440 | tf_op jit(solution)/shard_map/ppermute | solution.py:328
  41.7 6.1 %partial.5 = (bf16[4,128,1536]{2,1,0:T(8,128)(2,1)S(1)}, bf16[128,1536]{1,0:T(8,128)(2,1)S(1)}) custom-call(s32[4,8]{1,0:T(4,128)S(1)} %bitcast.18, bf16[4,128,128]{2,1,0:T(8,128)(2,1)S(1)} %get-tuple-element.68.held, bf16[3584,2048]{1,0:T(8,128)(2,1)} %weight.5, bf16[512,2048]{1,0:T(8,128)(2,1)S(1)} %get-tuple-element.84.refs_0_.rows), custom_call_target="tpu_custom_call" | custom-call | flops 3221225472 | bytes 6291456 | tf_op jit(solution)/shard_map/partial/pallas_call | solution.py:181
  47.7 2.2 %collective-permute-start.16 = (bf16[128,1536]{1,0:T(8,128)(2,1)S(1)}, bf16[128,1536]{1,0:T(8,128)(2,1)S(1)}, u32[]{:S(2)}, u32[]{:S(2)}) collective-permute-start(bf16[128,1536]{1,0:T(8,128)(2,1)S(1)} %get-tuple-element.97), channel_id=1, source_target_pairs={{12,0},{0,4},{4,8},{8,12},{13,1},{1,5},{5,9},{9,13},{14,2},{2,6},{... | collective-permute-start | bytes 1179656 | tf_op jit(solution)/shard_map/ppermute | solution.py:328
  50.0 4.5 %partial.4 = (bf16[4,128,1024]{2,1,0:T(8,128)(2,1)S(1)}, bf16[128,1024]{1,0:T(8,128)(2,1)S(1)}) custom-call(s32[4,8]{1,0:T(4,128)S(1)} %bitcast.19, bf16[4,128,128]{2,1,0:T(8,128)(2,1)S(1)} %get-tuple-element.68.held, bf16[3584,2048]{1,0:T(8,128)(2,1)} %weight.5, bf16[512,2048]{1,0:T(8,128)(2,1)S(1)} %get-tuple-element.84.refs_0_.rows), custom_call_target="tpu_custom_call" | custom-call | flops 2147483648 | bytes 4194304 | tf_op jit(solution)/shard_map/partial/pallas_call | solution.py:181
  55.1 4.4 %collective-permute-done.16.arrived = bf16[128,1536]{1,0:T(8,128)(2,1)S(1)} collective-permute-done((bf16[128,1536]{1,0:T(8,128)(2,1)S(1)}, bf16[128,1536]{1,0:T(8,128)(2,1)S(1)}, u32[]{:S(2)}, u32[]{:S(2)}) %collective-permute-start.16) | collective-permute-done | bytes 393248 | tf_op jit(solution)/shard_map/ppermute | solution.py:328
  59.6 2.5 %collective-permute-start.17 = (bf16[128,1536]{1,0:T(8,128)(2,1)S(1)}, bf16[128,1536]{1,0:T(8,128)(2,1)S(1)}, u32[]{:S(2)}, u32[]{:S(2)}) collective-permute-start(bf16[128,1536]{1,0:T(8,128)(2,1)S(1)} %add.11), channel_id=1, source_target_pairs={{12,0},{0,4},{4,8},{8,12},{13,1},{1,5},{5,9},{9,13},{14,2},{2,6},{... | collective-permute-start | bytes 1179656 | tf_op jit(solution)/shard_map/ppermute | solution.py:328
  62.7 2.9 %collective-permute-done.10.arrived = bf16[128,1024]{1,0:T(8,128)(2,1)S(1)} collective-permute-done((bf16[128,1024]{1,0:T(8,128)(2,1)S(1)}, bf16[128,1024]{1,0:T(8,128)(2,1)S(1)}, u32[]{:S(2)}, u32[]{:S(2)}) %collective-permute-start.10) | collective-permute-done | bytes 262176 | tf_op jit(solution)/shard_map/ppermute | solution.py:328
  65.7 2.1 %collective-permute-start.11 = (bf16[128,1024]{1,0:T(8,128)(2,1)S(1)}, bf16[128,1024]{1,0:T(8,128)(2,1)S(1)}, u32[]{:S(2)}, u32[]{:S(2)}) collective-permute-start(bf16[128,1024]{1,0:T(8,128)(2,1)S(1)} %add.9), channel_id=1, source_target_pairs={{12,0},{0,4},{4,8},{8,12},{13,1},{1,5},{5,9},{9,13},{14,2},{2,6},{... | collective-permute-start | bytes 786440 | tf_op jit(solution)/shard_map/ppermute | solution.py:328
  67.8 6.2 %collective-permute-done.17.arrived = bf16[128,1536]{1,0:T(8,128)(2,1)S(1)} collective-permute-done((bf16[128,1536]{1,0:T(8,128)(2,1)S(1)}, bf16[128,1536]{1,0:T(8,128)(2,1)S(1)}, u32[]{:S(2)}, u32[]{:S(2)}) %collective-permute-start.17) | collective-permute-done | bytes 393248 | tf_op jit(solution)/shard_map/ppermute | solution.py:328
  74.1 2.1 %collective-permute-start.18 = (bf16[128,1536]{1,0:T(8,128)(2,1)S(1)}, bf16[128,1536]{1,0:T(8,128)(2,1)S(1)}, u32[]{:S(2)}, u32[]{:S(2)}) collective-permute-start(bf16[128,1536]{1,0:T(8,128)(2,1)S(1)} %add.12), channel_id=1, source_target_pairs={{12,0},{0,4},{4,8},{8,12},{13,1},{1,5},{5,9},{9,13},{14,2},{2,6},{... | collective-permute-start | bytes 1179656 | tf_op jit(solution)/shard_map/ppermute | solution.py:328
  81.1 11.8 %collective-permute-done.12.refs_1_ = bf16[128,128]{1,0:T(8,128)(2,1)S(1)} collective-permute-done((bf16[128,128]{1,0:T(8,128)(2,1)S(1)}, bf16[128,128]{1,0:T(8,128)(2,1)S(1)}, u32[]{:S(2)}, u32[]{:S(2)}) %collective-permute-start.12) | collective-permute-done | bytes 32800 | tf_op jit(solution)/shard_map/ppermute | solution.py:328
  93.0 2.1 %collective-permute-start.20 = (bf16[128,1024]{1,0:T(8,128)(2,1)S(1)}, bf16[128,1024]{1,0:T(8,128)(2,1)S(1)}, u32[]{:S(2)}, u32[]{:S(2)}) collective-permute-start(bf16[128,1024]{1,0:T(8,128)(2,1)S(1)} %add.13), channel_id=1, source_target_pairs={{12,0},{0,4},{4,8},{8,12},{13,1},{1,5},{5,9},{9,13},{14,2},{2,6},{... | collective-permute-start | bytes 786440 | tf_op jit(solution)/shard_map/ppermute | solution.py:328
  96.3 1.6 %adam.1 = (f32[4,128,128]{2,1,0:T(8,128)}, f32[4,128,128]{2,1,0:T(8,128)}, f32[4,128,128]{2,1,0:T(8,128)}) custom-call(s32[4,8]{1,0:T(4,128)S(1)} %bitcast.21, bf16[128,128]{1,0:T(8,128)(2,1)S(1)} %get-tuple-element.99.refs_0_, bf16[128,128]{1,0:T(8,128)(2,1)S(1)} %collective-permute-done.12.refs_1_, bf16[128,128]{1,0:T(8,128)(2,1)S(1)} %collective-permute-done.13.refs_2_, ...), custom_call_target="tpu_custom_call" | custom-call | flops 65536 | bytes 131072 | tf_op jit(solution)/shard_map/adam/pallas_call | solution.py:314
  97.9 5.8 %collective-permute-done.20.arrived = bf16[128,1024]{1,0:T(8,128)(2,1)S(1)} collective-permute-done((bf16[128,1024]{1,0:T(8,128)(2,1)S(1)}, bf16[128,1024]{1,0:T(8,128)(2,1)S(1)}, u32[]{:S(2)}, u32[]{:S(2)}) %collective-permute-start.20) | collective-permute-done | bytes 262176 | tf_op jit(solution)/shard_map/ppermute | solution.py:328
  (43 shorter events, 16.9 us)
Async XLA Ops:
  0.6 20.6 %collective-permute-start.5 = (bf16[128,2048]{1,0:T(8,128)(2,1)}, bf16[128,2048]{1,0:T(8,128)(2,1)S(1)}, u32[]{:S(2)}, u32[]{:S(2)}) collective-permute-start(bf16[128,2048]{1,0:T(8,128)(2,1)} %own.1), channel_id=1, source_target_pairs={{2,0},{0,2},{3,1},{1,3},{6,4},{4,6},{7,5},{5,7},{10,8},{8,10},{11,... | collective-permute-start | bytes 1572872 | tf_op jit(solution)/shard_map/ppermute | solution.py:328
  4.9 15.6 %collective-permute-start.2 = (bf16[4,128,128]{2,1,0:T(8,128)(2,1)S(1)}, bf16[4,128,128]{2,1,0:T(8,128)(2,1)S(1)}, u32[]{:S(2)}, u32[]{:S(2)}) collective-permute-start(bf16[4,128,128]{2,1,0:T(8,128)(2,1)S(1)} %get-tuple-element.64.refs_1_), channel_id=1, source_target_pairs={{12,0},{0,4},{4,8},{8,12},{13,1},{1,5},{5,9},{9,13},{14,2},{2,6},{... | collective-permute-start | bytes 393224 | tf_op jit(solution)/shard_map/ppermute | solution.py:328
  6.6 14.0 %collective-permute-start.1 = (bf16[4,128,128]{2,1,0:T(8,128)(2,1)S(1)}, bf16[4,128,128]{2,1,0:T(8,128)(2,1)S(1)}, u32[]{:S(2)}, u32[]{:S(2)}) collective-permute-start(bf16[4,128,128]{2,1,0:T(8,128)(2,1)S(1)} %get-tuple-element.64.refs_1_), channel_id=1, source_target_pairs={{8,0},{12,4},{0,8},{4,12},{9,1},{13,5},{1,9},{5,13},{10,2},{14,6},... | collective-permute-start | bytes 393224 | tf_op jit(solution)/shard_map/ppermute | solution.py:328
  9.1 11.4 %collective-permute-start = (bf16[4,128,128]{2,1,0:T(8,128)(2,1)S(1)}, bf16[4,128,128]{2,1,0:T(8,128)(2,1)S(1)}, u32[]{:S(2)}, u32[]{:S(2)}) collective-permute-start(bf16[4,128,128]{2,1,0:T(8,128)(2,1)S(1)} %get-tuple-element.64.refs_1_), channel_id=1, source_target_pairs={{4,0},{8,4},{12,8},{0,12},{5,1},{9,5},{13,9},{1,13},{6,2},{10,6},{... | collective-permute-start | bytes 393224 | tf_op jit(solution)/shard_map/ppermute | solution.py:328
  11.2 18.3 %collective-permute-start.3 = (bf16[128,2048]{1,0:T(8,128)(2,1)}, bf16[128,2048]{1,0:T(8,128)(2,1)S(1)}, u32[]{:S(2)}, u32[]{:S(2)}) collective-permute-start(bf16[128,2048]{1,0:T(8,128)(2,1)} %own.1), channel_id=1, source_target_pairs={{1,0},{0,1},{3,2},{2,3},{5,4},{4,5},{7,6},{6,7},{9,8},{8,9},{11,10... | collective-permute-start | bytes 1572872 | tf_op jit(solution)/shard_map/ppermute | solution.py:328
  21.3 11.1 %collective-permute-start.6 = (bf16[128,2048]{1,0:T(8,128)(2,1)S(1)}, bf16[128,2048]{1,0:T(8,128)(2,1)S(1)}, u32[]{:S(2)}, u32[]{:S(2)}) collective-permute-start(bf16[128,2048]{1,0:T(8,128)(2,1)S(1)} %collective-permute-done.5.refs_1_), channel_id=1, source_target_pairs={{1,0},{0,1},{3,2},{2,3},{5,4},{4,5},{7,6},{6,7},{9,8},{8,9},{11,10... | collective-permute-start | bytes 1572872 | tf_op jit(solution)/shard_map/ppermute | solution.py:328
  21.4 8.1 %collective-permute-start.4 = (bf16[4,128,128]{2,1,0:T(8,128)(2,1)S(1)}, bf16[4,128,128]{2,1,0:T(8,128)(2,1)S(1)}, u32[]{:S(2)}, u32[]{:S(2)}) collective-permute-start(bf16[4,128,128]{2,1,0:T(8,128)(2,1)S(1)} %get-tuple-element.63), channel_id=1, source_target_pairs={{12,0},{0,4},{4,8},{8,12},{13,1},{1,5},{5,9},{9,13},{14,2},{2,6},{... | collective-permute-start | bytes 393224 | tf_op jit(solution)/shard_map/ppermute | solution.py:328
  23.1 9.3 %collective-permute-start.7 = (bf16[4,128,128]{2,1,0:T(8,128)(2,1)S(1)}, bf16[4,128,128]{2,1,0:T(8,128)(2,1)S(1)}, u32[]{:S(2)}, u32[]{:S(2)}) collective-permute-start(bf16[4,128,128]{2,1,0:T(8,128)(2,1)S(1)} %get-tuple-element.73), channel_id=1, source_target_pairs={{4,0},{8,4},{12,8},{0,12},{5,1},{9,5},{13,9},{1,13},{6,2},{10,6},{... | collective-permute-start | bytes 393224 | tf_op jit(solution)/shard_map/ppermute | solution.py:328
  25.2 12.2 %collective-permute-start.8 = (bf16[4,128,128]{2,1,0:T(8,128)(2,1)S(1)}, bf16[4,128,128]{2,1,0:T(8,128)(2,1)S(1)}, u32[]{:S(2)}, u32[]{:S(2)}) collective-permute-start(bf16[4,128,128]{2,1,0:T(8,128)(2,1)S(1)} %get-tuple-element.72), channel_id=1, source_target_pairs={{8,0},{12,4},{0,8},{4,12},{9,1},{13,5},{1,9},{5,13},{10,2},{14,6},... | collective-permute-start | bytes 393224 | tf_op jit(solution)/shard_map/ppermute | solution.py:328
  37.5 12.5 %collective-permute-start.9 = (bf16[128,1024]{1,0:T(8,128)(2,1)S(1)}, bf16[128,1024]{1,0:T(8,128)(2,1)S(1)}, u32[]{:S(2)}, u32[]{:S(2)}) collective-permute-start(bf16[128,1024]{1,0:T(8,128)(2,1)S(1)} %get-tuple-element.83), channel_id=1, source_target_pairs={{12,0},{0,4},{4,8},{8,12},{13,1},{1,5},{5,9},{9,13},{14,2},{2,6},{... | collective-permute-start | bytes 786440 | tf_op jit(solution)/shard_map/ppermute | solution.py:328
  47.7 11.8 %collective-permute-start.16 = (bf16[128,1536]{1,0:T(8,128)(2,1)S(1)}, bf16[128,1536]{1,0:T(8,128)(2,1)S(1)}, u32[]{:S(2)}, u32[]{:S(2)}) collective-permute-start(bf16[128,1536]{1,0:T(8,128)(2,1)S(1)} %get-tuple-element.97), channel_id=1, source_target_pairs={{12,0},{0,4},{4,8},{8,12},{13,1},{1,5},{5,9},{9,13},{14,2},{2,6},{... | collective-permute-start | bytes 1179656 | tf_op jit(solution)/shard_map/ppermute | solution.py:328
  54.5 11.1 %collective-permute-start.10 = (bf16[128,1024]{1,0:T(8,128)(2,1)S(1)}, bf16[128,1024]{1,0:T(8,128)(2,1)S(1)}, u32[]{:S(2)}, u32[]{:S(2)}) collective-permute-start(bf16[128,1024]{1,0:T(8,128)(2,1)S(1)} %get-tuple-element.86), channel_id=1, source_target_pairs={{12,0},{0,4},{4,8},{8,12},{13,1},{1,5},{5,9},{9,13},{14,2},{2,6},{... | collective-permute-start | bytes 786440 | tf_op jit(solution)/shard_map/ppermute | solution.py:328
  59.6 14.4 %collective-permute-start.17 = (bf16[128,1536]{1,0:T(8,128)(2,1)S(1)}, bf16[128,1536]{1,0:T(8,128)(2,1)S(1)}, u32[]{:S(2)}, u32[]{:S(2)}) collective-permute-start(bf16[128,1536]{1,0:T(8,128)(2,1)S(1)} %add.11), channel_id=1, source_target_pairs={{12,0},{0,4},{4,8},{8,12},{13,1},{1,5},{5,9},{9,13},{14,2},{2,6},{... | collective-permute-start | bytes 1179656 | tf_op jit(solution)/shard_map/ppermute | solution.py:328
  62.1 17.7 %collective-permute-start.19 = (bf16[128,1024]{1,0:T(8,128)(2,1)S(1)}, bf16[128,1024]{1,0:T(8,128)(2,1)S(1)}, u32[]{:S(2)}, u32[]{:S(2)}) collective-permute-start(bf16[128,1024]{1,0:T(8,128)(2,1)S(1)} %add.8), channel_id=1, source_target_pairs={{12,0},{0,4},{4,8},{8,12},{13,1},{1,5},{5,9},{9,13},{14,2},{2,6},{... | collective-permute-start | bytes 786440 | tf_op jit(solution)/shard_map/ppermute | solution.py:328
  65.7 30.6 %copy-start = (f32[1,1,4,128,128]{4,3,2,1,0:T(8,128)S(1)}, f32[1,1,4,128,128]{4,3,2,1,0:T(8,128)}, u32[]{:S(2)}) copy-start(f32[1,1,4,128,128]{4,3,2,1,0:T(8,128)} %param.13) | copy-start | bytes 786436
  65.7 30.6 %copy-start.1 = (f32[1,1,4,128,128]{4,3,2,1,0:T(8,128)S(1)}, f32[1,1,4,128,128]{4,3,2,1,0:T(8,128)}, u32[]{:S(2)}) copy-start(f32[1,1,4,128,128]{4,3,2,1,0:T(8,128)} %param.14) | copy-start | bytes 786436
  65.7 30.6 %copy-start.2 = (f32[1,1,4,128,128]{4,3,2,1,0:T(8,128)S(1)}, f32[1,1,4,128,128]{4,3,2,1,0:T(8,128)}, u32[]{:S(2)}) copy-start(f32[1,1,4,128,128]{4,3,2,1,0:T(8,128)} %param.15) | copy-start | bytes 786436
  65.7 29.3 %collective-permute-start.11 = (bf16[128,1024]{1,0:T(8,128)(2,1)S(1)}, bf16[128,1024]{1,0:T(8,128)(2,1)S(1)}, u32[]{:S(2)}, u32[]{:S(2)}) collective-permute-start(bf16[128,1024]{1,0:T(8,128)(2,1)S(1)} %add.9), channel_id=1, source_target_pairs={{12,0},{0,4},{4,8},{8,12},{13,1},{1,5},{5,9},{9,13},{14,2},{2,6},{... | collective-permute-start | bytes 786440 | tf_op jit(solution)/shard_map/ppermute | solution.py:328
  74.1 30.4 %collective-permute-start.18 = (bf16[128,1536]{1,0:T(8,128)(2,1)S(1)}, bf16[128,1536]{1,0:T(8,128)(2,1)S(1)}, u32[]{:S(2)}, u32[]{:S(2)}) collective-permute-start(bf16[128,1536]{1,0:T(8,128)(2,1)S(1)} %add.12), channel_id=1, source_target_pairs={{12,0},{0,4},{4,8},{8,12},{13,1},{1,5},{5,9},{9,13},{14,2},{2,6},{... | collective-permute-start | bytes 1179656 | tf_op jit(solution)/shard_map/ppermute | solution.py:328
  77.1 15.9 %collective-permute-start.12 = (bf16[128,128]{1,0:T(8,128)(2,1)S(1)}, bf16[128,128]{1,0:T(8,128)(2,1)S(1)}, u32[]{:S(2)}, u32[]{:S(2)}) collective-permute-start(bf16[128,128]{1,0:T(8,128)(2,1)S(1)} %get-tuple-element.92), channel_id=1, source_target_pairs={{12,0},{0,4},{4,8},{8,12},{13,1},{1,5},{5,9},{9,13},{14,2},{2,6},{... | collective-permute-start | bytes 98312 | tf_op jit(solution)/shard_map/ppermute | solution.py:328
  78.1 16.9 %collective-permute-start.13 = (bf16[128,128]{1,0:T(8,128)(2,1)S(1)}, bf16[128,128]{1,0:T(8,128)(2,1)S(1)}, u32[]{:S(2)}, u32[]{:S(2)}) collective-permute-start(bf16[128,128]{1,0:T(8,128)(2,1)S(1)} %get-tuple-element.93), channel_id=1, source_target_pairs={{8,0},{12,4},{0,8},{4,12},{9,1},{13,5},{1,9},{5,13},{10,2},{14,6},... | collective-permute-start | bytes 98312 | tf_op jit(solution)/shard_map/ppermute | solution.py:328
  79.8 15.2 %collective-permute-start.14 = (bf16[128,128]{1,0:T(8,128)(2,1)S(1)}, bf16[128,128]{1,0:T(8,128)(2,1)S(1)}, u32[]{:S(2)}, u32[]{:S(2)}) collective-permute-start(bf16[128,128]{1,0:T(8,128)(2,1)S(1)} %get-tuple-element.94), channel_id=1, source_target_pairs={{4,0},{8,4},{12,8},{0,12},{5,1},{9,5},{13,9},{1,13},{6,2},{10,6},{... | collective-permute-start | bytes 98312 | tf_op jit(solution)/shard_map/ppermute | solution.py:328
  93.0 10.8 %collective-permute-start.20 = (bf16[128,1024]{1,0:T(8,128)(2,1)S(1)}, bf16[128,1024]{1,0:T(8,128)(2,1)S(1)}, u32[]{:S(2)}, u32[]{:S(2)}) collective-permute-start(bf16[128,1024]{1,0:T(8,128)(2,1)S(1)} %add.13), channel_id=1, source_target_pairs={{12,0},{0,4},{4,8},{8,12},{13,1},{1,5},{5,9},{9,13},{14,2},{2,6},{... | collective-permute-start | bytes 786440 | tf_op jit(solution)/shard_map/ppermute | solution.py:328
  95.1 11.4 %collective-permute-start.15 = (bf16[128,1024]{1,0:T(8,128)(2,1)S(1)}, bf16[128,1024]{1,0:T(8,128)(2,1)S(1)}, u32[]{:S(2)}, u32[]{:S(2)}) collective-permute-start(bf16[128,1024]{1,0:T(8,128)(2,1)S(1)} %add.10), channel_id=1, source_target_pairs={{12,0},{0,4},{4,8},{8,12},{13,1},{1,5},{5,9},{9,13},{14,2},{2,6},{... | collective-permute-start | bytes 786440 | tf_op jit(solution)/shard_map/ppermute | solution.py:328

commit v6 on v5

v6 whole, which is shorter than its diff:
```python
import functools

import jax
import jax.numpy as jnp
from jax import lax
from jax.experimental import pallas as pl
from jax.experimental.pallas import tpu as pltpu
from jax.sharding import PartitionSpec as P

STEP = 100
BETA_ONE = 0.9
BETA_TWO = 0.999
RATE = 0.01
EPSILON = 1e-08
VMEM_LIMIT = 24 * 1024 * 1024
PARTS = 3
RIDE = 1
WAIT = 2000
NT = (((1,), (1,)), ((), ()))
TN = (((0,), (0,)), ((), ()))


def vmem():
    return pl.BlockSpec(memory_space=pltpu.VMEM)


def smem():
    return pl.BlockSpec(memory_space=pltpu.SMEM)


def hbm():
    return pl.BlockSpec(memory_space=pltpu.HBM)


def stay(array):
    return pltpu.with_memory_space_constraint(array, pltpu.HBM)


def cost(count):
    return pl.CostEstimate(flops=count, bytes_accessed=2 * count, transcendentals=0)


def params():
    return pltpu.CompilerParams(vmem_limit_bytes=VMEM_LIMIT)


def wrap(index, size):
    return lax.rem(index + size, size)


def live_count(table, row, slots):
    count = table[row, 2 * slots]
    for slot in range(1, slots):
        count = count + table[row, 2 * slots + slot]
    return count


def rank_before(table, row, spans, slots):
    me = lax.axis_index("seq")
    before = jnp.int32(0)
    for other in range(spans):
        ahead = wrap(me - other, spans) < wrap(me - row, spans)
        before = before + jnp.where(ahead, live_count(table, other, slots), 0)
    return before


def early_kernel(d_blocks, ids, live, values, hidden, out, hidden_here, stored, sems):
    value_copy = pltpu.make_async_copy(values, stored, sems.at[0])
    hidden_copy = pltpu.make_async_copy(hidden, hidden_here, sems.at[1])
    value_copy.start()
    hidden_copy.start()
    slots, block, _ = stored.shape
    tail = (out.shape[0] - slots * block, block)
    lane = lax.broadcasted_iota(jnp.int32, tail, 1)
    lists = jnp.zeros(tail, jnp.int32)
    for j in range(slots):
        lists = jnp.where(lane == j, lax.div(ids[0, j], d_blocks), lists)
        lists = jnp.where(lane == slots + j, lax.rem(ids[0, j], d_blocks), lists)
        lists = jnp.where(lane == 2 * slots + j, live[0, j], lists)
    out[slots * block :] = lists.astype(jnp.float32).astype(out.dtype)
    value_copy.wait()
    for j in range(slots):
        out[j * block : (j + 1) * block] = stored[j].astype(out.dtype)
    hidden_copy.wait()


def pick_kernel(spans, slots, block, *refs):
    stored, hidden, table, outs = refs[:spans], refs[spans], refs[spans + 1], refs[spans + 2 : -2]
    lists, sem = refs[-2:]
    for s in range(spans):
        tail = stored[s][slots * block :].astype(jnp.float32).astype(jnp.int32)
        lists[s : s + 1] = tail[:1]
    copy = pltpu.make_async_copy(lists, table, sem)
    copy.start()
    copy.wait()
    for s in range(spans):
        for j in range(slots):
            start = pl.multiple_of(table[(spans - s) % spans, j] * block, block)
            outs[s][j] = hidden[:, pl.ds(start, block)]


def lay_kernel(own, weight, *refs):
    others, (rows, first_weight, sems) = refs[:-3], refs[-3:]
    chunk = own.shape[0]
    weight_copy = pltpu.make_async_copy(
        weight.at[pl.ds(0, first_weight.shape[0])], first_weight, sems.at[0]
    )
    weight_copy.start()
    own_copy = pltpu.make_async_copy(own, rows.at[pl.ds(0, chunk)], sems.at[1])
    own_copy.start()
    for p, other in enumerate(others):
        rows[(p + 1) * chunk : (p + 2) * chunk] = other[...]
    own_copy.wait()
    weight_copy.wait()


def chunk_at(place):
    tensors, cores = lax.axis_size("tensor"), lax.axis_size("dp")
    t_place = lax.rem(lax.axis_index("tensor") + place // cores, tensors)
    d_place = lax.rem(lax.axis_index("dp") + place % cores, cores)
    return t_place * cores + d_place


def matmul_kernel(sizes, low, width, counts, table, weight, *refs):
    spans, slots, block = sizes
    step = pl.program_id(0)
    me = lax.axis_index("seq")
    pieces, stores, riders = counts
    given, refs = refs[:pieces], refs[pieces:]
    stored, refs = refs[:stores], refs[stores:]
    riding, refs = refs[:riders], refs[riders:]
    if stores:
        out, first, rows, held, total = refs

        @pl.when(step == 0)
        def _():
            at = 0
            for piece in given:
                rows[at : at + piece.shape[0]] = piece[...]
                at += piece.shape[0]
            before = rank_before(table, 0, spans, slots)
            for j in range(slots):
                rank = before + j
                owned = jnp.minimum(lax.div(rank, spans), slots - 1)
                place = pl.ds(pl.multiple_of(owned * block, block), block)
                for s in range(spans):

                    @pl.when(lax.rem(rank, spans) == wrap(me - s, spans))
                    def _():
                        held[j] = stored[s][place]

    else:
        (rows, held), (out, first, total) = given, refs
    chunk = rows.shape[0] // spans
    here = pl.ds(pl.multiple_of(step * width, width), width)
    weights = weight[here] if weight.shape[0] > width else weight[...]
    total[...] = lax.dot_general(rows[...], weights, NT, preferred_element_type=jnp.float32)
    count = live_count(table, 0, slots)
    for j in range(slots):
        f_start = table[0, j] * block - (low + step) * width

        @pl.when((j < count) & (f_start >= 0) & (f_start < width))
        def _():
            d_start = pl.multiple_of(table[0, slots + j] * block, block)
            place = pl.ds(pl.multiple_of(f_start, block), block)
            total[:, place] += lax.dot_general(
                rows[:, pl.ds(d_start, block)], held[j], NT, preferred_element_type=jnp.float32
            )

    first_chunk = wrap(me - 1, spans)
    for p in range(spans):
        result = total[p * chunk : (p + 1) * chunk].astype(out.dtype)
        out[chunk_at(p), :, here] = result

        @pl.when(chunk_at(p) == first_chunk)
        def _():
            first[:, here] = result

    at = out.shape[2]
    for rider in riding:
        first[:, at : at + block] = rider[...]
        at += block


def matmul_call(sizes, low, high, width, table, weight, given, stored=(), riding=()):
    spans, slots, block = sizes
    tokens = sum(piece.shape[0] for piece in given) if stored else given[0].shape[0]
    d_width, columns = weight.shape[1], (high - low) * width
    half = jnp.bfloat16
    shapes = [
        jax.ShapeDtypeStruct((spans, tokens // spans, columns), half),
        jax.ShapeDtypeStruct((tokens // spans, columns + len(riding) * block), half),
    ]
    if stored:
        shapes.append(jax.ShapeDtypeStruct((tokens, d_width), half))
        shapes.append(jax.ShapeDtypeStruct((slots, block, block), half))
    if weight.shape[0] == columns:
        weight_spec = vmem()
    else:
        weight, weight_spec = stay(weight), pl.BlockSpec((width, d_width), lambda i: (i + low, 0))
    inputs = [*given, *stored, *riding]
    return pl.pallas_call(
        functools.partial(
            matmul_kernel, sizes, low, width, (len(given), len(stored), len(riding))
        ),
        grid=(high - low,),
        out_shape=shapes,
        in_specs=[smem(), weight_spec] + [vmem()] * len(inputs),
        out_specs=[vmem()] * len(shapes),
        scratch_shapes=[pltpu.VMEM((tokens, width), jnp.float32)],
        compiler_params=params(),
        cost_estimate=pl.CostEstimate(
            flops=2 * tokens * d_width * columns,
            bytes_accessed=2 * d_width * columns,
            transcendentals=0,
        ),
        name="partial",
    )(table, weight, *inputs)


def add_kernel(t, riders, partials, arrived, out, *mine):
    spans, _, columns = partials.shape
    chunk = wrap(lax.axis_index("seq") - t, spans)
    result = partials[chunk].astype(jnp.float32) + arrived[:, :columns].astype(jnp.float32)
    out[:, :columns] = result.astype(out.dtype)
    if riders:
        block = mine[0].shape[1]
        mine[0][...] = arrived[:, columns : columns + block]
        out[:, columns:] = arrived[:, columns + block :]


def add_call(t, partials, arrived, block):
    chunk, columns = partials.shape[1:]
    riders = (arrived.shape[1] - columns) // block
    shapes = [jax.ShapeDtypeStruct((chunk, arrived.shape[1] - min(riders, 1) * block), arrived.dtype)]
    if riders:
        shapes.append(jax.ShapeDtypeStruct((chunk, block), arrived.dtype))
    return pl.pallas_call(
        functools.partial(add_kernel, t, riders),
        out_shape=shapes,
        in_specs=[vmem(), vmem()],
        out_specs=[vmem()] * len(shapes),
        compiler_params=params(),
        cost_estimate=cost(arrived.size),
        name="add",
    )(partials, arrived)


def last_kernel(low, partials, arrived, *refs):
    out, total, sem = refs[-3:]
    columns = partials.shape[2]
    result = partials[lax.axis_index("seq")].astype(jnp.float32)
    result = result + arrived[:, :columns].astype(jnp.float32)
    total[...] = result.astype(out.dtype)
    copy = pltpu.make_async_copy(total, out.at[:, pl.ds(low, columns)], sem)
    copy.start()
    copy.wait()


def last_call(low, partials, arrived, out, shape):
    _, chunk, columns = partials.shape
    given = [] if out is None else [out]
    return pl.pallas_call(
        functools.partial(last_kernel, low),
        out_shape=shape,
        in_specs=[vmem()] * 2 + [hbm()] * len(given),
        out_specs=hbm(),
        scratch_shapes=[pltpu.VMEM((chunk, columns), shape.dtype), pltpu.SemaphoreType.DMA],
        input_output_aliases={2: 0} if given else {},
        compiler_params=params(),
        cost_estimate=cost(arrived.size),
        name="last_sum",
    )(partials, arrived, *given)


def grad_kernel(spans, slots, block, table, rows, *refs):
    hidden, outs, (cols,) = refs[:spans], refs[spans : 2 * spans], refs[2 * spans :]
    me = lax.axis_index("seq")
    count, before = live_count(table, 0, slots), rank_before(table, 0, spans, slots)
    chunk = rows.shape[0] // spans
    for s in range(spans):
        cols[s] = hidden[s][...]
    for s in range(spans):
        slot = wrap(lax.rem(me + s, spans) - lax.rem(before, spans), spans)
        outs[s][...] = jnp.zeros_like(outs[s])

        @pl.when(slot < count)
        def _():
            d_start = pl.multiple_of(table[0, slots + slot] * block, block)
            total = jnp.zeros((block, block), jnp.float32)
            for p in range(spans):
                total = total + lax.dot_general(
                    cols[wrap(me - chunk_at(p), spans), slot],
                    rows[p * chunk : (p + 1) * chunk, pl.ds(d_start, block)],
                    TN,
                    preferred_element_type=jnp.float32,
                )
            outs[s][...] = total.astype(outs[s].dtype)


def grad_call(sizes, table, rows, hidden_cols):
    spans = sizes[0]
    slots, chunk, block = hidden_cols[0].shape
    return pl.pallas_call(
        functools.partial(grad_kernel, *sizes),
        out_shape=[jax.ShapeDtypeStruct((block, block), jnp.bfloat16)] * spans,
        in_specs=[smem()] + [vmem()] * (spans + 1),
        out_specs=[vmem()] * spans,
        scratch_shapes=[pltpu.VMEM((spans, slots, chunk, block), jnp.bfloat16)],
        compiler_params=params(),
        cost_estimate=cost(WAIT * rows.size),
        name="tile_grad",
    )(table, rows, *hidden_cols)


def adam_kernel(spans, slots, columns, table, *refs):
    arrived, refs = refs[:spans], refs[spans:]
    values, one, two, values_new, one_new, two_new, grads = refs
    me = lax.axis_index("seq")
    for s in range(spans - 1):
        grads[s] = arrived[s][...]
    grads[spans - 1] = arrived[-1][:, columns:]
    befores = [rank_before(table, s, spans, slots) for s in range(spans)]
    counts = [live_count(table, s, slots) for s in range(spans)]
    for owned in range(slots):
        rank = owned * spans + me
        source, live = jnp.int32(0), jnp.int32(0)
        for s in range(spans):
            holds = (befores[s] <= rank) & (rank < befores[s] + counts[s])
            source, live = jnp.where(holds, s, source), jnp.where(holds, 1, live)
        grad = grads[source].astype(jnp.float32)
        stored, old_one, old_two = values[owned], one[owned], two[owned]
        new_one = BETA_ONE * old_one + (1.0 - BETA_ONE) * grad
        new_two = BETA_TWO * old_two + (1.0 - BETA_TWO) * grad * grad
        stepped = (
            new_one
            / (1.0 - BETA_ONE**STEP)
            / (jnp.sqrt(new_two / (1.0 - BETA_TWO**STEP)) + EPSILON)
        )
        values_new[owned] = jnp.where(live > 0, stored - RATE * stepped, stored)
        one_new[owned] = jnp.where(live > 0, new_one, old_one)
        two_new[owned] = jnp.where(live > 0, new_two, old_two)


def adam_call(sizes, columns, table, grads, *states):
    spans, slots, block = sizes
    tile = jax.ShapeDtypeStruct((slots, block, block), jnp.float32)
    return pl.pallas_call(
        functools.partial(adam_kernel, spans, slots, columns),
        out_shape=(tile, tile, tile),
        in_specs=[smem()] + [vmem()] * (spans + 3),
        out_specs=(vmem(), vmem(), vmem()),
        scratch_shapes=[pltpu.VMEM((spans, block, block), jnp.bfloat16)],
        compiler_params=params(),
        cost_estimate=cost(slots * block * block),
        name="adam",
    )(table, *grads, *[state[0, 0] for state in states])


def take_from(array, axis, places):
    size = lax.axis_size(axis)
    return lax.ppermute(array, axis, [((i + places) % size, i) for i in range(size)])


def exchange(pieces):
    return [pieces[0]] + [take_from(pieces[s], "seq", -s) for s in range(1, len(pieces))]


def per_device(
    hidden_in, cotangent, down_weight, tile_ids, tile_live, values, moment_one, moment_two
):
    spans, cores = lax.axis_size("seq"), lax.axis_size("dp")
    slots, block = values.shape[2], values.shape[3]
    f_width, d_width = down_weight.shape
    d_blocks, f_blocks = d_width // block, f_width // block
    chunk = hidden_in.shape[0]
    sizes = (spans, slots, block)
    group = max(size for size in range(1, 5) if f_blocks % size == 0)
    width = group * block
    steps = f_blocks // group
    cuts = [(steps * part + 2) // PARTS for part in range(PARTS + 1)]
    ranges = list(zip(cuts[:-1], cuts[1:]))

    firsts = [take_from(cotangent, "tensor", t) for t in range(1, lax.axis_size("tensor"))]
    local = [take_from(cotangent, "dp", d) for d in range(1, cores)]

    payload, hidden_here = pl.pallas_call(
        functools.partial(early_kernel, d_blocks),
        out_shape=[
            jax.ShapeDtypeStruct((slots * block + 16, block), jnp.bfloat16),
            jax.ShapeDtypeStruct(hidden_in.shape, hidden_in.dtype),
        ],
        in_specs=[smem(), smem(), hbm(), hbm()],
        out_specs=[vmem(), vmem()],
        scratch_shapes=[
            pltpu.VMEM((slots, block, block), jnp.float32),
            pltpu.SemaphoreType.DMA((2,)),
        ],
        compiler_params=params(),
        cost_estimate=cost(hidden_in.size),
        name="early",
    )(tile_ids[0], tile_live[0], stay(values[0, 0]), stay(hidden_in))
    stored = exchange([payload] * spans)
    local_rows, first_weight = pl.pallas_call(
        lay_kernel,
        out_shape=[
            jax.ShapeDtypeStruct((cores * chunk, d_width), cotangent.dtype),
            jax.ShapeDtypeStruct((ranges[0][1] * width, d_width), down_weight.dtype),
        ],
        in_specs=[hbm(), hbm()] + [vmem()] * (cores - 1),
        out_specs=[vmem(), vmem()],
        scratch_shapes=[pltpu.SemaphoreType.DMA((2,))],
        compiler_params=params(),
        cost_estimate=cost(cores * chunk * d_width),
        name="lay",
    )(stay(cotangent), stay(down_weight), *local)

    firsts, stored, local_rows, first_weight = lax.optimization_barrier(
        (firsts, stored, local_rows, first_weight)
    )
    pieces = [local_rows]
    for first in firsts:
        pieces += [first] + [take_from(first, "dp", d) for d in range(1, cores)]

    table, *picked = pl.pallas_call(
        functools.partial(pick_kernel, *sizes),
        out_shape=[jax.ShapeDtypeStruct((spans, block), jnp.int32)]
        + [jax.ShapeDtypeStruct((slots, chunk, block), jnp.bfloat16)] * spans,
        in_specs=[vmem()] * (spans + 1),
        out_specs=[smem()] + [vmem()] * spans,
        scratch_shapes=[pltpu.VMEM((spans, block), jnp.int32), pltpu.SemaphoreType.DMA],
        compiler_params=params(),
        cost_estimate=cost(hidden_in.size),
        name="pick",
    )(*stored, hidden_here)
    hidden_cols = exchange(picked)

    partials, moving, grads = [], [], None
    for part, (low, high) in enumerate(ranges):
        if part == 0:
            partial, first, rows, held = matmul_call(
                sizes, low, high, width, table, first_weight, pieces, stored
            )
        else:
            riding = []
            if part == RIDE:
                grads = grad_call(sizes, table, rows, hidden_cols)
                riding = grads[1:]
            else:
                moving[0] = add_call(2, partials[0], moving[0], block)[0]
                rows, moving[0] = lax.optimization_barrier((rows, moving[0]))
            partial, first = matmul_call(
                sizes, low, high, width, table, down_weight, [rows, held], riding=riding
            )
        partials.append(partial)
        moving.append(take_from(first, "seq", -1))

    tiles = [grads[0]]
    for t in range(2, spans):
        for part in range(len(ranges)):
            if (t, part) != (2, 0):
                moving[part], *mine = add_call(t, partials[part], moving[part], block)
                tiles += mine
            moving[part] = take_from(moving[part], "seq", -1)
    tiles.append(moving[RIDE])
    new = adam_call(
        sizes, partials[RIDE].shape[2], table, tiles, values, moment_one, moment_two
    )

    hidden_grad = None
    shape = jax.ShapeDtypeStruct((chunk, f_width), jnp.bfloat16)
    for part, (low, _) in enumerate(ranges):
        if part == len(ranges) - 1:
            moving[part], new = lax.optimization_barrier((moving[part], new))
        hidden_grad = last_call(low * width, partials[part], moving[part], hidden_grad, shape)
    return (hidden_grad,) + tuple(array[None, None] for array in new)


def solution(mesh):
    shards = P(("groups", "seq"), ("tensor", "dp"))
    tiles = P(("groups", "seq"), ("tensor", "dp"), None, None, None)
    lists = P(("groups", "seq"), ("tensor", "dp"), None)
    return jax.shard_map(
        per_device,
        mesh=mesh,
        in_specs=(
            shards,
            P(("groups", "tensor", "dp"), "seq"),
            P(("tensor", "dp"), "seq"),
            lists,
            lists,
            tiles,
            tiles,
            tiles,
        ),
        out_specs=(shards, tiles, tiles, tiles),
        check_vma=False,
    )
```

time: 108 us -> 113 us (1.046)
  waiting for transfers between devices: 37 us -> 52.2 us
  blocking collectives: 9.29 us -> 0 us
  starting transfers between devices: 35.1 us -> 31.1 us
  Pallas kernels: 24.4 us -> 26.9 us
  local copies, waits for them, and re-layouts: 0.02 us -> 1.33 us
    ppermute x21 -> x18, waiting for transfers between devices: 37 us -> 52.2 us  [take_from(): lax.ppermute(array, axis, [((i + places) % size, i) for i in range(size)])]
    all_gather x1 -> x0, blocking collectives: 9.29 us -> none  [per_device(): table = lax.all_gather(table, 'seq', axis=0, tiled=True)]
    ppermute x21 -> x18, starting transfers between devices: 35.1 us -> 31.1 us  [take_from(): lax.ppermute(array, axis, [((i + places) % size, i) for i in range(size)])]
    pallas_call x13, Pallas kernels: 21.1 us -> 22.9 us  [the longest x3 14.8 us: matmul_call(): pl.pallas_call(functools.partial(matmul_kernel, sizes, low, width, (len(g...]
    unnamed x6 -> x10, local copies, waits for them, and re-layouts: 0.02 us -> 1.33 us
  transfers between devices with their start and end apart: 21 -> 18, of which waited for: 9 -> 10; matrix products, arithmetic and copies ran while one was open for 1% -> 0% of each run, Pallas kernels for 22% -> 22%
where the time goes in v6:
time: 113 us; the launch traced here: 112 us
  waiting for transfers between devices  52.2 us (46%)
  starting transfers between devices  31.1 us (28%)
  Pallas kernels  26.9 us (24%)
  local copies, waits for them, and re-layouts  1.33 us (1%)
    ppermute x18, waiting for transfers between devices, take_from(): lax.ppermute(array, axis, [((i + places) % size, i) for i in range(size)])  52.2 us
    ppermute x18, starting transfers between devices, take_from(): lax.ppermute(array, axis, [((i + places) % size, i) for i in range(size)])  31.1 us
    pallas_call x3, Pallas kernels, matmul_call(): pl.pallas_call(functools.partial(matmul_kernel, sizes, low, width, (len(g...  14.8 us
    pallas_call x1, Pallas kernels, per_device(): pl.pallas_call(lay_kernel, out_shape=[jax.ShapeDtypeStruct((cores * chunk...  2.88 us
    pallas_call x3, Pallas kernels, last_call(): pl.pallas_call(functools.partial(last_kernel, low), out_shape=shape, in_s...  2.43 us
  transfers between devices with their start and end apart: 18, of which 10 were waited for; matrix products, arithmetic and copies ran while one was open for 0% of the time, Pallas kernels for 22%

profile of v6, /device:TPU:0, one launch (start us, length us, event | category | flops | bytes accessed | tf_op | source)
XLA Modules:
  0.0 112.3 jit_solution(4719396513699491980)
XLA Ops:
  1.1 2.6 %collective-permute-start = (bf16[128,2048]{1,0:T(8,128)(2,1)}, bf16[128,2048]{1,0:T(8,128)(2,1)S(1)}, u32[]{:S(2)}, u32[]{:S(2)}) collective-permute-start(bf16[128,2048]{1,0:T(8,128)(2,1)} %own.1), channel_id=1, source_target_pairs={{2,0},{0,2},{3,1},{1,3},{6,4},{4,6},{7,5},{5,7},{10,8},{8,10},{11,... | collective-permute-start | bytes 1572872 | tf_op jit(solution)/shard_map/ppermute | solution.py:362
  5.0 1.8 %early.1 = (bf16[528,128]{1,0:T(8,128)(2,1)S(1)}, bf16[128,3584]{1,0:T(8,128)(2,1)S(1)}) custom-call(s32[1,4]{1,0:T(1,128)S(1)} %bitcast.12, s32[1,4]{1,0:T(1,128)S(1)} %bitcast.13, f32[4,128,128]{2,1,0:T(8,128)} %bitcast.8, bf16[128,3584]{1,0:T(8,128)(2,1)} %hidden.1), custom_call_target="tpu_custom_call" | custom-call | flops 458752 | bytes 917504 | tf_op jit(solution)/shard_map/early/pallas_call | solution.py:387
  6.9 3.7 %collective-permute-start.3 = (bf16[528,128]{1,0:T(8,128)(2,1)S(1)}, bf16[528,128]{1,0:T(8,128)(2,1)S(1)}, u32[]{:S(2)}, u32[]{:S(2)}) collective-permute-start(bf16[528,128]{1,0:T(8,128)(2,1)S(1)} %get-tuple-element.48.refs_0_.refs_3_), channel_id=1, source_target_pairs={{4,0},{8,4},{12,8},{0,12},{5,1},{9,5},{13,9},{1,13},{6,2},{10,6},{... | collective-permute-start | bytes 405512 | tf_op jit(solution)/shard_map/ppermute | solution.py:362
  11.5 2.9 %lay.1 = (bf16[256,2048]{1,0:T(8,128)(2,1)S(1)}, bf16[1536,2048]{1,0:T(8,128)(2,1)S(1)}) custom-call(bf16[128,2048]{1,0:T(8,128)(2,1)} %own.1, bf16[3584,2048]{1,0:T(8,128)(2,1)} %weight.5, bf16[128,2048]{1,0:T(8,128)(2,1)S(1)} %collective-permute-done.4.refs_0_), custom_call_target="tpu_custom_call" | custom-call | flops 524288 | bytes 1048576 | tf_op jit(solution)/shard_map/lay/pallas_call | solution.py:404
  14.5 8.0 %collective-permute-done.2.refs_2_.refs_5_ = bf16[528,128]{1,0:T(8,128)(2,1)S(1)} collective-permute-done((bf16[528,128]{1,0:T(8,128)(2,1)S(1)}, bf16[528,128]{1,0:T(8,128)(2,1)S(1)}, u32[]{:S(2)}, u32[]{:S(2)}) %collective-permute-start.2) | collective-permute-done | bytes 135200 | tf_op jit(solution)/shard_map/ppermute | solution.py:362
  22.6 1.3 %pick.1 = (s32[4,128]{1,0:T(4,128)S(1)}, bf16[4,128,128]{2,1,0:T(8,128)(2,1)S(1)}, bf16[4,128,128]{2,1,0:T(8,128)(2,1)S(1)}, bf16[4,128,128]{2,1,0:T(8,128)(2,1)S(1)}, bf16[4,128,128]{2,1,0:T(8,128)(2,1)S(1)}) custom-call(bf16[528,128]{1,0:T(8,128)(2,1)S(1)} %get-tuple-element.48.refs_0_.refs_3_, ...), custom_call_target="tpu_custom_call" | custom-call | flops 458752 | bytes 917504 | tf_op jit(solution)/shard_map/pick/pallas_call | solution.py:425
  24.5 2.0 %collective-permute-start.11 = (bf16[4,128,128]{2,1,0:T(8,128)(2,1)S(1)}, bf16[4,128,128]{2,1,0:T(8,128)(2,1)S(1)}, u32[]{:S(2)}, u32[]{:S(2)}) collective-permute-start(bf16[4,128,128]{2,1,0:T(8,128)(2,1)S(1)} %get-tuple-element.66), channel_id=1, source_target_pairs={{8,0},{12,4},{0,8},{4,12},{9,1},{13,5},{1,9},{5,13},{10,2},{14,6},... | collective-permute-start | bytes 393224 | tf_op jit(solution)/shard_map/ppermute | solution.py:362
  26.5 2.8 %collective-permute-start.12 = (bf16[4,128,128]{2,1,0:T(8,128)(2,1)S(1)}, bf16[4,128,128]{2,1,0:T(8,128)(2,1)S(1)}, u32[]{:S(2)}, u32[]{:S(2)}) collective-permute-start(bf16[4,128,128]{2,1,0:T(8,128)(2,1)S(1)} %get-tuple-element.67), channel_id=1, source_target_pairs={{4,0},{8,4},{12,8},{0,12},{5,1},{9,5},{13,9},{1,13},{6,2},{10,6},{... | collective-permute-start | bytes 393224 | tf_op jit(solution)/shard_map/ppermute | solution.py:362
  29.3 5.6 %partial.3 = (bf16[4,128,1536]{2,1,0:T(8,128)(2,1)S(1)}, bf16[128,1536]{1,0:T(8,128)(2,1)S(1)}, bf16[512,2048]{1,0:T(8,128)(2,1)S(1)}, bf16[4,128,128]{2,1,0:T(8,128)(2,1)S(1)}) custom-call(s32[4,128]{1,0:T(4,128)S(1)} %get-tuple-element.53.table, bf16[1536,2048]{1,0:T(8,128)(2,1)S(1)} %get-tuple-element.54.weight, ...), custom_call_target="tpu_custom_call" | custom-call | flops 3221225472 | bytes 6291456 | tf_op jit(solution)/shard_map/partial/pallas_call | solution.py:202
  35.1 2.3 %collective-permute-done.11.refs_2_ = bf16[4,128,128]{2,1,0:T(8,128)(2,1)S(1)} collective-permute-done((bf16[4,128,128]{2,1,0:T(8,128)(2,1)S(1)}, bf16[4,128,128]{2,1,0:T(8,128)(2,1)S(1)}, u32[]{:S(2)}, u32[]{:S(2)}) %collective-permute-start.11) | collective-permute-done | bytes 131104 | tf_op jit(solution)/shard_map/ppermute | solution.py:362
  37.3 1.6 %tile_grad.1 = (bf16[128,128]{1,0:T(8,128)(2,1)S(1)}, bf16[128,128]{1,0:T(8,128)(2,1)S(1)}, bf16[128,128]{1,0:T(8,128)(2,1)S(1)}, bf16[128,128]{1,0:T(8,128)(2,1)S(1)}) custom-call(s32[4,128]{1,0:T(4,128)S(1)} %get-tuple-element.53.table, bf16[512,2048]{1,0:T(8,128)(2,1)S(1)} %get-tuple-element.60.refs_0_.rows, ...), custom_call_target="tpu_custom_call" | custom-call | flops 2097152000 | bytes 4194304000 | tf_op jit(solution)/shard_map/tile_grad/pallas_call | solution.py:304
  38.9 4.5 %partial.5 = (bf16[4,128,1024]{2,1,0:T(8,128)(2,1)S(1)}, bf16[128,1408]{1,0:T(8,128)(2,1)S(1)}) custom-call(s32[4,128]{1,0:T(4,128)S(1)} %get-tuple-element.53.table, bf16[3584,2048]{1,0:T(8,128)(2,1)} %weight.5, bf16[512,2048]{1,0:T(8,128)(2,1)S(1)} %get-tuple-element.60.refs_0_.rows, bf16[4,128,128]{2,1,0:T(8,128)(2,1)S(1)} %get-tuple-element.61.refs_1_, ...), custom_call_target="tpu_custom_call" | custom-call | flops 2147483648 | bytes 4194304 | tf_op jit(solution)/shard_map/partial/pallas_call | solution.py:202
  43.4 10.8 %collective-permute-start.13 = (bf16[128,1408]{1,0:T(8,128)(2,1)S(1)}, bf16[128,1408]{1,0:T(8,128)(2,1)S(1)}, u32[]{:S(2)}, u32[]{:S(2)}) collective-permute-start(bf16[128,1408]{1,0:T(8,128)(2,1)S(1)} %get-tuple-element.73), channel_id=1, source_target_pairs={{12,0},{0,4},{4,8},{8,12},{13,1},{1,5},{5,9},{9,13},{14,2},{2,6},{... | collective-permute-start | bytes 1081352 | tf_op jit(solution)/shard_map/ppermute | solution.py:362
  54.3 4.6 %partial.4 = (bf16[4,128,1024]{2,1,0:T(8,128)(2,1)S(1)}, bf16[128,1024]{1,0:T(8,128)(2,1)S(1)}) custom-call(s32[4,128]{1,0:T(4,128)S(1)} %get-tuple-element.53.table, bf16[3584,2048]{1,0:T(8,128)(2,1)} %weight.5, bf16[512,2048]{1,0:T(8,128)(2,1)S(1)} %get-tuple-element.60.refs_0_.rows, bf16[4,128,128]{2,1,0:T(8,128)(2,1)S(1)} %get-tuple-element.61.refs_1_), custom_call_target="tpu_custom_call" | custom-call | flops 2147483648 | bytes 4194304 | tf_op jit(solution)/shard_map/partial/pallas_call | solution.py:202
  59.2 3.7 %collective-permute-done.13.arrived = bf16[128,1408]{1,0:T(8,128)(2,1)S(1)} collective-permute-done((bf16[128,1408]{1,0:T(8,128)(2,1)S(1)}, bf16[128,1408]{1,0:T(8,128)(2,1)S(1)}, u32[]{:S(2)}, u32[]{:S(2)}) %collective-permute-start.13) | collective-permute-done | bytes 360480 | tf_op jit(solution)/shard_map/ppermute | solution.py:362
  63.0 2.5 %collective-permute-start.14 = (bf16[128,1280]{1,0:T(8,128)(2,1)S(1)}, bf16[128,1280]{1,0:T(8,128)(2,1)S(1)}, u32[]{:S(2)}, u32[]{:S(2)}) collective-permute-start(bf16[128,1280]{1,0:T(8,128)(2,1)S(1)} %get-tuple-element.75), channel_id=1, source_target_pairs={{12,0},{0,4},{4,8},{8,12},{13,1},{1,5},{5,9},{9,13},{14,2},{2,6},{... | collective-permute-start | bytes 983048 | tf_op jit(solution)/shard_map/ppermute | solution.py:362
  65.6 4.5 %collective-permute-done.7.arrived = bf16[128,1024]{1,0:T(8,128)(2,1)S(1)} collective-permute-done((bf16[128,1024]{1,0:T(8,128)(2,1)S(1)}, bf16[128,1024]{1,0:T(8,128)(2,1)S(1)}, u32[]{:S(2)}, u32[]{:S(2)}) %collective-permute-start.7) | collective-permute-done | bytes 262176 | tf_op jit(solution)/shard_map/ppermute | solution.py:362
  70.1 1.1 collective-permute-start.8
  71.2 7.3 %collective-permute-done.16.arrived = bf16[128,1536]{1,0:T(8,128)(2,1)S(1)} collective-permute-done((bf16[128,1536]{1,0:T(8,128)(2,1)S(1)}, bf16[128,1536]{1,0:T(8,128)(2,1)S(1)}, u32[]{:S(2)}, u32[]{:S(2)}) %collective-permute-start.16) | collective-permute-done | bytes 393248 | tf_op jit(solution)/shard_map/ppermute | solution.py:362
  79.6 5.8 %collective-permute-done.14.arrived = bf16[128,1280]{1,0:T(8,128)(2,1)S(1)} collective-permute-done((bf16[128,1280]{1,0:T(8,128)(2,1)S(1)}, bf16[128,1280]{1,0:T(8,128)(2,1)S(1)}, u32[]{:S(2)}, u32[]{:S(2)}) %collective-permute-start.14) | collective-permute-done | bytes 327712 | tf_op jit(solution)/shard_map/ppermute | solution.py:362
  86.6 4.5 %collective-permute-done.8.arrived = bf16[128,1024]{1,0:T(8,128)(2,1)S(1)} collective-permute-done((bf16[128,1024]{1,0:T(8,128)(2,1)S(1)}, bf16[128,1024]{1,0:T(8,128)(2,1)S(1)}, u32[]{:S(2)}, u32[]{:S(2)}) %collective-permute-start.8) | collective-permute-done | bytes 262176 | tf_op jit(solution)/shard_map/ppermute | solution.py:362
  92.2 13.6 %collective-permute-done.15.refs_3_.arrived = bf16[128,1152]{1,0:T(8,128)(2,1)S(1)} collective-permute-done((bf16[128,1152]{1,0:T(8,128)(2,1)S(1)}, bf16[128,1152]{1,0:T(8,128)(2,1)S(1)}, u32[]{:S(2)}, u32[]{:S(2)}) %collective-permute-start.15) | collective-permute-done | bytes 294944 | tf_op jit(solution)/shard_map/ppermute | solution.py:362
  105.9 1.7 %adam.1 = (f32[4,128,128]{2,1,0:T(8,128)}, f32[4,128,128]{2,1,0:T(8,128)}, f32[4,128,128]{2,1,0:T(8,128)}) custom-call(s32[4,128]{1,0:T(4,128)S(1)} %get-tuple-element.53.table, bf16[128,128]{1,0:T(8,128)(2,1)S(1)} %get-tuple-element.68.refs_0_, bf16[128,128]{1,0:T(8,128)(2,1)S(1)} %get-tuple-element.74.refs_1_, ...), custom_call_target="tpu_custom_call" | custom-call | flops 65536 | bytes 131072 | tf_op jit(solution)/shard_map/adam/pallas_call | solution.py:348
  107.5 2.4 %collective-permute-done.9.arrived = bf16[128,1024]{1,0:T(8,128)(2,1)S(1)} collective-permute-done((bf16[128,1024]{1,0:T(8,128)(2,1)S(1)}, bf16[128,1024]{1,0:T(8,128)(2,1)S(1)}, u32[]{:S(2)}, u32[]{:S(2)}) %collective-permute-start.9) | collective-permute-done | bytes 262176 | tf_op jit(solution)/shard_map/ppermute | solution.py:362
  (39 shorter events, 10.1 us)
Async XLA Ops:
  0.6 10.9 %collective-permute-start.4 = (bf16[128,2048]{1,0:T(8,128)(2,1)}, bf16[128,2048]{1,0:T(8,128)(2,1)S(1)}, u32[]{:S(2)}, u32[]{:S(2)}) collective-permute-start(bf16[128,2048]{1,0:T(8,128)(2,1)} %own.1), channel_id=1, source_target_pairs={{1,0},{0,1},{3,2},{2,3},{5,4},{4,5},{7,6},{6,7},{9,8},{8,9},{11,10... | collective-permute-start | bytes 1572872 | tf_op jit(solution)/shard_map/ppermute | solution.py:362
  1.1 21.4 %collective-permute-start = (bf16[128,2048]{1,0:T(8,128)(2,1)}, bf16[128,2048]{1,0:T(8,128)(2,1)S(1)}, u32[]{:S(2)}, u32[]{:S(2)}) collective-permute-start(bf16[128,2048]{1,0:T(8,128)(2,1)} %own.1), channel_id=1, source_target_pairs={{2,0},{0,2},{3,1},{1,3},{6,4},{4,6},{7,5},{5,7},{10,8},{8,10},{11,... | collective-permute-start | bytes 1572872 | tf_op jit(solution)/shard_map/ppermute | solution.py:362
  3.7 0.7 copy-start.3
  4.4 0.7 copy-start.4
  6.9 7.7 %collective-permute-start.3 = (bf16[528,128]{1,0:T(8,128)(2,1)S(1)}, bf16[528,128]{1,0:T(8,128)(2,1)S(1)}, u32[]{:S(2)}, u32[]{:S(2)}) collective-permute-start(bf16[528,128]{1,0:T(8,128)(2,1)S(1)} %get-tuple-element.48.refs_0_.refs_3_), channel_id=1, source_target_pairs={{4,0},{8,4},{12,8},{0,12},{5,1},{9,5},{13,9},{1,13},{6,2},{10,6},{... | collective-permute-start | bytes 405512 | tf_op jit(solution)/shard_map/ppermute | solution.py:362
  10.5 12.0 %collective-permute-start.2 = (bf16[528,128]{1,0:T(8,128)(2,1)S(1)}, bf16[528,128]{1,0:T(8,128)(2,1)S(1)}, u32[]{:S(2)}, u32[]{:S(2)}) collective-permute-start(bf16[528,128]{1,0:T(8,128)(2,1)S(1)} %get-tuple-element.48.refs_0_.refs_3_), channel_id=1, source_target_pairs={{8,0},{12,4},{0,8},{4,12},{9,1},{13,5},{1,9},{5,13},{10,2},{14,6},... | collective-permute-start | bytes 405512 | tf_op jit(solution)/shard_map/ppermute | solution.py:362
  10.5 12.0 %collective-permute-start.1 = (bf16[528,128]{1,0:T(8,128)(2,1)S(1)}, bf16[528,128]{1,0:T(8,128)(2,1)S(1)}, u32[]{:S(2)}, u32[]{:S(2)}) collective-permute-start(bf16[528,128]{1,0:T(8,128)(2,1)S(1)} %get-tuple-element.48.refs_0_.refs_3_), channel_id=1, source_target_pairs={{12,0},{0,4},{4,8},{8,12},{13,1},{1,5},{5,9},{9,13},{14,2},{2,6},{... | collective-permute-start | bytes 405512 | tf_op jit(solution)/shard_map/ppermute | solution.py:362
  22.5 6.8 %collective-permute-start.5 = (bf16[128,2048]{1,0:T(8,128)(2,1)S(1)}, bf16[128,2048]{1,0:T(8,128)(2,1)S(1)}, u32[]{:S(2)}, u32[]{:S(2)}) collective-permute-start(bf16[128,2048]{1,0:T(8,128)(2,1)S(1)} %collective-permute-done.refs_1_), channel_id=1, source_target_pairs={{1,0},{0,1},{3,2},{2,3},{5,4},{4,5},{7,6},{6,7},{9,8},{8,9},{11,10... | collective-permute-start | bytes 1572872 | tf_op jit(solution)/shard_map/ppermute | solution.py:362
  23.8 11.2 %collective-permute-start.10 = (bf16[4,128,128]{2,1,0:T(8,128)(2,1)S(1)}, bf16[4,128,128]{2,1,0:T(8,128)(2,1)S(1)}, u32[]{:S(2)}, u32[]{:S(2)}) collective-permute-start(bf16[4,128,128]{2,1,0:T(8,128)(2,1)S(1)} %get-tuple-element.65), channel_id=1, source_target_pairs={{12,0},{0,4},{4,8},{8,12},{13,1},{1,5},{5,9},{9,13},{14,2},{2,6},{... | collective-permute-start | bytes 393224 | tf_op jit(solution)/shard_map/ppermute | solution.py:362
  24.5 12.8 %collective-permute-start.11 = (bf16[4,128,128]{2,1,0:T(8,128)(2,1)S(1)}, bf16[4,128,128]{2,1,0:T(8,128)(2,1)S(1)}, u32[]{:S(2)}, u32[]{:S(2)}) collective-permute-start(bf16[4,128,128]{2,1,0:T(8,128)(2,1)S(1)} %get-tuple-element.66), channel_id=1, source_target_pairs={{8,0},{12,4},{0,8},{4,12},{9,1},{13,5},{1,9},{5,13},{10,2},{14,6},... | collective-permute-start | bytes 393224 | tf_op jit(solution)/shard_map/ppermute | solution.py:362
  26.5 10.8 %collective-permute-start.12 = (bf16[4,128,128]{2,1,0:T(8,128)(2,1)S(1)}, bf16[4,128,128]{2,1,0:T(8,128)(2,1)S(1)}, u32[]{:S(2)}, u32[]{:S(2)}) collective-permute-start(bf16[4,128,128]{2,1,0:T(8,128)(2,1)S(1)} %get-tuple-element.67), channel_id=1, source_target_pairs={{4,0},{8,4},{12,8},{0,12},{5,1},{9,5},{13,9},{1,13},{6,2},{10,6},{... | collective-permute-start | bytes 393224 | tf_op jit(solution)/shard_map/ppermute | solution.py:362
  35.0 19.2 %collective-permute-start.6 = (bf16[128,1536]{1,0:T(8,128)(2,1)S(1)}, bf16[128,1536]{1,0:T(8,128)(2,1)S(1)}, u32[]{:S(2)}, u32[]{:S(2)}) collective-permute-start(bf16[128,1536]{1,0:T(8,128)(2,1)S(1)} %get-tuple-element.59), channel_id=1, source_target_pairs={{12,0},{0,4},{4,8},{8,12},{13,1},{1,5},{5,9},{9,13},{14,2},{2,6},{... | collective-permute-start | bytes 1179656 | tf_op jit(solution)/shard_map/ppermute | solution.py:362
  43.4 19.6 %collective-permute-start.13 = (bf16[128,1408]{1,0:T(8,128)(2,1)S(1)}, bf16[128,1408]{1,0:T(8,128)(2,1)S(1)}, u32[]{:S(2)}, u32[]{:S(2)}) collective-permute-start(bf16[128,1408]{1,0:T(8,128)(2,1)S(1)} %get-tuple-element.73), channel_id=1, source_target_pairs={{12,0},{0,4},{4,8},{8,12},{13,1},{1,5},{5,9},{9,13},{14,2},{2,6},{... | collective-permute-start | bytes 1081352 | tf_op jit(solution)/shard_map/ppermute | solution.py:362
  58.9 46.9 %copy-start = (f32[1,1,4,128,128]{4,3,2,1,0:T(8,128)S(1)}, f32[1,1,4,128,128]{4,3,2,1,0:T(8,128)}, u32[]{:S(2)}) copy-start(f32[1,1,4,128,128]{4,3,2,1,0:T(8,128)} %param.13) | copy-start | bytes 786436
  58.9 46.9 %copy-start.1 = (f32[1,1,4,128,128]{4,3,2,1,0:T(8,128)S(1)}, f32[1,1,4,128,128]{4,3,2,1,0:T(8,128)}, u32[]{:S(2)}) copy-start(f32[1,1,4,128,128]{4,3,2,1,0:T(8,128)} %param.14) | copy-start | bytes 786436
  58.9 46.9 %copy-start.2 = (f32[1,1,4,128,128]{4,3,2,1,0:T(8,128)S(1)}, f32[1,1,4,128,128]{4,3,2,1,0:T(8,128)}, u32[]{:S(2)}) copy-start(f32[1,1,4,128,128]{4,3,2,1,0:T(8,128)} %param.15) | copy-start | bytes 786436
  58.9 11.1 %collective-permute-start.7 = (bf16[128,1024]{1,0:T(8,128)(2,1)S(1)}, bf16[128,1024]{1,0:T(8,128)(2,1)S(1)}, u32[]{:S(2)}, u32[]{:S(2)}) collective-permute-start(bf16[128,1024]{1,0:T(8,128)(2,1)S(1)} %get-tuple-element.63), channel_id=1, source_target_pairs={{12,0},{0,4},{4,8},{8,12},{13,1},{1,5},{5,9},{9,13},{14,2},{2,6},{... | collective-permute-start | bytes 786440 | tf_op jit(solution)/shard_map/ppermute | solution.py:362
  59.0 19.5 %collective-permute-start.16 = (bf16[128,1536]{1,0:T(8,128)(2,1)S(1)}, bf16[128,1536]{1,0:T(8,128)(2,1)S(1)}, u32[]{:S(2)}, u32[]{:S(2)}) collective-permute-start(bf16[128,1536]{1,0:T(8,128)(2,1)S(1)} %add.6), channel_id=1, source_target_pairs={{12,0},{0,4},{4,8},{8,12},{13,1},{1,5},{5,9},{9,13},{14,2},{2,6},{... | collective-permute-start | bytes 1179656 | tf_op jit(solution)/shard_map/ppermute | solution.py:362
  63.0 22.4 %collective-permute-start.14 = (bf16[128,1280]{1,0:T(8,128)(2,1)S(1)}, bf16[128,1280]{1,0:T(8,128)(2,1)S(1)}, u32[]{:S(2)}, u32[]{:S(2)}) collective-permute-start(bf16[128,1280]{1,0:T(8,128)(2,1)S(1)} %get-tuple-element.75), channel_id=1, source_target_pairs={{12,0},{0,4},{4,8},{8,12},{13,1},{1,5},{5,9},{9,13},{14,2},{2,6},{... | collective-permute-start | bytes 983048 | tf_op jit(solution)/shard_map/ppermute | solution.py:362
  70.1 21.0 %collective-permute-start.8 = (bf16[128,1024]{1,0:T(8,128)(2,1)S(1)}, bf16[128,1024]{1,0:T(8,128)(2,1)S(1)}, u32[]{:S(2)}, u32[]{:S(2)}) collective-permute-start(bf16[128,1024]{1,0:T(8,128)(2,1)S(1)} %add.7), channel_id=1, source_target_pairs={{12,0},{0,4},{4,8},{8,12},{13,1},{1,5},{5,9},{9,13},{14,2},{2,6},{... | collective-permute-start | bytes 786440 | tf_op jit(solution)/shard_map/ppermute | solution.py:362
  78.6 31.3 %collective-permute-start.17 = (bf16[128,1536]{1,0:T(8,128)(2,1)S(1)}, bf16[128,1536]{1,0:T(8,128)(2,1)S(1)}, u32[]{:S(2)}, u32[]{:S(2)}) collective-permute-start(bf16[128,1536]{1,0:T(8,128)(2,1)S(1)} %add.11), channel_id=1, source_target_pairs={{12,0},{0,4},{4,8},{8,12},{13,1},{1,5},{5,9},{9,13},{14,2},{2,6},{... | collective-permute-start | bytes 1179656 | tf_op jit(solution)/shard_map/ppermute | solution.py:362
  85.6 20.3 %collective-permute-start.15 = (bf16[128,1152]{1,0:T(8,128)(2,1)S(1)}, bf16[128,1152]{1,0:T(8,128)(2,1)S(1)}, u32[]{:S(2)}, u32[]{:S(2)}) collective-permute-start(bf16[128,1152]{1,0:T(8,128)(2,1)S(1)} %get-tuple-element.77), channel_id=1, source_target_pairs={{12,0},{0,4},{4,8},{8,12},{13,1},{1,5},{5,9},{9,13},{14,2},{2,6},{... | collective-permute-start | bytes 884744 | tf_op jit(solution)/shard_map/ppermute | solution.py:362
  91.2 18.7 %collective-permute-start.9 = (bf16[128,1024]{1,0:T(8,128)(2,1)S(1)}, bf16[128,1024]{1,0:T(8,128)(2,1)S(1)}, u32[]{:S(2)}, u32[]{:S(2)}) collective-permute-start(bf16[128,1024]{1,0:T(8,128)(2,1)S(1)} %add.8), channel_id=1, source_target_pairs={{12,0},{0,4},{4,8},{8,12},{13,1},{1,5},{5,9},{9,13},{14,2},{2,6},{... | collective-permute-start | bytes 786440 | tf_op jit(solution)/shard_map/ppermute | solution.py:362

commit v7 on v6

v7 whole, which is shorter than its diff:
```python
import functools

import jax
import jax.numpy as jnp
from jax import lax
from jax.experimental import pallas as pl
from jax.experimental.pallas import tpu as pltpu
from jax.sharding import PartitionSpec as P

STEP = 100
BETA_ONE = 0.9
BETA_TWO = 0.999
RATE = 0.01
EPSILON = 1e-08
VMEM_LIMIT = 24 * 1024 * 1024
WAIT = 2000
LAG = 2
NT = (((1,), (1,)), ((), ()))
TN = (((0,), (0,)), ((), ()))


def vmem():
    return pl.BlockSpec(memory_space=pltpu.VMEM)


def smem():
    return pl.BlockSpec(memory_space=pltpu.SMEM)


def hbm():
    return pl.BlockSpec(memory_space=pltpu.HBM)


def stay(array):
    return pltpu.with_memory_space_constraint(array, pltpu.HBM)


def cost(count):
    return pl.CostEstimate(flops=count, bytes_accessed=2 * count, transcendentals=0)


def params():
    return pltpu.CompilerParams(vmem_limit_bytes=VMEM_LIMIT)


def wrap(index, size):
    return lax.rem(index + size, size)


def live_count(table, row, slots):
    count = table[row, 2 * slots]
    for slot in range(1, slots):
        count = count + table[row, 2 * slots + slot]
    return count


def rank_before(table, row, spans, slots):
    me = lax.axis_index("seq")
    before = jnp.int32(0)
    for other in range(spans):
        ahead = wrap(me - other, spans) < wrap(me - row, spans)
        before = before + jnp.where(ahead, live_count(table, other, slots), 0)
    return before


def early_kernel(values, hidden, values_half, hidden_here, stored, sems):
    value_copy = pltpu.make_async_copy(values, stored, sems.at[0])
    hidden_copy = pltpu.make_async_copy(hidden, hidden_here, sems.at[1])
    value_copy.start()
    hidden_copy.start()
    value_copy.wait()
    values_half[...] = stored[...].astype(values_half.dtype)
    hidden_copy.wait()


def pick_kernel(spans, slots, block, d_blocks, *refs):
    metas, (values, hidden, table), outs = refs[:spans], refs[spans : spans + 3], refs[spans + 3 :]
    me = lax.axis_index("seq")
    for s in range(spans):
        for j in range(slots):
            table[s, j] = lax.div(metas[s][0, j], d_blocks)
            table[s, slots + j] = lax.rem(metas[s][0, j], d_blocks)
            table[s, 2 * slots + j] = metas[s][0, slots + j]
    for s in range(spans):
        row = (spans - s) % spans
        before = rank_before(table, row, spans, slots)
        slot = wrap(me - lax.rem(before, spans), spans)
        tile = values[jnp.minimum(lax.div(before + slot, spans), slots - 1)]
        live = slot < live_count(table, row, slots)
        outs[s][...] = jnp.where(live, tile.astype(jnp.float32), 0.0).astype(tile.dtype)
        for j in range(slots):
            start = pl.multiple_of(table[row, j] * block, block)
            outs[spans + s][j] = hidden[:, pl.ds(start, block)]


def lay_kernel(own, weight, *refs):
    others, (rows, first_weight, sems) = refs[:-3], refs[-3:]
    chunk = own.shape[0]
    weight_copy = pltpu.make_async_copy(
        weight.at[pl.ds(0, first_weight.shape[0])], first_weight, sems.at[0]
    )
    weight_copy.start()
    own_copy = pltpu.make_async_copy(own, rows.at[pl.ds(0, chunk)], sems.at[1])
    own_copy.start()
    for p, other in enumerate(others):
        rows[(p + 1) * chunk : (p + 2) * chunk] = other[...]
    own_copy.wait()
    weight_copy.wait()


def chunk_at(place):
    tensors, cores = lax.axis_size("tensor"), lax.axis_size("dp")
    t_place = lax.rem(lax.axis_index("tensor") + place // cores, tensors)
    d_place = lax.rem(lax.axis_index("dp") + place % cores, cores)
    return t_place * cores + d_place


def matmul_kernel(sizes, low, width, firsts_of, stores, table, weight, *refs):
    spans, slots, block = sizes
    step = pl.program_id(0)
    me = lax.axis_index("seq")
    if stores:
        given, stored, (out, first, rows, held, total) = refs[: -stores - 5], refs[-stores - 5 : -5], refs[-5:]

        @pl.when(step == 0)
        def _():
            at = 0
            for piece in given:
                rows[at : at + piece.shape[0]] = piece[...]
                at += piece.shape[0]
            before = rank_before(table, 0, spans, slots)
            for j in range(slots):
                for s in range(spans):

                    @pl.when(lax.rem(before + j, spans) == wrap(me - s, spans))
                    def _():
                        held[j] = stored[s][...]

    else:
        rows, held, out, first, total = refs
    chunk = rows.shape[0] // spans
    here = pl.ds(pl.multiple_of(step * width, width), width)
    weights = weight[here] if weight.shape[0] > width else weight[...]
    total[...] = lax.dot_general(rows[...], weights, NT, preferred_element_type=jnp.float32)
    count = live_count(table, 0, slots)
    for j in range(slots):
        f_start = table[0, j] * block - (low + step) * width

        @pl.when((j < count) & (f_start >= 0) & (f_start < width))
        def _():
            d_start = pl.multiple_of(table[0, slots + j] * block, block)
            place = pl.ds(pl.multiple_of(f_start, block), block)
            total[:, place] += lax.dot_general(
                rows[:, pl.ds(d_start, block)], held[j], NT, preferred_element_type=jnp.float32
            )

    for p in range(spans):
        result = total[p * chunk : (p + 1) * chunk].astype(out.dtype)
        out[chunk_at(p), :, here] = result
        for k, first_chunk in enumerate(firsts_of(me)):

            @pl.when(chunk_at(p) == first_chunk)
            def _():
                first[k, :, here] = result


def matmul_call(sizes, low, high, width, firsts_of, table, weight, given, stored=()):
    spans, slots, block = sizes
    tokens = sum(piece.shape[0] for piece in given) if stored else given[0].shape[0]
    d_width, columns = weight.shape[1], (high - low) * width
    half = jnp.bfloat16
    shapes = [
        jax.ShapeDtypeStruct((spans, tokens // spans, columns), half),
        jax.ShapeDtypeStruct((len(firsts_of(0)), tokens // spans, columns), half),
    ]
    if stored:
        shapes.append(jax.ShapeDtypeStruct((tokens, d_width), half))
        shapes.append(jax.ShapeDtypeStruct((slots, block, block), half))
    if weight.shape[0] == columns:
        weight_spec = vmem()
    else:
        weight, weight_spec = stay(weight), pl.BlockSpec((width, d_width), lambda i: (i + low, 0))
    inputs = [*given, *stored]
    return pl.pallas_call(
        functools.partial(matmul_kernel, sizes, low, width, firsts_of, len(stored)),
        grid=(high - low,),
        out_shape=shapes,
        in_specs=[smem(), weight_spec] + [vmem()] * len(inputs),
        out_specs=[vmem()] * len(shapes),
        scratch_shapes=[pltpu.VMEM((tokens, width), jnp.float32)],
        compiler_params=params(),
        cost_estimate=pl.CostEstimate(
            flops=2 * tokens * d_width * columns,
            bytes_accessed=2 * d_width * columns,
            transcendentals=0,
        ),
        name="partial",
    )(table, weight, *inputs)


def add_kernel(chunks_of, partials, arrived, out):
    for k, chunk in enumerate(chunks_of(lax.axis_index("seq"))):
        result = partials[chunk].astype(jnp.float32) + arrived[k].astype(jnp.float32)
        out[k] = result.astype(out.dtype)


def add_call(chunks_of, partials, arrived):
    shape = (len(chunks_of(0)), *arrived.shape[1:])
    return pl.pallas_call(
        functools.partial(add_kernel, chunks_of),
        out_shape=jax.ShapeDtypeStruct(shape, arrived.dtype),
        in_specs=[vmem(), vmem()],
        out_specs=vmem(),
        compiler_params=params(),
        cost_estimate=cost(arrived.size),
        name="add",
    )(partials, arrived)


def last_kernel(low, places, partials, *refs):
    out, total, sem = refs[-3:]
    result = partials[lax.axis_index("seq")].astype(jnp.float32)
    for arrived, place in zip(refs, places):
        result = result + arrived[place].astype(jnp.float32)
    total[...] = result.astype(out.dtype)
    copy = pltpu.make_async_copy(total, out.at[:, pl.ds(low, total.shape[1])], sem)
    copy.start()
    copy.wait()


def last_call(low, partials, arrivals, out, shape):
    _, chunk, columns = partials.shape
    given = [] if out is None else [out]
    arrived, places = zip(*arrivals)
    return pl.pallas_call(
        functools.partial(last_kernel, low, places),
        out_shape=shape,
        in_specs=[vmem()] * (1 + len(arrived)) + [hbm()] * len(given),
        out_specs=hbm(),
        scratch_shapes=[pltpu.VMEM((chunk, columns), shape.dtype), pltpu.SemaphoreType.DMA],
        input_output_aliases={1 + len(arrived): 0} if given else {},
        compiler_params=params(),
        cost_estimate=cost(partials.size),
        name="last_sum",
    )(partials, *arrived, *given)


def grad_kernel(spans, slots, block, table, rows, *refs):
    hidden, outs, (cols,) = refs[:spans], refs[spans : 2 * spans], refs[2 * spans :]
    me = lax.axis_index("seq")
    count, before = live_count(table, 0, slots), rank_before(table, 0, spans, slots)
    chunk = rows.shape[0] // spans
    for s in range(spans):
        cols[s] = hidden[s][...]
    for s in range(spans):
        slot = wrap(lax.rem(me + s, spans) - lax.rem(before, spans), spans)
        outs[s][...] = jnp.zeros_like(outs[s])

        @pl.when(slot < count)
        def _():
            d_start = pl.multiple_of(table[0, slots + slot] * block, block)
            total = jnp.zeros((block, block), jnp.float32)
            for p in range(spans):
                total = total + lax.dot_general(
                    cols[wrap(me - chunk_at(p), spans), slot],
                    rows[p * chunk : (p + 1) * chunk, pl.ds(d_start, block)],
                    TN,
                    preferred_element_type=jnp.float32,
                )
            outs[s][...] = total.astype(outs[s].dtype)


def grad_call(sizes, table, rows, hidden_cols):
    spans = sizes[0]
    slots, chunk, block = hidden_cols[0].shape
    return pl.pallas_call(
        functools.partial(grad_kernel, *sizes),
        out_shape=[jax.ShapeDtypeStruct((block, block), jnp.bfloat16)] * spans,
        in_specs=[smem()] + [vmem()] * (spans + 1),
        out_specs=[vmem()] * spans,
        scratch_shapes=[pltpu.VMEM((spans, slots, chunk, block), jnp.bfloat16)],
        compiler_params=params(),
        cost_estimate=cost(WAIT * rows.size),
        name="tile_grad",
    )(table, rows, *hidden_cols)


def adam_kernel(spans, slots, table, *refs):
    arrived, refs = refs[:spans], refs[spans:]
    values, one, two, values_new, one_new, two_new, grads = refs
    me = lax.axis_index("seq")
    for s in range(spans):
        grads[s] = arrived[s][...]
    befores = [rank_before(table, s, spans, slots) for s in range(spans)]
    counts = [live_count(table, s, slots) for s in range(spans)]
    for owned in range(slots):
        rank = owned * spans + me
        source, live = jnp.int32(0), jnp.int32(0)
        for s in range(spans):
            holds = (befores[s] <= rank) & (rank < befores[s] + counts[s])
            source, live = jnp.where(holds, s, source), jnp.where(holds, 1, live)
        grad = grads[source].astype(jnp.float32)
        stored, old_one, old_two = values[owned], one[owned], two[owned]
        new_one = BETA_ONE * old_one + (1.0 - BETA_ONE) * grad
        new_two = BETA_TWO * old_two + (1.0 - BETA_TWO) * grad * grad
        stepped = (
            new_one
            / (1.0 - BETA_ONE**STEP)
            / (jnp.sqrt(new_two / (1.0 - BETA_TWO**STEP)) + EPSILON)
        )
        values_new[owned] = jnp.where(live > 0, stored - RATE * stepped, stored)
        one_new[owned] = jnp.where(live > 0, new_one, old_one)
        two_new[owned] = jnp.where(live > 0, new_two, old_two)


def adam_call(sizes, table, grads, *states):
    spans, slots, block = sizes
    tile = jax.ShapeDtypeStruct((slots, block, block), jnp.float32)
    return pl.pallas_call(
        functools.partial(adam_kernel, spans, slots),
        out_shape=(tile, tile, tile),
        in_specs=[smem()] + [vmem()] * (spans + 3),
        out_specs=(vmem(), vmem(), vmem()),
        scratch_shapes=[pltpu.VMEM((spans, block, block), jnp.bfloat16)],
        compiler_params=params(),
        cost_estimate=cost(slots * block * block),
        name="adam",
    )(table, *grads, *[state[0, 0] for state in states])


def take_from(array, axis, places):
    size = lax.axis_size(axis)
    return lax.ppermute(array, axis, [((i + places) % size, i) for i in range(size)])


def exchange(pieces):
    return [pieces[0]] + [take_from(pieces[s], "seq", -s) for s in range(1, len(pieces))]


class Ring:
    parts = [2, 3, 2]

    def __init__(self, spans):
        self.spans, self.steps = spans, spans - 1

    def first(self, me):
        return [wrap(me - 1, self.spans)]

    def move(self, step, sums):
        return take_from(sums, "seq", -1)

    def add(self, step, partials, moved):
        return add_call(lambda me: [wrap(me - step - 1, self.spans)], partials, moved[-1])

    def last(self, moved):
        return [(moved[-1], 0)]


class Line:
    parts = [2, 2, 2, 1]
    steps = 3

    def first(self, me):
        return [jnp.where(me < 2, 3, 0), jnp.where(me < 2, 2, 1)]

    def move(self, step, sums):
        pairs = [[(0, 1), (3, 2)], [(1, 2), (2, 1)], [(0, 1), (1, 0), (2, 3), (3, 2)]]
        return lax.ppermute(sums, "seq", pairs[step])

    def add(self, step, partials, moved):
        chunks_of = self.first if step == 1 else lambda me: [me + 1 - 2 * lax.rem(me, 2)]
        return add_call(chunks_of, partials, moved[-1])

    def last(self, moved):
        return [(moved[1], 1), (moved[2], 0)]


def per_device(
    hidden_in, cotangent, down_weight, tile_ids, tile_live, values, moment_one, moment_two
):
    spans, cores = lax.axis_size("seq"), lax.axis_size("dp")
    slots, block = values.shape[2], values.shape[3]
    f_width, d_width = down_weight.shape
    d_blocks, f_blocks = d_width // block, f_width // block
    chunk = hidden_in.shape[0]
    sizes = (spans, slots, block)
    group = max(size for size in range(1, 5) if f_blocks % size == 0)
    width = group * block
    plan = Line() if spans == 4 else Ring(spans)
    ends = [sum(plan.parts[:part]) for part in range(len(plan.parts) + 1)]
    cuts = [(f_blocks // group) * end // ends[-1] for end in ends]
    ranges = list(zip(cuts[:-1], cuts[1:]))

    firsts = [take_from(cotangent, "tensor", t) for t in range(1, lax.axis_size("tensor"))]
    local = [take_from(cotangent, "dp", d) for d in range(1, cores)]

    meta = jnp.concatenate([tile_ids[0], tile_live[0]], axis=1)
    metas = exchange([meta] * spans)
    values_half, hidden_here = pl.pallas_call(
        early_kernel,
        out_shape=[
            jax.ShapeDtypeStruct((slots, block, block), jnp.bfloat16),
            jax.ShapeDtypeStruct(hidden_in.shape, hidden_in.dtype),
        ],
        in_specs=[hbm(), hbm()],
        out_specs=[vmem(), vmem()],
        scratch_shapes=[
            pltpu.VMEM((slots, block, block), jnp.float32),
            pltpu.SemaphoreType.DMA((2,)),
        ],
        compiler_params=params(),
        cost_estimate=cost(hidden_in.size),
        name="early",
    )(stay(values[0, 0]), stay(hidden_in))
    local_rows, first_weight = pl.pallas_call(
        lay_kernel,
        out_shape=[
            jax.ShapeDtypeStruct((cores * chunk, d_width), cotangent.dtype),
            jax.ShapeDtypeStruct((ranges[0][1] * width, d_width), down_weight.dtype),
        ],
        in_specs=[hbm(), hbm()] + [vmem()] * (cores - 1),
        out_specs=[vmem(), vmem()],
        scratch_shapes=[pltpu.SemaphoreType.DMA((2,))],
        compiler_params=params(),
        cost_estimate=cost(cores * chunk * d_width),
        name="lay",
    )(stay(cotangent), stay(down_weight), *local)
    hidden_here, local_rows, first_weight = lax.optimization_barrier(
        (hidden_here, local_rows, first_weight)
    )
    table, *picked = pl.pallas_call(
        functools.partial(pick_kernel, *sizes, d_blocks),
        out_shape=[jax.ShapeDtypeStruct((spans, 3 * slots), jnp.int32)]
        + [jax.ShapeDtypeStruct((block, block), jnp.bfloat16)] * spans
        + [jax.ShapeDtypeStruct((slots, chunk, block), jnp.bfloat16)] * spans,
        in_specs=[smem()] * spans + [vmem(), vmem()],
        out_specs=[smem()] + [vmem()] * (2 * spans),
        compiler_params=params(),
        cost_estimate=cost(hidden_in.size),
        name="pick",
    )(*metas, values_half, hidden_here)
    stored = exchange(picked[:spans])
    hidden_cols = exchange(picked[spans:])

    firsts, stored = lax.optimization_barrier((firsts, stored))
    pieces = [local_rows]
    for first in firsts:
        pieces += [first] + [take_from(first, "dp", d) for d in range(1, cores)]

    partials, moved = [], []
    for part, (low, high) in enumerate(ranges):
        if part == 0:
            partial, first, rows, held = matmul_call(
                sizes, low, high, width, plan.first, table, first_weight, pieces, stored
            )
        else:
            if part == 2:
                send = grad_call(sizes, table, rows, hidden_cols)
                moved[0][-1], send = lax.optimization_barrier((moved[0][-1], send))
            if part > 1:
                sums = plan.add(1, partials[part - 2], moved[part - 2])
                rows, sums = lax.optimization_barrier((rows, sums))
                moved[part - 2].append(plan.move(1, sums))
            partial, first = matmul_call(
                sizes, low, high, width, plan.first, table, down_weight, [rows, held]
            )
        partials.append(partial)
        moved.append([plan.move(0, first)])

    grads = exchange(send)
    turn = partials[-1]
    todo = [(step, part) for step in range(1, plan.steps) for part in range(len(ranges))]
    todo = [(step, part) for step, part in todo if len(moved[part]) <= step]
    for step, part in sorted(todo, key=lambda item: (item[1] + LAG * item[0], -item[0])):
        if (step, part) == (plan.steps - 1, len(ranges) - 1):
            turn = (turn, grads)
        moved[part][-1], turn = lax.optimization_barrier((moved[part][-1], turn))
        turn = plan.add(step, partials[part], moved[part])
        moved[part].append(plan.move(step, turn))
    new = adam_call(sizes, table, grads, values, moment_one, moment_two)

    hidden_grad = None
    shape = jax.ShapeDtypeStruct((chunk, f_width), jnp.bfloat16)
    for part, (low, _) in enumerate(ranges):
        if part == len(ranges) - 1:
            moved[part][-1], new = lax.optimization_barrier((moved[part][-1], new))
        hidden_grad = last_call(
            low * width, partials[part], plan.last(moved[part]), hidden_grad, shape
        )
    return (hidden_grad,) + tuple(array[None, None] for array in new)


def solution(mesh):
    shards = P(("groups", "seq"), ("tensor", "dp"))
    tiles = P(("groups", "seq"), ("tensor", "dp"), None, None, None)
    lists = P(("groups", "seq"), ("tensor", "dp"), None)
    return jax.shard_map(
        per_device,
        mesh=mesh,
        in_specs=(
            shards,
            P(("groups", "tensor", "dp"), "seq"),
            P(("tensor", "dp"), "seq"),
            lists,
            lists,
            tiles,
            tiles,
            tiles,
        ),
        out_specs=(shards, tiles, tiles, tiles),
        check_vma=False,
    )
```

time: 113 us -> 123 us (1.088)
  starting transfers between devices: 31.1 us -> 46 us
  waiting for transfers between devices: 52.2 us -> 46.7 us
  local copies, waits for them, and re-layouts: 1.33 us -> 0.02 us
    ppermute x0 -> x12, starting transfers between devices: none -> 29.9 us  [move(): return lax.ppermute(sums, 'seq', pairs[step])]
    ppermute x18 -> x15, waiting for transfers between devices: 52.2 us -> 36.6 us  [take_from(): lax.ppermute(array, axis, [((i + places) % size, i) for i in range(size)])]
    ppermute x18 -> x15, starting transfers between devices: 31.1 us -> 16.1 us  [take_from(): lax.ppermute(array, axis, [((i + places) % size, i) for i in range(size)])]
    ppermute x0 -> x12, waiting for transfers between devices: none -> 10.1 us  [move(): return lax.ppermute(sums, 'seq', pairs[step])]
    pallas_call x15 -> x19, Pallas kernels: 22.5 us -> 24.1 us  [the longest x4 15.9 us: matmul_call(): pl.pallas_call(functools.partial(matmul_kernel, sizes, low, width, firsts...]
    unnamed x10 -> x6, local copies, waits for them, and re-layouts: 1.33 us -> 0.02 us
  transfers between devices with their start and end apart: 18 -> 27, of which waited for: 10 -> 14; matrix products, arithmetic and copies ran while one was open for 0% -> 1% of each run, Pallas kernels for 22% -> 18%
where the time goes in v7:
time: 123 us; the launch traced here: 122 us
  waiting for transfers between devices  46.7 us (38%)
  starting transfers between devices  46 us (37%)
  Pallas kernels  27.3 us (22%)
    ppermute x15, waiting for transfers between devices, take_from(): lax.ppermute(array, axis, [((i + places) % size, i) for i in range(size)])  36.6 us
    ppermute x12, starting transfers between devices, move(): return lax.ppermute(sums, 'seq', pairs[step])  29.9 us
    ppermute x15, starting transfers between devices, take_from(): lax.ppermute(array, axis, [((i + places) % size, i) for i in range(size)])  16.1 us
    pallas_call x4, Pallas kernels, matmul_call(): pl.pallas_call(functools.partial(matmul_kernel, sizes, low, width, firsts...  15.9 us
    ppermute x12, waiting for transfers between devices, move(): return lax.ppermute(sums, 'seq', pairs[step])  10.1 us
    pallas_call x4, Pallas kernels, last_call(): pl.pallas_call(functools.partial(last_kernel, low, places), out_shape=sha...  3.17 us
  transfers between devices with their start and end apart: 27, of which 14 were waited for; matrix products, arithmetic and copies ran while one was open for 1% of the time, Pallas kernels for 18%

profile of v7, /device:TPU:0, one launch (start us, length us, event | category | flops | bytes accessed | tf_op | source)
XLA Modules:
  0.0 121.7 jit_solution(7242181953799109235)
XLA Ops:
  1.1 2.6 %collective-permute-start.4 = (bf16[128,2048]{1,0:T(8,128)(2,1)}, bf16[128,2048]{1,0:T(8,128)(2,1)S(1)}, u32[]{:S(2)}, u32[]{:S(2)}) collective-permute-start(bf16[128,2048]{1,0:T(8,128)(2,1)} %own.1), channel_id=1, source_target_pairs={{2,0},{0,2},{3,1},{1,3},{6,4},{4,6},{7,5},{5,7},{10,8},{8,10},{11,... | collective-permute-start | bytes 1572872 | tf_op jit(solution)/shard_map/ppermute | solution.py:333
  4.5 3.6 %collective-permute-start.2 = (s32[1,8]{1,0:T(1,128)S(1)}, s32[1,8]{1,0:T(1,128)S(1)}, u32[]{:S(2)}, u32[]{:S(2)}) collective-permute-start(s32[1,8]{1,0:T(1,128)S(1)} %pad_add_fusion.refs_0_), channel_id=1, source_target_pairs={{4,0},{8,4},{12,8},{0,12},{5,1},{9,5},{13,9},{1,13},{6,2},{10,6},{... | collective-permute-start | bytes 104 | tf_op jit(solution)/shard_map/ppermute | solution.py:333
  10.4 2.3 %lay.1 = (bf16[256,2048]{1,0:T(8,128)(2,1)S(1)}, bf16[1024,2048]{1,0:T(8,128)(2,1)S(1)}) custom-call(bf16[128,2048]{1,0:T(8,128)(2,1)} %own.1, bf16[3584,2048]{1,0:T(8,128)(2,1)} %weight.7, bf16[128,2048]{1,0:T(8,128)(2,1)S(1)} %collective-permute-done.3.refs_0_), custom_call_target="tpu_custom_call" | custom-call | flops 524288 | bytes 1048576 | tf_op jit(solution)/shard_map/lay/pallas_call | solution.py:415
  14.8 1.9 %collective-permute-start.5 = (bf16[128,128]{1,0:T(8,128)(2,1)S(1)}, bf16[128,128]{1,0:T(8,128)(2,1)S(1)}, u32[]{:S(2)}, u32[]{:S(2)}) collective-permute-start(bf16[128,128]{1,0:T(8,128)(2,1)S(1)} %get-tuple-element.70), channel_id=1, source_target_pairs={{12,0},{0,4},{4,8},{8,12},{13,1},{1,5},{5,9},{9,13},{14,2},{2,6},{... | collective-permute-start | bytes 98312 | tf_op jit(solution)/shard_map/ppermute | solution.py:333
  21.8 1.9 %collective-permute-done.8.refs_2_ = bf16[128,2048]{1,0:T(8,128)(2,1)S(1)} collective-permute-done((bf16[128,2048]{1,0:T(8,128)(2,1)S(1)}, bf16[128,2048]{1,0:T(8,128)(2,1)S(1)}, u32[]{:S(2)}, u32[]{:S(2)}) %collective-permute-start.8) | collective-permute-done | bytes 524320 | tf_op jit(solution)/shard_map/ppermute | solution.py:333
  23.8 3.7 %partial.4 = (bf16[4,128,1024]{2,1,0:T(8,128)(2,1)S(1)}, bf16[2,128,1024]{2,1,0:T(8,128)(2,1)S(1)}, bf16[512,2048]{1,0:T(8,128)(2,1)S(1)}, bf16[4,128,128]{2,1,0:T(8,128)(2,1)S(1)}) custom-call(s32[4,12]{1,0:T(4,128)S(1)} %get-tuple-element.66.table, bf16[1024,2048]{1,0:T(8,128)(2,1)S(1)} %get-tuple-element.67.weight, ...), custom_call_target="tpu_custom_call" | custom-call | flops 2147483648 | bytes 4194304 | tf_op jit(solution)/shard_map/partial/pallas_call | solution.py:184
  27.5 3.3 %collective-permute-start.9 = (bf16[2,128,1024]{2,1,0:T(8,128)(2,1)S(1)}, bf16[2,128,1024]{2,1,0:T(8,128)(2,1)S(1)}, u32[]{:S(2)}, u32[]{:S(2)}) collective-permute-start(bf16[2,128,1024]{2,1,0:T(8,128)(2,1)S(1)} %get-tuple-element.80), channel_id=1, source_target_pairs={{0,4},{12,8},{1,5},{13,9},{2,6},{14,10},{3,7},{15,11},{16,20},{28,... | collective-permute-start | bytes 1572872 | tf_op jit(solution)/shard_map/ppermute | solution.py:368
  30.8 2.5 %collective-permute-start.11 = (bf16[4,128,128]{2,1,0:T(8,128)(2,1)S(1)}, bf16[4,128,128]{2,1,0:T(8,128)(2,1)S(1)}, u32[]{:S(2)}, u32[]{:S(2)}) collective-permute-start(bf16[4,128,128]{2,1,0:T(8,128)(2,1)S(1)} %get-tuple-element.83), channel_id=1, source_target_pairs={{8,0},{12,4},{0,8},{4,12},{9,1},{13,5},{1,9},{5,13},{10,2},{14,6},... | collective-permute-start | bytes 393224 | tf_op jit(solution)/shard_map/ppermute | solution.py:333
  34.6 4.5 %partial.5 = (bf16[4,128,1024]{2,1,0:T(8,128)(2,1)S(1)}, bf16[2,128,1024]{2,1,0:T(8,128)(2,1)S(1)}) custom-call(s32[4,12]{1,0:T(4,128)S(1)} %get-tuple-element.66.table, bf16[3584,2048]{1,0:T(8,128)(2,1)} %weight.7, bf16[512,2048]{1,0:T(8,128)(2,1)S(1)} %get-tuple-element.94.rows.refs_0_, bf16[4,128,128]{2,1,0:T(8,128)(2,1)S(1)} %get-tuple-element.91.refs_1_), custom_call_target="tpu_custom_call" | custom-call | flops 2147483648 | bytes 4194304 | tf_op jit(solution)/shard_map/partial/pallas_call | solution.py:184
  39.1 2.7 %collective-permute-start.13 = (bf16[2,128,1024]{2,1,0:T(8,128)(2,1)S(1)}, bf16[2,128,1024]{2,1,0:T(8,128)(2,1)S(1)}, u32[]{:S(2)}, u32[]{:S(2)}) collective-permute-start(bf16[2,128,1024]{2,1,0:T(8,128)(2,1)S(1)} %get-tuple-element.93), channel_id=1, source_target_pairs={{0,4},{12,8},{1,5},{13,9},{2,6},{14,10},{3,7},{15,11},{16,20},{28,... | collective-permute-start | bytes 1572872 | tf_op jit(solution)/shard_map/ppermute | solution.py:368
  41.8 6.4 %collective-permute-done.10.refs_1_ = bf16[4,128,128]{2,1,0:T(8,128)(2,1)S(1)} collective-permute-done((bf16[4,128,128]{2,1,0:T(8,128)(2,1)S(1)}, bf16[4,128,128]{2,1,0:T(8,128)(2,1)S(1)}, u32[]{:S(2)}, u32[]{:S(2)}) %collective-permute-start.10) | collective-permute-done | bytes 131104 | tf_op jit(solution)/shard_map/ppermute | solution.py:333
  48.6 2.8 %collective-permute-done.12.refs_3_ = bf16[4,128,128]{2,1,0:T(8,128)(2,1)S(1)} collective-permute-done((bf16[4,128,128]{2,1,0:T(8,128)(2,1)S(1)}, bf16[4,128,128]{2,1,0:T(8,128)(2,1)S(1)}, u32[]{:S(2)}, u32[]{:S(2)}) %collective-permute-start.12) | collective-permute-done | bytes 131104 | tf_op jit(solution)/shard_map/ppermute | solution.py:333
  53.1 4.5 %partial.7 = (bf16[4,128,1024]{2,1,0:T(8,128)(2,1)S(1)}, bf16[2,128,1024]{2,1,0:T(8,128)(2,1)S(1)}) custom-call(s32[4,12]{1,0:T(4,128)S(1)} %get-tuple-element.66.table, bf16[3584,2048]{1,0:T(8,128)(2,1)} %weight.7, bf16[512,2048]{1,0:T(8,128)(2,1)S(1)} %get-tuple-element.94.rows.refs_0_, bf16[4,128,128]{2,1,0:T(8,128)(2,1)S(1)} %get-tuple-element.91.refs_1_), custom_call_target="tpu_custom_call" | custom-call | flops 2147483648 | bytes 4194304 | tf_op jit(solution)/shard_map/partial/pallas_call | solution.py:184
  57.6 7.1 %collective-permute-start.16 = (bf16[2,128,1024]{2,1,0:T(8,128)(2,1)S(1)}, bf16[2,128,1024]{2,1,0:T(8,128)(2,1)S(1)}, u32[]{:S(2)}, u32[]{:S(2)}) collective-permute-start(bf16[2,128,1024]{2,1,0:T(8,128)(2,1)S(1)} %get-tuple-element.99), channel_id=1, source_target_pairs={{0,4},{12,8},{1,5},{13,9},{2,6},{14,10},{3,7},{15,11},{16,20},{28,... | collective-permute-start | bytes 1572872 | tf_op jit(solution)/shard_map/ppermute | solution.py:368
  65.6 3.2 %partial.6 = (bf16[4,128,512]{2,1,0:T(8,128)(2,1)S(1)}, bf16[2,128,512]{2,1,0:T(8,128)(2,1)S(1)}) custom-call(s32[4,12]{1,0:T(4,128)S(1)} %get-tuple-element.66.table, bf16[3584,2048]{1,0:T(8,128)(2,1)} %weight.7, bf16[512,2048]{1,0:T(8,128)(2,1)S(1)} %get-tuple-element.94.rows.refs_0_, bf16[4,128,128]{2,1,0:T(8,128)(2,1)S(1)} %get-tuple-element.91.refs_1_), custom_call_target="tpu_custom_call" | custom-call | flops 1073741824 | bytes 2097152 | tf_op jit(solution)/shard_map/partial/pallas_call | solution.py:184
  68.9 4.8 %collective-permute-done.16.arrived = bf16[2,128,1024]{2,1,0:T(8,128)(2,1)S(1)} collective-permute-done((bf16[2,128,1024]{2,1,0:T(8,128)(2,1)S(1)}, bf16[2,128,1024]{2,1,0:T(8,128)(2,1)S(1)}, u32[]{:S(2)}, u32[]{:S(2)}) %collective-permute-start.16) | collective-permute-done | bytes 524320 | tf_op jit(solution)/shard_map/ppermute | solution.py:368
  74.5 5.9 %collective-permute-start.14 = (bf16[2,128,512]{2,1,0:T(8,128)(2,1)S(1)}, bf16[2,128,512]{2,1,0:T(8,128)(2,1)S(1)}, u32[]{:S(2)}, u32[]{:S(2)}) collective-permute-start(bf16[2,128,512]{2,1,0:T(8,128)(2,1)S(1)} %get-tuple-element.96), channel_id=1, source_target_pairs={{0,4},{12,8},{1,5},{13,9},{2,6},{14,10},{3,7},{15,11},{16,20},{28,... | collective-permute-start | bytes 786440 | tf_op jit(solution)/shard_map/ppermute | solution.py:368
  80.5 3.8 %collective-permute-done.14.arrived = bf16[2,128,512]{2,1,0:T(8,128)(2,1)S(1)} collective-permute-done((bf16[2,128,512]{2,1,0:T(8,128)(2,1)S(1)}, bf16[2,128,512]{2,1,0:T(8,128)(2,1)S(1)}, u32[]{:S(2)}, u32[]{:S(2)}) %collective-permute-start.14) | collective-permute-done | bytes 262176 | tf_op jit(solution)/shard_map/ppermute | solution.py:368
  85.0 5.5 %collective-permute-start.26 = (bf16[1,128,1024]{2,1,0:T(8,128)(2,1)S(1)}, bf16[1,128,1024]{2,1,0:T(8,128)(2,1)S(1)}, u32[]{:S(2)}, u32[]{:S(2)}) collective-permute-start(bf16[1,128,1024]{2,1,0:T(8,128)(2,1)S(1)} %add.12), channel_id=1, source_target_pairs={{0,4},{4,0},{8,12},{12,8},{1,5},{5,1},{9,13},{13,9},{2,6},{6,2},{1... | collective-permute-start | bytes 786440 | tf_op jit(solution)/shard_map/ppermute | solution.py:368
  90.7 2.5 %collective-permute-start.24 = (bf16[1,128,1024]{2,1,0:T(8,128)(2,1)S(1)}, bf16[1,128,1024]{2,1,0:T(8,128)(2,1)S(1)}, u32[]{:S(2)}, u32[]{:S(2)}) collective-permute-start(bf16[1,128,1024]{2,1,0:T(8,128)(2,1)S(1)} %add.16), channel_id=1, source_target_pairs={{0,4},{4,0},{8,12},{12,8},{1,5},{5,1},{9,13},{13,9},{2,6},{6,2},{1... | collective-permute-start | bytes 786440 | tf_op jit(solution)/shard_map/ppermute | solution.py:368
  93.3 12.9 %collective-permute-done.20.refs_1_ = bf16[128,128]{1,0:T(8,128)(2,1)S(1)} collective-permute-done((bf16[128,128]{1,0:T(8,128)(2,1)S(1)}, bf16[128,128]{1,0:T(8,128)(2,1)S(1)}, u32[]{:S(2)}, u32[]{:S(2)}) %collective-permute-start.20) | collective-permute-done | bytes 32800 | tf_op jit(solution)/shard_map/ppermute | solution.py:333
  106.2 5.0 %collective-permute-done.21.refs_2_ = bf16[128,128]{1,0:T(8,128)(2,1)S(1)} collective-permute-done((bf16[128,128]{1,0:T(8,128)(2,1)S(1)}, bf16[128,128]{1,0:T(8,128)(2,1)S(1)}, u32[]{:S(2)}, u32[]{:S(2)}) %collective-permute-start.21) | collective-permute-done | bytes 32800 | tf_op jit(solution)/shard_map/ppermute | solution.py:333
  111.3 3.8 %collective-permute-done.22.refs_3_ = bf16[128,128]{1,0:T(8,128)(2,1)S(1)} collective-permute-done((bf16[128,128]{1,0:T(8,128)(2,1)S(1)}, bf16[128,128]{1,0:T(8,128)(2,1)S(1)}, u32[]{:S(2)}, u32[]{:S(2)}) %collective-permute-start.22) | collective-permute-done | bytes 32800 | tf_op jit(solution)/shard_map/ppermute | solution.py:333
  115.3 1.6 %adam.1 = (f32[4,128,128]{2,1,0:T(8,128)}, f32[4,128,128]{2,1,0:T(8,128)}, f32[4,128,128]{2,1,0:T(8,128)}) custom-call(s32[4,12]{1,0:T(4,128)S(1)} %get-tuple-element.66.table, bf16[128,128]{1,0:T(8,128)(2,1)S(1)} %get-tuple-element.106.refs_0_, bf16[128,128]{1,0:T(8,128)(2,1)S(1)} %collective-permute-done.20.refs_1_, ...), custom_call_target="tpu_custom_call" | custom-call | flops 65536 | bytes 131072 | tf_op jit(solution)/shard_map/adam/pallas_call | solution.py:319
  (58 shorter events, 22.1 us)
Async XLA Ops:
  0.6 9.7 %collective-permute-start.3 = (bf16[128,2048]{1,0:T(8,128)(2,1)}, bf16[128,2048]{1,0:T(8,128)(2,1)S(1)}, u32[]{:S(2)}, u32[]{:S(2)}) collective-permute-start(bf16[128,2048]{1,0:T(8,128)(2,1)} %own.1), channel_id=1, source_target_pairs={{1,0},{0,1},{3,2},{2,3},{5,4},{4,5},{7,6},{6,7},{9,8},{8,9},{11,10... | collective-permute-start | bytes 1572872 | tf_op jit(solution)/shard_map/ppermute | solution.py:333
  1.1 18.0 %collective-permute-start.4 = (bf16[128,2048]{1,0:T(8,128)(2,1)}, bf16[128,2048]{1,0:T(8,128)(2,1)S(1)}, u32[]{:S(2)}, u32[]{:S(2)}) collective-permute-start(bf16[128,2048]{1,0:T(8,128)(2,1)} %own.1), channel_id=1, source_target_pairs={{2,0},{0,2},{3,1},{1,3},{6,4},{4,6},{7,5},{5,7},{10,8},{8,10},{11,... | collective-permute-start | bytes 1572872 | tf_op jit(solution)/shard_map/ppermute | solution.py:333
  4.5 8.3 %collective-permute-start.2 = (s32[1,8]{1,0:T(1,128)S(1)}, s32[1,8]{1,0:T(1,128)S(1)}, u32[]{:S(2)}, u32[]{:S(2)}) collective-permute-start(s32[1,8]{1,0:T(1,128)S(1)} %pad_add_fusion.refs_0_), channel_id=1, source_target_pairs={{4,0},{8,4},{12,8},{0,12},{5,1},{9,5},{13,9},{1,13},{6,2},{10,6},{... | collective-permute-start | bytes 104 | tf_op jit(solution)/shard_map/ppermute | solution.py:333
  8.1 4.7 %collective-permute-start.1 = (s32[1,8]{1,0:T(1,128)S(1)}, s32[1,8]{1,0:T(1,128)S(1)}, u32[]{:S(2)}, u32[]{:S(2)}) collective-permute-start(s32[1,8]{1,0:T(1,128)S(1)} %pad_add_fusion.refs_0_), channel_id=1, source_target_pairs={{8,0},{12,4},{0,8},{4,12},{9,1},{13,5},{1,9},{5,13},{10,2},{14,6},... | collective-permute-start | bytes 104 | tf_op jit(solution)/shard_map/ppermute | solution.py:333
  8.1 5.3 %collective-permute-start = (s32[1,8]{1,0:T(1,128)S(1)}, s32[1,8]{1,0:T(1,128)S(1)}, u32[]{:S(2)}, u32[]{:S(2)}) collective-permute-start(s32[1,8]{1,0:T(1,128)S(1)} %pad_add_fusion.refs_0_), channel_id=1, source_target_pairs={{12,0},{0,4},{4,8},{8,12},{13,1},{1,5},{5,9},{9,13},{14,2},{2,6},{... | collective-permute-start | bytes 104 | tf_op jit(solution)/shard_map/ppermute | solution.py:333
  14.8 5.9 %collective-permute-start.5 = (bf16[128,128]{1,0:T(8,128)(2,1)S(1)}, bf16[128,128]{1,0:T(8,128)(2,1)S(1)}, u32[]{:S(2)}, u32[]{:S(2)}) collective-permute-start(bf16[128,128]{1,0:T(8,128)(2,1)S(1)} %get-tuple-element.70), channel_id=1, source_target_pairs={{12,0},{0,4},{4,8},{8,12},{13,1},{1,5},{5,9},{9,13},{14,2},{2,6},{... | collective-permute-start | bytes 98312 | tf_op jit(solution)/shard_map/ppermute | solution.py:333
  16.7 5.1 %collective-permute-start.6 = (bf16[128,128]{1,0:T(8,128)(2,1)S(1)}, bf16[128,128]{1,0:T(8,128)(2,1)S(1)}, u32[]{:S(2)}, u32[]{:S(2)}) collective-permute-start(bf16[128,128]{1,0:T(8,128)(2,1)S(1)} %get-tuple-element.71), channel_id=1, source_target_pairs={{8,0},{12,4},{0,8},{4,12},{9,1},{13,5},{1,9},{5,13},{10,2},{14,6},... | collective-permute-start | bytes 98312 | tf_op jit(solution)/shard_map/ppermute | solution.py:333
  27.5 24.8 %collective-permute-start.9 = (bf16[2,128,1024]{2,1,0:T(8,128)(2,1)S(1)}, bf16[2,128,1024]{2,1,0:T(8,128)(2,1)S(1)}, u32[]{:S(2)}, u32[]{:S(2)}) collective-permute-start(bf16[2,128,1024]{2,1,0:T(8,128)(2,1)S(1)} %get-tuple-element.80), channel_id=1, source_target_pairs={{0,4},{12,8},{1,5},{13,9},{2,6},{14,10},{3,7},{15,11},{16,20},{28,... | collective-permute-start | bytes 1572872 | tf_op jit(solution)/shard_map/ppermute | solution.py:368
  30.7 17.5 %collective-permute-start.10 = (bf16[4,128,128]{2,1,0:T(8,128)(2,1)S(1)}, bf16[4,128,128]{2,1,0:T(8,128)(2,1)S(1)}, u32[]{:S(2)}, u32[]{:S(2)}) collective-permute-start(bf16[4,128,128]{2,1,0:T(8,128)(2,1)S(1)} %get-tuple-element.82), channel_id=1, source_target_pairs={{12,0},{0,4},{4,8},{8,12},{13,1},{1,5},{5,9},{9,13},{14,2},{2,6},{... | collective-permute-start | bytes 393224 | tf_op jit(solution)/shard_map/ppermute | solution.py:333
  30.8 17.8 %collective-permute-start.11 = (bf16[4,128,128]{2,1,0:T(8,128)(2,1)S(1)}, bf16[4,128,128]{2,1,0:T(8,128)(2,1)S(1)}, u32[]{:S(2)}, u32[]{:S(2)}) collective-permute-start(bf16[4,128,128]{2,1,0:T(8,128)(2,1)S(1)} %get-tuple-element.83), channel_id=1, source_target_pairs={{8,0},{12,4},{0,8},{4,12},{9,1},{13,5},{1,9},{5,13},{10,2},{14,6},... | collective-permute-start | bytes 393224 | tf_op jit(solution)/shard_map/ppermute | solution.py:333
  33.3 18.1 %collective-permute-start.12 = (bf16[4,128,128]{2,1,0:T(8,128)(2,1)S(1)}, bf16[4,128,128]{2,1,0:T(8,128)(2,1)S(1)}, u32[]{:S(2)}, u32[]{:S(2)}) collective-permute-start(bf16[4,128,128]{2,1,0:T(8,128)(2,1)S(1)} %get-tuple-element.84), channel_id=1, source_target_pairs={{4,0},{8,4},{12,8},{0,12},{5,1},{9,5},{13,9},{1,13},{6,2},{10,6},{... | collective-permute-start | bytes 393224 | tf_op jit(solution)/shard_map/ppermute | solution.py:333
  39.1 25.6 %collective-permute-start.13 = (bf16[2,128,1024]{2,1,0:T(8,128)(2,1)S(1)}, bf16[2,128,1024]{2,1,0:T(8,128)(2,1)S(1)}, u32[]{:S(2)}, u32[]{:S(2)}) collective-permute-start(bf16[2,128,1024]{2,1,0:T(8,128)(2,1)S(1)} %get-tuple-element.93), channel_id=1, source_target_pairs={{0,4},{12,8},{1,5},{13,9},{2,6},{14,10},{3,7},{15,11},{16,20},{28,... | collective-permute-start | bytes 1572872 | tf_op jit(solution)/shard_map/ppermute | solution.py:368
  52.4 16.4 %collective-permute-start.17 = (bf16[2,128,1024]{2,1,0:T(8,128)(2,1)S(1)}, bf16[2,128,1024]{2,1,0:T(8,128)(2,1)S(1)}, u32[]{:S(2)}, u32[]{:S(2)}) collective-permute-start(bf16[2,128,1024]{2,1,0:T(8,128)(2,1)S(1)} %add.10), channel_id=1, source_target_pairs={{4,8},{8,4},{5,9},{9,5},{6,10},{10,6},{7,11},{11,7},{20,24},{24,20... | collective-permute-start | bytes 1572872 | tf_op jit(solution)/shard_map/ppermute | solution.py:368
  57.6 16.1 %collective-permute-start.16 = (bf16[2,128,1024]{2,1,0:T(8,128)(2,1)S(1)}, bf16[2,128,1024]{2,1,0:T(8,128)(2,1)S(1)}, u32[]{:S(2)}, u32[]{:S(2)}) collective-permute-start(bf16[2,128,1024]{2,1,0:T(8,128)(2,1)S(1)} %get-tuple-element.99), channel_id=1, source_target_pairs={{0,4},{12,8},{1,5},{13,9},{2,6},{14,10},{3,7},{15,11},{16,20},{28,... | collective-permute-start | bytes 1572872 | tf_op jit(solution)/shard_map/ppermute | solution.py:368
  64.9 15.6 %collective-permute-start.15 = (bf16[2,128,1024]{2,1,0:T(8,128)(2,1)S(1)}, bf16[2,128,1024]{2,1,0:T(8,128)(2,1)S(1)}, u32[]{:S(2)}, u32[]{:S(2)}) collective-permute-start(bf16[2,128,1024]{2,1,0:T(8,128)(2,1)S(1)} %add.11), channel_id=1, source_target_pairs={{4,8},{8,4},{5,9},{9,5},{6,10},{10,6},{7,11},{11,7},{20,24},{24,20... | collective-permute-start | bytes 1572872 | tf_op jit(solution)/shard_map/ppermute | solution.py:368
  73.8 16.8 %collective-permute-start.19 = (bf16[2,128,1024]{2,1,0:T(8,128)(2,1)S(1)}, bf16[2,128,1024]{2,1,0:T(8,128)(2,1)S(1)}, u32[]{:S(2)}, u32[]{:S(2)}) collective-permute-start(bf16[2,128,1024]{2,1,0:T(8,128)(2,1)S(1)} %add.13), channel_id=1, source_target_pairs={{4,8},{8,4},{5,9},{9,5},{6,10},{10,6},{7,11},{11,7},{20,24},{24,20... | collective-permute-start | bytes 1572872 | tf_op jit(solution)/shard_map/ppermute | solution.py:368
  74.5 9.7 %collective-permute-start.14 = (bf16[2,128,512]{2,1,0:T(8,128)(2,1)S(1)}, bf16[2,128,512]{2,1,0:T(8,128)(2,1)S(1)}, u32[]{:S(2)}, u32[]{:S(2)}) collective-permute-start(bf16[2,128,512]{2,1,0:T(8,128)(2,1)S(1)} %get-tuple-element.96), channel_id=1, source_target_pairs={{0,4},{12,8},{1,5},{13,9},{2,6},{14,10},{3,7},{15,11},{16,20},{28,... | collective-permute-start | bytes 786440 | tf_op jit(solution)/shard_map/ppermute | solution.py:368
  84.4 30.7 %collective-permute-start.18 = (bf16[2,128,512]{2,1,0:T(8,128)(2,1)S(1)}, bf16[2,128,512]{2,1,0:T(8,128)(2,1)S(1)}, u32[]{:S(2)}, u32[]{:S(2)}) collective-permute-start(bf16[2,128,512]{2,1,0:T(8,128)(2,1)S(1)} %add.15), channel_id=1, source_target_pairs={{4,8},{8,4},{5,9},{9,5},{6,10},{10,6},{7,11},{11,7},{20,24},{24,20... | collective-permute-start | bytes 786440 | tf_op jit(solution)/shard_map/ppermute | solution.py:368
  85.0 31.9 %collective-permute-start.26 = (bf16[1,128,1024]{2,1,0:T(8,128)(2,1)S(1)}, bf16[1,128,1024]{2,1,0:T(8,128)(2,1)S(1)}, u32[]{:S(2)}, u32[]{:S(2)}) collective-permute-start(bf16[1,128,1024]{2,1,0:T(8,128)(2,1)S(1)} %add.12), channel_id=1, source_target_pairs={{0,4},{4,0},{8,12},{12,8},{1,5},{5,1},{9,13},{13,9},{2,6},{6,2},{1... | collective-permute-start | bytes 786440 | tf_op jit(solution)/shard_map/ppermute | solution.py:368
  90.6 27.2 %collective-permute-start.25 = (bf16[1,128,1024]{2,1,0:T(8,128)(2,1)S(1)}, bf16[1,128,1024]{2,1,0:T(8,128)(2,1)S(1)}, u32[]{:S(2)}, u32[]{:S(2)}) collective-permute-start(bf16[1,128,1024]{2,1,0:T(8,128)(2,1)S(1)} %add.14), channel_id=1, source_target_pairs={{0,4},{4,0},{8,12},{12,8},{1,5},{5,1},{9,13},{13,9},{2,6},{6,2},{1... | collective-permute-start | bytes 786440 | tf_op jit(solution)/shard_map/ppermute | solution.py:368
  90.7 29.4 %collective-permute-start.24 = (bf16[1,128,1024]{2,1,0:T(8,128)(2,1)S(1)}, bf16[1,128,1024]{2,1,0:T(8,128)(2,1)S(1)}, u32[]{:S(2)}, u32[]{:S(2)}) collective-permute-start(bf16[1,128,1024]{2,1,0:T(8,128)(2,1)S(1)} %add.16), channel_id=1, source_target_pairs={{0,4},{4,0},{8,12},{12,8},{1,5},{5,1},{9,13},{13,9},{2,6},{6,2},{1... | collective-permute-start | bytes 786440 | tf_op jit(solution)/shard_map/ppermute | solution.py:368
  93.2 13.0 %collective-permute-start.20 = (bf16[128,128]{1,0:T(8,128)(2,1)S(1)}, bf16[128,128]{1,0:T(8,128)(2,1)S(1)}, u32[]{:S(2)}, u32[]{:S(2)}) collective-permute-start(bf16[128,128]{1,0:T(8,128)(2,1)S(1)} %get-tuple-element.107), channel_id=1, source_target_pairs={{12,0},{0,4},{4,8},{8,12},{13,1},{1,5},{5,9},{9,13},{14,2},{2,6},{... | collective-permute-start | bytes 98312 | tf_op jit(solution)/shard_map/ppermute | solution.py:333
  106.2 5.0 %collective-permute-start.21 = (bf16[128,128]{1,0:T(8,128)(2,1)S(1)}, bf16[128,128]{1,0:T(8,128)(2,1)S(1)}, u32[]{:S(2)}, u32[]{:S(2)}) collective-permute-start(bf16[128,128]{1,0:T(8,128)(2,1)S(1)} %get-tuple-element.108), channel_id=1, source_target_pairs={{8,0},{12,4},{0,8},{4,12},{9,1},{13,5},{1,9},{5,13},{10,2},{14,6},... | collective-permute-start | bytes 98312 | tf_op jit(solution)/shard_map/ppermute | solution.py:333
  115.1 5.0 %collective-permute-start.23 = (bf16[1,128,512]{2,1,0:T(8,128)(2,1)S(1)}, bf16[1,128,512]{2,1,0:T(8,128)(2,1)S(1)}, u32[]{:S(2)}, u32[]{:S(2)}) collective-permute-start(bf16[1,128,512]{2,1,0:T(8,128)(2,1)S(1)} %add.17), channel_id=1, source_target_pairs={{0,4},{4,0},{8,12},{12,8},{1,5},{5,1},{9,13},{13,9},{2,6},{6,2},{1... | collective-permute-start | bytes 393224 | tf_op jit(solution)/shard_map/ppermute | solution.py:368
  (6 other events, 149.3 us)

commit v8 on v7

--- a/solution.py
+++ b/solution.py
@@ -13,8 +13,9 @@
 RATE = 0.01
 EPSILON = 1e-08
 VMEM_LIMIT = 24 * 1024 * 1024
-WAIT = 2000
-LAG = 2
+MATMUL = 4096
+PARTS = (3, 2, 2)
+RIDE = 2
 NT = (((1,), (1,)), ((), ()))
 TN = (((0,), (0,)), ((), ()))
 
@@ -115,12 +116,14 @@
     return t_place * cores + d_place
 
 
-def matmul_kernel(sizes, low, width, firsts_of, stores, table, weight, *refs):
+def matmul_kernel(sizes, low, width, ends, stores, table, weight, *refs):
     spans, slots, block = sizes
     step = pl.program_id(0)
     me = lax.axis_index("seq")
+    parts, total = len(ends), refs[-1]
     if stores:
-        given, stored, (out, first, rows, held, total) = refs[: -stores - 5], refs[-stores - 5 : -5], refs[-5:]
+        given, stored = refs[: -stores - 2 * parts - 3], refs[-stores - 2 * parts - 3 : -2 * parts - 3]
+        outs, (rows, held) = refs[-2 * parts - 3 : -3], refs[-3:-1]
 
         @pl.when(step == 0)
         def _():
@@ -137,7 +140,7 @@
                         held[j] = stored[s][...]
 
     else:
-        rows, held, out, first, total = refs
+        (rows, held), outs = refs[:2], refs[2:-1]
     chunk = rows.shape[0] // spans
     here = pl.ds(pl.multiple_of(step * width, width), width)
     weights = weight[here] if weight.shape[0] > width else weight[...]
@@ -154,95 +157,127 @@
                 rows[:, pl.ds(d_start, block)], held[j], NT, preferred_element_type=jnp.float32
             )
 
-    for p in range(spans):
-        result = total[p * chunk : (p + 1) * chunk].astype(out.dtype)
-        out[chunk_at(p), :, here] = result
-        for k, first_chunk in enumerate(firsts_of(me)):
-
-            @pl.when(chunk_at(p) == first_chunk)
-            def _():
-                first[k, :, here] = result
-
-
-def matmul_call(sizes, low, high, width, firsts_of, table, weight, given, stored=()):
+    for part, (begin, end) in enumerate(zip((0, *ends), ends)):
+
+        @pl.when((step >= begin) & (step < end))
+        def _():
+            out, first = outs[2 * part : 2 * part + 2]
+            here = pl.ds(pl.multiple_of((step - begin) * width, width), width)
+            for p in range(spans):
+                result = total[p * chunk : (p + 1) * chunk].astype(out.dtype)
+                out[chunk_at(p), :, here] = result
+
+                @pl.when(chunk_at(p) == wrap(me - 1, spans))
+                def _():
+                    first[:, here] = result
+
+
+def matmul_call(sizes, low, ends, width, table, weight, given, stored=()):
     spans, slots, block = sizes
     tokens = sum(piece.shape[0] for piece in given) if stored else given[0].shape[0]
-    d_width, columns = weight.shape[1], (high - low) * width
-    half = jnp.bfloat16
-    shapes = [
-        jax.ShapeDtypeStruct((spans, tokens // spans, columns), half),
-        jax.ShapeDtypeStruct((len(firsts_of(0)), tokens // spans, columns), half),
-    ]
+    d_width, chunk, half = weight.shape[1], tokens // spans, jnp.bfloat16
+    shapes = []
+    for begin, end in zip((0, *ends), ends):
+        columns = (end - begin) * width
+        shapes.append(jax.ShapeDtypeStruct((spans, chunk, columns), half))
+        shapes.append(jax.ShapeDtypeStruct((chunk, columns), half))
     if stored:
         shapes.append(jax.ShapeDtypeStruct((tokens, d_width), half))
         shapes.append(jax.ShapeDtypeStruct((slots, block, block), half))
-    if weight.shape[0] == columns:
+    if weight.shape[0] == ends[-1] * width:
         weight_spec = vmem()
     else:
         weight, weight_spec = stay(weight), pl.BlockSpec((width, d_width), lambda i: (i + low, 0))
     inputs = [*given, *stored]
     return pl.pallas_call(
-        functools.partial(matmul_kernel, sizes, low, width, firsts_of, len(stored)),
-        grid=(high - low,),
+        functools.partial(matmul_kernel, sizes, low, width, ends, len(stored)),
+        grid=(ends[-1],),
         out_shape=shapes,
         in_specs=[smem(), weight_spec] + [vmem()] * len(inputs),
         out_specs=[vmem()] * len(shapes),
         scratch_shapes=[pltpu.VMEM((tokens, width), jnp.float32)],
         compiler_params=params(),
-        cost_estimate=pl.CostEstimate(
-            flops=2 * tokens * d_width * columns,
-            bytes_accessed=2 * d_width * columns,
-            transcendentals=0,
-        ),
+        cost_estimate=cost(MATMUL * tokens * ends[-1] * width),
         name="partial",
     )(table, weight, *inputs)
 
 
-def add_kernel(chunks_of, partials, arrived, out):
-    for k, chunk in enumerate(chunks_of(lax.axis_index("seq"))):
-        result = partials[chunk].astype(jnp.float32) + arrived[k].astype(jnp.float32)
-        out[k] = result.astype(out.dtype)
-
-
-def add_call(chunks_of, partials, arrived):
-    shape = (len(chunks_of(0)), *arrived.shape[1:])
-    return pl.pallas_call(
-        functools.partial(add_kernel, chunks_of),
-        out_shape=jax.ShapeDtypeStruct(shape, arrived.dtype),
+def attach_kernel(first, *refs):
+    riders, out = refs[:-1], refs[-1]
+    at = first.shape[1]
+    out[:, :at] = first[...]
+    for rider in riders:
+        out[:, at : at + rider.shape[1]] = rider[...]
+        at += rider.shape[1]
+
+
+def attach_call(first, riders):
+    chunk, columns = first.shape
+    columns += sum(rider.shape[1] for rider in riders)
+    return pl.pallas_call(
+        attach_kernel,
+        out_shape=jax.ShapeDtypeStruct((chunk, columns), first.dtype),
+        in_specs=[vmem()] * (1 + len(riders)),
+        out_specs=vmem(),
+        compiler_params=params(),
+        cost_estimate=cost(first.size),
+        name="attach",
+    )(first, *riders)
+
+
+def add_kernel(t, riders, partials, arrived, out, *mine):
+    spans, _, columns = partials.shape
+    chunk = wrap(lax.axis_index("seq") - t, spans)
+    result = partials[chunk].astype(jnp.float32) + arrived[:, :columns].astype(jnp.float32)
+    out[:, :columns] = result.astype(out.dtype)
+    if riders:
+        block = mine[0].shape[1]
+        mine[0][...] = arrived[:, columns : columns + block]
+        out[:, columns:] = arrived[:, columns + block :]
+
+
+def add_call(t, partials, arrived, block):
+    chunk, columns = partials.shape[1:]
+    riders = (arrived.shape[1] - columns) // block
+    shapes = [jax.ShapeDtypeStruct((chunk, arrived.shape[1] - min(riders, 1) * block), arrived.dtype)]
+    if riders:
+        shapes.append(jax.ShapeDtypeStruct((chunk, block), arrived.dtype))
+    return pl.pallas_call(
+        functools.partial(add_kernel, t, riders),
+        out_shape=shapes,
         in_specs=[vmem(), vmem()],
-        out_specs=vmem(),
+        out_specs=[vmem()] * len(shapes),
         compiler_params=params(),
         cost_estimate=cost(arrived.size),
         name="add",
     )(partials, arrived)
 
 
-def last_kernel(low, places, partials, *refs):
+def last_kernel(low, partials, arrived, *refs):
     out, total, sem = refs[-3:]
+    columns = total.shape[1]
     result = partials[lax.axis_index("seq")].astype(jnp.float32)
-    for arrived, place in zip(refs, places):
-        result = result + arrived[place].astype(jnp.float32)
+    result = result + arrived[:, :columns].astype(jnp.float32)
     total[...] = result.astype(out.dtype)
-    copy = pltpu.make_async_copy(total, out.at[:, pl.ds(low, total.shape[1])], sem)
+    copy = pltpu.make_async_copy(total, out.at[:, pl.ds(low, columns)], sem)
     copy.start()
     copy.wait()
 
 
-def last_call(low, partials, arrivals, out, shape):
+def last_call(low, partials, arrived, out, shape):
     _, chunk, columns = partials.shape
     given = [] if out is None else [out]
-    arrived, places = zip(*arrivals)
-    return pl.pallas_call(
-        functools.partial(last_kernel, low, places),
+    return pl.pallas_call(
+        functools.partial(last_kernel, low),
         out_shape=shape,
-        in_specs=[vmem()] * (1 + len(arrived)) + [hbm()] * len(given),
+        in_specs=[vmem()] * 2 + [hbm()] * len(given),
         out_specs=hbm(),
         scratch_shapes=[pltpu.VMEM((chunk, columns), shape.dtype), pltpu.SemaphoreType.DMA],
-        input_output_aliases={1 + len(arrived): 0} if given else {},
+        input_output_aliases={2: 0} if given else {},
         compiler_params=params(),
         cost_estimate=cost(partials.size),
         name="last_sum",
-    )(partials, *arrived, *given)
+    )(partials, arrived, *given)
 
 
 def grad_kernel(spans, slots, block, table, rows, *refs):
@@ -280,17 +315,18 @@
         out_specs=[vmem()] * spans,
         scratch_shapes=[pltpu.VMEM((spans, slots, chunk, block), jnp.bfloat16)],
         compiler_params=params(),
-        cost_estimate=cost(WAIT * rows.size),
+        cost_estimate=cost(rows.size),
         name="tile_grad",
     )(table, rows, *hidden_cols)
 
 
-def adam_kernel(spans, slots, table, *refs):
+def adam_kernel(spans, slots, columns, table, *refs):
     arrived, refs = refs[:spans], refs[spans:]
     values, one, two, values_new, one_new, two_new, grads = refs
     me = lax.axis_index("seq")
-    for s in range(spans):
+    for s in range(spans - 1):
         grads[s] = arrived[s][...]
+    grads[spans - 1] = arrived[-1][:, columns:]
     befores = [rank_before(table, s, spans, slots) for s in range(spans)]
     counts = [live_count(table, s, slots) for s in range(spans)]
     for owned in range(slots):
@@ -313,11 +349,11 @@
         two_new[owned] = jnp.where(live > 0, new_two, old_two)
 
 
-def adam_call(sizes, table, grads, *states):
+def adam_call(sizes, columns, table, grads, *states):
     spans, slots, block = sizes
     tile = jax.ShapeDtypeStruct((slots, block, block), jnp.float32)
     return pl.pallas_call(
-        functools.partial(adam_kernel, spans, slots),
+        functools.partial(adam_kernel, spans, slots, columns),
         out_shape=(tile, tile, tile),
         in_specs=[smem()] + [vmem()] * (spans + 3),
         out_specs=(vmem(), vmem(), vmem()),
@@ -335,44 +371,6 @@
 
 def exchange(pieces):
     return [pieces[0]] + [take_from(pieces[s], "seq", -s) for s in range(1, len(pieces))]
-
-
-class Ring:
-    parts = [2, 3, 2]
-
-    def __init__(self, spans):
-        self.spans, self.steps = spans, spans - 1
-
-    def first(self, me):
-        return [wrap(me - 1, self.spans)]
-
-    def move(self, step, sums):
-        return take_from(sums, "seq", -1)
-
-    def add(self, step, partials, moved):
-        return add_call(lambda me: [wrap(me - step - 1, self.spans)], partials, moved[-1])
-
-    def last(self, moved):
-        return [(moved[-1], 0)]
-
-
-class Line:
-    parts = [2, 2, 2, 1]
-    steps = 3
-
-    def first(self, me):
-        return [jnp.where(me < 2, 3, 0), jnp.where(me < 2, 2, 1)]
-
-    def move(self, step, sums):
-        pairs = [[(0, 1), (3, 2)], [(1, 2), (2, 1)], [(0, 1), (1, 0), (2, 3), (3, 2)]]
-        return lax.ppermute(sums, "seq", pairs[step])
-
-    def add(self, step, partials, moved):
-        chunks_of = self.first if step == 1 else lambda me: [me + 1 - 2 * lax.rem(me, 2)]
-        return add_call(chunks_of, partials, moved[-1])
-
-    def last(self, moved):
-        return [(moved[1], 1), (moved[2], 0)]
 
 
 def per_device(
@@ -386,8 +384,7 @@
     sizes = (spans, slots, block)
     group = max(size for size in range(1, 5) if f_blocks % size == 0)
     width = group * block
-    plan = Line() if spans == 4 else Ring(spans)
-    ends = [sum(plan.parts[:part]) for part in range(len(plan.parts) + 1)]
+    ends = [sum(PARTS[:part]) for part in range(len(PARTS) + 1)]
     cuts = [(f_blocks // group) * end // ends[-1] for end in ends]
     ranges = list(zip(cuts[:-1], cuts[1:]))
 
@@ -447,46 +444,33 @@
     for first in firsts:
         pieces += [first] + [take_from(first, "dp", d) for d in range(1, cores)]
 
-    partials, moved = [], []
-    for part, (low, high) in enumerate(ranges):
-        if part == 0:
-            partial, first, rows, held = matmul_call(
-                sizes, low, high, width, plan.first, table, first_weight, pieces, stored
-            )
-        else:
-            if part == 2:
-                send = grad_call(sizes, table, rows, hidden_cols)
-                moved[0][-1], send = lax.optimization_barrier((moved[0][-1], send))
-            if part > 1:
-                sums = plan.add(1, partials[part - 2], moved[part - 2])
-                rows, sums = lax.optimization_barrier((rows, sums))
-                moved[part - 2].append(plan.move(1, sums))
-            partial, first = matmul_call(
-                sizes, low, high, width, plan.first, table, down_weight, [rows, held]
-            )
-        partials.append(partial)
-        moved.append([plan.move(0, first)])
-
-    grads = exchange(send)
-    turn = partials[-1]
-    todo = [(step, part) for step in range(1, plan.steps) for part in range(len(ranges))]
-    todo = [(step, part) for step, part in todo if len(moved[part]) <= step]
-    for step, part in sorted(todo, key=lambda item: (item[1] + LAG * item[0], -item[0])):
-        if (step, part) == (plan.steps - 1, len(ranges) - 1):
-            turn = (turn, grads)
-        moved[part][-1], turn = lax.optimization_barrier((moved[part][-1], turn))
-        turn = plan.add(step, partials[part], moved[part])
-        moved[part].append(plan.move(step, turn))
-    new = adam_call(sizes, table, grads, values, moment_one, moment_two)
+    pieces = list(pieces)
+    partial, first, rows, held = matmul_call(
+        sizes, 0, (cuts[1],), width, table, first_weight, pieces, stored
+    )
+    later = tuple(cut - cuts[1] for cut in cuts[2:])
+    more = matmul_call(sizes, cuts[1], later, width, table, down_weight, [rows, held])
+    partials, begins = [partial, *more[::2]], [first, *more[1::2]]
+    grads = grad_call(sizes, table, rows, hidden_cols)
+    begins[RIDE] = attach_call(begins[RIDE], grads[1:])
+    moving = [take_from(begin, "seq", -1) for begin in begins]
+
+    tiles = [grads[0]]
+    for t in range(2, spans):
+        for part in range(len(ranges)):
+            moving[part], *mine = add_call(t, partials[part], moving[part], block)
+            tiles += mine
+            moving[part] = take_from(moving[part], "seq", -1)
+    tiles.append(moving[RIDE])
+    columns = partials[RIDE].shape[2]
+    new = adam_call(sizes, columns, table, tiles, values, moment_one, moment_two)
 
     hidden_grad = None
     shape = jax.ShapeDtypeStruct((chunk, f_width), jnp.bfloat16)
     for part, (low, _) in enumerate(ranges):
         if part == len(ranges) - 1:
-            moved[part][-1], new = lax.optimization_barrier((moved[part][-1], new))
-        hidden_grad = last_call(
-            low * width, partials[part], plan.last(moved[part]), hidden_grad, shape
-        )
+            moving[part], new = lax.optimization_barrier((moving[part], new))
+        hidden_grad = last_call(low * width, partials[part], moving[part], hidden_grad, shape)
     return (hidden_grad,) + tuple(array[None, None] for array in new)
 
 

time: 123 us -> 113 us (0.919)
  waiting for transfers between devices: 46.7 us -> 41.4 us
  Pallas kernels: 27.3 us -> 24.2 us
    ppermute x12 -> x0, starting transfers between devices: 29.9 us -> none  [move(): return lax.ppermute(sums, 'seq', pairs[step])]
    ppermute x15 -> x21, starting transfers between devices: 16.1 us -> 45 us  [take_from(): lax.ppermute(array, axis, [((i + places) % size, i) for i in range(size)])]
    ppermute x12 -> x0, waiting for transfers between devices: 10.1 us -> none  [move(): return lax.ppermute(sums, 'seq', pairs[step])]
    ppermute x15 -> x21, waiting for transfers between devices: 36.6 us -> 41.4 us  [take_from(): lax.ppermute(array, axis, [((i + places) % size, i) for i in range(size)])]
    pallas_call x17 -> x13, Pallas kernels: 21.4 us -> 17.6 us  [the longest x2 12.9 us: matmul_call(): pl.pallas_call(functools.partial(matmul_kernel, sizes, low, width, ends,...]
  transfers between devices with their start and end apart: 27 -> 21, of which waited for: 14 -> 11; matrix products, arithmetic and copies ran while one was open for 1% -> 1% of each run, Pallas kernels for 18% -> 20%
where the time goes in v8:
time: 113 us; the launch traced here: 112 us
  starting transfers between devices  45 us (40%)
  waiting for transfers between devices  41.4 us (37%)
  Pallas kernels  24.2 us (21%)
    ppermute x21, starting transfers between devices, take_from(): lax.ppermute(array, axis, [((i + places) % size, i) for i in range(size)])  45 us
    ppermute x21, waiting for transfers between devices, take_from(): lax.ppermute(array, axis, [((i + places) % size, i) for i in range(size)])  41.4 us
    pallas_call x2, Pallas kernels, matmul_call(): pl.pallas_call(functools.partial(matmul_kernel, sizes, low, width, ends,...  12.9 us
    pallas_call x1, Pallas kernels, per_device(): pl.pallas_call(lay_kernel, out_shape=[jax.ShapeDtypeStruct((cores * chunk...  2.88 us
    pallas_call x3, Pallas kernels, last_call(): pl.pallas_call(functools.partial(last_kernel, low), out_shape=shape, in_s...  2.42 us
  transfers between devices with their start and end apart: 21, of which 11 were waited for; matrix products, arithmetic and copies ran while one was open for 1% of the time, Pallas kernels for 20%

profile of v8, /device:TPU:0, one launch (start us, length us, event | category | flops | bytes accessed | tf_op | source)
XLA Modules:
  0.0 112.3 jit_solution(4723885893742882776)
XLA Ops:
  1.1 2.6 %collective-permute-start.4 = (bf16[128,2048]{1,0:T(8,128)(2,1)}, bf16[128,2048]{1,0:T(8,128)(2,1)S(1)}, u32[]{:S(2)}, u32[]{:S(2)}) collective-permute-start(bf16[128,2048]{1,0:T(8,128)(2,1)} %own.1), channel_id=1, source_target_pairs={{2,0},{0,2},{3,1},{1,3},{6,4},{4,6},{7,5},{5,7},{10,8},{8,10},{11,... | collective-permute-start | bytes 1572872 | tf_op jit(solution)/shard_map/ppermute | solution.py:369
  4.5 3.6 %collective-permute-start.2 = (s32[1,8]{1,0:T(1,128)S(1)}, s32[1,8]{1,0:T(1,128)S(1)}, u32[]{:S(2)}, u32[]{:S(2)}) collective-permute-start(s32[1,8]{1,0:T(1,128)S(1)} %pad_add_fusion.refs_0_), channel_id=1, source_target_pairs={{4,0},{8,4},{12,8},{0,12},{5,1},{9,5},{13,9},{1,13},{6,2},{10,6},{... | collective-permute-start | bytes 104 | tf_op jit(solution)/shard_map/ppermute | solution.py:369
  10.4 2.9 %lay.1 = (bf16[256,2048]{1,0:T(8,128)(2,1)S(1)}, bf16[1536,2048]{1,0:T(8,128)(2,1)S(1)}) custom-call(bf16[128,2048]{1,0:T(8,128)(2,1)} %own.1, bf16[3584,2048]{1,0:T(8,128)(2,1)} %weight.3, bf16[128,2048]{1,0:T(8,128)(2,1)S(1)} %collective-permute-done.3.refs_0_), custom_call_target="tpu_custom_call" | custom-call | flops 524288 | bytes 1048576 | tf_op jit(solution)/shard_map/lay/pallas_call | solution.py:412
  13.4 1.4 %pick.1 = (s32[4,12]{1,0:T(4,128)S(1)}, bf16[128,128]{1,0:T(8,128)(2,1)S(1)}, bf16[128,128]{1,0:T(8,128)(2,1)S(1)}, bf16[128,128]{1,0:T(8,128)(2,1)S(1)}, bf16[1...) custom-call(s32[1,8]{1,0:T(1,128)S(1)} %pad_add_fusion.refs_0_, ...), custom_call_target="tpu_custom_call" | custom-call | flops 458752 | bytes 917504 | tf_op jit(solution)/shard_map/pick/pallas_call | solution.py:428
  14.8 2.4 %collective-permute-start.5 = (bf16[128,128]{1,0:T(8,128)(2,1)S(1)}, bf16[128,128]{1,0:T(8,128)(2,1)S(1)}, u32[]{:S(2)}, u32[]{:S(2)}) collective-permute-start(bf16[128,128]{1,0:T(8,128)(2,1)S(1)} %get-tuple-element.57), channel_id=1, source_target_pairs={{12,0},{0,4},{4,8},{8,12},{13,1},{1,5},{5,9},{9,13},{14,2},{2,6},{... | collective-permute-start | bytes 98312 | tf_op jit(solution)/shard_map/ppermute | solution.py:369
  18.1 1.5 %collective-permute-start.7 = (bf16[128,128]{1,0:T(8,128)(2,1)S(1)}, bf16[128,128]{1,0:T(8,128)(2,1)S(1)}, u32[]{:S(2)}, u32[]{:S(2)}) collective-permute-start(bf16[128,128]{1,0:T(8,128)(2,1)S(1)} %get-tuple-element.59), channel_id=1, source_target_pairs={{4,0},{8,4},{12,8},{0,12},{5,1},{9,5},{13,9},{1,13},{6,2},{10,6},{... | collective-permute-start | bytes 98312 | tf_op jit(solution)/shard_map/ppermute | solution.py:369
  20.7 1.4 %collective-permute-done.6.refs_5_ = bf16[128,128]{1,0:T(8,128)(2,1)S(1)} collective-permute-done((bf16[128,128]{1,0:T(8,128)(2,1)S(1)}, bf16[128,128]{1,0:T(8,128)(2,1)S(1)}, u32[]{:S(2)}, u32[]{:S(2)}) %collective-permute-start.6) | collective-permute-done | bytes 32800 | tf_op jit(solution)/shard_map/ppermute | solution.py:369
  23.2 2.8 %collective-permute-start.10 = (bf16[4,128,128]{2,1,0:T(8,128)(2,1)S(1)}, bf16[4,128,128]{2,1,0:T(8,128)(2,1)S(1)}, u32[]{:S(2)}, u32[]{:S(2)}) collective-permute-start(bf16[4,128,128]{2,1,0:T(8,128)(2,1)S(1)} %get-tuple-element.71), channel_id=1, source_target_pairs={{8,0},{12,4},{0,8},{4,12},{9,1},{13,5},{1,9},{5,13},{10,2},{14,6},... | collective-permute-start | bytes 393224 | tf_op jit(solution)/shard_map/ppermute | solution.py:369
  27.0 5.2 %partial.2 = (bf16[4,128,1536]{2,1,0:T(8,128)(2,1)S(1)}, bf16[128,1536]{1,0:T(8,128)(2,1)S(1)}, bf16[512,2048]{1,0:T(8,128)(2,1)S(1)}, bf16[4,128,128]{2,1,0:T(8,128)(2,1)S(1)}) custom-call(s32[4,12]{1,0:T(4,128)S(1)} %get-tuple-element.53.table, bf16[1536,2048]{1,0:T(8,128)(2,1)S(1)} %get-tuple-element.54.weight, ...), custom_call_target="tpu_custom_call" | custom-call | flops 3221225472 | bytes 6442450944 | tf_op jit(solution)/shard_map/partial/pallas_call | solution.py:192
  33.3 7.7 %partial.3 = (bf16[4,128,1024]{2,1,0:T(8,128)(2,1)S(1)}, bf16[128,1024]{1,0:T(8,128)(2,1)S(1)}, bf16[4,128,1024]{2,1,0:T(8,128)(2,1)S(1)}, bf16[128,1024]{1,0:T(8,128)(2,1)S(1)}) custom-call(s32[4,12]{1,0:T(4,128)S(1)} %get-tuple-element.53.table, bf16[3584,2048]{1,0:T(8,128)(2,1)} %weight.3, bf16[512,2048]{1,0:T(8,128)(2,1)S(1)} %get-tuple-element.65.refs_0_.rows, ...), custom_call_target="tpu_custom_call" | custom-call | flops 4294967296 | bytes 8589934592 | tf_op jit(solution)/shard_map/partial/pallas_call | solution.py:192
  42.2 14.0 %collective-permute-start.12 = (bf16[128,1408]{1,0:T(8,128)(2,1)S(1)}, bf16[128,1408]{1,0:T(8,128)(2,1)S(1)}, u32[]{:S(2)}, u32[]{:S(2)}) collective-permute-start(bf16[128,1408]{1,0:T(8,128)(2,1)S(1)} %attach.1), channel_id=1, source_target_pairs={{12,0},{0,4},{4,8},{8,12},{13,1},{1,5},{5,9},{9,13},{14,2},{2,6},{... | collective-permute-start | bytes 1081352 | tf_op jit(solution)/shard_map/ppermute | solution.py:369
  56.5 8.6 %collective-permute-done.12.arrived = bf16[128,1408]{1,0:T(8,128)(2,1)S(1)} collective-permute-done((bf16[128,1408]{1,0:T(8,128)(2,1)S(1)}, bf16[128,1408]{1,0:T(8,128)(2,1)S(1)}, u32[]{:S(2)}, u32[]{:S(2)}) %collective-permute-start.12) | collective-permute-done | bytes 360480 | tf_op jit(solution)/shard_map/ppermute | solution.py:369
  65.2 2.5 %collective-permute-start.13 = (bf16[128,1280]{1,0:T(8,128)(2,1)S(1)}, bf16[128,1280]{1,0:T(8,128)(2,1)S(1)}, u32[]{:S(2)}, u32[]{:S(2)}) collective-permute-start(bf16[128,1280]{1,0:T(8,128)(2,1)S(1)} %get-tuple-element.76), channel_id=1, source_target_pairs={{12,0},{0,4},{4,8},{8,12},{13,1},{1,5},{5,9},{9,13},{14,2},{2,6},{... | collective-permute-start | bytes 983048 | tf_op jit(solution)/shard_map/ppermute | solution.py:369
  67.7 3.0 %collective-permute-done.15.arrived = bf16[128,1024]{1,0:T(8,128)(2,1)S(1)} collective-permute-done((bf16[128,1024]{1,0:T(8,128)(2,1)S(1)}, bf16[128,1024]{1,0:T(8,128)(2,1)S(1)}, u32[]{:S(2)}, u32[]{:S(2)}) %collective-permute-start.15) | collective-permute-done | bytes 262176 | tf_op jit(solution)/shard_map/ppermute | solution.py:369
  70.8 2.5 %collective-permute-start.16 = (bf16[128,1024]{1,0:T(8,128)(2,1)S(1)}, bf16[128,1024]{1,0:T(8,128)(2,1)S(1)}, u32[]{:S(2)}, u32[]{:S(2)}) collective-permute-start(bf16[128,1024]{1,0:T(8,128)(2,1)S(1)} %add.10), channel_id=1, source_target_pairs={{12,0},{0,4},{4,8},{8,12},{13,1},{1,5},{5,9},{9,13},{14,2},{2,6},{... | collective-permute-start | bytes 786440 | tf_op jit(solution)/shard_map/ppermute | solution.py:369
  73.3 5.8 %collective-permute-done.19.arrived = bf16[128,1536]{1,0:T(8,128)(2,1)S(1)} collective-permute-done((bf16[128,1536]{1,0:T(8,128)(2,1)S(1)}, bf16[128,1536]{1,0:T(8,128)(2,1)S(1)}, u32[]{:S(2)}, u32[]{:S(2)}) %collective-permute-start.19) | collective-permute-done | bytes 393248 | tf_op jit(solution)/shard_map/ppermute | solution.py:369
  79.2 2.5 %collective-permute-start.20 = (bf16[128,1536]{1,0:T(8,128)(2,1)S(1)}, bf16[128,1536]{1,0:T(8,128)(2,1)S(1)}, u32[]{:S(2)}, u32[]{:S(2)}) collective-permute-start(bf16[128,1536]{1,0:T(8,128)(2,1)S(1)} %add.13), channel_id=1, source_target_pairs={{12,0},{0,4},{4,8},{8,12},{13,1},{1,5},{5,9},{9,13},{14,2},{2,6},{... | collective-permute-start | bytes 1179656 | tf_op jit(solution)/shard_map/ppermute | solution.py:369
  81.8 4.4 %collective-permute-done.13.arrived = bf16[128,1280]{1,0:T(8,128)(2,1)S(1)} collective-permute-done((bf16[128,1280]{1,0:T(8,128)(2,1)S(1)}, bf16[128,1280]{1,0:T(8,128)(2,1)S(1)}, u32[]{:S(2)}, u32[]{:S(2)}) %collective-permute-start.13) | collective-permute-done | bytes 327712 | tf_op jit(solution)/shard_map/ppermute | solution.py:369
  86.2 2.5 %collective-permute-start.14 = (bf16[128,1152]{1,0:T(8,128)(2,1)S(1)}, bf16[128,1152]{1,0:T(8,128)(2,1)S(1)}, u32[]{:S(2)}, u32[]{:S(2)}) collective-permute-start(bf16[128,1152]{1,0:T(8,128)(2,1)S(1)} %get-tuple-element.77), channel_id=1, source_target_pairs={{12,0},{0,4},{4,8},{8,12},{13,1},{1,5},{5,9},{9,13},{14,2},{2,6},{... | collective-permute-start | bytes 884744 | tf_op jit(solution)/shard_map/ppermute | solution.py:369
  88.8 3.0 %collective-permute-done.16.arrived = bf16[128,1024]{1,0:T(8,128)(2,1)S(1)} collective-permute-done((bf16[128,1024]{1,0:T(8,128)(2,1)S(1)}, bf16[128,1024]{1,0:T(8,128)(2,1)S(1)}, u32[]{:S(2)}, u32[]{:S(2)}) %collective-permute-start.16) | collective-permute-done | bytes 262176 | tf_op jit(solution)/shard_map/ppermute | solution.py:369
  91.8 2.5 %collective-permute-start.17 = (bf16[128,1024]{1,0:T(8,128)(2,1)S(1)}, bf16[128,1024]{1,0:T(8,128)(2,1)S(1)}, u32[]{:S(2)}, u32[]{:S(2)}) collective-permute-start(bf16[128,1024]{1,0:T(8,128)(2,1)S(1)} %add.11), channel_id=1, source_target_pairs={{12,0},{0,4},{4,8},{8,12},{13,1},{1,5},{5,9},{9,13},{14,2},{2,6},{... | collective-permute-start | bytes 786440 | tf_op jit(solution)/shard_map/ppermute | solution.py:369
  94.4 12.1 %collective-permute-done.14.refs_3_.arrived = bf16[128,1152]{1,0:T(8,128)(2,1)S(1)} collective-permute-done((bf16[128,1152]{1,0:T(8,128)(2,1)S(1)}, bf16[128,1152]{1,0:T(8,128)(2,1)S(1)}, u32[]{:S(2)}, u32[]{:S(2)}) %collective-permute-start.14) | collective-permute-done | bytes 294944 | tf_op jit(solution)/shard_map/ppermute | solution.py:369
  106.5 1.7 %adam.1 = (f32[4,128,128]{2,1,0:T(8,128)}, f32[4,128,128]{2,1,0:T(8,128)}, f32[4,128,128]{2,1,0:T(8,128)}) custom-call(s32[4,12]{1,0:T(4,128)S(1)} %get-tuple-element.53.table, bf16[128,128]{1,0:T(8,128)(2,1)S(1)} %get-tuple-element.78.refs_0_, bf16[128,128]{1,0:T(8,128)(2,1)S(1)} %get-tuple-element.79.refs_1_, ...), custom_call_target="tpu_custom_call" | custom-call | flops 65536 | bytes 131072 | tf_op jit(solution)/shard_map/adam/pallas_call | solution.py:355
  109.0 1.6 %collective-permute-done.17.arrived = bf16[128,1024]{1,0:T(8,128)(2,1)S(1)} collective-permute-done((bf16[128,1024]{1,0:T(8,128)(2,1)S(1)}, bf16[128,1024]{1,0:T(8,128)(2,1)S(1)}, u32[]{:S(2)}, u32[]{:S(2)}) %collective-permute-start.17) | collective-permute-done | bytes 262176 | tf_op jit(solution)/shard_map/ppermute | solution.py:369
  (42 shorter events, 13.0 us)
Async XLA Ops:
  0.6 9.7 %collective-permute-start.3 = (bf16[128,2048]{1,0:T(8,128)(2,1)}, bf16[128,2048]{1,0:T(8,128)(2,1)S(1)}, u32[]{:S(2)}, u32[]{:S(2)}) collective-permute-start(bf16[128,2048]{1,0:T(8,128)(2,1)} %own.1), channel_id=1, source_target_pairs={{1,0},{0,1},{3,2},{2,3},{5,4},{4,5},{7,6},{6,7},{9,8},{8,9},{11,10... | collective-permute-start | bytes 1572872 | tf_op jit(solution)/shard_map/ppermute | solution.py:369
  1.1 18.5 %collective-permute-start.4 = (bf16[128,2048]{1,0:T(8,128)(2,1)}, bf16[128,2048]{1,0:T(8,128)(2,1)S(1)}, u32[]{:S(2)}, u32[]{:S(2)}) collective-permute-start(bf16[128,2048]{1,0:T(8,128)(2,1)} %own.1), channel_id=1, source_target_pairs={{2,0},{0,2},{3,1},{1,3},{6,4},{4,6},{7,5},{5,7},{10,8},{8,10},{11,... | collective-permute-start | bytes 1572872 | tf_op jit(solution)/shard_map/ppermute | solution.py:369
  4.5 8.8 %collective-permute-start.2 = (s32[1,8]{1,0:T(1,128)S(1)}, s32[1,8]{1,0:T(1,128)S(1)}, u32[]{:S(2)}, u32[]{:S(2)}) collective-permute-start(s32[1,8]{1,0:T(1,128)S(1)} %pad_add_fusion.refs_0_), channel_id=1, source_target_pairs={{4,0},{8,4},{12,8},{0,12},{5,1},{9,5},{13,9},{1,13},{6,2},{10,6},{... | collective-permute-start | bytes 104 | tf_op jit(solution)/shard_map/ppermute | solution.py:369
  8.1 5.2 %collective-permute-start.1 = (s32[1,8]{1,0:T(1,128)S(1)}, s32[1,8]{1,0:T(1,128)S(1)}, u32[]{:S(2)}, u32[]{:S(2)}) collective-permute-start(s32[1,8]{1,0:T(1,128)S(1)} %pad_add_fusion.refs_0_), channel_id=1, source_target_pairs={{8,0},{12,4},{0,8},{4,12},{9,1},{13,5},{1,9},{5,13},{10,2},{14,6},... | collective-permute-start | bytes 104 | tf_op jit(solution)/shard_map/ppermute | solution.py:369
  8.1 5.3 %collective-permute-start = (s32[1,8]{1,0:T(1,128)S(1)}, s32[1,8]{1,0:T(1,128)S(1)}, u32[]{:S(2)}, u32[]{:S(2)}) collective-permute-start(s32[1,8]{1,0:T(1,128)S(1)} %pad_add_fusion.refs_0_), channel_id=1, source_target_pairs={{12,0},{0,4},{4,8},{8,12},{13,1},{1,5},{5,9},{9,13},{14,2},{2,6},{... | collective-permute-start | bytes 104 | tf_op jit(solution)/shard_map/ppermute | solution.py:369
  14.8 5.9 %collective-permute-start.5 = (bf16[128,128]{1,0:T(8,128)(2,1)S(1)}, bf16[128,128]{1,0:T(8,128)(2,1)S(1)}, u32[]{:S(2)}, u32[]{:S(2)}) collective-permute-start(bf16[128,128]{1,0:T(8,128)(2,1)S(1)} %get-tuple-element.57), channel_id=1, source_target_pairs={{12,0},{0,4},{4,8},{8,12},{13,1},{1,5},{5,9},{9,13},{14,2},{2,6},{... | collective-permute-start | bytes 98312 | tf_op jit(solution)/shard_map/ppermute | solution.py:369
  17.2 4.8 %collective-permute-start.6 = (bf16[128,128]{1,0:T(8,128)(2,1)S(1)}, bf16[128,128]{1,0:T(8,128)(2,1)S(1)}, u32[]{:S(2)}, u32[]{:S(2)}) collective-permute-start(bf16[128,128]{1,0:T(8,128)(2,1)S(1)} %get-tuple-element.58), channel_id=1, source_target_pairs={{8,0},{12,4},{0,8},{4,12},{9,1},{13,5},{1,9},{5,13},{10,2},{14,6},... | collective-permute-start | bytes 98312 | tf_op jit(solution)/shard_map/ppermute | solution.py:369
  18.1 4.3 %collective-permute-start.7 = (bf16[128,128]{1,0:T(8,128)(2,1)S(1)}, bf16[128,128]{1,0:T(8,128)(2,1)S(1)}, u32[]{:S(2)}, u32[]{:S(2)}) collective-permute-start(bf16[128,128]{1,0:T(8,128)(2,1)S(1)} %get-tuple-element.59), channel_id=1, source_target_pairs={{4,0},{8,4},{12,8},{0,12},{5,1},{9,5},{13,9},{1,13},{6,2},{10,6},{... | collective-permute-start | bytes 98312 | tf_op jit(solution)/shard_map/ppermute | solution.py:369
  22.4 4.6 %collective-permute-start.8 = (bf16[128,2048]{1,0:T(8,128)(2,1)S(1)}, bf16[128,2048]{1,0:T(8,128)(2,1)S(1)}, u32[]{:S(2)}, u32[]{:S(2)}) collective-permute-start(bf16[128,2048]{1,0:T(8,128)(2,1)S(1)} %collective-permute-done.4.refs_1_), channel_id=1, source_target_pairs={{1,0},{0,1},{3,2},{2,3},{5,4},{4,5},{7,6},{6,7},{9,8},{8,9},{11,10... | collective-permute-start | bytes 1572872 | tf_op jit(solution)/shard_map/ppermute | solution.py:369
  22.4 18.6 %collective-permute-start.9 = (bf16[4,128,128]{2,1,0:T(8,128)(2,1)S(1)}, bf16[4,128,128]{2,1,0:T(8,128)(2,1)S(1)}, u32[]{:S(2)}, u32[]{:S(2)}) collective-permute-start(bf16[4,128,128]{2,1,0:T(8,128)(2,1)S(1)} %get-tuple-element.70), channel_id=1, source_target_pairs={{12,0},{0,4},{4,8},{8,12},{13,1},{1,5},{5,9},{9,13},{14,2},{2,6},{... | collective-permute-start | bytes 393224 | tf_op jit(solution)/shard_map/ppermute | solution.py:369
  23.2 17.9 %collective-permute-start.10 = (bf16[4,128,128]{2,1,0:T(8,128)(2,1)S(1)}, bf16[4,128,128]{2,1,0:T(8,128)(2,1)S(1)}, u32[]{:S(2)}, u32[]{:S(2)}) collective-permute-start(bf16[4,128,128]{2,1,0:T(8,128)(2,1)S(1)} %get-tuple-element.71), channel_id=1, source_target_pairs={{8,0},{12,4},{0,8},{4,12},{9,1},{13,5},{1,9},{5,13},{10,2},{14,6},... | collective-permute-start | bytes 393224 | tf_op jit(solution)/shard_map/ppermute | solution.py:369
  26.0 15.1 %collective-permute-start.11 = (bf16[4,128,128]{2,1,0:T(8,128)(2,1)S(1)}, bf16[4,128,128]{2,1,0:T(8,128)(2,1)S(1)}, u32[]{:S(2)}, u32[]{:S(2)}) collective-permute-start(bf16[4,128,128]{2,1,0:T(8,128)(2,1)S(1)} %get-tuple-element.72), channel_id=1, source_target_pairs={{4,0},{8,4},{12,8},{0,12},{5,1},{9,5},{13,9},{1,13},{6,2},{10,6},{... | collective-permute-start | bytes 393224 | tf_op jit(solution)/shard_map/ppermute | solution.py:369
  32.2 24.0 %collective-permute-start.18 = (bf16[128,1536]{1,0:T(8,128)(2,1)S(1)}, bf16[128,1536]{1,0:T(8,128)(2,1)S(1)}, u32[]{:S(2)}, u32[]{:S(2)}) collective-permute-start(bf16[128,1536]{1,0:T(8,128)(2,1)S(1)} %get-tuple-element.88), channel_id=1, source_target_pairs={{12,0},{0,4},{4,8},{8,12},{13,1},{1,5},{5,9},{9,13},{14,2},{2,6},{... | collective-permute-start | bytes 1179656 | tf_op jit(solution)/shard_map/ppermute | solution.py:369
  42.2 64.4 %copy-start = (f32[1,1,4,128,128]{4,3,2,1,0:T(8,128)S(1)}, f32[1,1,4,128,128]{4,3,2,1,0:T(8,128)}, u32[]{:S(2)}) copy-start(f32[1,1,4,128,128]{4,3,2,1,0:T(8,128)} %param.13) | copy-start | bytes 786436
  42.2 64.4 %copy-start.1 = (f32[1,1,4,128,128]{4,3,2,1,0:T(8,128)S(1)}, f32[1,1,4,128,128]{4,3,2,1,0:T(8,128)}, u32[]{:S(2)}) copy-start(f32[1,1,4,128,128]{4,3,2,1,0:T(8,128)} %param.14) | copy-start | bytes 786436
  42.2 64.3 %copy-start.2 = (f32[1,1,4,128,128]{4,3,2,1,0:T(8,128)S(1)}, f32[1,1,4,128,128]{4,3,2,1,0:T(8,128)}, u32[]{:S(2)}) copy-start(f32[1,1,4,128,128]{4,3,2,1,0:T(8,128)} %param.15) | copy-start | bytes 786436
  42.2 22.9 %collective-permute-start.12 = (bf16[128,1408]{1,0:T(8,128)(2,1)S(1)}, bf16[128,1408]{1,0:T(8,128)(2,1)S(1)}, u32[]{:S(2)}, u32[]{:S(2)}) collective-permute-start(bf16[128,1408]{1,0:T(8,128)(2,1)S(1)} %attach.1), channel_id=1, source_target_pairs={{12,0},{0,4},{4,8},{8,12},{13,1},{1,5},{5,9},{9,13},{14,2},{2,6},{... | collective-permute-start | bytes 1081352 | tf_op jit(solution)/shard_map/ppermute | solution.py:369
  56.2 14.5 %collective-permute-start.15 = (bf16[128,1024]{1,0:T(8,128)(2,1)S(1)}, bf16[128,1024]{1,0:T(8,128)(2,1)S(1)}, u32[]{:S(2)}, u32[]{:S(2)}) collective-permute-start(bf16[128,1024]{1,0:T(8,128)(2,1)S(1)} %get-tuple-element.86), channel_id=1, source_target_pairs={{12,0},{0,4},{4,8},{8,12},{13,1},{1,5},{5,9},{9,13},{14,2},{2,6},{... | collective-permute-start | bytes 786440 | tf_op jit(solution)/shard_map/ppermute | solution.py:369
  56.4 22.7 %collective-permute-start.19 = (bf16[128,1536]{1,0:T(8,128)(2,1)S(1)}, bf16[128,1536]{1,0:T(8,128)(2,1)S(1)}, u32[]{:S(2)}, u32[]{:S(2)}) collective-permute-start(bf16[128,1536]{1,0:T(8,128)(2,1)S(1)} %add.12), channel_id=1, source_target_pairs={{12,0},{0,4},{4,8},{8,12},{13,1},{1,5},{5,9},{9,13},{14,2},{2,6},{... | collective-permute-start | bytes 1179656 | tf_op jit(solution)/shard_map/ppermute | solution.py:369
  65.2 21.0 %collective-permute-start.13 = (bf16[128,1280]{1,0:T(8,128)(2,1)S(1)}, bf16[128,1280]{1,0:T(8,128)(2,1)S(1)}, u32[]{:S(2)}, u32[]{:S(2)}) collective-permute-start(bf16[128,1280]{1,0:T(8,128)(2,1)S(1)} %get-tuple-element.76), channel_id=1, source_target_pairs={{12,0},{0,4},{4,8},{8,12},{13,1},{1,5},{5,9},{9,13},{14,2},{2,6},{... | collective-permute-start | bytes 983048 | tf_op jit(solution)/shard_map/ppermute | solution.py:369
  70.8 21.0 %collective-permute-start.16 = (bf16[128,1024]{1,0:T(8,128)(2,1)S(1)}, bf16[128,1024]{1,0:T(8,128)(2,1)S(1)}, u32[]{:S(2)}, u32[]{:S(2)}) collective-permute-start(bf16[128,1024]{1,0:T(8,128)(2,1)S(1)} %add.10), channel_id=1, source_target_pairs={{12,0},{0,4},{4,8},{8,12},{13,1},{1,5},{5,9},{9,13},{14,2},{2,6},{... | collective-permute-start | bytes 786440 | tf_op jit(solution)/shard_map/ppermute | solution.py:369
  79.2 28.9 %collective-permute-start.20 = (bf16[128,1536]{1,0:T(8,128)(2,1)S(1)}, bf16[128,1536]{1,0:T(8,128)(2,1)S(1)}, u32[]{:S(2)}, u32[]{:S(2)}) collective-permute-start(bf16[128,1536]{1,0:T(8,128)(2,1)S(1)} %add.13), channel_id=1, source_target_pairs={{12,0},{0,4},{4,8},{8,12},{13,1},{1,5},{5,9},{9,13},{14,2},{2,6},{... | collective-permute-start | bytes 1179656 | tf_op jit(solution)/shard_map/ppermute | solution.py:369
  86.2 20.3 %collective-permute-start.14 = (bf16[128,1152]{1,0:T(8,128)(2,1)S(1)}, bf16[128,1152]{1,0:T(8,128)(2,1)S(1)}, u32[]{:S(2)}, u32[]{:S(2)}) collective-permute-start(bf16[128,1152]{1,0:T(8,128)(2,1)S(1)} %get-tuple-element.77), channel_id=1, source_target_pairs={{12,0},{0,4},{4,8},{8,12},{13,1},{1,5},{5,9},{9,13},{14,2},{2,6},{... | collective-permute-start | bytes 884744 | tf_op jit(solution)/shard_map/ppermute | solution.py:369
  91.8 18.8 %collective-permute-start.17 = (bf16[128,1024]{1,0:T(8,128)(2,1)S(1)}, bf16[128,1024]{1,0:T(8,128)(2,1)S(1)}, u32[]{:S(2)}, u32[]{:S(2)}) collective-permute-start(bf16[128,1024]{1,0:T(8,128)(2,1)S(1)} %add.11), channel_id=1, source_target_pairs={{12,0},{0,4},{4,8},{8,12},{13,1},{1,5},{5,9},{9,13},{14,2},{2,6},{... | collective-permute-start | bytes 786440 | tf_op jit(solution)/shard_map/ppermute | solution.py:369

commit v9 on v8

--- a/solution.py
+++ b/solution.py
@@ -88,10 +88,10 @@
         slot = wrap(me - lax.rem(before, spans), spans)
         tile = values[jnp.minimum(lax.div(before + slot, spans), slots - 1)]
         live = slot < live_count(table, row, slots)
-        outs[s][...] = jnp.where(live, tile.astype(jnp.float32), 0.0).astype(tile.dtype)
+        outs[s][slots] = jnp.where(live, tile.astype(jnp.float32), 0.0).astype(tile.dtype)
         for j in range(slots):
             start = pl.multiple_of(table[row, j] * block, block)
-            outs[spans + s][j] = hidden[:, pl.ds(start, block)]
+            outs[s][j] = hidden[:, pl.ds(start, block)]
 
 
 def lay_kernel(own, weight, *refs):
@@ -116,40 +116,47 @@
     return t_place * cores + d_place
 
 
-def matmul_kernel(sizes, low, width, ends, stores, table, weight, *refs):
-    spans, slots, block = sizes
+def early_matmul_kernel(width, weight, *refs):
+    pieces, (out, rows) = refs[:-2], refs[-2:]
     step = pl.program_id(0)
-    me = lax.axis_index("seq")
-    parts, total = len(ends), refs[-1]
-    if stores:
-        given, stored = refs[: -stores - 2 * parts - 3], refs[-stores - 2 * parts - 3 : -2 * parts - 3]
-        outs, (rows, held) = refs[-2 * parts - 3 : -3], refs[-3:-1]
-
-        @pl.when(step == 0)
-        def _():
-            at = 0
-            for piece in given:
-                rows[at : at + piece.shape[0]] = piece[...]
-                at += piece.shape[0]
-            before = rank_before(table, 0, spans, slots)
-            for j in range(slots):
-                for s in range(spans):
-
-                    @pl.when(lax.rem(before + j, spans) == wrap(me - s, spans))
-                    def _():
-                        held[j] = stored[s][...]
-
-    else:
-        (rows, held), outs = refs[:2], refs[2:-1]
-    chunk = rows.shape[0] // spans
+
+    @pl.when(step == 0)
+    def _():
+        at = 0
+        for piece in pieces:
+            rows[at : at + piece.shape[0]] = piece[...]
+            at += piece.shape[0]
+
     here = pl.ds(pl.multiple_of(step * width, width), width)
-    weights = weight[here] if weight.shape[0] > width else weight[...]
-    total[...] = lax.dot_general(rows[...], weights, NT, preferred_element_type=jnp.float32)
+    out[:, here] = lax.dot_general(
+        rows[...], weight[here], NT, preferred_element_type=jnp.float32
+    )
+
+
+def early_matmul_call(width, weight, pieces):
+    tokens, (columns, d_width) = sum(piece.shape[0] for piece in pieces), weight.shape
+    return pl.pallas_call(
+        functools.partial(early_matmul_kernel, width),
+        grid=(columns // width,),
+        out_shape=[
+            jax.ShapeDtypeStruct((tokens, columns), jnp.float32),
+            jax.ShapeDtypeStruct((tokens, d_width), weight.dtype),
+        ],
+        in_specs=[vmem()] * (1 + len(pieces)),
+        out_specs=[vmem()] * 2,
+        compiler_params=params(),
+        cost_estimate=cost(MATMUL * tokens * columns),
+        name="partial",
+    )(weight, *pieces)
+
+
+def add_delta(table, rows, held, total, low):
+    slots, block, _ = held.shape
     count = live_count(table, 0, slots)
     for j in range(slots):
-        f_start = table[0, j] * block - (low + step) * width
-
-        @pl.when((j < count) & (f_start >= 0) & (f_start < width))
+        f_start = table[0, j] * block - low
+
+        @pl.when((j < count) & (f_start >= 0) & (f_start < total.shape[1]))
         def _():
             d_start = pl.multiple_of(table[0, slots + j] * block, block)
             place = pl.ds(pl.multiple_of(f_start, block), block)
@@ -157,49 +164,90 @@
                 rows[:, pl.ds(d_start, block)], held[j], NT, preferred_element_type=jnp.float32
             )
 
+
+def put_chunks(total, out, first, here):
+    spans, chunk = out.shape[:2]
+    me = lax.axis_index("seq")
+    for p in range(spans):
+        result = total[p * chunk : (p + 1) * chunk].astype(out.dtype)
+        out[chunk_at(p), :, here] = result
+
+        @pl.when(chunk_at(p) == wrap(me - 1, spans))
+        def _():
+            first[:, here] = result
+
+
+def delta_kernel(spans, slots, block, table, early, rows, *refs):
+    stored, (out, first, held, total) = refs[:spans], refs[spans:]
+    me = lax.axis_index("seq")
+    before = rank_before(table, 0, spans, slots)
+    for j in range(slots):
+        for s in range(spans):
+
+            @pl.when(lax.rem(before + j, spans) == wrap(me - s, spans))
+            def _():
+                held[j] = stored[s][slots]
+
+    total[...] = early[...]
+    add_delta(table, rows, held, total, 0)
+    put_chunks(total, out, first, pl.ds(0, total.shape[1]))
+
+
+def delta_call(sizes, table, early, rows, stored):
+    spans, slots, block = sizes
+    tokens, columns = early.shape
+    return pl.pallas_call(
+        functools.partial(delta_kernel, *sizes),
+        out_shape=[
+            jax.ShapeDtypeStruct((spans, tokens // spans, columns), rows.dtype),
+            jax.ShapeDtypeStruct((tokens // spans, columns), rows.dtype),
+            jax.ShapeDtypeStruct((slots, block, block), rows.dtype),
+        ],
+        in_specs=[smem()] + [vmem()] * (2 + spans),
+        out_specs=[vmem()] * 3,
+        scratch_shapes=[pltpu.VMEM((tokens, columns), jnp.float32)],
+        compiler_params=params(),
+        cost_estimate=cost(early.size),
+        name="delta",
+    )(table, early, rows, *stored)
+
+
+def matmul_kernel(low, ends, table, weight, rows, held, *refs):
+    outs, total = refs[:-1], refs[-1]
+    step, width = pl.program_id(0), weight.shape[0]
+    total[...] = lax.dot_general(rows[...], weight[...], NT, preferred_element_type=jnp.float32)
+    add_delta(table, rows, held, total, (low + step) * width)
     for part, (begin, end) in enumerate(zip((0, *ends), ends)):
 
         @pl.when((step >= begin) & (step < end))
         def _():
-            out, first = outs[2 * part : 2 * part + 2]
             here = pl.ds(pl.multiple_of((step - begin) * width, width), width)
-            for p in range(spans):
-                result = total[p * chunk : (p + 1) * chunk].astype(out.dtype)
-                out[chunk_at(p), :, here] = result
-
-                @pl.when(chunk_at(p) == wrap(me - 1, spans))
-                def _():
-                    first[:, here] = result
-
-
-def matmul_call(sizes, low, ends, width, table, weight, given, stored=()):
-    spans, slots, block = sizes
-    tokens = sum(piece.shape[0] for piece in given) if stored else given[0].shape[0]
-    d_width, chunk, half = weight.shape[1], tokens // spans, jnp.bfloat16
+            put_chunks(total, *outs[2 * part : 2 * part + 2], here)
+
+
+def matmul_call(spans, low, ends, width, table, weight, rows, held):
+    tokens, d_width = rows.shape
     shapes = []
     for begin, end in zip((0, *ends), ends):
         columns = (end - begin) * width
-        shapes.append(jax.ShapeDtypeStruct((spans, chunk, columns), half))
-        shapes.append(jax.ShapeDtypeStruct((chunk, columns), half))
-    if stored:
-        shapes.append(jax.ShapeDtypeStruct((tokens, d_width), half))
-        shapes.append(jax.ShapeDtypeStruct((slots, block, block), half))
-    if weight.shape[0] == ends[-1] * width:
-        weight_spec = vmem()
-    else:
-        weight, weight_spec = stay(weight), pl.BlockSpec((width, d_width), lambda i: (i + low, 0))
-    inputs = [*given, *stored]
-    return pl.pallas_call(
-        functools.partial(matmul_kernel, sizes, low, width, ends, len(stored)),
+        shapes.append(jax.ShapeDtypeStruct((spans, tokens // spans, columns), rows.dtype))
+        shapes.append(jax.ShapeDtypeStruct((tokens // spans, columns), rows.dtype))
+    return pl.pallas_call(
+        functools.partial(matmul_kernel, low, ends),
         grid=(ends[-1],),
         out_shape=shapes,
-        in_specs=[smem(), weight_spec] + [vmem()] * len(inputs),
+        in_specs=[
+            smem(),
+            pl.BlockSpec((width, d_width), lambda i: (i + low, 0)),
+            vmem(),
+            vmem(),
+        ],
         out_specs=[vmem()] * len(shapes),
         scratch_shapes=[pltpu.VMEM((tokens, width), jnp.float32)],
         compiler_params=params(),
         cost_estimate=cost(MATMUL * tokens * ends[-1] * width),
         name="partial",
-    )(table, weight, *inputs)
+    )(table, stay(weight), rows, held)
 
 
 def attach_kernel(first, *refs):
@@ -286,7 +334,7 @@
     count, before = live_count(table, 0, slots), rank_before(table, 0, spans, slots)
     chunk = rows.shape[0] // spans
     for s in range(spans):
-        cols[s] = hidden[s][...]
+        cols[s] = hidden[s][:slots]
     for s in range(spans):
         slot = wrap(lax.rem(me + s, spans) - lax.rem(before, spans), spans)
         outs[s][...] = jnp.zeros_like(outs[s])
@@ -308,6 +356,7 @@
 def grad_call(sizes, table, rows, hidden_cols):
     spans = sizes[0]
     slots, chunk, block = hidden_cols[0].shape
+    slots -= 1
     return pl.pallas_call(
         functools.partial(grad_kernel, *sizes),
         out_shape=[jax.ShapeDtypeStruct((block, block), jnp.bfloat16)] * spans,
@@ -422,36 +471,29 @@
         cost_estimate=cost(cores * chunk * d_width),
         name="lay",
     )(stay(cotangent), stay(down_weight), *local)
-    hidden_here, local_rows, first_weight = lax.optimization_barrier(
-        (hidden_here, local_rows, first_weight)
-    )
     table, *picked = pl.pallas_call(
         functools.partial(pick_kernel, *sizes, d_blocks),
         out_shape=[jax.ShapeDtypeStruct((spans, 3 * slots), jnp.int32)]
-        + [jax.ShapeDtypeStruct((block, block), jnp.bfloat16)] * spans
-        + [jax.ShapeDtypeStruct((slots, chunk, block), jnp.bfloat16)] * spans,
+        + [jax.ShapeDtypeStruct((slots + 1, chunk, block), jnp.bfloat16)] * spans,
         in_specs=[smem()] * spans + [vmem(), vmem()],
-        out_specs=[smem()] + [vmem()] * (2 * spans),
+        out_specs=[smem()] + [vmem()] * spans,
         compiler_params=params(),
         cost_estimate=cost(hidden_in.size),
         name="pick",
     )(*metas, values_half, hidden_here)
-    stored = exchange(picked[:spans])
-    hidden_cols = exchange(picked[spans:])
-
-    firsts, stored = lax.optimization_barrier((firsts, stored))
+    crossed = exchange(picked)
+
+    firsts, crossed[1] = lax.optimization_barrier((firsts, crossed[1]))
     pieces = [local_rows]
     for first in firsts:
         pieces += [first] + [take_from(first, "dp", d) for d in range(1, cores)]
 
-    pieces = list(pieces)
-    partial, first, rows, held = matmul_call(
-        sizes, 0, (cuts[1],), width, table, first_weight, pieces, stored
-    )
+    early, rows = early_matmul_call(width, first_weight, pieces)
+    partial, first, held = delta_call(sizes, table, early, rows, crossed)
     later = tuple(cut - cuts[1] for cut in cuts[2:])
-    more = matmul_call(sizes, cuts[1], later, width, table, down_weight, [rows, held])
+    more = matmul_call(spans, cuts[1], later, width, table, down_weight, rows, held)
     partials, begins = [partial, *more[::2]], [first, *more[1::2]]
-    grads = grad_call(sizes, table, rows, hidden_cols)
+    grads = grad_call(sizes, table, rows, crossed)
     begins[RIDE] = attach_call(begins[RIDE], grads[1:])
     moving = [take_from(begin, "seq", -1) for begin in begins]
 

time: 113 us -> 106 us (0.938); the launches traced: 112 us -> 107 us
  starting transfers between devices: 45 us -> 13.8 us
  waiting for transfers between devices: 41.4 us -> 66.8 us
    ppermute x21 -> x18, starting transfers between devices: 45 us -> 13.8 us  [take_from(): lax.ppermute(array, axis, [((i + places) % size, i) for i in range(size)])]
    ppermute x21 -> x18, waiting for transfers between devices: 41.4 us -> 66.8 us  [take_from(): lax.ppermute(array, axis, [((i + places) % size, i) for i in range(size)])]
    pallas_call x2 -> x3, Pallas kernels: 12.9 us -> 13 us  [the longest x1 7.83 us: matmul_call(): pl.pallas_call(functools.partial(matmul_kernel, low, ends), grid=(ends[-1...]
  transfers between devices with their start and end apart: 21 -> 18, of which waited for: 11 -> 12; matrix products, arithmetic and copies ran while one was open for 1% -> 1% of each run, Pallas kernels for 20% -> 20%
where the time goes in v9:
time: 106 us; the launch traced here: 107 us
  waiting for transfers between devices  66.8 us (63%)
  Pallas kernels  24.5 us (23%)
  starting transfers between devices  13.8 us (13%)
    ppermute x18, waiting for transfers between devices, take_from(): lax.ppermute(array, axis, [((i + places) % size, i) for i in range(size)])  66.8 us
    ppermute x18, starting transfers between devices, take_from(): lax.ppermute(array, axis, [((i + places) % size, i) for i in range(size)])  13.8 us
    pallas_call x1, Pallas kernels, matmul_call(): pl.pallas_call(functools.partial(matmul_kernel, low, ends), grid=(ends[-1...  7.83 us
    pallas_call x1, Pallas kernels, early_matmul_call(): pl.pallas_call(functools.partial(early_matmul_kernel, width), grid=(colum...  4.03 us
    pallas_call x1, Pallas kernels, per_device(): pl.pallas_call(lay_kernel, out_shape=[jax.ShapeDtypeStruct((cores * chunk...  2.88 us
    pallas_call x3, Pallas kernels, last_call(): pl.pallas_call(functools.partial(last_kernel, low), out_shape=shape, in_s...  2.42 us
  transfers between devices with their start and end apart: 18, of which 12 were waited for; matrix products, arithmetic and copies ran while one was open for 1% of the time, Pallas kernels for 20%

profile of v9, /device:TPU:0, one launch (start us, length us, event | category | flops | bytes accessed | tf_op | source)
XLA Modules:
  0.0 106.6 jit_solution(11595836131588207727)
XLA Ops:
  0.6 3.0 %collective-permute-start.4 = (bf16[128,2048]{1,0:T(8,128)(2,1)}, bf16[128,2048]{1,0:T(8,128)(2,1)S(1)}, u32[]{:S(2)}, u32[]{:S(2)}) collective-permute-start(bf16[128,2048]{1,0:T(8,128)(2,1)} %own.1), channel_id=1, source_target_pairs={{2,0},{0,2},{3,1},{1,3},{6,4},{4,6},{7,5},{5,7},{10,8},{8,10},{11,... | collective-permute-start | bytes 1572872 | tf_op jit(solution)/shard_map/ppermute | solution.py:418
  4.4 3.6 %collective-permute-start.2 = (s32[1,8]{1,0:T(1,128)S(1)}, s32[1,8]{1,0:T(1,128)S(1)}, u32[]{:S(2)}, u32[]{:S(2)}) collective-permute-start(s32[1,8]{1,0:T(1,128)S(1)} %pad_add_fusion.refs_0_), channel_id=1, source_target_pairs={{4,0},{8,4},{12,8},{0,12},{5,1},{9,5},{13,9},{1,13},{6,2},{10,6},{... | collective-permute-start | bytes 104 | tf_op jit(solution)/shard_map/ppermute | solution.py:418
  8.0 1.0 collective-permute-start
  9.0 1.3 %early.1 = (bf16[4,128,128]{2,1,0:T(8,128)(2,1)S(1)}, bf16[128,3584]{1,0:T(8,128)(2,1)S(1)}) custom-call(f32[4,128,128]{2,1,0:T(8,128)} %bitcast.8, bf16[128,3584]{1,0:T(8,128)(2,1)} %hidden.1), custom_call_target="tpu_custom_call" | custom-call | flops 458752 | bytes 917504 | tf_op jit(solution)/shard_map/early/pallas_call | solution.py:445
  10.3 2.1 %collective-permute-done.1.refs_2_ = s32[1,8]{1,0:T(1,128)S(1)} collective-permute-done((s32[1,8]{1,0:T(1,128)S(1)}, s32[1,8]{1,0:T(1,128)S(1)}, u32[]{:S(2)}, u32[]{:S(2)}) %collective-permute-start.1) | collective-permute-done | bytes 64 | tf_op jit(solution)/shard_map/ppermute | solution.py:418
  13.3 1.4 %pick.1 = (s32[4,12]{1,0:T(4,128)S(1)}, bf16[5,128,128]{2,1,0:T(8,128)(2,1)S(1)}, bf16[5,128,128]{2,1,0:T(8,128)(2,1)S(1)}, bf16[5,128,128]{2,1,0:T(8,128)(2,1)S(1)}, bf16[5,128,128]{2,1,0:T(8,128)(2,1)S(1)}) custom-call(s32[1,8]{1,0:T(1,128)S(1)} %pad_add_fusion.refs_0_, s32[1,8]{1,0:T(1,128)S(1)} %collective-permute-done.refs_1_, ...), custom_call_target="tpu_custom_call" | custom-call | flops 458752 | bytes 917504 | tf_op jit(solution)/shard_map/pick/pallas_call | solution.py:474
  14.9 7.0 %collective-permute-done.5.refs_1_ = bf16[5,128,128]{2,1,0:T(8,128)(2,1)S(1)} collective-permute-done((bf16[5,128,128]{2,1,0:T(8,128)(2,1)S(1)}, bf16[5,128,128]{2,1,0:T(8,128)(2,1)S(1)}, u32[]{:S(2)}, u32[]{:S(2)}) %collective-permute-start.5) | collective-permute-done | bytes 163872 | tf_op jit(solution)/shard_map/ppermute | solution.py:418
  22.5 2.9 %lay.1 = (bf16[256,2048]{1,0:T(8,128)(2,1)S(1)}, bf16[1536,2048]{1,0:T(8,128)(2,1)S(1)}) custom-call(bf16[128,2048]{1,0:T(8,128)(2,1)} %own.1, bf16[3584,2048]{1,0:T(8,128)(2,1)} %weight.3, bf16[128,2048]{1,0:T(8,128)(2,1)S(1)} %collective-permute-done.3.refs_0_), custom_call_target="tpu_custom_call" | custom-call | flops 524288 | bytes 1048576 | tf_op jit(solution)/shard_map/lay/pallas_call | solution.py:461
  25.4 4.0 %partial.2 = (f32[512,1536]{1,0:T(8,128)S(1)}, bf16[512,2048]{1,0:T(8,128)(2,1)S(1)}) custom-call(bf16[1536,2048]{1,0:T(8,128)(2,1)S(1)} %get-tuple-element.42.weight, bf16[256,2048]{1,0:T(8,128)(2,1)S(1)} %get-tuple-element.43.refs_0_, bf16[128,2048]{1,0:T(8,128)(2,1)S(1)} %collective-permute-done.4.refs_1_, ...), custom_call_target="tpu_custom_call" | custom-call | flops 3221225472 | bytes 6442450944 | tf_op jit(solution)/shard_map/partial/pallas_call | solution.py:138
  29.4 1.3 %collective-permute-done.7.refs_2_ = bf16[5,128,128]{2,1,0:T(8,128)(2,1)S(1)} collective-permute-done((bf16[5,128,128]{2,1,0:T(8,128)(2,1)S(1)}, bf16[5,128,128]{2,1,0:T(8,128)(2,1)S(1)}, u32[]{:S(2)}, u32[]{:S(2)}) %collective-permute-start.7) | collective-permute-done | bytes 163872 | tf_op jit(solution)/shard_map/ppermute | solution.py:418
  30.7 1.4 %collective-permute-done.8.refs_3_ = bf16[5,128,128]{2,1,0:T(8,128)(2,1)S(1)} collective-permute-done((bf16[5,128,128]{2,1,0:T(8,128)(2,1)S(1)}, bf16[5,128,128]{2,1,0:T(8,128)(2,1)S(1)}, u32[]{:S(2)}, u32[]{:S(2)}) %collective-permute-start.8) | collective-permute-done | bytes 163872 | tf_op jit(solution)/shard_map/ppermute | solution.py:418
  32.0 1.1 %delta.1 = (bf16[4,128,1536]{2,1,0:T(8,128)(2,1)S(1)}, bf16[128,1536]{1,0:T(8,128)(2,1)S(1)}, bf16[4,128,128]{2,1,0:T(8,128)(2,1)S(1)}) custom-call(s32[4,12]{1,0:T(4,128)S(1)} %get-tuple-element.41.table, f32[512,1536]{1,0:T(8,128)S(1)} %get-tuple-element.47.early, bf16[512,2048]{1,0:T(8,128)(2,1)S(1)} %get-tuple-element.46.rows, ...), custom_call_target="tpu_custom_call" | custom-call | flops 786432 | bytes 1572864 | tf_op jit(solution)/shard_map/delta/pallas_call | solution.py:199
  33.2 2.7 %collective-permute-start.15 = (bf16[128,1536]{1,0:T(8,128)(2,1)S(1)}, bf16[128,1536]{1,0:T(8,128)(2,1)S(1)}, u32[]{:S(2)}, u32[]{:S(2)}) collective-permute-start(bf16[128,1536]{1,0:T(8,128)(2,1)S(1)} %get-tuple-element.70), channel_id=1, source_target_pairs={{12,0},{0,4},{4,8},{8,12},{13,1},{1,5},{5,9},{9,13},{14,2},{2,6},{... | collective-permute-start | bytes 1179656 | tf_op jit(solution)/shard_map/ppermute | solution.py:418
  35.9 7.8 %partial.3 = (bf16[4,128,1024]{2,1,0:T(8,128)(2,1)S(1)}, bf16[128,1024]{1,0:T(8,128)(2,1)S(1)}, bf16[4,128,1024]{2,1,0:T(8,128)(2,1)S(1)}, bf16[128,1024]{1,0:T(8,128)(2,1)S(1)}) custom-call(s32[4,12]{1,0:T(4,128)S(1)} %get-tuple-element.41.table, bf16[3584,2048]{1,0:T(8,128)(2,1)} %weight.3, bf16[512,2048]{1,0:T(8,128)(2,1)S(1)} %get-tuple-element.46.rows, ...), custom_call_target="tpu_custom_call" | custom-call | flops 4294967296 | bytes 8589934592 | tf_op jit(solution)/shard_map/partial/pallas_call | solution.py:235
  43.7 1.3 %tile_grad.1 = (bf16[128,128]{1,0:T(8,128)(2,1)S(1)}, bf16[128,128]{1,0:T(8,128)(2,1)S(1)}, bf16[128,128]{1,0:T(8,128)(2,1)S(1)}, bf16[128,128]{1,0:T(8,128)(2,1)S(1)}) custom-call(s32[4,12]{1,0:T(4,128)S(1)} %get-tuple-element.41.table, bf16[512,2048]{1,0:T(8,128)(2,1)S(1)} %get-tuple-element.46.rows, bf16[5,128,128]{2,1,0:T(8,128)(2,1)S(1)} %get-tuple-element.48.refs_0_, ...), custom_call_target="tpu_custom_call" | custom-call | flops 1048576 | bytes 2097152 | tf_op jit(solution)/shard_map/tile_grad/pallas_call | solution.py:360
  45.2 2.2 %collective-permute-start.12 = (bf16[128,1024]{1,0:T(8,128)(2,1)S(1)}, bf16[128,1024]{1,0:T(8,128)(2,1)S(1)}, u32[]{:S(2)}, u32[]{:S(2)}) collective-permute-start(bf16[128,1024]{1,0:T(8,128)(2,1)S(1)} %get-tuple-element.68), channel_id=1, source_target_pairs={{12,0},{0,4},{4,8},{8,12},{13,1},{1,5},{5,9},{9,13},{14,2},{2,6},{... | collective-permute-start | bytes 786440 | tf_op jit(solution)/shard_map/ppermute | solution.py:418
  47.7 10.5 %collective-permute-done.9.arrived = bf16[128,1408]{1,0:T(8,128)(2,1)S(1)} collective-permute-done((bf16[128,1408]{1,0:T(8,128)(2,1)S(1)}, bf16[128,1408]{1,0:T(8,128)(2,1)S(1)}, u32[]{:S(2)}, u32[]{:S(2)}) %collective-permute-start.9) | collective-permute-done | bytes 360480 | tf_op jit(solution)/shard_map/ppermute | solution.py:418
  58.4 5.5 %collective-permute-done.12.arrived = bf16[128,1024]{1,0:T(8,128)(2,1)S(1)} collective-permute-done((bf16[128,1024]{1,0:T(8,128)(2,1)S(1)}, bf16[128,1024]{1,0:T(8,128)(2,1)S(1)}, u32[]{:S(2)}, u32[]{:S(2)}) %collective-permute-start.12) | collective-permute-done | bytes 262176 | tf_op jit(solution)/shard_map/ppermute | solution.py:418
  64.0 8.3 %collective-permute-done.16.arrived = bf16[128,1536]{1,0:T(8,128)(2,1)S(1)} collective-permute-done((bf16[128,1536]{1,0:T(8,128)(2,1)S(1)}, bf16[128,1536]{1,0:T(8,128)(2,1)S(1)}, u32[]{:S(2)}, u32[]{:S(2)}) %collective-permute-start.16) | collective-permute-done | bytes 393248 | tf_op jit(solution)/shard_map/ppermute | solution.py:418
  72.4 6.8 %collective-permute-done.10.arrived = bf16[128,1280]{1,0:T(8,128)(2,1)S(1)} collective-permute-done((bf16[128,1280]{1,0:T(8,128)(2,1)S(1)}, bf16[128,1280]{1,0:T(8,128)(2,1)S(1)}, u32[]{:S(2)}, u32[]{:S(2)}) %collective-permute-start.10) | collective-permute-done | bytes 327712 | tf_op jit(solution)/shard_map/ppermute | solution.py:418
  79.4 5.5 %collective-permute-done.13.arrived = bf16[128,1024]{1,0:T(8,128)(2,1)S(1)} collective-permute-done((bf16[128,1024]{1,0:T(8,128)(2,1)S(1)}, bf16[128,1024]{1,0:T(8,128)(2,1)S(1)}, u32[]{:S(2)}, u32[]{:S(2)}) %collective-permute-start.13) | collective-permute-done | bytes 262176 | tf_op jit(solution)/shard_map/ppermute | solution.py:418
  85.1 14.6 %collective-permute-done.11.refs_3_.arrived = bf16[128,1152]{1,0:T(8,128)(2,1)S(1)} collective-permute-done((bf16[128,1152]{1,0:T(8,128)(2,1)S(1)}, bf16[128,1152]{1,0:T(8,128)(2,1)S(1)}, u32[]{:S(2)}, u32[]{:S(2)}) %collective-permute-start.11) | collective-permute-done | bytes 294944 | tf_op jit(solution)/shard_map/ppermute | solution.py:418
  99.7 1.7 %adam.1 = (f32[4,128,128]{2,1,0:T(8,128)}, f32[4,128,128]{2,1,0:T(8,128)}, f32[4,128,128]{2,1,0:T(8,128)}) custom-call(s32[4,12]{1,0:T(4,128)S(1)} %get-tuple-element.41.table, bf16[128,128]{1,0:T(8,128)(2,1)S(1)} %get-tuple-element.60.refs_0_, bf16[128,128]{1,0:T(8,128)(2,1)S(1)} %get-tuple-element.61.refs_1_, ...), custom_call_target="tpu_custom_call" | custom-call | flops 65536 | bytes 131072 | tf_op jit(solution)/shard_map/adam/pallas_call | solution.py:404
  102.2 2.9 %collective-permute-done.14.arrived = bf16[128,1024]{1,0:T(8,128)(2,1)S(1)} collective-permute-done((bf16[128,1024]{1,0:T(8,128)(2,1)S(1)}, bf16[128,1024]{1,0:T(8,128)(2,1)S(1)}, u32[]{:S(2)}, u32[]{:S(2)}) %collective-permute-start.14) | collective-permute-done | bytes 262176 | tf_op jit(solution)/shard_map/ppermute | solution.py:418
  (37 shorter events, 5.9 us)
Async XLA Ops:
  0.6 21.3 %collective-permute-start.4 = (bf16[128,2048]{1,0:T(8,128)(2,1)}, bf16[128,2048]{1,0:T(8,128)(2,1)S(1)}, u32[]{:S(2)}, u32[]{:S(2)}) collective-permute-start(bf16[128,2048]{1,0:T(8,128)(2,1)} %own.1), channel_id=1, source_target_pairs={{2,0},{0,2},{3,1},{1,3},{6,4},{4,6},{7,5},{5,7},{10,8},{8,10},{11,... | collective-permute-start | bytes 1572872 | tf_op jit(solution)/shard_map/ppermute | solution.py:418
  4.4 5.9 %collective-permute-start.2 = (s32[1,8]{1,0:T(1,128)S(1)}, s32[1,8]{1,0:T(1,128)S(1)}, u32[]{:S(2)}, u32[]{:S(2)}) collective-permute-start(s32[1,8]{1,0:T(1,128)S(1)} %pad_add_fusion.refs_0_), channel_id=1, source_target_pairs={{4,0},{8,4},{12,8},{0,12},{5,1},{9,5},{13,9},{1,13},{6,2},{10,6},{... | collective-permute-start | bytes 104 | tf_op jit(solution)/shard_map/ppermute | solution.py:418
  8.0 4.4 %collective-permute-start.1 = (s32[1,8]{1,0:T(1,128)S(1)}, s32[1,8]{1,0:T(1,128)S(1)}, u32[]{:S(2)}, u32[]{:S(2)}) collective-permute-start(s32[1,8]{1,0:T(1,128)S(1)} %pad_add_fusion.refs_0_), channel_id=1, source_target_pairs={{8,0},{12,4},{0,8},{4,12},{9,1},{13,5},{1,9},{5,13},{10,2},{14,6},... | collective-permute-start | bytes 104 | tf_op jit(solution)/shard_map/ppermute | solution.py:418
  8.0 5.3 %collective-permute-start = (s32[1,8]{1,0:T(1,128)S(1)}, s32[1,8]{1,0:T(1,128)S(1)}, u32[]{:S(2)}, u32[]{:S(2)}) collective-permute-start(s32[1,8]{1,0:T(1,128)S(1)} %pad_add_fusion.refs_0_), channel_id=1, source_target_pairs={{12,0},{0,4},{4,8},{8,12},{13,1},{1,5},{5,9},{9,13},{14,2},{2,6},{... | collective-permute-start | bytes 104 | tf_op jit(solution)/shard_map/ppermute | solution.py:418
  14.7 7.2 %collective-permute-start.5 = (bf16[5,128,128]{2,1,0:T(8,128)(2,1)S(1)}, bf16[5,128,128]{2,1,0:T(8,128)(2,1)S(1)}, u32[]{:S(2)}, u32[]{:S(2)}) collective-permute-start(bf16[5,128,128]{2,1,0:T(8,128)(2,1)S(1)} %get-tuple-element.44), channel_id=1, source_target_pairs={{12,0},{0,4},{4,8},{8,12},{13,1},{1,5},{5,9},{9,13},{14,2},{2,6},{... | collective-permute-start | bytes 491528 | tf_op jit(solution)/shard_map/ppermute | solution.py:418
  14.8 7.7 %collective-permute-start.3 = (bf16[128,2048]{1,0:T(8,128)(2,1)}, bf16[128,2048]{1,0:T(8,128)(2,1)S(1)}, u32[]{:S(2)}, u32[]{:S(2)}) collective-permute-start(bf16[128,2048]{1,0:T(8,128)(2,1)} %own.1), channel_id=1, source_target_pairs={{1,0},{0,1},{3,2},{2,3},{5,4},{4,5},{7,6},{6,7},{9,8},{8,9},{11,10... | collective-permute-start | bytes 1572872 | tf_op jit(solution)/shard_map/ppermute | solution.py:418
  21.9 3.5 %collective-permute-start.6 = (bf16[128,2048]{1,0:T(8,128)(2,1)S(1)}, bf16[128,2048]{1,0:T(8,128)(2,1)S(1)}, u32[]{:S(2)}, u32[]{:S(2)}) collective-permute-start(bf16[128,2048]{1,0:T(8,128)(2,1)S(1)} %collective-permute-done.4.refs_1_), channel_id=1, source_target_pairs={{1,0},{0,1},{3,2},{2,3},{5,4},{4,5},{7,6},{6,7},{9,8},{8,9},{11,10... | collective-permute-start | bytes 1572872 | tf_op jit(solution)/shard_map/ppermute | solution.py:418
  21.9 8.8 %collective-permute-start.7 = (bf16[5,128,128]{2,1,0:T(8,128)(2,1)S(1)}, bf16[5,128,128]{2,1,0:T(8,128)(2,1)S(1)}, u32[]{:S(2)}, u32[]{:S(2)}) collective-permute-start(bf16[5,128,128]{2,1,0:T(8,128)(2,1)S(1)} %get-tuple-element.50), channel_id=1, source_target_pairs={{8,0},{12,4},{0,8},{4,12},{9,1},{13,5},{1,9},{5,13},{10,2},{14,6},... | collective-permute-start | bytes 491528 | tf_op jit(solution)/shard_map/ppermute | solution.py:418
  21.9 10.1 %collective-permute-start.8 = (bf16[5,128,128]{2,1,0:T(8,128)(2,1)S(1)}, bf16[5,128,128]{2,1,0:T(8,128)(2,1)S(1)}, u32[]{:S(2)}, u32[]{:S(2)}) collective-permute-start(bf16[5,128,128]{2,1,0:T(8,128)(2,1)S(1)} %get-tuple-element.51), channel_id=1, source_target_pairs={{4,0},{8,4},{12,8},{0,12},{5,1},{9,5},{13,9},{1,13},{6,2},{10,6},{... | collective-permute-start | bytes 491528 | tf_op jit(solution)/shard_map/ppermute | solution.py:418
  33.2 14.2 %collective-permute-start.15 = (bf16[128,1536]{1,0:T(8,128)(2,1)S(1)}, bf16[128,1536]{1,0:T(8,128)(2,1)S(1)}, u32[]{:S(2)}, u32[]{:S(2)}) collective-permute-start(bf16[128,1536]{1,0:T(8,128)(2,1)S(1)} %get-tuple-element.70), channel_id=1, source_target_pairs={{12,0},{0,4},{4,8},{8,12},{13,1},{1,5},{5,9},{9,13},{14,2},{2,6},{... | collective-permute-start | bytes 1179656 | tf_op jit(solution)/shard_map/ppermute | solution.py:418
  45.1 13.1 %collective-permute-start.9 = (bf16[128,1408]{1,0:T(8,128)(2,1)S(1)}, bf16[128,1408]{1,0:T(8,128)(2,1)S(1)}, u32[]{:S(2)}, u32[]{:S(2)}) collective-permute-start(bf16[128,1408]{1,0:T(8,128)(2,1)S(1)} %attach.1), channel_id=1, source_target_pairs={{12,0},{0,4},{4,8},{8,12},{13,1},{1,5},{5,9},{9,13},{14,2},{2,6},{... | collective-permute-start | bytes 1081352 | tf_op jit(solution)/shard_map/ppermute | solution.py:418
  45.2 18.7 %collective-permute-start.12 = (bf16[128,1024]{1,0:T(8,128)(2,1)S(1)}, bf16[128,1024]{1,0:T(8,128)(2,1)S(1)}, u32[]{:S(2)}, u32[]{:S(2)}) collective-permute-start(bf16[128,1024]{1,0:T(8,128)(2,1)S(1)} %get-tuple-element.68), channel_id=1, source_target_pairs={{12,0},{0,4},{4,8},{8,12},{13,1},{1,5},{5,9},{9,13},{14,2},{2,6},{... | collective-permute-start | bytes 786440 | tf_op jit(solution)/shard_map/ppermute | solution.py:418
  47.5 24.8 %collective-permute-start.16 = (bf16[128,1536]{1,0:T(8,128)(2,1)S(1)}, bf16[128,1536]{1,0:T(8,128)(2,1)S(1)}, u32[]{:S(2)}, u32[]{:S(2)}) collective-permute-start(bf16[128,1536]{1,0:T(8,128)(2,1)S(1)} %add.12), channel_id=1, source_target_pairs={{12,0},{0,4},{4,8},{8,12},{13,1},{1,5},{5,9},{9,13},{14,2},{2,6},{... | collective-permute-start | bytes 1179656 | tf_op jit(solution)/shard_map/ppermute | solution.py:418
  58.3 21.0 %collective-permute-start.10 = (bf16[128,1280]{1,0:T(8,128)(2,1)S(1)}, bf16[128,1280]{1,0:T(8,128)(2,1)S(1)}, u32[]{:S(2)}, u32[]{:S(2)}) collective-permute-start(bf16[128,1280]{1,0:T(8,128)(2,1)S(1)} %get-tuple-element.58), channel_id=1, source_target_pairs={{12,0},{0,4},{4,8},{8,12},{13,1},{1,5},{5,9},{9,13},{14,2},{2,6},{... | collective-permute-start | bytes 983048 | tf_op jit(solution)/shard_map/ppermute | solution.py:418
  63.8 35.8 %copy-start = (f32[1,1,4,128,128]{4,3,2,1,0:T(8,128)S(1)}, f32[1,1,4,128,128]{4,3,2,1,0:T(8,128)}, u32[]{:S(2)}) copy-start(f32[1,1,4,128,128]{4,3,2,1,0:T(8,128)} %param.13) | copy-start | bytes 786436
  63.8 35.8 %copy-start.1 = (f32[1,1,4,128,128]{4,3,2,1,0:T(8,128)S(1)}, f32[1,1,4,128,128]{4,3,2,1,0:T(8,128)}, u32[]{:S(2)}) copy-start(f32[1,1,4,128,128]{4,3,2,1,0:T(8,128)} %param.14) | copy-start | bytes 786436
  63.8 35.8 %copy-start.2 = (f32[1,1,4,128,128]{4,3,2,1,0:T(8,128)S(1)}, f32[1,1,4,128,128]{4,3,2,1,0:T(8,128)}, u32[]{:S(2)}) copy-start(f32[1,1,4,128,128]{4,3,2,1,0:T(8,128)} %param.15) | copy-start | bytes 786436
  63.9 21.0 %collective-permute-start.13 = (bf16[128,1024]{1,0:T(8,128)(2,1)S(1)}, bf16[128,1024]{1,0:T(8,128)(2,1)S(1)}, u32[]{:S(2)}, u32[]{:S(2)}) collective-permute-start(bf16[128,1024]{1,0:T(8,128)(2,1)S(1)} %add.10), channel_id=1, source_target_pairs={{12,0},{0,4},{4,8},{8,12},{13,1},{1,5},{5,9},{9,13},{14,2},{2,6},{... | collective-permute-start | bytes 786440 | tf_op jit(solution)/shard_map/ppermute | solution.py:418
  72.4 28.9 %collective-permute-start.17 = (bf16[128,1536]{1,0:T(8,128)(2,1)S(1)}, bf16[128,1536]{1,0:T(8,128)(2,1)S(1)}, u32[]{:S(2)}, u32[]{:S(2)}) collective-permute-start(bf16[128,1536]{1,0:T(8,128)(2,1)S(1)} %add.13), channel_id=1, source_target_pairs={{12,0},{0,4},{4,8},{8,12},{13,1},{1,5},{5,9},{9,13},{14,2},{2,6},{... | collective-permute-start | bytes 1179656 | tf_op jit(solution)/shard_map/ppermute | solution.py:418
  79.4 20.3 %collective-permute-start.11 = (bf16[128,1152]{1,0:T(8,128)(2,1)S(1)}, bf16[128,1152]{1,0:T(8,128)(2,1)S(1)}, u32[]{:S(2)}, u32[]{:S(2)}) collective-permute-start(bf16[128,1152]{1,0:T(8,128)(2,1)S(1)} %get-tuple-element.59), channel_id=1, source_target_pairs={{12,0},{0,4},{4,8},{8,12},{13,1},{1,5},{5,9},{9,13},{14,2},{2,6},{... | collective-permute-start | bytes 884744 | tf_op jit(solution)/shard_map/ppermute | solution.py:418
  85.0 20.1 %collective-permute-start.14 = (bf16[128,1024]{1,0:T(8,128)(2,1)S(1)}, bf16[128,1024]{1,0:T(8,128)(2,1)S(1)}, u32[]{:S(2)}, u32[]{:S(2)}) collective-permute-start(bf16[128,1024]{1,0:T(8,128)(2,1)S(1)} %add.11), channel_id=1, source_target_pairs={{12,0},{0,4},{4,8},{8,12},{13,1},{1,5},{5,9},{9,13},{14,2},{2,6},{... | collective-permute-start | bytes 786440 | tf_op jit(solution)/shard_map/ppermute | solution.py:418

commit v10 on v9

--- a/solution.py
+++ b/solution.py
@@ -14,8 +14,10 @@
 EPSILON = 1e-08
 VMEM_LIMIT = 24 * 1024 * 1024
 MATMUL = 4096
-PARTS = (3, 2, 2)
+EARLY = 1
+PARTS = (2, 3, 2)
 RIDE = 2
+LAST = 0
 NT = (((1,), (1,)), ((), ()))
 TN = (((0,), (0,)), ((), ()))
 
@@ -145,7 +147,7 @@
         in_specs=[vmem()] * (1 + len(pieces)),
         out_specs=[vmem()] * 2,
         compiler_params=params(),
-        cost_estimate=cost(MATMUL * tokens * columns),
+        cost_estimate=cost(EARLY * tokens * columns),
         name="partial",
     )(weight, *pieces)
 
@@ -418,6 +420,17 @@
     return lax.ppermute(array, axis, [((i + places) % size, i) for i in range(size)])
 
 
+def take_chunk(own, place):
+    tensors, cores = lax.axis_size("tensor"), lax.axis_size("dp")
+    t_place, d_place = divmod(place, cores)
+    pairs = []
+    for t in range(tensors):
+        for d in range(cores):
+            source = (t + t_place) % tensors * cores + (d + d_place) % cores
+            pairs.append((source, t * cores + d))
+    return lax.ppermute(own, ("tensor", "dp"), pairs)
+
+
 def exchange(pieces):
     return [pieces[0]] + [take_from(pieces[s], "seq", -s) for s in range(1, len(pieces))]
 
@@ -437,8 +450,8 @@
     cuts = [(f_blocks // group) * end // ends[-1] for end in ends]
     ranges = list(zip(cuts[:-1], cuts[1:]))
 
-    firsts = [take_from(cotangent, "tensor", t) for t in range(1, lax.axis_size("tensor"))]
-    local = [take_from(cotangent, "dp", d) for d in range(1, cores)]
+    local = [take_chunk(cotangent, place) for place in range(1, cores)]
+    remote = [take_chunk(cotangent, place) for place in range(cores, spans)]
 
     meta = jnp.concatenate([tile_ids[0], tile_live[0]], axis=1)
     metas = exchange([meta] * spans)
@@ -483,25 +496,29 @@
     )(*metas, values_half, hidden_here)
     crossed = exchange(picked)
 
-    firsts, crossed[1] = lax.optimization_barrier((firsts, crossed[1]))
-    pieces = [local_rows]
-    for first in firsts:
-        pieces += [first] + [take_from(first, "dp", d) for d in range(1, cores)]
-
-    early, rows = early_matmul_call(width, first_weight, pieces)
+    early, rows = early_matmul_call(width, first_weight, [local_rows, *remote])
     partial, first, held = delta_call(sizes, table, early, rows, crossed)
-    later = tuple(cut - cuts[1] for cut in cuts[2:])
-    more = matmul_call(spans, cuts[1], later, width, table, down_weight, rows, held)
-    partials, begins = [partial, *more[::2]], [first, *more[1::2]]
-    grads = grad_call(sizes, table, rows, crossed)
-    begins[RIDE] = attach_call(begins[RIDE], grads[1:])
-    moving = [take_from(begin, "seq", -1) for begin in begins]
+    partials, moving = [partial], [take_from(first, "seq", -1)]
+    for part in range(1, len(ranges)):
+        low, high = ranges[part]
+        if part == RIDE:
+            moving[0] = add_call(2, partials[0], moving[0], block)[0]
+            rows, moving[0] = lax.optimization_barrier((rows, moving[0]))
+        partial, first = matmul_call(
+            spans, low, (high - low,), width, table, down_weight, rows, held
+        )
+        if part == RIDE:
+            grads = grad_call(sizes, table, rows, crossed)
+            first = attach_call(first, grads[1:])
+        partials.append(partial)
+        moving.append(take_from(first, "seq", -1))
 
     tiles = [grads[0]]
     for t in range(2, spans):
         for part in range(len(ranges)):
-            moving[part], *mine = add_call(t, partials[part], moving[part], block)
-            tiles += mine
+            if (t, part) != (2, 0):
+                moving[part], *mine = add_call(t, partials[part], moving[part], block)
+                tiles += mine
             moving[part] = take_from(moving[part], "seq", -1)
     tiles.append(moving[RIDE])
     columns = partials[RIDE].shape[2]
@@ -509,10 +526,13 @@
 
     hidden_grad = None
     shape = jax.ShapeDtypeStruct((chunk, f_width), jnp.bfloat16)
-    for part, (low, _) in enumerate(ranges):
-        if part == len(ranges) - 1:
+    order = [part for part in range(len(ranges)) if part != LAST] + [LAST]
+    for part in order:
+        if part == LAST:
             moving[part], new = lax.optimization_barrier((moving[part], new))
-        hidden_grad = last_call(low * width, partials[part], moving[part], hidden_grad, shape)
+        hidden_grad = last_call(
+            ranges[part][0] * width, partials[part], moving[part], hidden_grad, shape
+        )
     return (hidden_grad,) + tuple(array[None, None] for array in new)
 
 

time: 106 us -> 103 us (0.972)
  waiting for transfers between devices: 66.8 us -> 58.3 us
  starting transfers between devices: 13.8 us -> 17.1 us
  Pallas kernels: 24.5 us -> 26.1 us
    ppermute x18 -> x15, waiting for transfers between devices: 66.8 us -> 53.8 us  [take_from(): lax.ppermute(array, axis, [((i + places) % size, i) for i in range(size)])]
    ppermute x0 -> x3, waiting for transfers between devices: none -> 4.49 us  [take_chunk(): return lax.ppermute(own, ('tensor', 'dp'), pairs)]
    pallas_call x1 -> x2, Pallas kernels: 7.83 us -> 11.2 us  [matmul_call(): pl.pallas_call(functools.partial(matmul_kernel, low, ends), grid=(ends[-1...]
    ppermute x0 -> x3, starting transfers between devices: none -> 3.18 us  [take_chunk(): return lax.ppermute(own, ('tensor', 'dp'), pairs)]
    pallas_call x1, Pallas kernels: 4.03 us -> 2.72 us  [early_matmul_call(): pl.pallas_call(functools.partial(early_matmul_kernel, width), grid=(colum...]
    ppermute x18 -> x15, starting transfers between devices: 13.8 us -> 13.9 us  [take_from(): lax.ppermute(array, axis, [((i + places) % size, i) for i in range(size)])]
  transfers between devices with their start and end apart: 18 -> 18, of which waited for: 12 -> 11; matrix products, arithmetic and copies ran while one was open for 1% -> 1% of each run, Pallas kernels for 20% -> 23%
where the time goes in v10:
time: 103 us
  waiting for transfers between devices  58.3 us (57%)
  Pallas kernels  26.1 us (25%)
  starting transfers between devices  17.1 us (17%)
    ppermute x15, waiting for transfers between devices, take_from(): lax.ppermute(array, axis, [((i + places) % size, i) for i in range(size)])  53.8 us
    ppermute x15, starting transfers between devices, take_from(): lax.ppermute(array, axis, [((i + places) % size, i) for i in range(size)])  13.9 us
    pallas_call x2, Pallas kernels, matmul_call(): pl.pallas_call(functools.partial(matmul_kernel, low, ends), grid=(ends[-1...  11.2 us
    ppermute x3, waiting for transfers between devices, take_chunk(): return lax.ppermute(own, ('tensor', 'dp'), pairs)  4.49 us
    ppermute x3, starting transfers between devices, take_chunk(): return lax.ppermute(own, ('tensor', 'dp'), pairs)  3.18 us
    pallas_call x1, Pallas kernels, early_matmul_call(): pl.pallas_call(functools.partial(early_matmul_kernel, width), grid=(colum...  2.72 us
    pallas_call x3, Pallas kernels, last_call(): pl.pallas_call(functools.partial(last_kernel, low), out_shape=shape, in_s...  2.42 us
    pallas_call x1, Pallas kernels, per_device(): pl.pallas_call(lay_kernel, out_shape=[jax.ShapeDtypeStruct((cores * chunk...  2.32 us
  transfers between devices with their start and end apart: 18, of which 11 were waited for; matrix products, arithmetic and copies ran while one was open for 1% of the time, Pallas kernels for 23%

profile of v10, /device:TPU:0, one launch (start us, length us, event | category | flops | bytes accessed | tf_op | source)
XLA Modules:
  0.0 103.1 jit_solution(6647284210958355811)
XLA Ops:
  1.1 2.6 %collective-permute-start.5 = (bf16[128,2048]{1,0:T(8,128)(2,1)}, bf16[128,2048]{1,0:T(8,128)(2,1)S(1)}, u32[]{:S(2)}, u32[]{:S(2)}) collective-permute-start(bf16[128,2048]{1,0:T(8,128)(2,1)} %own.1), channel_id=1, source_target_pairs={{3,0},{2,1},{1,2},{0,3},{7,4},{6,5},{5,6},{4,7},{11,8},{10,9},{9,1... | collective-permute-start | bytes 1572872 | tf_op jit(solution)/shard_map/ppermute | solution.py:431
  4.6 4.1 %collective-permute-start.2 = (s32[1,8]{1,0:T(1,128)S(1)}, s32[1,8]{1,0:T(1,128)S(1)}, u32[]{:S(2)}, u32[]{:S(2)}) collective-permute-start(s32[1,8]{1,0:T(1,128)S(1)} %pad_add_fusion.refs_0_), channel_id=1, source_target_pairs={{4,0},{8,4},{12,8},{0,12},{5,1},{9,5},{13,9},{1,13},{6,2},{10,6},{... | collective-permute-start | bytes 104 | tf_op jit(solution)/shard_map/ppermute | solution.py:420
  8.7 1.3 %early.1 = (bf16[4,128,128]{2,1,0:T(8,128)(2,1)S(1)}, bf16[128,3584]{1,0:T(8,128)(2,1)S(1)}) custom-call(f32[4,128,128]{2,1,0:T(8,128)} %bitcast.8, bf16[128,3584]{1,0:T(8,128)(2,1)} %hidden.1), custom_call_target="tpu_custom_call" | custom-call | flops 458752 | bytes 917504 | tf_op jit(solution)/shard_map/early/pallas_call | solution.py:458
  11.0 2.1 %collective-permute-done.1.refs_2_ = s32[1,8]{1,0:T(1,128)S(1)} collective-permute-done((s32[1,8]{1,0:T(1,128)S(1)}, s32[1,8]{1,0:T(1,128)S(1)}, u32[]{:S(2)}, u32[]{:S(2)}) %collective-permute-start.1) | collective-permute-done | bytes 64 | tf_op jit(solution)/shard_map/ppermute | solution.py:420
  13.1 2.4 %collective-permute-done.refs_1_ = s32[1,8]{1,0:T(1,128)S(1)} collective-permute-done((s32[1,8]{1,0:T(1,128)S(1)}, s32[1,8]{1,0:T(1,128)S(1)}, u32[]{:S(2)}, u32[]{:S(2)}) %collective-permute-start) | collective-permute-done | bytes 64 | tf_op jit(solution)/shard_map/ppermute | solution.py:420
  15.5 1.4 %pick.1 = (s32[4,12]{1,0:T(4,128)S(1)}, bf16[5,128,128]{2,1,0:T(8,128)(2,1)S(1)}, bf16[5,128,128]{2,1,0:T(8,128)(2,1)S(1)}, bf16[5,128,128]{2,1,0:T(8,128)(2,1)S(1)}, bf16[5,128,128]{2,1,0:T(8,128)(2,1)S(1)}) custom-call(s32[1,8]{1,0:T(1,128)S(1)} %pad_add_fusion.refs_0_, s32[1,8]{1,0:T(1,128)S(1)} %collective-permute-done.refs_1_, ...), custom_call_target="tpu_custom_call" | custom-call | flops 458752 | bytes 917504 | tf_op jit(solution)/shard_map/pick/pallas_call | solution.py:487
  17.0 2.6 %collective-permute-start.7 = (bf16[5,128,128]{2,1,0:T(8,128)(2,1)S(1)}, bf16[5,128,128]{2,1,0:T(8,128)(2,1)S(1)}, u32[]{:S(2)}, u32[]{:S(2)}) collective-permute-start(bf16[5,128,128]{2,1,0:T(8,128)(2,1)S(1)} %get-tuple-element.48), channel_id=1, source_target_pairs={{8,0},{12,4},{0,8},{4,12},{9,1},{13,5},{1,9},{5,13},{10,2},{14,6},... | collective-permute-start | bytes 491528 | tf_op jit(solution)/shard_map/ppermute | solution.py:420
  19.5 1.3 %collective-permute-start.8 = (bf16[5,128,128]{2,1,0:T(8,128)(2,1)S(1)}, bf16[5,128,128]{2,1,0:T(8,128)(2,1)S(1)}, u32[]{:S(2)}, u32[]{:S(2)}) collective-permute-start(bf16[5,128,128]{2,1,0:T(8,128)(2,1)S(1)} %get-tuple-element.49), channel_id=1, source_target_pairs={{4,0},{8,4},{12,8},{0,12},{5,1},{9,5},{13,9},{1,13},{6,2},{10,6},{... | collective-permute-start | bytes 491528 | tf_op jit(solution)/shard_map/ppermute | solution.py:420
  20.8 2.3 %lay.1 = (bf16[256,2048]{1,0:T(8,128)(2,1)S(1)}, bf16[1024,2048]{1,0:T(8,128)(2,1)S(1)}) custom-call(bf16[128,2048]{1,0:T(8,128)(2,1)} %own.1, bf16[3584,2048]{1,0:T(8,128)(2,1)} %weight.5, bf16[128,2048]{1,0:T(8,128)(2,1)S(1)} %collective-permute-done.3.refs_0_), custom_call_target="tpu_custom_call" | custom-call | flops 524288 | bytes 1048576 | tf_op jit(solution)/shard_map/lay/pallas_call | solution.py:474
  23.2 4.5 %collective-permute-done.4.refs_1_ = bf16[128,2048]{1,0:T(8,128)(2,1)S(1)} collective-permute-done((bf16[128,2048]{1,0:T(8,128)(2,1)}, bf16[128,2048]{1,0:T(8,128)(2,1)S(1)}, u32[]{:S(2)}, u32[]{:S(2)}) %collective-permute-start.4) | collective-permute-done | bytes 524320 | tf_op jit(solution)/shard_map/ppermute | solution.py:431
  27.7 2.7 %partial.3 = (f32[512,1024]{1,0:T(8,128)S(1)}, bf16[512,2048]{1,0:T(8,128)(2,1)S(1)}) custom-call(bf16[1024,2048]{1,0:T(8,128)(2,1)S(1)} %get-tuple-element.42.weight, bf16[256,2048]{1,0:T(8,128)(2,1)S(1)} %get-tuple-element.43.refs_0_, bf16[128,2048]{1,0:T(8,128)(2,1)S(1)} %collective-permute-done.4.refs_1_, ...), custom_call_target="tpu_custom_call" | custom-call | flops 524288 | bytes 1048576 | tf_op jit(solution)/shard_map/partial/pallas_call | solution.py:140
  31.4 3.4 %collective-permute-start.9 = (bf16[128,1024]{1,0:T(8,128)(2,1)S(1)}, bf16[128,1024]{1,0:T(8,128)(2,1)S(1)}, u32[]{:S(2)}, u32[]{:S(2)}) collective-permute-start(bf16[128,1024]{1,0:T(8,128)(2,1)S(1)} %get-tuple-element.51), channel_id=1, source_target_pairs={{12,0},{0,4},{4,8},{8,12},{13,1},{1,5},{5,9},{9,13},{14,2},{2,6},{... | collective-permute-start | bytes 786440 | tf_op jit(solution)/shard_map/ppermute | solution.py:420
  34.8 6.4 %partial.5 = (bf16[4,128,1536]{2,1,0:T(8,128)(2,1)S(1)}, bf16[128,1536]{1,0:T(8,128)(2,1)S(1)}) custom-call(s32[4,12]{1,0:T(4,128)S(1)} %get-tuple-element.41.table, bf16[3584,2048]{1,0:T(8,128)(2,1)} %weight.5, bf16[512,2048]{1,0:T(8,128)(2,1)S(1)} %get-tuple-element.53.rows, bf16[4,128,128]{2,1,0:T(8,128)(2,1)S(1)} %get-tuple-element.55.held), custom_call_target="tpu_custom_call" | custom-call | flops 3221225472 | bytes 6442450944 | tf_op jit(solution)/shard_map/partial/pallas_call | solution.py:237
  41.4 1.6 %tile_grad.1 = (bf16[128,128]{1,0:T(8,128)(2,1)S(1)}, bf16[128,128]{1,0:T(8,128)(2,1)S(1)}, bf16[128,128]{1,0:T(8,128)(2,1)S(1)}, bf16[128,128]{1,0:T(8,128)(2,1)S(1)}) custom-call(s32[4,12]{1,0:T(4,128)S(1)} %get-tuple-element.41.table, bf16[512,2048]{1,0:T(8,128)(2,1)S(1)} %get-tuple-element.53.rows, bf16[5,128,128]{2,1,0:T(8,128)(2,1)S(1)} %get-tuple-element.46.refs_0_, ...), custom_call_target="tpu_custom_call" | custom-call | flops 1048576 | bytes 2097152 | tf_op jit(solution)/shard_map/tile_grad/pallas_call | solution.py:362
  43.0 4.8 %partial.4 = (bf16[4,128,1024]{2,1,0:T(8,128)(2,1)S(1)}, bf16[128,1024]{1,0:T(8,128)(2,1)S(1)}) custom-call(s32[4,12]{1,0:T(4,128)S(1)} %get-tuple-element.41.table, bf16[3584,2048]{1,0:T(8,128)(2,1)} %weight.5, bf16[512,2048]{1,0:T(8,128)(2,1)S(1)} %get-tuple-element.53.rows, bf16[4,128,128]{2,1,0:T(8,128)(2,1)S(1)} %get-tuple-element.55.held), custom_call_target="tpu_custom_call" | custom-call | flops 2147483648 | bytes 4294967296 | tf_op jit(solution)/shard_map/partial/pallas_call | solution.py:237
  48.7 5.7 %collective-permute-done.15.arrived = bf16[128,1536]{1,0:T(8,128)(2,1)S(1)} collective-permute-done((bf16[128,1536]{1,0:T(8,128)(2,1)S(1)}, bf16[128,1536]{1,0:T(8,128)(2,1)S(1)}, u32[]{:S(2)}, u32[]{:S(2)}) %collective-permute-start.15) | collective-permute-done | bytes 393248 | tf_op jit(solution)/shard_map/ppermute | solution.py:420
  54.6 7.5 %collective-permute-done.12.arrived = bf16[128,1408]{1,0:T(8,128)(2,1)S(1)} collective-permute-done((bf16[128,1408]{1,0:T(8,128)(2,1)S(1)}, bf16[128,1408]{1,0:T(8,128)(2,1)S(1)}, u32[]{:S(2)}, u32[]{:S(2)}) %collective-permute-start.12) | collective-permute-done | bytes 360480 | tf_op jit(solution)/shard_map/ppermute | solution.py:420
  62.4 8.1 %collective-permute-done.16.arrived = bf16[128,1536]{1,0:T(8,128)(2,1)S(1)} collective-permute-done((bf16[128,1536]{1,0:T(8,128)(2,1)S(1)}, bf16[128,1536]{1,0:T(8,128)(2,1)S(1)}, u32[]{:S(2)}, u32[]{:S(2)}) %collective-permute-start.16) | collective-permute-done | bytes 393248 | tf_op jit(solution)/shard_map/ppermute | solution.py:420
  70.7 6.8 %collective-permute-done.13.arrived = bf16[128,1280]{1,0:T(8,128)(2,1)S(1)} collective-permute-done((bf16[128,1280]{1,0:T(8,128)(2,1)S(1)}, bf16[128,1280]{1,0:T(8,128)(2,1)S(1)}, u32[]{:S(2)}, u32[]{:S(2)}) %collective-permute-start.13) | collective-permute-done | bytes 327712 | tf_op jit(solution)/shard_map/ppermute | solution.py:420
  77.7 5.4 %collective-permute-done.10.arrived = bf16[128,1024]{1,0:T(8,128)(2,1)S(1)} collective-permute-done((bf16[128,1024]{1,0:T(8,128)(2,1)S(1)}, bf16[128,1024]{1,0:T(8,128)(2,1)S(1)}, u32[]{:S(2)}, u32[]{:S(2)}) %collective-permute-start.10) | collective-permute-done | bytes 262176 | tf_op jit(solution)/shard_map/ppermute | solution.py:420
  83.3 8.3 %collective-permute-done.17.arrived = bf16[128,1536]{1,0:T(8,128)(2,1)S(1)} collective-permute-done((bf16[128,1536]{1,0:T(8,128)(2,1)S(1)}, bf16[128,1536]{1,0:T(8,128)(2,1)S(1)}, u32[]{:S(2)}, u32[]{:S(2)}) %collective-permute-start.17) | collective-permute-done | bytes 393248 | tf_op jit(solution)/shard_map/ppermute | solution.py:420
  92.5 5.5 %collective-permute-done.14.refs_3_.arrived = bf16[128,1152]{1,0:T(8,128)(2,1)S(1)} collective-permute-done((bf16[128,1152]{1,0:T(8,128)(2,1)S(1)}, bf16[128,1152]{1,0:T(8,128)(2,1)S(1)}, u32[]{:S(2)}, u32[]{:S(2)}) %collective-permute-start.14) | collective-permute-done | bytes 294944 | tf_op jit(solution)/shard_map/ppermute | solution.py:420
  97.9 1.7 %adam.1 = (f32[4,128,128]{2,1,0:T(8,128)}, f32[4,128,128]{2,1,0:T(8,128)}, f32[4,128,128]{2,1,0:T(8,128)}) custom-call(s32[4,12]{1,0:T(4,128)S(1)} %get-tuple-element.41.table, bf16[128,128]{1,0:T(8,128)(2,1)S(1)} %get-tuple-element.54.refs_0_, bf16[128,128]{1,0:T(8,128)(2,1)S(1)} %get-tuple-element.61.refs_1_, ...), custom_call_target="tpu_custom_call" | custom-call | flops 65536 | bytes 131072 | tf_op jit(solution)/shard_map/adam/pallas_call | solution.py:406
  99.6 1.9 %collective-permute-done.11.arrived = bf16[128,1024]{1,0:T(8,128)(2,1)S(1)} collective-permute-done((bf16[128,1024]{1,0:T(8,128)(2,1)S(1)}, bf16[128,1024]{1,0:T(8,128)(2,1)S(1)}, u32[]{:S(2)}, u32[]{:S(2)}) %collective-permute-start.11) | collective-permute-done | bytes 262176 | tf_op jit(solution)/shard_map/ppermute | solution.py:420
  (38 shorter events, 7.9 us)
Async XLA Ops:
  0.6 18.9 %collective-permute-start.3 = (bf16[128,2048]{1,0:T(8,128)(2,1)}, bf16[128,2048]{1,0:T(8,128)(2,1)S(1)}, u32[]{:S(2)}, u32[]{:S(2)}) collective-permute-start(bf16[128,2048]{1,0:T(8,128)(2,1)} %own.1), channel_id=1, source_target_pairs={{1,0},{0,1},{3,2},{2,3},{5,4},{4,5},{7,6},{6,7},{9,8},{8,9},{11,10... | collective-permute-start | bytes 1572872 | tf_op jit(solution)/shard_map/ppermute | solution.py:431
  1.1 22.0 %collective-permute-start.5 = (bf16[128,2048]{1,0:T(8,128)(2,1)}, bf16[128,2048]{1,0:T(8,128)(2,1)S(1)}, u32[]{:S(2)}, u32[]{:S(2)}) collective-permute-start(bf16[128,2048]{1,0:T(8,128)(2,1)} %own.1), channel_id=1, source_target_pairs={{3,0},{2,1},{1,2},{0,3},{7,4},{6,5},{5,6},{4,7},{11,8},{10,9},{9,1... | collective-permute-start | bytes 1572872 | tf_op jit(solution)/shard_map/ppermute | solution.py:431
  3.8 23.9 %collective-permute-start.4 = (bf16[128,2048]{1,0:T(8,128)(2,1)}, bf16[128,2048]{1,0:T(8,128)(2,1)S(1)}, u32[]{:S(2)}, u32[]{:S(2)}) collective-permute-start(bf16[128,2048]{1,0:T(8,128)(2,1)} %own.1), channel_id=1, source_target_pairs={{2,0},{3,1},{0,2},{1,3},{6,4},{7,5},{4,6},{5,7},{10,8},{11,9},{8,1... | collective-permute-start | bytes 1572872 | tf_op jit(solution)/shard_map/ppermute | solution.py:431
  4.6 5.4 %collective-permute-start.2 = (s32[1,8]{1,0:T(1,128)S(1)}, s32[1,8]{1,0:T(1,128)S(1)}, u32[]{:S(2)}, u32[]{:S(2)}) collective-permute-start(s32[1,8]{1,0:T(1,128)S(1)} %pad_add_fusion.refs_0_), channel_id=1, source_target_pairs={{4,0},{8,4},{12,8},{0,12},{5,1},{9,5},{13,9},{1,13},{6,2},{10,6},{... | collective-permute-start | bytes 104 | tf_op jit(solution)/shard_map/ppermute | solution.py:420
  8.6 4.4 %collective-permute-start.1 = (s32[1,8]{1,0:T(1,128)S(1)}, s32[1,8]{1,0:T(1,128)S(1)}, u32[]{:S(2)}, u32[]{:S(2)}) collective-permute-start(s32[1,8]{1,0:T(1,128)S(1)} %pad_add_fusion.refs_0_), channel_id=1, source_target_pairs={{8,0},{12,4},{0,8},{4,12},{9,1},{13,5},{1,9},{5,13},{10,2},{14,6},... | collective-permute-start | bytes 104 | tf_op jit(solution)/shard_map/ppermute | solution.py:420
  10.0 5.6 %collective-permute-start = (s32[1,8]{1,0:T(1,128)S(1)}, s32[1,8]{1,0:T(1,128)S(1)}, u32[]{:S(2)}, u32[]{:S(2)}) collective-permute-start(s32[1,8]{1,0:T(1,128)S(1)} %pad_add_fusion.refs_0_), channel_id=1, source_target_pairs={{12,0},{0,4},{4,8},{8,12},{13,1},{1,5},{5,9},{9,13},{14,2},{2,6},{... | collective-permute-start | bytes 104 | tf_op jit(solution)/shard_map/ppermute | solution.py:420
  16.9 13.5 %collective-permute-start.6 = (bf16[5,128,128]{2,1,0:T(8,128)(2,1)S(1)}, bf16[5,128,128]{2,1,0:T(8,128)(2,1)S(1)}, u32[]{:S(2)}, u32[]{:S(2)}) collective-permute-start(bf16[5,128,128]{2,1,0:T(8,128)(2,1)S(1)} %get-tuple-element.47), channel_id=1, source_target_pairs={{12,0},{0,4},{4,8},{8,12},{13,1},{1,5},{5,9},{9,13},{14,2},{2,6},{... | collective-permute-start | bytes 491528 | tf_op jit(solution)/shard_map/ppermute | solution.py:420
  17.0 13.4 %collective-permute-start.7 = (bf16[5,128,128]{2,1,0:T(8,128)(2,1)S(1)}, bf16[5,128,128]{2,1,0:T(8,128)(2,1)S(1)}, u32[]{:S(2)}, u32[]{:S(2)}) collective-permute-start(bf16[5,128,128]{2,1,0:T(8,128)(2,1)S(1)} %get-tuple-element.48), channel_id=1, source_target_pairs={{8,0},{12,4},{0,8},{4,12},{9,1},{13,5},{1,9},{5,13},{10,2},{14,6},... | collective-permute-start | bytes 491528 | tf_op jit(solution)/shard_map/ppermute | solution.py:420
  19.5 10.9 %collective-permute-start.8 = (bf16[5,128,128]{2,1,0:T(8,128)(2,1)S(1)}, bf16[5,128,128]{2,1,0:T(8,128)(2,1)S(1)}, u32[]{:S(2)}, u32[]{:S(2)}) collective-permute-start(bf16[5,128,128]{2,1,0:T(8,128)(2,1)S(1)} %get-tuple-element.49), channel_id=1, source_target_pairs={{4,0},{8,4},{12,8},{0,12},{5,1},{9,5},{13,9},{1,13},{6,2},{10,6},{... | collective-permute-start | bytes 491528 | tf_op jit(solution)/shard_map/ppermute | solution.py:420
  31.4 9.9 %collective-permute-start.9 = (bf16[128,1024]{1,0:T(8,128)(2,1)S(1)}, bf16[128,1024]{1,0:T(8,128)(2,1)S(1)}, u32[]{:S(2)}, u32[]{:S(2)}) collective-permute-start(bf16[128,1024]{1,0:T(8,128)(2,1)S(1)} %get-tuple-element.51), channel_id=1, source_target_pairs={{12,0},{0,4},{4,8},{8,12},{13,1},{1,5},{5,9},{9,13},{14,2},{2,6},{... | collective-permute-start | bytes 786440 | tf_op jit(solution)/shard_map/ppermute | solution.py:420
  41.2 13.2 %collective-permute-start.15 = (bf16[128,1536]{1,0:T(8,128)(2,1)S(1)}, bf16[128,1536]{1,0:T(8,128)(2,1)S(1)}, u32[]{:S(2)}, u32[]{:S(2)}) collective-permute-start(bf16[128,1536]{1,0:T(8,128)(2,1)S(1)} %get-tuple-element.70), channel_id=1, source_target_pairs={{12,0},{0,4},{4,8},{8,12},{13,1},{1,5},{5,9},{9,13},{14,2},{2,6},{... | collective-permute-start | bytes 1179656 | tf_op jit(solution)/shard_map/ppermute | solution.py:420
  47.8 14.3 %collective-permute-start.12 = (bf16[128,1408]{1,0:T(8,128)(2,1)S(1)}, bf16[128,1408]{1,0:T(8,128)(2,1)S(1)}, u32[]{:S(2)}, u32[]{:S(2)}) collective-permute-start(bf16[128,1408]{1,0:T(8,128)(2,1)S(1)} %attach.1), channel_id=1, source_target_pairs={{12,0},{0,4},{4,8},{8,12},{13,1},{1,5},{5,9},{9,13},{14,2},{2,6},{... | collective-permute-start | bytes 1081352 | tf_op jit(solution)/shard_map/ppermute | solution.py:420
  54.5 16.0 %collective-permute-start.16 = (bf16[128,1536]{1,0:T(8,128)(2,1)S(1)}, bf16[128,1536]{1,0:T(8,128)(2,1)S(1)}, u32[]{:S(2)}, u32[]{:S(2)}) collective-permute-start(bf16[128,1536]{1,0:T(8,128)(2,1)S(1)} %add.12), channel_id=1, source_target_pairs={{12,0},{0,4},{4,8},{8,12},{13,1},{1,5},{5,9},{9,13},{14,2},{2,6},{... | collective-permute-start | bytes 1179656 | tf_op jit(solution)/shard_map/ppermute | solution.py:420
  62.2 15.4 %collective-permute-start.13 = (bf16[128,1280]{1,0:T(8,128)(2,1)S(1)}, bf16[128,1280]{1,0:T(8,128)(2,1)S(1)}, u32[]{:S(2)}, u32[]{:S(2)}) collective-permute-start(bf16[128,1280]{1,0:T(8,128)(2,1)S(1)} %get-tuple-element.62), channel_id=1, source_target_pairs={{12,0},{0,4},{4,8},{8,12},{13,1},{1,5},{5,9},{9,13},{14,2},{2,6},{... | collective-permute-start | bytes 983048 | tf_op jit(solution)/shard_map/ppermute | solution.py:420
  62.3 20.9 %collective-permute-start.10 = (bf16[128,1024]{1,0:T(8,128)(2,1)S(1)}, bf16[128,1024]{1,0:T(8,128)(2,1)S(1)}, u32[]{:S(2)}, u32[]{:S(2)}) collective-permute-start(bf16[128,1024]{1,0:T(8,128)(2,1)S(1)} %add.8), channel_id=1, source_target_pairs={{12,0},{0,4},{4,8},{8,12},{13,1},{1,5},{5,9},{9,13},{14,2},{2,6},{... | collective-permute-start | bytes 786440 | tf_op jit(solution)/shard_map/ppermute | solution.py:420
  70.6 21.0 %collective-permute-start.17 = (bf16[128,1536]{1,0:T(8,128)(2,1)S(1)}, bf16[128,1536]{1,0:T(8,128)(2,1)S(1)}, u32[]{:S(2)}, u32[]{:S(2)}) collective-permute-start(bf16[128,1536]{1,0:T(8,128)(2,1)S(1)} %add.13), channel_id=1, source_target_pairs={{12,0},{0,4},{4,8},{8,12},{13,1},{1,5},{5,9},{9,13},{14,2},{2,6},{... | collective-permute-start | bytes 1179656 | tf_op jit(solution)/shard_map/ppermute | solution.py:420
  77.6 20.3 %copy-start = (f32[1,1,4,128,128]{4,3,2,1,0:T(8,128)S(1)}, f32[1,1,4,128,128]{4,3,2,1,0:T(8,128)}, u32[]{:S(2)}) copy-start(f32[1,1,4,128,128]{4,3,2,1,0:T(8,128)} %param.13) | copy-start | bytes 786436
  77.7 20.3 %copy-start.1 = (f32[1,1,4,128,128]{4,3,2,1,0:T(8,128)S(1)}, f32[1,1,4,128,128]{4,3,2,1,0:T(8,128)}, u32[]{:S(2)}) copy-start(f32[1,1,4,128,128]{4,3,2,1,0:T(8,128)} %param.14) | copy-start | bytes 786436
  77.7 20.3 %copy-start.2 = (f32[1,1,4,128,128]{4,3,2,1,0:T(8,128)S(1)}, f32[1,1,4,128,128]{4,3,2,1,0:T(8,128)}, u32[]{:S(2)}) copy-start(f32[1,1,4,128,128]{4,3,2,1,0:T(8,128)} %param.15) | copy-start | bytes 786436
  77.7 20.2 %collective-permute-start.14 = (bf16[128,1152]{1,0:T(8,128)(2,1)S(1)}, bf16[128,1152]{1,0:T(8,128)(2,1)S(1)}, u32[]{:S(2)}, u32[]{:S(2)}) collective-permute-start(bf16[128,1152]{1,0:T(8,128)(2,1)S(1)} %get-tuple-element.64), channel_id=1, source_target_pairs={{12,0},{0,4},{4,8},{8,12},{13,1},{1,5},{5,9},{9,13},{14,2},{2,6},{... | collective-permute-start | bytes 884744 | tf_op jit(solution)/shard_map/ppermute | solution.py:420
  83.3 18.2 %collective-permute-start.11 = (bf16[128,1024]{1,0:T(8,128)(2,1)S(1)}, bf16[128,1024]{1,0:T(8,128)(2,1)S(1)}, u32[]{:S(2)}, u32[]{:S(2)}) collective-permute-start(bf16[128,1024]{1,0:T(8,128)(2,1)S(1)} %add.9), channel_id=1, source_target_pairs={{12,0},{0,4},{4,8},{8,12},{13,1},{1,5},{5,9},{9,13},{14,2},{2,6},{... | collective-permute-start | bytes 786440 | tf_op jit(solution)/shard_map/ppermute | solution.py:420

commit v11 on v10

--- a/solution.py
+++ b/solution.py
@@ -18,6 +18,7 @@
 PARTS = (2, 3, 2)
 RIDE = 2
 LAST = 0
+LAID = 2
 NT = (((1,), (1,)), ((), ()))
 TN = (((0,), (0,)), ((), ()))
 
@@ -66,14 +67,22 @@
     return before
 
 
-def early_kernel(values, hidden, values_half, hidden_here, stored, sems):
-    value_copy = pltpu.make_async_copy(values, stored, sems.at[0])
-    hidden_copy = pltpu.make_async_copy(hidden, hidden_here, sems.at[1])
-    value_copy.start()
-    hidden_copy.start()
-    value_copy.wait()
+def early_kernel(values, hidden, own, *refs):
+    others, (values_half, hidden_here, rows, stored, sems) = refs[:-5], refs[-5:]
+    chunk = own.shape[0]
+    copies = [
+        pltpu.make_async_copy(values, stored, sems.at[0]),
+        pltpu.make_async_copy(hidden, hidden_here, sems.at[1]),
+        pltpu.make_async_copy(own, rows.at[pl.ds(0, chunk)], sems.at[2]),
+    ]
+    for copy in copies:
+        copy.start()
+    for p, other in enumerate(others):
+        rows[(p + 1) * chunk : (p + 2) * chunk] = other[...]
+    copies[0].wait()
     values_half[...] = stored[...].astype(values_half.dtype)
-    hidden_copy.wait()
+    copies[1].wait()
+    copies[2].wait()
 
 
 def pick_kernel(spans, slots, block, d_blocks, *refs):
@@ -96,19 +105,10 @@
             outs[s][j] = hidden[:, pl.ds(start, block)]
 
 
-def lay_kernel(own, weight, *refs):
-    others, (rows, first_weight, sems) = refs[:-3], refs[-3:]
-    chunk = own.shape[0]
-    weight_copy = pltpu.make_async_copy(
-        weight.at[pl.ds(0, first_weight.shape[0])], first_weight, sems.at[0]
-    )
-    weight_copy.start()
-    own_copy = pltpu.make_async_copy(own, rows.at[pl.ds(0, chunk)], sems.at[1])
-    own_copy.start()
-    for p, other in enumerate(others):
-        rows[(p + 1) * chunk : (p + 2) * chunk] = other[...]
-    own_copy.wait()
-    weight_copy.wait()
+def lay_kernel(weight, first_weight, sem):
+    copy = pltpu.make_async_copy(weight.at[pl.ds(0, first_weight.shape[0])], first_weight, sem)
+    copy.start()
+    copy.wait()
 
 
 def chunk_at(place):
@@ -135,8 +135,8 @@
     )
 
 
-def early_matmul_call(width, weight, pieces):
-    tokens, (columns, d_width) = sum(piece.shape[0] for piece in pieces), weight.shape
+def early_matmul_call(width, columns, weight, pieces):
+    tokens, d_width = sum(piece.shape[0] for piece in pieces), weight.shape[1]
     return pl.pallas_call(
         functools.partial(early_matmul_kernel, width),
         grid=(columns // width,),
@@ -216,8 +216,12 @@
 
 def matmul_kernel(low, ends, table, weight, rows, held, *refs):
     outs, total = refs[:-1], refs[-1]
-    step, width = pl.program_id(0), weight.shape[0]
-    total[...] = lax.dot_general(rows[...], weight[...], NT, preferred_element_type=jnp.float32)
+    step, width = pl.program_id(0), total.shape[1]
+    if weight.shape[0] == width:
+        weights = weight[...]
+    else:
+        weights = weight[pl.ds(pl.multiple_of((low + step) * width, width), width)]
+    total[...] = lax.dot_general(rows[...], weights, NT, preferred_element_type=jnp.float32)
     add_delta(table, rows, held, total, (low + step) * width)
     for part, (begin, end) in enumerate(zip((0, *ends), ends)):
 
@@ -227,8 +231,12 @@
             put_chunks(total, *outs[2 * part : 2 * part + 2], here)
 
 
-def matmul_call(spans, low, ends, width, table, weight, rows, held):
+def matmul_call(spans, low, ends, width, table, weight, in_vmem, rows, held):
     tokens, d_width = rows.shape
+    if in_vmem:
+        weight_spec = vmem()
+    else:
+        weight, weight_spec = stay(weight), pl.BlockSpec((width, d_width), lambda i: (i + low, 0))
     shapes = []
     for begin, end in zip((0, *ends), ends):
         columns = (end - begin) * width
@@ -238,18 +246,13 @@
         functools.partial(matmul_kernel, low, ends),
         grid=(ends[-1],),
         out_shape=shapes,
-        in_specs=[
-            smem(),
-            pl.BlockSpec((width, d_width), lambda i: (i + low, 0)),
-            vmem(),
-            vmem(),
-        ],
+        in_specs=[smem(), weight_spec, vmem(), vmem()],
         out_specs=[vmem()] * len(shapes),
         scratch_shapes=[pltpu.VMEM((tokens, width), jnp.float32)],
         compiler_params=params(),
         cost_estimate=cost(MATMUL * tokens * ends[-1] * width),
         name="partial",
-    )(table, stay(weight), rows, held)
+    )(table, weight, rows, held)
 
 
 def attach_kernel(first, *refs):
@@ -455,35 +458,23 @@
 
     meta = jnp.concatenate([tile_ids[0], tile_live[0]], axis=1)
     metas = exchange([meta] * spans)
-    values_half, hidden_here = pl.pallas_call(
+    values_half, hidden_here, local_rows = pl.pallas_call(
         early_kernel,
         out_shape=[
             jax.ShapeDtypeStruct((slots, block, block), jnp.bfloat16),
             jax.ShapeDtypeStruct(hidden_in.shape, hidden_in.dtype),
+            jax.ShapeDtypeStruct((cores * chunk, d_width), cotangent.dtype),
         ],
-        in_specs=[hbm(), hbm()],
-        out_specs=[vmem(), vmem()],
+        in_specs=[hbm()] * 3 + [vmem()] * (cores - 1),
+        out_specs=[vmem()] * 3,
         scratch_shapes=[
             pltpu.VMEM((slots, block, block), jnp.float32),
-            pltpu.SemaphoreType.DMA((2,)),
+            pltpu.SemaphoreType.DMA((3,)),
         ],
         compiler_params=params(),
         cost_estimate=cost(hidden_in.size),
         name="early",
-    )(stay(values[0, 0]), stay(hidden_in))
-    local_rows, first_weight = pl.pallas_call(
-        lay_kernel,
-        out_shape=[
-            jax.ShapeDtypeStruct((cores * chunk, d_width), cotangent.dtype),
-            jax.ShapeDtypeStruct((ranges[0][1] * width, d_width), down_weight.dtype),
-        ],
-        in_specs=[hbm(), hbm()] + [vmem()] * (cores - 1),
-        out_specs=[vmem(), vmem()],
-        scratch_shapes=[pltpu.SemaphoreType.DMA((2,))],
-        compiler_params=params(),
-        cost_estimate=cost(cores * chunk * d_width),
-        name="lay",
-    )(stay(cotangent), stay(down_weight), *local)
+    )(stay(values[0, 0]), stay(hidden_in), stay(cotangent), *local)
     table, *picked = pl.pallas_call(
         functools.partial(pick_kernel, *sizes, d_blocks),
         out_shape=[jax.ShapeDtypeStruct((spans, 3 * slots), jnp.int32)]
@@ -496,7 +487,21 @@
     )(*metas, values_half, hidden_here)
     crossed = exchange(picked)
 
-    early, rows = early_matmul_call(width, first_weight, [local_rows, *remote])
+    laid = ranges[LAID - 1][1]
+    first_weight = pl.pallas_call(
+        lay_kernel,
+        out_shape=jax.ShapeDtypeStruct((laid * width, d_width), down_weight.dtype),
+        in_specs=[hbm()],
+        out_specs=vmem(),
+        scratch_shapes=[pltpu.SemaphoreType.DMA],
+        compiler_params=params(),
+        cost_estimate=cost(laid * width * d_width),
+        name="lay",
+    )(stay(down_weight))
+
+    early, rows = early_matmul_call(
+        width, ranges[0][1] * width, first_weight, [local_rows, *remote]
+    )
     partial, first, held = delta_call(sizes, table, early, rows, crossed)
     partials, moving = [partial], [take_from(first, "seq", -1)]
     for part in range(1, len(ranges)):
@@ -505,7 +510,15 @@
             moving[0] = add_call(2, partials[0], moving[0], block)[0]
             rows, moving[0] = lax.optimization_barrier((rows, moving[0]))
         partial, first = matmul_call(
-            spans, low, (high - low,), width, table, down_weight, rows, held
+            spans,
+            low,
+            (high - low,),
+            width,
+            table,
+            first_weight if part < LAID else down_weight,
+            part < LAID,
+            rows,
+            held,
         )
         if part == RIDE:
             grads = grad_call(sizes, table, rows, crossed)
@@ -522,13 +535,14 @@
             moving[part] = take_from(moving[part], "seq", -1)
     tiles.append(moving[RIDE])
     columns = partials[RIDE].shape[2]
-    new = adam_call(sizes, columns, table, tiles, values, moment_one, moment_two)
 
     hidden_grad = None
     shape = jax.ShapeDtypeStruct((chunk, f_width), jnp.bfloat16)
     order = [part for part in range(len(ranges)) if part != LAST] + [LAST]
     for part in order:
         if part == LAST:
+            tiles[0], hidden_grad = lax.optimization_barrier((tiles[0], hidden_grad))
+            new = adam_call(sizes, columns, table, tiles, values, moment_one, moment_two)
             moving[part], new = lax.optimization_barrier((moving[part], new))
         hidden_grad = last_call(
             ranges[part][0] * width, partials[part], moving[part], hidden_grad, shape

time: 103 us -> 101 us (0.981)
  waiting for transfers between devices: 58.3 us -> 54.6 us
  starting transfers between devices: 17.1 us -> 18.6 us
    ppermute x15, waiting for transfers between devices: 53.8 us -> 50.5 us  [take_from(): lax.ppermute(array, axis, [((i + places) % size, i) for i in range(size)])]
    pallas_call x2, Pallas kernels: 11.2 us -> 9.47 us  [matmul_call(): pl.pallas_call(functools.partial(matmul_kernel, low, ends), grid=(ends[-1...]
    pallas_call x1, Pallas kernels: 2.32 us -> 3.99 us  [per_device(): pl.pallas_call(lay_kernel, out_shape=jax.ShapeDtypeStruct((laid * width,...]
    ppermute x15, starting transfers between devices: 13.9 us -> 15.4 us  [take_from(): lax.ppermute(array, axis, [((i + places) % size, i) for i in range(size)])]
  transfers between devices with their start and end apart: 18 -> 18, of which waited for: 11 -> 12; matrix products, arithmetic and copies ran while one was open for 1% -> 1% of each run, Pallas kernels for 23% -> 24%
where the time goes in v11:
time: 101 us; the launch traced here: 100 us
  waiting for transfers between devices  54.6 us (54%)
  Pallas kernels  25.5 us (25%)
  starting transfers between devices  18.6 us (18%)
    ppermute x15, waiting for transfers between devices, take_from(): lax.ppermute(array, axis, [((i + places) % size, i) for i in range(size)])  50.5 us
    ppermute x15, starting transfers between devices, take_from(): lax.ppermute(array, axis, [((i + places) % size, i) for i in range(size)])  15.4 us
    pallas_call x2, Pallas kernels, matmul_call(): pl.pallas_call(functools.partial(matmul_kernel, low, ends), grid=(ends[-1...  9.47 us
    ppermute x3, waiting for transfers between devices, take_chunk(): return lax.ppermute(own, ('tensor', 'dp'), pairs)  4.18 us
    pallas_call x1, Pallas kernels, per_device(): pl.pallas_call(lay_kernel, out_shape=jax.ShapeDtypeStruct((laid * width,...  3.99 us
    ppermute x3, starting transfers between devices, take_chunk(): return lax.ppermute(own, ('tensor', 'dp'), pairs)  3.18 us
    pallas_call x1, Pallas kernels, early_matmul_call(): pl.pallas_call(functools.partial(early_matmul_kernel, width), grid=(colum...  2.74 us
    pallas_call x3, Pallas kernels, last_call(): pl.pallas_call(functools.partial(last_kernel, low), out_shape=shape, in_s...  2.41 us
  transfers between devices with their start and end apart: 18, of which 12 were waited for; matrix products, arithmetic and copies ran while one was open for 1% of the time, Pallas kernels for 24%

profile of v11, /device:TPU:0, one launch (start us, length us, event | category | flops | bytes accessed | tf_op | source)
XLA Modules:
  0.0 100.3 jit_solution(4631517363848949777)
XLA Ops:
  1.1 2.6 %collective-permute-start.5 = (bf16[128,2048]{1,0:T(8,128)(2,1)}, bf16[128,2048]{1,0:T(8,128)(2,1)S(1)}, u32[]{:S(2)}, u32[]{:S(2)}) collective-permute-start(bf16[128,2048]{1,0:T(8,128)(2,1)} %own.1), channel_id=1, source_target_pairs={{3,0},{2,1},{1,2},{0,3},{7,4},{6,5},{5,6},{4,7},{11,8},{10,9},{9,1... | collective-permute-start | bytes 1572872 | tf_op jit(solution)/shard_map/ppermute | solution.py:434
  4.6 4.1 %collective-permute-start.2 = (s32[1,8]{1,0:T(1,128)S(1)}, s32[1,8]{1,0:T(1,128)S(1)}, u32[]{:S(2)}, u32[]{:S(2)}) collective-permute-start(s32[1,8]{1,0:T(1,128)S(1)} %pad_add_fusion.refs_0_), channel_id=1, source_target_pairs={{4,0},{8,4},{12,8},{0,12},{5,1},{9,5},{13,9},{1,13},{6,2},{10,6},{... | collective-permute-start | bytes 104 | tf_op jit(solution)/shard_map/ppermute | solution.py:423
  9.7 1.4 %early.1 = (bf16[4,128,128]{2,1,0:T(8,128)(2,1)S(1)}, bf16[128,3584]{1,0:T(8,128)(2,1)S(1)}, bf16[256,2048]{1,0:T(8,128)(2,1)S(1)}) custom-call(f32[4,128,128]{2,1,0:T(8,128)} %bitcast.8, bf16[128,3584]{1,0:T(8,128)(2,1)} %hidden.1, bf16[128,2048]{1,0:T(8,128)(2,1)} %own.1, bf16[128,2048]{1,0:T(8,128)(2,1)S(1)} %collective-permute-done.3.refs_0_), custom_call_target="tpu_custom_call" | custom-call | flops 458752 | bytes 917504 | tf_op jit(solution)/shard_map/early/pallas_call | solution.py:461
  11.1 2.0 %collective-permute-done.1.refs_2_ = s32[1,8]{1,0:T(1,128)S(1)} collective-permute-done((s32[1,8]{1,0:T(1,128)S(1)}, s32[1,8]{1,0:T(1,128)S(1)}, u32[]{:S(2)}, u32[]{:S(2)}) %collective-permute-start.1) | collective-permute-done | bytes 64 | tf_op jit(solution)/shard_map/ppermute | solution.py:423
  14.0 1.4 %pick.1 = (s32[4,12]{1,0:T(4,128)S(1)}, bf16[5,128,128]{2,1,0:T(8,128)(2,1)S(1)}, bf16[5,128,128]{2,1,0:T(8,128)(2,1)S(1)}, bf16[5,128,128]{2,1,0:T(8,128)(2,1)S(1)}, bf16[5,128,128]{2,1,0:T(8,128)(2,1)S(1)}) custom-call(s32[1,8]{1,0:T(1,128)S(1)} %pad_add_fusion.refs_0_, s32[1,8]{1,0:T(1,128)S(1)} %collective-permute-done.refs_1_, ...), custom_call_target="tpu_custom_call" | custom-call | flops 458752 | bytes 917504 | tf_op jit(solution)/shard_map/pick/pallas_call | solution.py:478
  16.6 2.8 %collective-permute-start.8 = (bf16[5,128,128]{2,1,0:T(8,128)(2,1)S(1)}, bf16[5,128,128]{2,1,0:T(8,128)(2,1)S(1)}, u32[]{:S(2)}, u32[]{:S(2)}) collective-permute-start(bf16[5,128,128]{2,1,0:T(8,128)(2,1)S(1)} %get-tuple-element.49), channel_id=1, source_target_pairs={{4,0},{8,4},{12,8},{0,12},{5,1},{9,5},{13,9},{1,13},{6,2},{10,6},{... | collective-permute-start | bytes 491528 | tf_op jit(solution)/shard_map/ppermute | solution.py:423
  19.5 4.0 %lay.1.weight = bf16[2560,2048]{1,0:T(8,128)(2,1)S(1)} custom-call(bf16[3584,2048]{1,0:T(8,128)(2,1)} %weight.3), custom_call_target="tpu_custom_call" | custom-call | flops 5242880 | bytes 10485760 | tf_op jit(solution)/shard_map/lay/pallas_call | solution.py:491
  23.5 4.2 %collective-permute-done.4.refs_1_ = bf16[128,2048]{1,0:T(8,128)(2,1)S(1)} collective-permute-done((bf16[128,2048]{1,0:T(8,128)(2,1)}, bf16[128,2048]{1,0:T(8,128)(2,1)S(1)}, u32[]{:S(2)}, u32[]{:S(2)}) %collective-permute-start.4) | collective-permute-done | bytes 524320 | tf_op jit(solution)/shard_map/ppermute | solution.py:434
  27.7 2.7 %partial.3 = (f32[512,1024]{1,0:T(8,128)S(1)}, bf16[512,2048]{1,0:T(8,128)(2,1)S(1)}) custom-call(bf16[2560,2048]{1,0:T(8,128)(2,1)S(1)} %lay.1.weight, bf16[256,2048]{1,0:T(8,128)(2,1)S(1)} %get-tuple-element.43.refs_0_, bf16[128,2048]{1,0:T(8,128)(2,1)S(1)} %collective-permute-done.4.refs_1_, bf16[128,2048]{1,0:T(8,128)(2,1)S(1)} %collective-permute-done.5.refs_2_), custom_call_target="tpu_custom_call" | custom-call | flops 524288 | bytes 1048576 | tf_op jit(solution)/shard_map/partial/pallas_call | solution.py:140
  31.4 2.0 %collective-permute-start.9 = (bf16[128,1024]{1,0:T(8,128)(2,1)S(1)}, bf16[128,1024]{1,0:T(8,128)(2,1)S(1)}, u32[]{:S(2)}, u32[]{:S(2)}) collective-permute-start(bf16[128,1024]{1,0:T(8,128)(2,1)S(1)} %get-tuple-element.51), channel_id=1, source_target_pairs={{12,0},{0,4},{4,8},{8,12},{13,1},{1,5},{5,9},{9,13},{14,2},{2,6},{... | collective-permute-start | bytes 786440 | tf_op jit(solution)/shard_map/ppermute | solution.py:423
  33.5 5.0 %partial.5 = (bf16[4,128,1536]{2,1,0:T(8,128)(2,1)S(1)}, bf16[128,1536]{1,0:T(8,128)(2,1)S(1)}) custom-call(s32[4,12]{1,0:T(4,128)S(1)} %get-tuple-element.42.table, bf16[2560,2048]{1,0:T(8,128)(2,1)S(1)} %lay.1.weight, bf16[512,2048]{1,0:T(8,128)(2,1)S(1)} %get-tuple-element.53.rows, bf16[4,128,128]{2,1,0:T(8,128)(2,1)S(1)} %get-tuple-element.55.held), custom_call_target="tpu_custom_call" | custom-call | flops 3221225472 | bytes 6442450944 | tf_op jit(solution)/shard_map/partial/pallas_call | solution.py:245
  38.5 1.3 %collective-permute-start.15 = (bf16[128,1536]{1,0:T(8,128)(2,1)S(1)}, bf16[128,1536]{1,0:T(8,128)(2,1)S(1)}, u32[]{:S(2)}, u32[]{:S(2)}) collective-permute-start(bf16[128,1536]{1,0:T(8,128)(2,1)S(1)} %get-tuple-element.64), channel_id=1, source_target_pairs={{12,0},{0,4},{4,8},{8,12},{13,1},{1,5},{5,9},{9,13},{14,2},{2,6},{... | collective-permute-start | bytes 1179656 | tf_op jit(solution)/shard_map/ppermute | solution.py:423
  39.8 1.6 %collective-permute-done.9.arrived = bf16[128,1024]{1,0:T(8,128)(2,1)S(1)} collective-permute-done((bf16[128,1024]{1,0:T(8,128)(2,1)S(1)}, bf16[128,1024]{1,0:T(8,128)(2,1)S(1)}, u32[]{:S(2)}, u32[]{:S(2)}) %collective-permute-start.9) | collective-permute-done | bytes 262176 | tf_op jit(solution)/shard_map/ppermute | solution.py:423
  42.3 4.5 %partial.4 = (bf16[4,128,1024]{2,1,0:T(8,128)(2,1)S(1)}, bf16[128,1024]{1,0:T(8,128)(2,1)S(1)}) custom-call(s32[4,12]{1,0:T(4,128)S(1)} %get-tuple-element.42.table, bf16[3584,2048]{1,0:T(8,128)(2,1)} %weight.3, bf16[512,2048]{1,0:T(8,128)(2,1)S(1)} %get-tuple-element.53.rows, bf16[4,128,128]{2,1,0:T(8,128)(2,1)S(1)} %get-tuple-element.55.held), custom_call_target="tpu_custom_call" | custom-call | flops 2147483648 | bytes 4294967296 | tf_op jit(solution)/shard_map/partial/pallas_call | solution.py:245
  47.0 3.2 %collective-permute-done.15.arrived = bf16[128,1536]{1,0:T(8,128)(2,1)S(1)} collective-permute-done((bf16[128,1536]{1,0:T(8,128)(2,1)S(1)}, bf16[128,1536]{1,0:T(8,128)(2,1)S(1)}, u32[]{:S(2)}, u32[]{:S(2)}) %collective-permute-start.15) | collective-permute-done | bytes 393248 | tf_op jit(solution)/shard_map/ppermute | solution.py:423
  50.4 1.2 %collective-permute-start.16 = (bf16[128,1536]{1,0:T(8,128)(2,1)S(1)}, bf16[128,1536]{1,0:T(8,128)(2,1)S(1)}, u32[]{:S(2)}, u32[]{:S(2)}) collective-permute-start(bf16[128,1536]{1,0:T(8,128)(2,1)S(1)} %add.12), channel_id=1, source_target_pairs={{12,0},{0,4},{4,8},{8,12},{13,1},{1,5},{5,9},{9,13},{14,2},{2,6},{... | collective-permute-start | bytes 1179656 | tf_op jit(solution)/shard_map/ppermute | solution.py:423
  51.6 8.4 %collective-permute-done.12.arrived = bf16[128,1408]{1,0:T(8,128)(2,1)S(1)} collective-permute-done((bf16[128,1408]{1,0:T(8,128)(2,1)S(1)}, bf16[128,1408]{1,0:T(8,128)(2,1)S(1)}, u32[]{:S(2)}, u32[]{:S(2)}) %collective-permute-start.12) | collective-permute-done | bytes 360480 | tf_op jit(solution)/shard_map/ppermute | solution.py:423
  61.4 7.1 %collective-permute-done.16.arrived = bf16[128,1536]{1,0:T(8,128)(2,1)S(1)} collective-permute-done((bf16[128,1536]{1,0:T(8,128)(2,1)S(1)}, bf16[128,1536]{1,0:T(8,128)(2,1)S(1)}, u32[]{:S(2)}, u32[]{:S(2)}) %collective-permute-start.16) | collective-permute-done | bytes 393248 | tf_op jit(solution)/shard_map/ppermute | solution.py:423
  68.6 6.8 %collective-permute-done.13.arrived = bf16[128,1280]{1,0:T(8,128)(2,1)S(1)} collective-permute-done((bf16[128,1280]{1,0:T(8,128)(2,1)S(1)}, bf16[128,1280]{1,0:T(8,128)(2,1)S(1)}, u32[]{:S(2)}, u32[]{:S(2)}) %collective-permute-start.13) | collective-permute-done | bytes 327712 | tf_op jit(solution)/shard_map/ppermute | solution.py:423
  75.6 5.5 %collective-permute-done.10.arrived = bf16[128,1024]{1,0:T(8,128)(2,1)S(1)} collective-permute-done((bf16[128,1024]{1,0:T(8,128)(2,1)S(1)}, bf16[128,1024]{1,0:T(8,128)(2,1)S(1)}, u32[]{:S(2)}, u32[]{:S(2)}) %collective-permute-start.10) | collective-permute-done | bytes 262176 | tf_op jit(solution)/shard_map/ppermute | solution.py:423
  81.3 8.3 %collective-permute-done.17.arrived = bf16[128,1536]{1,0:T(8,128)(2,1)S(1)} collective-permute-done((bf16[128,1536]{1,0:T(8,128)(2,1)S(1)}, bf16[128,1536]{1,0:T(8,128)(2,1)S(1)}, u32[]{:S(2)}, u32[]{:S(2)}) %collective-permute-start.17) | collective-permute-done | bytes 393248 | tf_op jit(solution)/shard_map/ppermute | solution.py:423
  90.4 5.4 %collective-permute-done.14.arrived.refs_3_ = bf16[128,1152]{1,0:T(8,128)(2,1)S(1)} collective-permute-done((bf16[128,1152]{1,0:T(8,128)(2,1)S(1)}, bf16[128,1152]{1,0:T(8,128)(2,1)S(1)}, u32[]{:S(2)}, u32[]{:S(2)}) %collective-permute-start.14) | collective-permute-done | bytes 294944 | tf_op jit(solution)/shard_map/ppermute | solution.py:423
  96.7 1.7 %adam.1 = (f32[4,128,128]{2,1,0:T(8,128)}, f32[4,128,128]{2,1,0:T(8,128)}, f32[4,128,128]{2,1,0:T(8,128)}) custom-call(s32[4,12]{1,0:T(4,128)S(1)} %get-tuple-element.42.table, bf16[128,128]{1,0:T(8,128)(2,1)S(1)} %get-tuple-element.65.refs_0_, bf16[128,128]{1,0:T(8,128)(2,1)S(1)} %get-tuple-element.66.refs_1_, ...), custom_call_target="tpu_custom_call" | custom-call | flops 65536 | bytes 131072 | tf_op jit(solution)/shard_map/adam/pallas_call | solution.py:409
  98.3 1.2 %collective-permute-done.11.arrived = bf16[128,1024]{1,0:T(8,128)(2,1)S(1)} collective-permute-done((bf16[128,1024]{1,0:T(8,128)(2,1)S(1)}, bf16[128,1024]{1,0:T(8,128)(2,1)S(1)}, u32[]{:S(2)}, u32[]{:S(2)}) %collective-permute-start.11) | collective-permute-done | bytes 262176 | tf_op jit(solution)/shard_map/ppermute | solution.py:423
  (38 shorter events, 11.0 us)
Async XLA Ops:
  0.6 8.0 %collective-permute-start.3 = (bf16[128,2048]{1,0:T(8,128)(2,1)}, bf16[128,2048]{1,0:T(8,128)(2,1)S(1)}, u32[]{:S(2)}, u32[]{:S(2)}) collective-permute-start(bf16[128,2048]{1,0:T(8,128)(2,1)} %own.1), channel_id=1, source_target_pairs={{1,0},{0,1},{3,2},{2,3},{5,4},{4,5},{7,6},{6,7},{9,8},{8,9},{11,10... | collective-permute-start | bytes 1572872 | tf_op jit(solution)/shard_map/ppermute | solution.py:434
  1.1 22.3 %collective-permute-start.5 = (bf16[128,2048]{1,0:T(8,128)(2,1)}, bf16[128,2048]{1,0:T(8,128)(2,1)S(1)}, u32[]{:S(2)}, u32[]{:S(2)}) collective-permute-start(bf16[128,2048]{1,0:T(8,128)(2,1)} %own.1), channel_id=1, source_target_pairs={{3,0},{2,1},{1,2},{0,3},{7,4},{6,5},{5,6},{4,7},{11,8},{10,9},{9,1... | collective-permute-start | bytes 1572872 | tf_op jit(solution)/shard_map/ppermute | solution.py:434
  3.8 23.9 %collective-permute-start.4 = (bf16[128,2048]{1,0:T(8,128)(2,1)}, bf16[128,2048]{1,0:T(8,128)(2,1)S(1)}, u32[]{:S(2)}, u32[]{:S(2)}) collective-permute-start(bf16[128,2048]{1,0:T(8,128)(2,1)} %own.1), channel_id=1, source_target_pairs={{2,0},{3,1},{0,2},{1,3},{6,4},{7,5},{4,6},{5,7},{10,8},{11,9},{8,1... | collective-permute-start | bytes 1572872 | tf_op jit(solution)/shard_map/ppermute | solution.py:434
  4.6 6.5 %collective-permute-start.2 = (s32[1,8]{1,0:T(1,128)S(1)}, s32[1,8]{1,0:T(1,128)S(1)}, u32[]{:S(2)}, u32[]{:S(2)}) collective-permute-start(s32[1,8]{1,0:T(1,128)S(1)} %pad_add_fusion.refs_0_), channel_id=1, source_target_pairs={{4,0},{8,4},{12,8},{0,12},{5,1},{9,5},{13,9},{1,13},{6,2},{10,6},{... | collective-permute-start | bytes 104 | tf_op jit(solution)/shard_map/ppermute | solution.py:423
  8.6 4.4 %collective-permute-start.1 = (s32[1,8]{1,0:T(1,128)S(1)}, s32[1,8]{1,0:T(1,128)S(1)}, u32[]{:S(2)}, u32[]{:S(2)}) collective-permute-start(s32[1,8]{1,0:T(1,128)S(1)} %pad_add_fusion.refs_0_), channel_id=1, source_target_pairs={{8,0},{12,4},{0,8},{4,12},{9,1},{13,5},{1,9},{5,13},{10,2},{14,6},... | collective-permute-start | bytes 104 | tf_op jit(solution)/shard_map/ppermute | solution.py:423
  8.7 5.3 %collective-permute-start = (s32[1,8]{1,0:T(1,128)S(1)}, s32[1,8]{1,0:T(1,128)S(1)}, u32[]{:S(2)}, u32[]{:S(2)}) collective-permute-start(s32[1,8]{1,0:T(1,128)S(1)} %pad_add_fusion.refs_0_), channel_id=1, source_target_pairs={{12,0},{0,4},{4,8},{8,12},{13,1},{1,5},{5,9},{9,13},{14,2},{2,6},{... | collective-permute-start | bytes 104 | tf_op jit(solution)/shard_map/ppermute | solution.py:423
  15.4 15.0 %collective-permute-start.6 = (bf16[5,128,128]{2,1,0:T(8,128)(2,1)S(1)}, bf16[5,128,128]{2,1,0:T(8,128)(2,1)S(1)}, u32[]{:S(2)}, u32[]{:S(2)}) collective-permute-start(bf16[5,128,128]{2,1,0:T(8,128)(2,1)S(1)} %get-tuple-element.47), channel_id=1, source_target_pairs={{12,0},{0,4},{4,8},{8,12},{13,1},{1,5},{5,9},{9,13},{14,2},{2,6},{... | collective-permute-start | bytes 491528 | tf_op jit(solution)/shard_map/ppermute | solution.py:423
  15.5 15.0 %collective-permute-start.7 = (bf16[5,128,128]{2,1,0:T(8,128)(2,1)S(1)}, bf16[5,128,128]{2,1,0:T(8,128)(2,1)S(1)}, u32[]{:S(2)}, u32[]{:S(2)}) collective-permute-start(bf16[5,128,128]{2,1,0:T(8,128)(2,1)S(1)} %get-tuple-element.48), channel_id=1, source_target_pairs={{8,0},{12,4},{0,8},{4,12},{9,1},{13,5},{1,9},{5,13},{10,2},{14,6},... | collective-permute-start | bytes 491528 | tf_op jit(solution)/shard_map/ppermute | solution.py:423
  16.6 13.8 %collective-permute-start.8 = (bf16[5,128,128]{2,1,0:T(8,128)(2,1)S(1)}, bf16[5,128,128]{2,1,0:T(8,128)(2,1)S(1)}, u32[]{:S(2)}, u32[]{:S(2)}) collective-permute-start(bf16[5,128,128]{2,1,0:T(8,128)(2,1)S(1)} %get-tuple-element.49), channel_id=1, source_target_pairs={{4,0},{8,4},{12,8},{0,12},{5,1},{9,5},{13,9},{1,13},{6,2},{10,6},{... | collective-permute-start | bytes 491528 | tf_op jit(solution)/shard_map/ppermute | solution.py:423
  31.4 9.9 %collective-permute-start.9 = (bf16[128,1024]{1,0:T(8,128)(2,1)S(1)}, bf16[128,1024]{1,0:T(8,128)(2,1)S(1)}, u32[]{:S(2)}, u32[]{:S(2)}) collective-permute-start(bf16[128,1024]{1,0:T(8,128)(2,1)S(1)} %get-tuple-element.51), channel_id=1, source_target_pairs={{12,0},{0,4},{4,8},{8,12},{13,1},{1,5},{5,9},{9,13},{14,2},{2,6},{... | collective-permute-start | bytes 786440 | tf_op jit(solution)/shard_map/ppermute | solution.py:423
  38.5 11.8 %collective-permute-start.15 = (bf16[128,1536]{1,0:T(8,128)(2,1)S(1)}, bf16[128,1536]{1,0:T(8,128)(2,1)S(1)}, u32[]{:S(2)}, u32[]{:S(2)}) collective-permute-start(bf16[128,1536]{1,0:T(8,128)(2,1)S(1)} %get-tuple-element.64), channel_id=1, source_target_pairs={{12,0},{0,4},{4,8},{8,12},{13,1},{1,5},{5,9},{9,13},{14,2},{2,6},{... | collective-permute-start | bytes 1179656 | tf_op jit(solution)/shard_map/ppermute | solution.py:423
  46.8 13.2 %collective-permute-start.12 = (bf16[128,1408]{1,0:T(8,128)(2,1)S(1)}, bf16[128,1408]{1,0:T(8,128)(2,1)S(1)}, u32[]{:S(2)}, u32[]{:S(2)}) collective-permute-start(bf16[128,1408]{1,0:T(8,128)(2,1)S(1)} %attach.1), channel_id=1, source_target_pairs={{12,0},{0,4},{4,8},{8,12},{13,1},{1,5},{5,9},{9,13},{14,2},{2,6},{... | collective-permute-start | bytes 1081352 | tf_op jit(solution)/shard_map/ppermute | solution.py:423
  50.4 18.1 %collective-permute-start.16 = (bf16[128,1536]{1,0:T(8,128)(2,1)S(1)}, bf16[128,1536]{1,0:T(8,128)(2,1)S(1)}, u32[]{:S(2)}, u32[]{:S(2)}) collective-permute-start(bf16[128,1536]{1,0:T(8,128)(2,1)S(1)} %add.12), channel_id=1, source_target_pairs={{12,0},{0,4},{4,8},{8,12},{13,1},{1,5},{5,9},{9,13},{14,2},{2,6},{... | collective-permute-start | bytes 1179656 | tf_op jit(solution)/shard_map/ppermute | solution.py:423
  60.1 15.4 %collective-permute-start.13 = (bf16[128,1280]{1,0:T(8,128)(2,1)S(1)}, bf16[128,1280]{1,0:T(8,128)(2,1)S(1)}, u32[]{:S(2)}, u32[]{:S(2)}) collective-permute-start(bf16[128,1280]{1,0:T(8,128)(2,1)S(1)} %get-tuple-element.61), channel_id=1, source_target_pairs={{12,0},{0,4},{4,8},{8,12},{13,1},{1,5},{5,9},{9,13},{14,2},{2,6},{... | collective-permute-start | bytes 983048 | tf_op jit(solution)/shard_map/ppermute | solution.py:423
  60.2 20.9 %collective-permute-start.10 = (bf16[128,1024]{1,0:T(8,128)(2,1)S(1)}, bf16[128,1024]{1,0:T(8,128)(2,1)S(1)}, u32[]{:S(2)}, u32[]{:S(2)}) collective-permute-start(bf16[128,1024]{1,0:T(8,128)(2,1)S(1)} %add.8), channel_id=1, source_target_pairs={{12,0},{0,4},{4,8},{8,12},{13,1},{1,5},{5,9},{9,13},{14,2},{2,6},{... | collective-permute-start | bytes 786440 | tf_op jit(solution)/shard_map/ppermute | solution.py:423
  68.6 21.0 %collective-permute-start.17 = (bf16[128,1536]{1,0:T(8,128)(2,1)S(1)}, bf16[128,1536]{1,0:T(8,128)(2,1)S(1)}, u32[]{:S(2)}, u32[]{:S(2)}) collective-permute-start(bf16[128,1536]{1,0:T(8,128)(2,1)S(1)} %add.13), channel_id=1, source_target_pairs={{12,0},{0,4},{4,8},{8,12},{13,1},{1,5},{5,9},{9,13},{14,2},{2,6},{... | collective-permute-start | bytes 1179656 | tf_op jit(solution)/shard_map/ppermute | solution.py:423
  75.6 20.3 %collective-permute-start.14 = (bf16[128,1152]{1,0:T(8,128)(2,1)S(1)}, bf16[128,1152]{1,0:T(8,128)(2,1)S(1)}, u32[]{:S(2)}, u32[]{:S(2)}) collective-permute-start(bf16[128,1152]{1,0:T(8,128)(2,1)S(1)} %get-tuple-element.62), channel_id=1, source_target_pairs={{12,0},{0,4},{4,8},{8,12},{13,1},{1,5},{5,9},{9,13},{14,2},{2,6},{... | collective-permute-start | bytes 884744 | tf_op jit(solution)/shard_map/ppermute | solution.py:423
  81.2 18.4 %collective-permute-start.11 = (bf16[128,1024]{1,0:T(8,128)(2,1)S(1)}, bf16[128,1024]{1,0:T(8,128)(2,1)S(1)}, u32[]{:S(2)}, u32[]{:S(2)}) collective-permute-start(bf16[128,1024]{1,0:T(8,128)(2,1)S(1)} %add.9), channel_id=1, source_target_pairs={{12,0},{0,4},{4,8},{8,12},{13,1},{1,5},{5,9},{9,13},{14,2},{2,6},{... | collective-permute-start | bytes 786440 | tf_op jit(solution)/shard_map/ppermute | solution.py:423
  90.4 6.2 %copy-start = (f32[1,1,4,128,128]{4,3,2,1,0:T(8,128)S(1)}, f32[1,1,4,128,128]{4,3,2,1,0:T(8,128)}, u32[]{:S(2)}) copy-start(f32[1,1,4,128,128]{4,3,2,1,0:T(8,128)} %param.13) | copy-start | bytes 786436
  90.4 6.2 %copy-start.1 = (f32[1,1,4,128,128]{4,3,2,1,0:T(8,128)S(1)}, f32[1,1,4,128,128]{4,3,2,1,0:T(8,128)}, u32[]{:S(2)}) copy-start(f32[1,1,4,128,128]{4,3,2,1,0:T(8,128)} %param.14) | copy-start | bytes 786436
  90.4 6.2 %copy-start.2 = (f32[1,1,4,128,128]{4,3,2,1,0:T(8,128)S(1)}, f32[1,1,4,128,128]{4,3,2,1,0:T(8,128)}, u32[]{:S(2)}) copy-start(f32[1,1,4,128,128]{4,3,2,1,0:T(8,128)} %param.15) | copy-start | bytes 786436

commit v12 on v11

--- a/solution.py
+++ b/solution.py
@@ -15,6 +15,7 @@
 VMEM_LIMIT = 24 * 1024 * 1024
 MATMUL = 4096
 EARLY = 1
+AHEAD = 100000
 PARTS = (2, 3, 2)
 RIDE = 2
 LAST = 0
@@ -454,7 +455,7 @@
     ranges = list(zip(cuts[:-1], cuts[1:]))
 
     local = [take_chunk(cotangent, place) for place in range(1, cores)]
-    remote = [take_chunk(cotangent, place) for place in range(cores, spans)]
+    firsts = [take_from(cotangent, "tensor", t) for t in range(1, lax.axis_size("tensor"))]
 
     meta = jnp.concatenate([tile_ids[0], tile_live[0]], axis=1)
     metas = exchange([meta] * spans)
@@ -495,10 +496,14 @@
         out_specs=vmem(),
         scratch_shapes=[pltpu.SemaphoreType.DMA],
         compiler_params=params(),
-        cost_estimate=cost(laid * width * d_width),
+        cost_estimate=cost(AHEAD * laid * width * d_width),
         name="lay",
     )(stay(down_weight))
 
+    firsts, picked = lax.optimization_barrier((firsts, picked))
+    remote = []
+    for first in firsts:
+        remote += [first] + [take_from(first, "dp", d) for d in range(1, cores)]
     early, rows = early_matmul_call(
         width, ranges[0][1] * width, first_weight, [local_rows, *remote]
     )

time: 101 us -> 101 us (level)
  Pallas kernels: 25.5 us -> 29.1 us
  waiting for transfers between devices: 54.6 us -> 52.8 us
  starting transfers between devices: 18.6 us -> 16.9 us
    ppermute x3 -> x1, waiting for transfers between devices: 4.18 us -> 0.01 us  [take_chunk(): return lax.ppermute(own, ('tensor', 'dp'), pairs)]
    ppermute x3 -> x1, starting transfers between devices: 3.18 us -> 0.52 us  [take_chunk(): return lax.ppermute(own, ('tensor', 'dp'), pairs)]
    ppermute x15 -> x17, waiting for transfers between devices: 50.5 us -> 52.8 us  [take_from(): lax.ppermute(array, axis, [((i + places) % size, i) for i in range(size)])]
    pallas_call x1, Pallas kernels: 2.74 us -> 3.97 us  [early_matmul_call(): pl.pallas_call(functools.partial(early_matmul_kernel, width), grid=(colum...]
    pallas_call x1, Pallas kernels: 0.87 us -> 2.08 us  [grad_call(): pl.pallas_call(functools.partial(grad_kernel, *sizes), out_shape=[jax.Sha...]
    ppermute x15 -> x17, starting transfers between devices: 15.4 us -> 16.3 us  [take_from(): lax.ppermute(array, axis, [((i + places) % size, i) for i in range(size)])]
  transfers between devices with their start and end apart: 18 -> 18, of which waited for: 12 -> 12; matrix products, arithmetic and copies ran while one was open for 1% -> 1% of each run, Pallas kernels for 24% -> 27%
where the time goes in v12:
time: 101 us; the launch traced here: 100 us
  waiting for transfers between devices  52.8 us (52%)
  Pallas kernels  29.1 us (29%)
  starting transfers between devices  16.9 us (17%)
    ppermute x17, waiting for transfers between devices, take_from(): lax.ppermute(array, axis, [((i + places) % size, i) for i in range(size)])  52.8 us
    ppermute x17, starting transfers between devices, take_from(): lax.ppermute(array, axis, [((i + places) % size, i) for i in range(size)])  16.3 us
    pallas_call x2, Pallas kernels, matmul_call(): pl.pallas_call(functools.partial(matmul_kernel, low, ends), grid=(ends[-1...  9.84 us
    pallas_call x1, Pallas kernels, per_device(): pl.pallas_call(lay_kernel, out_shape=jax.ShapeDtypeStruct((laid * width,...  3.99 us
    pallas_call x1, Pallas kernels, early_matmul_call(): pl.pallas_call(functools.partial(early_matmul_kernel, width), grid=(colum...  3.97 us
    pallas_call x3, Pallas kernels, last_call(): pl.pallas_call(functools.partial(last_kernel, low), out_shape=shape, in_s...  2.41 us
    pallas_call x1, Pallas kernels, grad_call(): pl.pallas_call(functools.partial(grad_kernel, *sizes), out_shape=[jax.Sha...  2.08 us
  transfers between devices with their start and end apart: 18, of which 12 were waited for; matrix products, arithmetic and copies ran while one was open for 1% of the time, Pallas kernels for 27%

profile of v12, /device:TPU:0, one launch (start us, length us, event | category | flops | bytes accessed | tf_op | source)
XLA Modules:
  0.0 100.4 jit_solution(9346422871298547572)
XLA Ops:
  1.1 2.6 %collective-permute-start.4 = (bf16[128,2048]{1,0:T(8,128)(2,1)}, bf16[128,2048]{1,0:T(8,128)(2,1)}, u32[]{:S(2)}, u32[]{:S(2)}) collective-permute-start(bf16[128,2048]{1,0:T(8,128)(2,1)} %own.1), channel_id=1, source_target_pairs={{2,0},{0,2},{3,1},{1,3},{6,4},{4,6},{7,5},{5,7},{10,8},{8,10},{11,... | collective-permute-start | bytes 1572872 | tf_op jit(solution)/shard_map/ppermute | solution.py:424
  4.5 3.6 %collective-permute-start.2 = (s32[1,8]{1,0:T(1,128)S(1)}, s32[1,8]{1,0:T(1,128)S(1)}, u32[]{:S(2)}, u32[]{:S(2)}) collective-permute-start(s32[1,8]{1,0:T(1,128)S(1)} %pad_add_fusion.refs_0_), channel_id=1, source_target_pairs={{4,0},{8,4},{12,8},{0,12},{5,1},{9,5},{13,9},{1,13},{6,2},{10,6},{... | collective-permute-start | bytes 104 | tf_op jit(solution)/shard_map/ppermute | solution.py:424
  9.1 1.4 %early.1 = (bf16[4,128,128]{2,1,0:T(8,128)(2,1)S(1)}, bf16[128,3584]{1,0:T(8,128)(2,1)S(1)}, bf16[256,2048]{1,0:T(8,128)(2,1)S(1)}) custom-call(f32[4,128,128]{2,1,0:T(8,128)} %bitcast.8, bf16[128,3584]{1,0:T(8,128)(2,1)} %hidden.1, bf16[128,2048]{1,0:T(8,128)(2,1)} %own.1, bf16[128,2048]{1,0:T(8,128)(2,1)S(1)} %collective-permute-done.3.refs_0_), custom_call_target="tpu_custom_call" | custom-call | flops 458752 | bytes 917504 | tf_op jit(solution)/shard_map/early/pallas_call | solution.py:462
  10.5 2.0 %collective-permute-done.1.refs_2_ = s32[1,8]{1,0:T(1,128)S(1)} collective-permute-done((s32[1,8]{1,0:T(1,128)S(1)}, s32[1,8]{1,0:T(1,128)S(1)}, u32[]{:S(2)}, u32[]{:S(2)}) %collective-permute-start.1) | collective-permute-done | bytes 64 | tf_op jit(solution)/shard_map/ppermute | solution.py:424
  13.4 1.5 %pick.1 = (s32[4,12]{1,0:T(4,128)S(1)}, bf16[5,128,128]{2,1,0:T(8,128)(2,1)S(1)}, bf16[5,128,128]{2,1,0:T(8,128)(2,1)}, bf16[5,128,128]{2,1,0:T(8,128)(2,1)}, bf16[5,128,128]{2,1,0:T(8,128)(2,1)}) custom-call(s32[1,8]{1,0:T(1,128)S(1)} %pad_add_fusion.refs_0_, s32[1,8]{1,0:T(1,128)S(1)} %collective-permute-done.refs_1_, ...), custom_call_target="tpu_custom_call" | custom-call | flops 458752 | bytes 917504 | tf_op jit(solution)/shard_map/pick/pallas_call | solution.py:479
  15.0 1.2 %collective-permute-start.7 = (bf16[5,128,128]{2,1,0:T(8,128)(2,1)}, bf16[5,128,128]{2,1,0:T(8,128)(2,1)}, u32[]{:S(2)}, u32[]{:S(2)}) collective-permute-start(bf16[5,128,128]{2,1,0:T(8,128)(2,1)} %get-tuple-element.47), channel_id=1, source_target_pairs={{8,0},{12,4},{0,8},{4,12},{9,1},{13,5},{1,9},{5,13},{10,2},{14,6},... | collective-permute-start | bytes 491528 | tf_op jit(solution)/shard_map/ppermute | solution.py:424
  16.2 2.8 %collective-permute-start.8 = (bf16[5,128,128]{2,1,0:T(8,128)(2,1)}, bf16[5,128,128]{2,1,0:T(8,128)(2,1)}, u32[]{:S(2)}, u32[]{:S(2)}) collective-permute-start(bf16[5,128,128]{2,1,0:T(8,128)(2,1)} %get-tuple-element.48), channel_id=1, source_target_pairs={{4,0},{8,4},{12,8},{0,12},{5,1},{9,5},{13,9},{1,13},{6,2},{10,6},{... | collective-permute-start | bytes 491528 | tf_op jit(solution)/shard_map/ppermute | solution.py:424
  19.0 4.0 %lay.1.weight = bf16[2560,2048]{1,0:T(8,128)(2,1)S(1)} custom-call(bf16[3584,2048]{1,0:T(8,128)(2,1)} %weight.3), custom_call_target="tpu_custom_call" | custom-call | flops 524288000000 | bytes 1048576000000 | tf_op jit(solution)/shard_map/lay/pallas_call | solution.py:492
  23.0 4.0 %partial.3 = (f32[512,1024]{1,0:T(8,128)S(1)}, bf16[512,2048]{1,0:T(8,128)(2,1)S(1)}) custom-call(bf16[2560,2048]{1,0:T(8,128)(2,1)S(1)} %lay.1.weight, bf16[256,2048]{1,0:T(8,128)(2,1)S(1)} %get-tuple-element.44.refs_0_, bf16[128,2048]{1,0:T(8,128)(2,1)} %collective-permute-done.4.refs_1_, bf16[128,2048]{1,0:T(8,128)(2,1)} %collective-permute-done.5.refs_2_), custom_call_target="tpu_custom_call" | custom-call | flops 524288 | bytes 1048576 | tf_op jit(solution)/shard_map/partial/pallas_call | solution.py:141
  27.0 2.1 %collective-permute-done.7.refs_2_ = bf16[5,128,128]{2,1,0:T(8,128)(2,1)} collective-permute-done((bf16[5,128,128]{2,1,0:T(8,128)(2,1)}, bf16[5,128,128]{2,1,0:T(8,128)(2,1)}, u32[]{:S(2)}, u32[]{:S(2)}) %collective-permute-start.7) | collective-permute-done | bytes 163872 | tf_op jit(solution)/shard_map/ppermute | solution.py:424
  29.1 1.7 %delta.1 = (bf16[4,128,1024]{2,1,0:T(8,128)(2,1)S(1)}, bf16[128,1024]{1,0:T(8,128)(2,1)S(1)}, bf16[4,128,128]{2,1,0:T(8,128)(2,1)S(1)}) custom-call(s32[4,12]{1,0:T(4,128)S(1)} %get-tuple-element.43.table, f32[512,1024]{1,0:T(8,128)S(1)} %get-tuple-element.50.early, bf16[512,2048]{1,0:T(8,128)(2,1)S(1)} %get-tuple-element.55.rows, ...), custom_call_target="tpu_custom_call" | custom-call | flops 524288 | bytes 1048576 | tf_op jit(solution)/shard_map/delta/pallas_call | solution.py:202
  30.8 3.1 %collective-permute-start.9 = (bf16[128,1024]{1,0:T(8,128)(2,1)S(1)}, bf16[128,1024]{1,0:T(8,128)(2,1)S(1)}, u32[]{:S(2)}, u32[]{:S(2)}) collective-permute-start(bf16[128,1024]{1,0:T(8,128)(2,1)S(1)} %get-tuple-element.53), channel_id=1, source_target_pairs={{12,0},{0,4},{4,8},{8,12},{13,1},{1,5},{5,9},{9,13},{14,2},{2,6},{... | collective-permute-start | bytes 786440 | tf_op jit(solution)/shard_map/ppermute | solution.py:424
  34.0 5.2 %partial.5 = (bf16[4,128,1536]{2,1,0:T(8,128)(2,1)S(1)}, bf16[128,1536]{1,0:T(8,128)(2,1)S(1)}) custom-call(s32[4,12]{1,0:T(4,128)S(1)} %get-tuple-element.43.table, bf16[2560,2048]{1,0:T(8,128)(2,1)S(1)} %lay.1.weight, bf16[512,2048]{1,0:T(8,128)(2,1)S(1)} %get-tuple-element.55.rows, bf16[4,128,128]{2,1,0:T(8,128)(2,1)S(1)} %get-tuple-element.57.held), custom_call_target="tpu_custom_call" | custom-call | flops 3221225472 | bytes 6442450944 | tf_op jit(solution)/shard_map/partial/pallas_call | solution.py:246
  39.6 2.1 %tile_grad.1 = (bf16[128,128]{1,0:T(8,128)(2,1)S(1)}, bf16[128,128]{1,0:T(8,128)(2,1)S(1)}, bf16[128,128]{1,0:T(8,128)(2,1)S(1)}, bf16[128,128]{1,0:T(8,128)(2,1)S(1)}) custom-call(s32[4,12]{1,0:T(4,128)S(1)} %get-tuple-element.43.table, bf16[512,2048]{1,0:T(8,128)(2,1)S(1)} %get-tuple-element.55.rows, bf16[5,128,128]{2,1,0:T(8,128)(2,1)S(1)} %get-tuple-element.45.refs_0_, ...), custom_call_target="tpu_custom_call" | custom-call | flops 1048576 | bytes 2097152 | tf_op jit(solution)/shard_map/tile_grad/pallas_call | solution.py:366
  41.7 4.6 %partial.4 = (bf16[4,128,1024]{2,1,0:T(8,128)(2,1)S(1)}, bf16[128,1024]{1,0:T(8,128)(2,1)S(1)}) custom-call(s32[4,12]{1,0:T(4,128)S(1)} %get-tuple-element.43.table, bf16[3584,2048]{1,0:T(8,128)(2,1)} %weight.3, bf16[512,2048]{1,0:T(8,128)(2,1)S(1)} %get-tuple-element.55.rows, bf16[4,128,128]{2,1,0:T(8,128)(2,1)S(1)} %get-tuple-element.57.held), custom_call_target="tpu_custom_call" | custom-call | flops 2147483648 | bytes 4294967296 | tf_op jit(solution)/shard_map/partial/pallas_call | solution.py:246
  46.3 1.5 %collective-permute-start.12 = (bf16[128,1408]{1,0:T(8,128)(2,1)S(1)}, bf16[128,1408]{1,0:T(8,128)(2,1)S(1)}, u32[]{:S(2)}, u32[]{:S(2)}) collective-permute-start(bf16[128,1408]{1,0:T(8,128)(2,1)S(1)} %attach.1), channel_id=1, source_target_pairs={{12,0},{0,4},{4,8},{8,12},{13,1},{1,5},{5,9},{9,13},{14,2},{2,6},{... | collective-permute-start | bytes 1081352 | tf_op jit(solution)/shard_map/ppermute | solution.py:424
  47.8 4.7 %collective-permute-done.15.arrived = bf16[128,1536]{1,0:T(8,128)(2,1)S(1)} collective-permute-done((bf16[128,1536]{1,0:T(8,128)(2,1)S(1)}, bf16[128,1536]{1,0:T(8,128)(2,1)S(1)}, u32[]{:S(2)}, u32[]{:S(2)}) %collective-permute-start.15) | collective-permute-done | bytes 393248 | tf_op jit(solution)/shard_map/ppermute | solution.py:424
  52.7 7.5 %collective-permute-done.12.arrived = bf16[128,1408]{1,0:T(8,128)(2,1)S(1)} collective-permute-done((bf16[128,1408]{1,0:T(8,128)(2,1)S(1)}, bf16[128,1408]{1,0:T(8,128)(2,1)S(1)}, u32[]{:S(2)}, u32[]{:S(2)}) %collective-permute-start.12) | collective-permute-done | bytes 360480 | tf_op jit(solution)/shard_map/ppermute | solution.py:424
  60.5 8.2 %collective-permute-done.16.arrived = bf16[128,1536]{1,0:T(8,128)(2,1)S(1)} collective-permute-done((bf16[128,1536]{1,0:T(8,128)(2,1)S(1)}, bf16[128,1536]{1,0:T(8,128)(2,1)S(1)}, u32[]{:S(2)}, u32[]{:S(2)}) %collective-permute-start.16) | collective-permute-done | bytes 393248 | tf_op jit(solution)/shard_map/ppermute | solution.py:424
  68.9 6.8 %collective-permute-done.13.arrived = bf16[128,1280]{1,0:T(8,128)(2,1)S(1)} collective-permute-done((bf16[128,1280]{1,0:T(8,128)(2,1)S(1)}, bf16[128,1280]{1,0:T(8,128)(2,1)S(1)}, u32[]{:S(2)}, u32[]{:S(2)}) %collective-permute-start.13) | collective-permute-done | bytes 327712 | tf_op jit(solution)/shard_map/ppermute | solution.py:424
  75.9 5.5 %collective-permute-done.10.arrived = bf16[128,1024]{1,0:T(8,128)(2,1)S(1)} collective-permute-done((bf16[128,1024]{1,0:T(8,128)(2,1)S(1)}, bf16[128,1024]{1,0:T(8,128)(2,1)S(1)}, u32[]{:S(2)}, u32[]{:S(2)}) %collective-permute-start.10) | collective-permute-done | bytes 262176 | tf_op jit(solution)/shard_map/ppermute | solution.py:424
  81.5 8.3 %collective-permute-done.17.arrived = bf16[128,1536]{1,0:T(8,128)(2,1)S(1)} collective-permute-done((bf16[128,1536]{1,0:T(8,128)(2,1)S(1)}, bf16[128,1536]{1,0:T(8,128)(2,1)S(1)}, u32[]{:S(2)}, u32[]{:S(2)}) %collective-permute-start.17) | collective-permute-done | bytes 393248 | tf_op jit(solution)/shard_map/ppermute | solution.py:424
  90.7 5.4 %collective-permute-done.14.arrived.refs_3_ = bf16[128,1152]{1,0:T(8,128)(2,1)S(1)} collective-permute-done((bf16[128,1152]{1,0:T(8,128)(2,1)S(1)}, bf16[128,1152]{1,0:T(8,128)(2,1)S(1)}, u32[]{:S(2)}, u32[]{:S(2)}) %collective-permute-start.14) | collective-permute-done | bytes 294944 | tf_op jit(solution)/shard_map/ppermute | solution.py:424
  96.9 1.7 %adam.1 = (f32[4,128,128]{2,1,0:T(8,128)}, f32[4,128,128]{2,1,0:T(8,128)}, f32[4,128,128]{2,1,0:T(8,128)}) custom-call(s32[4,12]{1,0:T(4,128)S(1)} %get-tuple-element.43.table, bf16[128,128]{1,0:T(8,128)(2,1)S(1)} %get-tuple-element.67.refs_0_, bf16[128,128]{1,0:T(8,128)(2,1)S(1)} %get-tuple-element.68.refs_1_, ...), custom_call_target="tpu_custom_call" | custom-call | flops 65536 | bytes 131072 | tf_op jit(solution)/shard_map/adam/pallas_call | solution.py:410
  (38 shorter events, 8.0 us)
Async XLA Ops:
  0.6 8.4 %collective-permute-start.3 = (bf16[128,2048]{1,0:T(8,128)(2,1)}, bf16[128,2048]{1,0:T(8,128)(2,1)S(1)}, u32[]{:S(2)}, u32[]{:S(2)}) collective-permute-start(bf16[128,2048]{1,0:T(8,128)(2,1)} %own.1), channel_id=1, source_target_pairs={{1,0},{0,1},{3,2},{2,3},{5,4},{4,5},{7,6},{6,7},{9,8},{8,9},{11,10... | collective-permute-start | bytes 1572872 | tf_op jit(solution)/shard_map/ppermute | solution.py:435
  1.1 17.9 %collective-permute-start.4 = (bf16[128,2048]{1,0:T(8,128)(2,1)}, bf16[128,2048]{1,0:T(8,128)(2,1)}, u32[]{:S(2)}, u32[]{:S(2)}) collective-permute-start(bf16[128,2048]{1,0:T(8,128)(2,1)} %own.1), channel_id=1, source_target_pairs={{2,0},{0,2},{3,1},{1,3},{6,4},{4,6},{7,5},{5,7},{10,8},{8,10},{11,... | collective-permute-start | bytes 1572872 | tf_op jit(solution)/shard_map/ppermute | solution.py:424
  4.5 6.1 %collective-permute-start.2 = (s32[1,8]{1,0:T(1,128)S(1)}, s32[1,8]{1,0:T(1,128)S(1)}, u32[]{:S(2)}, u32[]{:S(2)}) collective-permute-start(s32[1,8]{1,0:T(1,128)S(1)} %pad_add_fusion.refs_0_), channel_id=1, source_target_pairs={{4,0},{8,4},{12,8},{0,12},{5,1},{9,5},{13,9},{1,13},{6,2},{10,6},{... | collective-permute-start | bytes 104 | tf_op jit(solution)/shard_map/ppermute | solution.py:424
  8.1 4.4 %collective-permute-start.1 = (s32[1,8]{1,0:T(1,128)S(1)}, s32[1,8]{1,0:T(1,128)S(1)}, u32[]{:S(2)}, u32[]{:S(2)}) collective-permute-start(s32[1,8]{1,0:T(1,128)S(1)} %pad_add_fusion.refs_0_), channel_id=1, source_target_pairs={{8,0},{12,4},{0,8},{4,12},{9,1},{13,5},{1,9},{5,13},{10,2},{14,6},... | collective-permute-start | bytes 104 | tf_op jit(solution)/shard_map/ppermute | solution.py:424
  8.1 5.3 %collective-permute-start = (s32[1,8]{1,0:T(1,128)S(1)}, s32[1,8]{1,0:T(1,128)S(1)}, u32[]{:S(2)}, u32[]{:S(2)}) collective-permute-start(s32[1,8]{1,0:T(1,128)S(1)} %pad_add_fusion.refs_0_), channel_id=1, source_target_pairs={{12,0},{0,4},{4,8},{8,12},{13,1},{1,5},{5,9},{9,13},{14,2},{2,6},{... | collective-permute-start | bytes 104 | tf_op jit(solution)/shard_map/ppermute | solution.py:424
  14.9 12.1 %collective-permute-start.6 = (bf16[5,128,128]{2,1,0:T(8,128)(2,1)}, bf16[5,128,128]{2,1,0:T(8,128)(2,1)}, u32[]{:S(2)}, u32[]{:S(2)}) collective-permute-start(bf16[5,128,128]{2,1,0:T(8,128)(2,1)} %get-tuple-element.46), channel_id=1, source_target_pairs={{12,0},{0,4},{4,8},{8,12},{13,1},{1,5},{5,9},{9,13},{14,2},{2,6},{... | collective-permute-start | bytes 491528 | tf_op jit(solution)/shard_map/ppermute | solution.py:424
  15.0 14.1 %collective-permute-start.7 = (bf16[5,128,128]{2,1,0:T(8,128)(2,1)}, bf16[5,128,128]{2,1,0:T(8,128)(2,1)}, u32[]{:S(2)}, u32[]{:S(2)}) collective-permute-start(bf16[5,128,128]{2,1,0:T(8,128)(2,1)} %get-tuple-element.47), channel_id=1, source_target_pairs={{8,0},{12,4},{0,8},{4,12},{9,1},{13,5},{1,9},{5,13},{10,2},{14,6},... | collective-permute-start | bytes 491528 | tf_op jit(solution)/shard_map/ppermute | solution.py:424
  16.2 12.9 %collective-permute-start.8 = (bf16[5,128,128]{2,1,0:T(8,128)(2,1)}, bf16[5,128,128]{2,1,0:T(8,128)(2,1)}, u32[]{:S(2)}, u32[]{:S(2)}) collective-permute-start(bf16[5,128,128]{2,1,0:T(8,128)(2,1)} %get-tuple-element.48), channel_id=1, source_target_pairs={{4,0},{8,4},{12,8},{0,12},{5,1},{9,5},{13,9},{1,13},{6,2},{10,6},{... | collective-permute-start | bytes 491528 | tf_op jit(solution)/shard_map/ppermute | solution.py:424
  19.0 4.0 %collective-permute-start.5 = (bf16[128,2048]{1,0:T(8,128)(2,1)}, bf16[128,2048]{1,0:T(8,128)(2,1)}, u32[]{:S(2)}, u32[]{:S(2)}) collective-permute-start(bf16[128,2048]{1,0:T(8,128)(2,1)} %collective-permute-done.4.refs_1_), channel_id=1, source_target_pairs={{1,0},{0,1},{3,2},{2,3},{5,4},{4,5},{7,6},{6,7},{9,8},{8,9},{11,10... | collective-permute-start | bytes 1572872 | tf_op jit(solution)/shard_map/ppermute | solution.py:424
  30.8 8.7 %collective-permute-start.9 = (bf16[128,1024]{1,0:T(8,128)(2,1)S(1)}, bf16[128,1024]{1,0:T(8,128)(2,1)S(1)}, u32[]{:S(2)}, u32[]{:S(2)}) collective-permute-start(bf16[128,1024]{1,0:T(8,128)(2,1)S(1)} %get-tuple-element.53), channel_id=1, source_target_pairs={{12,0},{0,4},{4,8},{8,12},{13,1},{1,5},{5,9},{9,13},{14,2},{2,6},{... | collective-permute-start | bytes 786440 | tf_op jit(solution)/shard_map/ppermute | solution.py:424
  39.2 13.4 %collective-permute-start.15 = (bf16[128,1536]{1,0:T(8,128)(2,1)S(1)}, bf16[128,1536]{1,0:T(8,128)(2,1)S(1)}, u32[]{:S(2)}, u32[]{:S(2)}) collective-permute-start(bf16[128,1536]{1,0:T(8,128)(2,1)S(1)} %get-tuple-element.66), channel_id=1, source_target_pairs={{12,0},{0,4},{4,8},{8,12},{13,1},{1,5},{5,9},{9,13},{14,2},{2,6},{... | collective-permute-start | bytes 1179656 | tf_op jit(solution)/shard_map/ppermute | solution.py:424
  46.3 14.0 %collective-permute-start.12 = (bf16[128,1408]{1,0:T(8,128)(2,1)S(1)}, bf16[128,1408]{1,0:T(8,128)(2,1)S(1)}, u32[]{:S(2)}, u32[]{:S(2)}) collective-permute-start(bf16[128,1408]{1,0:T(8,128)(2,1)S(1)} %attach.1), channel_id=1, source_target_pairs={{12,0},{0,4},{4,8},{8,12},{13,1},{1,5},{5,9},{9,13},{14,2},{2,6},{... | collective-permute-start | bytes 1081352 | tf_op jit(solution)/shard_map/ppermute | solution.py:424
  52.7 16.0 %collective-permute-start.16 = (bf16[128,1536]{1,0:T(8,128)(2,1)S(1)}, bf16[128,1536]{1,0:T(8,128)(2,1)S(1)}, u32[]{:S(2)}, u32[]{:S(2)}) collective-permute-start(bf16[128,1536]{1,0:T(8,128)(2,1)S(1)} %add.12), channel_id=1, source_target_pairs={{12,0},{0,4},{4,8},{8,12},{13,1},{1,5},{5,9},{9,13},{14,2},{2,6},{... | collective-permute-start | bytes 1179656 | tf_op jit(solution)/shard_map/ppermute | solution.py:424
  60.4 15.4 %collective-permute-start.13 = (bf16[128,1280]{1,0:T(8,128)(2,1)S(1)}, bf16[128,1280]{1,0:T(8,128)(2,1)S(1)}, u32[]{:S(2)}, u32[]{:S(2)}) collective-permute-start(bf16[128,1280]{1,0:T(8,128)(2,1)S(1)} %get-tuple-element.63), channel_id=1, source_target_pairs={{12,0},{0,4},{4,8},{8,12},{13,1},{1,5},{5,9},{9,13},{14,2},{2,6},{... | collective-permute-start | bytes 983048 | tf_op jit(solution)/shard_map/ppermute | solution.py:424
  60.4 20.9 %collective-permute-start.10 = (bf16[128,1024]{1,0:T(8,128)(2,1)S(1)}, bf16[128,1024]{1,0:T(8,128)(2,1)S(1)}, u32[]{:S(2)}, u32[]{:S(2)}) collective-permute-start(bf16[128,1024]{1,0:T(8,128)(2,1)S(1)} %add.8), channel_id=1, source_target_pairs={{12,0},{0,4},{4,8},{8,12},{13,1},{1,5},{5,9},{9,13},{14,2},{2,6},{... | collective-permute-start | bytes 786440 | tf_op jit(solution)/shard_map/ppermute | solution.py:424
  68.8 21.0 %collective-permute-start.17 = (bf16[128,1536]{1,0:T(8,128)(2,1)S(1)}, bf16[128,1536]{1,0:T(8,128)(2,1)S(1)}, u32[]{:S(2)}, u32[]{:S(2)}) collective-permute-start(bf16[128,1536]{1,0:T(8,128)(2,1)S(1)} %add.13), channel_id=1, source_target_pairs={{12,0},{0,4},{4,8},{8,12},{13,1},{1,5},{5,9},{9,13},{14,2},{2,6},{... | collective-permute-start | bytes 1179656 | tf_op jit(solution)/shard_map/ppermute | solution.py:424
  75.8 20.3 %collective-permute-start.14 = (bf16[128,1152]{1,0:T(8,128)(2,1)S(1)}, bf16[128,1152]{1,0:T(8,128)(2,1)S(1)}, u32[]{:S(2)}, u32[]{:S(2)}) collective-permute-start(bf16[128,1152]{1,0:T(8,128)(2,1)S(1)} %get-tuple-element.64), channel_id=1, source_target_pairs={{12,0},{0,4},{4,8},{8,12},{13,1},{1,5},{5,9},{9,13},{14,2},{2,6},{... | collective-permute-start | bytes 884744 | tf_op jit(solution)/shard_map/ppermute | solution.py:424
  81.4 18.2 %collective-permute-start.11 = (bf16[128,1024]{1,0:T(8,128)(2,1)S(1)}, bf16[128,1024]{1,0:T(8,128)(2,1)S(1)}, u32[]{:S(2)}, u32[]{:S(2)}) collective-permute-start(bf16[128,1024]{1,0:T(8,128)(2,1)S(1)} %add.9), channel_id=1, source_target_pairs={{12,0},{0,4},{4,8},{8,12},{13,1},{1,5},{5,9},{9,13},{14,2},{2,6},{... | collective-permute-start | bytes 786440 | tf_op jit(solution)/shard_map/ppermute | solution.py:424
  90.7 6.2 %copy-start = (f32[1,1,4,128,128]{4,3,2,1,0:T(8,128)S(1)}, f32[1,1,4,128,128]{4,3,2,1,0:T(8,128)}, u32[]{:S(2)}) copy-start(f32[1,1,4,128,128]{4,3,2,1,0:T(8,128)} %param.13) | copy-start | bytes 786436
  90.7 6.2 %copy-start.1 = (f32[1,1,4,128,128]{4,3,2,1,0:T(8,128)S(1)}, f32[1,1,4,128,128]{4,3,2,1,0:T(8,128)}, u32[]{:S(2)}) copy-start(f32[1,1,4,128,128]{4,3,2,1,0:T(8,128)} %param.14) | copy-start | bytes 786436
  90.7 6.2 %copy-start.2 = (f32[1,1,4,128,128]{4,3,2,1,0:T(8,128)S(1)}, f32[1,1,4,128,128]{4,3,2,1,0:T(8,128)}, u32[]{:S(2)}) copy-start(f32[1,1,4,128,128]{4,3,2,1,0:T(8,128)} %param.15) | copy-start | bytes 786436

commit v13 on v12

--- a/solution.py
+++ b/solution.py
@@ -12,10 +12,10 @@
 BETA_TWO = 0.999
 RATE = 0.01
 EPSILON = 1e-08
-VMEM_LIMIT = 24 * 1024 * 1024
+VMEM_LIMIT = 12 * 1024 * 1024
 MATMUL = 4096
 EARLY = 1
-AHEAD = 100000
+AHEAD = 5000
 PARTS = (2, 3, 2)
 RIDE = 2
 LAST = 0
@@ -180,8 +180,8 @@
             first[:, here] = result
 
 
-def delta_kernel(spans, slots, block, table, early, rows, *refs):
-    stored, (out, first, held, total) = refs[:spans], refs[spans:]
+def held_kernel(spans, slots, block, table, *refs):
+    stored, held = refs[:-1], refs[-1]
     me = lax.axis_index("seq")
     before = rank_before(table, 0, spans, slots)
     for j in range(slots):
@@ -191,38 +191,44 @@
             def _():
                 held[j] = stored[s][slots]
 
-    total[...] = early[...]
-    add_delta(table, rows, held, total, 0)
+
+def delta_kernel(sizes, low, stores, table, early, rows, *refs):
+    given, (out, first, *more, total) = refs[:stores], refs[stores:]
+    if stores > 1:
+        (held,) = more
+        held_kernel(*sizes, table, *given, held)
+    else:
+        (held,) = given
+    total[...] = early[:, low : low + total.shape[1]]
+    add_delta(table, rows, held, total, low)
     put_chunks(total, out, first, pl.ds(0, total.shape[1]))
 
 
-def delta_call(sizes, table, early, rows, stored):
+def delta_call(sizes, low, high, table, early, rows, given):
     spans, slots, block = sizes
-    tokens, columns = early.shape
-    return pl.pallas_call(
-        functools.partial(delta_kernel, *sizes),
-        out_shape=[
-            jax.ShapeDtypeStruct((spans, tokens // spans, columns), rows.dtype),
-            jax.ShapeDtypeStruct((tokens // spans, columns), rows.dtype),
-            jax.ShapeDtypeStruct((slots, block, block), rows.dtype),
-        ],
-        in_specs=[smem()] + [vmem()] * (2 + spans),
-        out_specs=[vmem()] * 3,
+    tokens, columns = early.shape[0], high - low
+    shapes = [
+        jax.ShapeDtypeStruct((spans, tokens // spans, columns), rows.dtype),
+        jax.ShapeDtypeStruct((tokens // spans, columns), rows.dtype),
+    ]
+    if len(given) > 1:
+        shapes.append(jax.ShapeDtypeStruct((slots, block, block), rows.dtype))
+    return pl.pallas_call(
+        functools.partial(delta_kernel, sizes, low, len(given)),
+        out_shape=shapes,
+        in_specs=[smem()] + [vmem()] * (2 + len(given)),
+        out_specs=[vmem()] * len(shapes),
         scratch_shapes=[pltpu.VMEM((tokens, columns), jnp.float32)],
         compiler_params=params(),
         cost_estimate=cost(early.size),
         name="delta",
-    )(table, early, rows, *stored)
+    )(table, early, rows, *given)
 
 
 def matmul_kernel(low, ends, table, weight, rows, held, *refs):
     outs, total = refs[:-1], refs[-1]
     step, width = pl.program_id(0), total.shape[1]
-    if weight.shape[0] == width:
-        weights = weight[...]
-    else:
-        weights = weight[pl.ds(pl.multiple_of((low + step) * width, width), width)]
-    total[...] = lax.dot_general(rows[...], weights, NT, preferred_element_type=jnp.float32)
+    total[...] = lax.dot_general(rows[...], weight[...], NT, preferred_element_type=jnp.float32)
     add_delta(table, rows, held, total, (low + step) * width)
     for part, (begin, end) in enumerate(zip((0, *ends), ends)):
 
@@ -232,12 +238,9 @@
             put_chunks(total, *outs[2 * part : 2 * part + 2], here)
 
 
-def matmul_call(spans, low, ends, width, table, weight, in_vmem, rows, held):
+def matmul_call(spans, low, ends, width, table, weight, rows, held):
     tokens, d_width = rows.shape
-    if in_vmem:
-        weight_spec = vmem()
-    else:
-        weight, weight_spec = stay(weight), pl.BlockSpec((width, d_width), lambda i: (i + low, 0))
+    weight_spec = pl.BlockSpec((width, d_width), lambda i: (i + low, 0))
     shapes = []
     for begin, end in zip((0, *ends), ends):
         columns = (end - begin) * width
@@ -253,7 +256,7 @@
         compiler_params=params(),
         cost_estimate=cost(MATMUL * tokens * ends[-1] * width),
         name="partial",
-    )(table, weight, rows, held)
+    )(table, stay(weight), rows, held)
 
 
 def attach_kernel(first, *refs):
@@ -504,27 +507,21 @@
     remote = []
     for first in firsts:
         remote += [first] + [take_from(first, "dp", d) for d in range(1, cores)]
-    early, rows = early_matmul_call(
-        width, ranges[0][1] * width, first_weight, [local_rows, *remote]
-    )
-    partial, first, held = delta_call(sizes, table, early, rows, crossed)
-    partials, moving = [partial], [take_from(first, "seq", -1)]
-    for part in range(1, len(ranges)):
-        low, high = ranges[part]
-        if part == RIDE:
+    early, rows = early_matmul_call(width, laid * width, first_weight, [local_rows, *remote])
+    partials, moving, held = [], [], None
+    for part, (low, high) in enumerate(ranges):
+        if part < LAID:
+            given = [held] if part else crossed
+            partial, first, *more = delta_call(
+                sizes, low * width, high * width, table, early, rows, given
+            )
+            held = more[0] if more else held
+        else:
             moving[0] = add_call(2, partials[0], moving[0], block)[0]
             rows, moving[0] = lax.optimization_barrier((rows, moving[0]))
-        partial, first = matmul_call(
-            spans,
-            low,
-            (high - low,),
-            width,
-            table,
-            first_weight if part < LAID else down_weight,
-            part < LAID,
-            rows,
-            held,
-        )
+            partial, first = matmul_call(
+                spans, low, (high - low,), width, table, down_weight, rows, held
+            )
         if part == RIDE:
             grads = grad_call(sizes, table, rows, crossed)
             first = attach_call(first, grads[1:])

time: 101 us -> 101 us (level)
  waiting for transfers between devices: 52.8 us -> 57.2 us
  Pallas kernels: 29.1 us -> 25.5 us
    pallas_call x2 -> x1, Pallas kernels: 9.84 us -> 4.44 us  [matmul_call(): pl.pallas_call(functools.partial(matmul_kernel, low, ends), grid=(ends[-1...]
    ppermute x17, waiting for transfers between devices: 52.8 us -> 57.2 us  [take_from(): lax.ppermute(array, axis, [((i + places) % size, i) for i in range(size)])]
    pallas_call x1, Pallas kernels: 3.97 us -> 6.62 us  [early_matmul_call(): pl.pallas_call(functools.partial(early_matmul_kernel, width), grid=(colum...]
    pallas_call x1, Pallas kernels: 2.08 us -> 0.87 us  [grad_call(): pl.pallas_call(functools.partial(grad_kernel, *sizes), out_shape=[jax.Sha...]
    pallas_call x1 -> x2, Pallas kernels: 1.68 us -> 2.18 us  [delta_call(): pl.pallas_call(functools.partial(delta_kernel, sizes, low, len(given)), o...]
  transfers between devices with their start and end apart: 18 -> 18, of which waited for: 12 -> 11; matrix products, arithmetic and copies ran while one was open for 1% -> 1% of each run, Pallas kernels for 27% -> 24%
where the time goes in v13:
time: 101 us
  waiting for transfers between devices  57.2 us (57%)
  Pallas kernels  25.5 us (25%)
  starting transfers between devices  16.6 us (16%)
    ppermute x17, waiting for transfers between devices, take_from(): lax.ppermute(array, axis, [((i + places) % size, i) for i in range(size)])  57.2 us
    ppermute x17, starting transfers between devices, take_from(): lax.ppermute(array, axis, [((i + places) % size, i) for i in range(size)])  16.1 us
    pallas_call x1, Pallas kernels, early_matmul_call(): pl.pallas_call(functools.partial(early_matmul_kernel, width), grid=(colum...  6.62 us
    pallas_call x1, Pallas kernels, matmul_call(): pl.pallas_call(functools.partial(matmul_kernel, low, ends), grid=(ends[-1...  4.44 us
    pallas_call x1, Pallas kernels, per_device(): pl.pallas_call(lay_kernel, out_shape=jax.ShapeDtypeStruct((laid * width,...  3.99 us
    pallas_call x3, Pallas kernels, last_call(): pl.pallas_call(functools.partial(last_kernel, low), out_shape=shape, in_s...  2.41 us
    pallas_call x2, Pallas kernels, delta_call(): pl.pallas_call(functools.partial(delta_kernel, sizes, low, len(given)), o...  2.18 us
  transfers between devices with their start and end apart: 18, of which 11 were waited for; matrix products, arithmetic and copies ran while one was open for 1% of the time, Pallas kernels for 24%

profile of v13, /device:TPU:0, one launch (start us, length us, event | category | flops | bytes accessed | tf_op | source)
XLA Modules:
  0.0 101.0 jit_solution(9815082646389434141)
XLA Ops:
  1.1 2.6 %collective-permute-start.4 = (bf16[128,2048]{1,0:T(8,128)(2,1)}, bf16[128,2048]{1,0:T(8,128)(2,1)S(1)}, u32[]{:S(2)}, u32[]{:S(2)}) collective-permute-start(bf16[128,2048]{1,0:T(8,128)(2,1)} %own.1), channel_id=1, source_target_pairs={{2,0},{0,2},{3,1},{1,3},{6,4},{4,6},{7,5},{5,7},{10,8},{8,10},{11,... | collective-permute-start | bytes 1572872 | tf_op jit(solution)/shard_map/ppermute | solution.py:427
  4.5 3.6 %collective-permute-start.2 = (s32[1,8]{1,0:T(1,128)S(1)}, s32[1,8]{1,0:T(1,128)S(1)}, u32[]{:S(2)}, u32[]{:S(2)}) collective-permute-start(s32[1,8]{1,0:T(1,128)S(1)} %pad_add_fusion.refs_0_), channel_id=1, source_target_pairs={{4,0},{8,4},{12,8},{0,12},{5,1},{9,5},{13,9},{1,13},{6,2},{10,6},{... | collective-permute-start | bytes 104 | tf_op jit(solution)/shard_map/ppermute | solution.py:427
  8.1 1.0 %collective-permute-start = (s32[1,8]{1,0:T(1,128)S(1)}, s32[1,8]{1,0:T(1,128)S(1)}, u32[]{:S(2)}, u32[]{:S(2)}) collective-permute-start(s32[1,8]{1,0:T(1,128)S(1)} %pad_add_fusion.refs_0_), channel_id=1, source_target_pairs={{12,0},{0,4},{4,8},{8,12},{13,1},{1,5},{5,9},{9,13},{14,2},{2,6},{... | collective-permute-start | bytes 104 | tf_op jit(solution)/shard_map/ppermute | solution.py:427
  9.1 1.4 %early.1 = (bf16[4,128,128]{2,1,0:T(8,128)(2,1)S(1)}, bf16[128,3584]{1,0:T(8,128)(2,1)S(1)}, bf16[256,2048]{1,0:T(8,128)(2,1)S(1)}) custom-call(f32[4,128,128]{2,1,0:T(8,128)} %bitcast.8, bf16[128,3584]{1,0:T(8,128)(2,1)} %hidden.1, bf16[128,2048]{1,0:T(8,128)(2,1)} %own.1, bf16[128,2048]{1,0:T(8,128)(2,1)S(1)} %collective-permute-done.3.refs_0_), custom_call_target="tpu_custom_call" | custom-call | flops 458752 | bytes 917504 | tf_op jit(solution)/shard_map/early/pallas_call | solution.py:465
  10.5 2.0 %collective-permute-done.1.refs_2_ = s32[1,8]{1,0:T(1,128)S(1)} collective-permute-done((s32[1,8]{1,0:T(1,128)S(1)}, s32[1,8]{1,0:T(1,128)S(1)}, u32[]{:S(2)}, u32[]{:S(2)}) %collective-permute-start.1) | collective-permute-done | bytes 64 | tf_op jit(solution)/shard_map/ppermute | solution.py:427
  13.4 1.4 %pick.1 = (s32[4,12]{1,0:T(4,128)S(1)}, bf16[5,128,128]{2,1,0:T(8,128)(2,1)S(1)}, bf16[5,128,128]{2,1,0:T(8,128)(2,1)S(1)}, bf16[5,128,128]{2,1,0:T(8,128)(2,1)S(1)}, bf16[5,128,128]{2,1,0:T(8,128)(2,1)S(1)}) custom-call(s32[1,8]{1,0:T(1,128)S(1)} %pad_add_fusion.refs_0_, s32[1,8]{1,0:T(1,128)S(1)} %collective-permute-done.refs_1_, ...), custom_call_target="tpu_custom_call" | custom-call | flops 458752 | bytes 917504 | tf_op jit(solution)/shard_map/pick/pallas_call | solution.py:482
  14.9 1.2 %collective-permute-start.7 = (bf16[5,128,128]{2,1,0:T(8,128)(2,1)S(1)}, bf16[5,128,128]{2,1,0:T(8,128)(2,1)S(1)}, u32[]{:S(2)}, u32[]{:S(2)}) collective-permute-start(bf16[5,128,128]{2,1,0:T(8,128)(2,1)S(1)} %get-tuple-element.47), channel_id=1, source_target_pairs={{8,0},{12,4},{0,8},{4,12},{9,1},{13,5},{1,9},{5,13},{10,2},{14,6},... | collective-permute-start | bytes 491528 | tf_op jit(solution)/shard_map/ppermute | solution.py:427
  16.1 2.8 %collective-permute-start.8 = (bf16[5,128,128]{2,1,0:T(8,128)(2,1)S(1)}, bf16[5,128,128]{2,1,0:T(8,128)(2,1)S(1)}, u32[]{:S(2)}, u32[]{:S(2)}) collective-permute-start(bf16[5,128,128]{2,1,0:T(8,128)(2,1)S(1)} %get-tuple-element.48), channel_id=1, source_target_pairs={{4,0},{8,4},{12,8},{0,12},{5,1},{9,5},{13,9},{1,13},{6,2},{10,6},{... | collective-permute-start | bytes 491528 | tf_op jit(solution)/shard_map/ppermute | solution.py:427
  18.9 4.0 %lay.1.weight = bf16[2560,2048]{1,0:T(8,128)(2,1)S(1)} custom-call(bf16[3584,2048]{1,0:T(8,128)(2,1)} %weight.3), custom_call_target="tpu_custom_call" | custom-call | flops 26214400000 | bytes 52428800000 | tf_op jit(solution)/shard_map/lay/pallas_call | solution.py:495
  22.9 6.6 %partial.2 = (f32[512,2560]{1,0:T(8,128)S(1)}, bf16[512,2048]{1,0:T(8,128)(2,1)S(1)}) custom-call(bf16[2560,2048]{1,0:T(8,128)(2,1)S(1)} %lay.1.weight, bf16[256,2048]{1,0:T(8,128)(2,1)S(1)} %get-tuple-element.44.refs_0_, bf16[128,2048]{1,0:T(8,128)(2,1)S(1)} %collective-permute-done.4.refs_1_, bf16[128,2048]{1,0:T(8,128)(2,1)S(1)} %collective-permute-done.5.refs_2_), custom_call_target="tpu_custom_call" | custom-call | flops 1310720 | bytes 2621440 | tf_op jit(solution)/shard_map/partial/pallas_call | solution.py:141
  30.6 2.6 %collective-permute-start.9 = (bf16[128,1024]{1,0:T(8,128)(2,1)S(1)}, bf16[128,1024]{1,0:T(8,128)(2,1)S(1)}, u32[]{:S(2)}, u32[]{:S(2)}) collective-permute-start(bf16[128,1024]{1,0:T(8,128)(2,1)S(1)} %get-tuple-element.53), channel_id=1, source_target_pairs={{12,0},{0,4},{4,8},{8,12},{13,1},{1,5},{5,9},{9,13},{14,2},{2,6},{... | collective-permute-start | bytes 786440 | tf_op jit(solution)/shard_map/ppermute | solution.py:427
  33.2 1.2 %delta.3 = (bf16[4,128,1536]{2,1,0:T(8,128)(2,1)S(1)}, bf16[128,1536]{1,0:T(8,128)(2,1)S(1)}) custom-call(s32[4,12]{1,0:T(4,128)S(1)} %get-tuple-element.43.table, f32[512,2560]{1,0:T(8,128)S(1)} %get-tuple-element.50.early, bf16[512,2048]{1,0:T(8,128)(2,1)S(1)} %get-tuple-element.55.rows, bf16[4,128,128]{2,1,0:T(8,128)(2,1)S(1)} %get-tuple-element.57.held.refs_0_), custom_call_target="tpu_custom_call" | custom-call | flops 1310720 | bytes 2621440 | tf_op jit(solution)/shard_map/delta/pallas_call | solution.py:216
  34.7 6.9 %collective-permute-done.9.arrived = bf16[128,1024]{1,0:T(8,128)(2,1)S(1)} collective-permute-done((bf16[128,1024]{1,0:T(8,128)(2,1)S(1)}, bf16[128,1024]{1,0:T(8,128)(2,1)S(1)}, u32[]{:S(2)}, u32[]{:S(2)}) %collective-permute-start.9) | collective-permute-done | bytes 262176 | tf_op jit(solution)/shard_map/ppermute | solution.py:427
  42.6 4.4 %partial.3 = (bf16[4,128,1024]{2,1,0:T(8,128)(2,1)S(1)}, bf16[128,1024]{1,0:T(8,128)(2,1)S(1)}) custom-call(s32[4,12]{1,0:T(4,128)S(1)} %get-tuple-element.43.table, bf16[3584,2048]{1,0:T(8,128)(2,1)} %weight.3, bf16[512,2048]{1,0:T(8,128)(2,1)S(1)} %get-tuple-element.55.rows, bf16[4,128,128]{2,1,0:T(8,128)(2,1)S(1)} %get-tuple-element.57.held.refs_0_), custom_call_target="tpu_custom_call" | custom-call | flops 2147483648 | bytes 4294967296 | tf_op jit(solution)/shard_map/partial/pallas_call | solution.py:249
  47.0 1.6 %collective-permute-start.12 = (bf16[128,1408]{1,0:T(8,128)(2,1)S(1)}, bf16[128,1408]{1,0:T(8,128)(2,1)S(1)}, u32[]{:S(2)}, u32[]{:S(2)}) collective-permute-start(bf16[128,1408]{1,0:T(8,128)(2,1)S(1)} %attach.1), channel_id=1, source_target_pairs={{12,0},{0,4},{4,8},{8,12},{13,1},{1,5},{5,9},{9,13},{14,2},{2,6},{... | collective-permute-start | bytes 1081352 | tf_op jit(solution)/shard_map/ppermute | solution.py:427
  48.6 1.1 %collective-permute-done.15.arrived = bf16[128,1536]{1,0:T(8,128)(2,1)S(1)} collective-permute-done((bf16[128,1536]{1,0:T(8,128)(2,1)S(1)}, bf16[128,1536]{1,0:T(8,128)(2,1)S(1)}, u32[]{:S(2)}, u32[]{:S(2)}) %collective-permute-start.15) | collective-permute-done | bytes 393248 | tf_op jit(solution)/shard_map/ppermute | solution.py:427
  49.9 10.3 %collective-permute-done.12.arrived = bf16[128,1408]{1,0:T(8,128)(2,1)S(1)} collective-permute-done((bf16[128,1408]{1,0:T(8,128)(2,1)S(1)}, bf16[128,1408]{1,0:T(8,128)(2,1)S(1)}, u32[]{:S(2)}, u32[]{:S(2)}) %collective-permute-start.12) | collective-permute-done | bytes 360480 | tf_op jit(solution)/shard_map/ppermute | solution.py:427
  60.5 8.2 %collective-permute-done.16.arrived = bf16[128,1536]{1,0:T(8,128)(2,1)S(1)} collective-permute-done((bf16[128,1536]{1,0:T(8,128)(2,1)S(1)}, bf16[128,1536]{1,0:T(8,128)(2,1)S(1)}, u32[]{:S(2)}, u32[]{:S(2)}) %collective-permute-start.16) | collective-permute-done | bytes 393248 | tf_op jit(solution)/shard_map/ppermute | solution.py:427
  68.8 6.8 %collective-permute-done.13.arrived = bf16[128,1280]{1,0:T(8,128)(2,1)S(1)} collective-permute-done((bf16[128,1280]{1,0:T(8,128)(2,1)S(1)}, bf16[128,1280]{1,0:T(8,128)(2,1)S(1)}, u32[]{:S(2)}, u32[]{:S(2)}) %collective-permute-start.13) | collective-permute-done | bytes 327712 | tf_op jit(solution)/shard_map/ppermute | solution.py:427
  75.8 5.5 %collective-permute-done.10.arrived = bf16[128,1024]{1,0:T(8,128)(2,1)S(1)} collective-permute-done((bf16[128,1024]{1,0:T(8,128)(2,1)S(1)}, bf16[128,1024]{1,0:T(8,128)(2,1)S(1)}, u32[]{:S(2)}, u32[]{:S(2)}) %collective-permute-start.10) | collective-permute-done | bytes 262176 | tf_op jit(solution)/shard_map/ppermute | solution.py:427
  81.5 8.3 %collective-permute-done.17.arrived = bf16[128,1536]{1,0:T(8,128)(2,1)S(1)} collective-permute-done((bf16[128,1536]{1,0:T(8,128)(2,1)S(1)}, bf16[128,1536]{1,0:T(8,128)(2,1)S(1)}, u32[]{:S(2)}, u32[]{:S(2)}) %collective-permute-start.17) | collective-permute-done | bytes 393248 | tf_op jit(solution)/shard_map/ppermute | solution.py:427
  90.6 5.5 %collective-permute-done.14.arrived.refs_3_ = bf16[128,1152]{1,0:T(8,128)(2,1)S(1)} collective-permute-done((bf16[128,1152]{1,0:T(8,128)(2,1)S(1)}, bf16[128,1152]{1,0:T(8,128)(2,1)S(1)}, u32[]{:S(2)}, u32[]{:S(2)}) %collective-permute-start.14) | collective-permute-done | bytes 294944 | tf_op jit(solution)/shard_map/ppermute | solution.py:427
  96.9 1.7 %adam.1 = (f32[4,128,128]{2,1,0:T(8,128)}, f32[4,128,128]{2,1,0:T(8,128)}, f32[4,128,128]{2,1,0:T(8,128)}) custom-call(s32[4,12]{1,0:T(4,128)S(1)} %get-tuple-element.43.table, bf16[128,128]{1,0:T(8,128)(2,1)S(1)} %get-tuple-element.67.refs_0_, bf16[128,128]{1,0:T(8,128)(2,1)S(1)} %get-tuple-element.68.refs_1_, ...), custom_call_target="tpu_custom_call" | custom-call | flops 65536 | bytes 131072 | tf_op jit(solution)/shard_map/adam/pallas_call | solution.py:413
  98.5 1.7 %collective-permute-done.11.arrived = bf16[128,1024]{1,0:T(8,128)(2,1)S(1)} collective-permute-done((bf16[128,1024]{1,0:T(8,128)(2,1)S(1)}, bf16[128,1024]{1,0:T(8,128)(2,1)S(1)}, u32[]{:S(2)}, u32[]{:S(2)}) %collective-permute-start.11) | collective-permute-done | bytes 262176 | tf_op jit(solution)/shard_map/ppermute | solution.py:427
  (38 shorter events, 7.7 us)
Async XLA Ops:
  0.6 8.4 %collective-permute-start.3 = (bf16[128,2048]{1,0:T(8,128)(2,1)}, bf16[128,2048]{1,0:T(8,128)(2,1)S(1)}, u32[]{:S(2)}, u32[]{:S(2)}) collective-permute-start(bf16[128,2048]{1,0:T(8,128)(2,1)} %own.1), channel_id=1, source_target_pairs={{1,0},{0,1},{3,2},{2,3},{5,4},{4,5},{7,6},{6,7},{9,8},{8,9},{11,10... | collective-permute-start | bytes 1572872 | tf_op jit(solution)/shard_map/ppermute | solution.py:438
  1.1 17.8 %collective-permute-start.4 = (bf16[128,2048]{1,0:T(8,128)(2,1)}, bf16[128,2048]{1,0:T(8,128)(2,1)S(1)}, u32[]{:S(2)}, u32[]{:S(2)}) collective-permute-start(bf16[128,2048]{1,0:T(8,128)(2,1)} %own.1), channel_id=1, source_target_pairs={{2,0},{0,2},{3,1},{1,3},{6,4},{4,6},{7,5},{5,7},{10,8},{8,10},{11,... | collective-permute-start | bytes 1572872 | tf_op jit(solution)/shard_map/ppermute | solution.py:427
  4.5 6.1 %collective-permute-start.2 = (s32[1,8]{1,0:T(1,128)S(1)}, s32[1,8]{1,0:T(1,128)S(1)}, u32[]{:S(2)}, u32[]{:S(2)}) collective-permute-start(s32[1,8]{1,0:T(1,128)S(1)} %pad_add_fusion.refs_0_), channel_id=1, source_target_pairs={{4,0},{8,4},{12,8},{0,12},{5,1},{9,5},{13,9},{1,13},{6,2},{10,6},{... | collective-permute-start | bytes 104 | tf_op jit(solution)/shard_map/ppermute | solution.py:427
  8.1 4.4 %collective-permute-start.1 = (s32[1,8]{1,0:T(1,128)S(1)}, s32[1,8]{1,0:T(1,128)S(1)}, u32[]{:S(2)}, u32[]{:S(2)}) collective-permute-start(s32[1,8]{1,0:T(1,128)S(1)} %pad_add_fusion.refs_0_), channel_id=1, source_target_pairs={{8,0},{12,4},{0,8},{4,12},{9,1},{13,5},{1,9},{5,13},{10,2},{14,6},... | collective-permute-start | bytes 104 | tf_op jit(solution)/shard_map/ppermute | solution.py:427
  8.1 5.3 %collective-permute-start = (s32[1,8]{1,0:T(1,128)S(1)}, s32[1,8]{1,0:T(1,128)S(1)}, u32[]{:S(2)}, u32[]{:S(2)}) collective-permute-start(s32[1,8]{1,0:T(1,128)S(1)} %pad_add_fusion.refs_0_), channel_id=1, source_target_pairs={{12,0},{0,4},{4,8},{8,12},{13,1},{1,5},{5,9},{9,13},{14,2},{2,6},{... | collective-permute-start | bytes 104 | tf_op jit(solution)/shard_map/ppermute | solution.py:427
  14.8 14.7 %collective-permute-start.6 = (bf16[5,128,128]{2,1,0:T(8,128)(2,1)S(1)}, bf16[5,128,128]{2,1,0:T(8,128)(2,1)S(1)}, u32[]{:S(2)}, u32[]{:S(2)}) collective-permute-start(bf16[5,128,128]{2,1,0:T(8,128)(2,1)S(1)} %get-tuple-element.46), channel_id=1, source_target_pairs={{12,0},{0,4},{4,8},{8,12},{13,1},{1,5},{5,9},{9,13},{14,2},{2,6},{... | collective-permute-start | bytes 491528 | tf_op jit(solution)/shard_map/ppermute | solution.py:427
  14.9 14.7 %collective-permute-start.7 = (bf16[5,128,128]{2,1,0:T(8,128)(2,1)S(1)}, bf16[5,128,128]{2,1,0:T(8,128)(2,1)S(1)}, u32[]{:S(2)}, u32[]{:S(2)}) collective-permute-start(bf16[5,128,128]{2,1,0:T(8,128)(2,1)S(1)} %get-tuple-element.47), channel_id=1, source_target_pairs={{8,0},{12,4},{0,8},{4,12},{9,1},{13,5},{1,9},{5,13},{10,2},{14,6},... | collective-permute-start | bytes 491528 | tf_op jit(solution)/shard_map/ppermute | solution.py:427
  16.1 13.5 %collective-permute-start.8 = (bf16[5,128,128]{2,1,0:T(8,128)(2,1)S(1)}, bf16[5,128,128]{2,1,0:T(8,128)(2,1)S(1)}, u32[]{:S(2)}, u32[]{:S(2)}) collective-permute-start(bf16[5,128,128]{2,1,0:T(8,128)(2,1)S(1)} %get-tuple-element.48), channel_id=1, source_target_pairs={{4,0},{8,4},{12,8},{0,12},{5,1},{9,5},{13,9},{1,13},{6,2},{10,6},{... | collective-permute-start | bytes 491528 | tf_op jit(solution)/shard_map/ppermute | solution.py:427
  18.9 4.0 %collective-permute-start.5 = (bf16[128,2048]{1,0:T(8,128)(2,1)S(1)}, bf16[128,2048]{1,0:T(8,128)(2,1)S(1)}, u32[]{:S(2)}, u32[]{:S(2)}) collective-permute-start(bf16[128,2048]{1,0:T(8,128)(2,1)S(1)} %collective-permute-done.4.refs_1_), channel_id=1, source_target_pairs={{1,0},{0,1},{3,2},{2,3},{5,4},{4,5},{7,6},{6,7},{9,8},{8,9},{11,10... | collective-permute-start | bytes 1572872 | tf_op jit(solution)/shard_map/ppermute | solution.py:427
  30.6 11.0 %collective-permute-start.9 = (bf16[128,1024]{1,0:T(8,128)(2,1)S(1)}, bf16[128,1024]{1,0:T(8,128)(2,1)S(1)}, u32[]{:S(2)}, u32[]{:S(2)}) collective-permute-start(bf16[128,1024]{1,0:T(8,128)(2,1)S(1)} %get-tuple-element.53), channel_id=1, source_target_pairs={{12,0},{0,4},{4,8},{8,12},{13,1},{1,5},{5,9},{9,13},{14,2},{2,6},{... | collective-permute-start | bytes 786440 | tf_op jit(solution)/shard_map/ppermute | solution.py:427
  34.4 15.3 %collective-permute-start.15 = (bf16[128,1536]{1,0:T(8,128)(2,1)S(1)}, bf16[128,1536]{1,0:T(8,128)(2,1)S(1)}, u32[]{:S(2)}, u32[]{:S(2)}) collective-permute-start(bf16[128,1536]{1,0:T(8,128)(2,1)S(1)} %get-tuple-element.66), channel_id=1, source_target_pairs={{12,0},{0,4},{4,8},{8,12},{13,1},{1,5},{5,9},{9,13},{14,2},{2,6},{... | collective-permute-start | bytes 1179656 | tf_op jit(solution)/shard_map/ppermute | solution.py:427
  47.0 13.2 %collective-permute-start.12 = (bf16[128,1408]{1,0:T(8,128)(2,1)S(1)}, bf16[128,1408]{1,0:T(8,128)(2,1)S(1)}, u32[]{:S(2)}, u32[]{:S(2)}) collective-permute-start(bf16[128,1408]{1,0:T(8,128)(2,1)S(1)} %attach.1), channel_id=1, source_target_pairs={{12,0},{0,4},{4,8},{8,12},{13,1},{1,5},{5,9},{9,13},{14,2},{2,6},{... | collective-permute-start | bytes 1081352 | tf_op jit(solution)/shard_map/ppermute | solution.py:427
  49.9 18.8 %collective-permute-start.16 = (bf16[128,1536]{1,0:T(8,128)(2,1)S(1)}, bf16[128,1536]{1,0:T(8,128)(2,1)S(1)}, u32[]{:S(2)}, u32[]{:S(2)}) collective-permute-start(bf16[128,1536]{1,0:T(8,128)(2,1)S(1)} %add.12), channel_id=1, source_target_pairs={{12,0},{0,4},{4,8},{8,12},{13,1},{1,5},{5,9},{9,13},{14,2},{2,6},{... | collective-permute-start | bytes 1179656 | tf_op jit(solution)/shard_map/ppermute | solution.py:427
  60.3 36.5 %copy-start = (f32[1,1,4,128,128]{4,3,2,1,0:T(8,128)S(1)}, f32[1,1,4,128,128]{4,3,2,1,0:T(8,128)}, u32[]{:S(2)}) copy-start(f32[1,1,4,128,128]{4,3,2,1,0:T(8,128)} %param.13) | copy-start | bytes 786436
  60.3 36.5 %copy-start.1 = (f32[1,1,4,128,128]{4,3,2,1,0:T(8,128)S(1)}, f32[1,1,4,128,128]{4,3,2,1,0:T(8,128)}, u32[]{:S(2)}) copy-start(f32[1,1,4,128,128]{4,3,2,1,0:T(8,128)} %param.14) | copy-start | bytes 786436
  60.3 36.5 %copy-start.2 = (f32[1,1,4,128,128]{4,3,2,1,0:T(8,128)S(1)}, f32[1,1,4,128,128]{4,3,2,1,0:T(8,128)}, u32[]{:S(2)}) copy-start(f32[1,1,4,128,128]{4,3,2,1,0:T(8,128)} %param.15) | copy-start | bytes 786436
  60.4 15.3 %collective-permute-start.13 = (bf16[128,1280]{1,0:T(8,128)(2,1)S(1)}, bf16[128,1280]{1,0:T(8,128)(2,1)S(1)}, u32[]{:S(2)}, u32[]{:S(2)}) collective-permute-start(bf16[128,1280]{1,0:T(8,128)(2,1)S(1)} %get-tuple-element.63), channel_id=1, source_target_pairs={{12,0},{0,4},{4,8},{8,12},{13,1},{1,5},{5,9},{9,13},{14,2},{2,6},{... | collective-permute-start | bytes 983048 | tf_op jit(solution)/shard_map/ppermute | solution.py:427
  60.4 20.9 %collective-permute-start.10 = (bf16[128,1024]{1,0:T(8,128)(2,1)S(1)}, bf16[128,1024]{1,0:T(8,128)(2,1)S(1)}, u32[]{:S(2)}, u32[]{:S(2)}) collective-permute-start(bf16[128,1024]{1,0:T(8,128)(2,1)S(1)} %add.8), channel_id=1, source_target_pairs={{12,0},{0,4},{4,8},{8,12},{13,1},{1,5},{5,9},{9,13},{14,2},{2,6},{... | collective-permute-start | bytes 786440 | tf_op jit(solution)/shard_map/ppermute | solution.py:427
  68.8 21.0 %collective-permute-start.17 = (bf16[128,1536]{1,0:T(8,128)(2,1)S(1)}, bf16[128,1536]{1,0:T(8,128)(2,1)S(1)}, u32[]{:S(2)}, u32[]{:S(2)}) collective-permute-start(bf16[128,1536]{1,0:T(8,128)(2,1)S(1)} %add.13), channel_id=1, source_target_pairs={{12,0},{0,4},{4,8},{8,12},{13,1},{1,5},{5,9},{9,13},{14,2},{2,6},{... | collective-permute-start | bytes 1179656 | tf_op jit(solution)/shard_map/ppermute | solution.py:427
  75.8 20.3 %collective-permute-start.14 = (bf16[128,1152]{1,0:T(8,128)(2,1)S(1)}, bf16[128,1152]{1,0:T(8,128)(2,1)S(1)}, u32[]{:S(2)}, u32[]{:S(2)}) collective-permute-start(bf16[128,1152]{1,0:T(8,128)(2,1)S(1)} %get-tuple-element.64), channel_id=1, source_target_pairs={{12,0},{0,4},{4,8},{8,12},{13,1},{1,5},{5,9},{9,13},{14,2},{2,6},{... | collective-permute-start | bytes 884744 | tf_op jit(solution)/shard_map/ppermute | solution.py:427
  81.4 18.8 %collective-permute-start.11 = (bf16[128,1024]{1,0:T(8,128)(2,1)S(1)}, bf16[128,1024]{1,0:T(8,128)(2,1)S(1)}, u32[]{:S(2)}, u32[]{:S(2)}) collective-permute-start(bf16[128,1024]{1,0:T(8,128)(2,1)S(1)} %add.9), channel_id=1, source_target_pairs={{12,0},{0,4},{4,8},{8,12},{13,1},{1,5},{5,9},{9,13},{14,2},{2,6},{... | collective-permute-start | bytes 786440 | tf_op jit(solution)/shard_map/ppermute | solution.py:427

commit v14 on v13

--- a/solution.py
+++ b/solution.py
@@ -16,9 +16,9 @@
 MATMUL = 4096
 EARLY = 1
 AHEAD = 5000
-PARTS = (2, 3, 2)
+PARTS = (3, 2, 2)
 RIDE = 2
-LAST = 0
+LAST = 1
 LAID = 2
 NT = (((1,), (1,)), ((), ()))
 TN = (((0,), (0,)), ((), ()))
@@ -517,8 +517,6 @@
             )
             held = more[0] if more else held
         else:
-            moving[0] = add_call(2, partials[0], moving[0], block)[0]
-            rows, moving[0] = lax.optimization_barrier((rows, moving[0]))
             partial, first = matmul_call(
                 spans, low, (high - low,), width, table, down_weight, rows, held
             )
@@ -531,9 +529,8 @@
     tiles = [grads[0]]
     for t in range(2, spans):
         for part in range(len(ranges)):
-            if (t, part) != (2, 0):
-                moving[part], *mine = add_call(t, partials[part], moving[part], block)
-                tiles += mine
+            moving[part], *mine = add_call(t, partials[part], moving[part], block)
+            tiles += mine
             moving[part] = take_from(moving[part], "seq", -1)
     tiles.append(moving[RIDE])
     columns = partials[RIDE].shape[2]

time: 101 us -> 100 us (0.990)
  waiting for transfers between devices: 57.2 us -> 53.9 us
  starting transfers between devices: 16.6 us -> 18.7 us
    ppermute x17, waiting for transfers between devices: 57.2 us -> 53.9 us  [take_from(): lax.ppermute(array, axis, [((i + places) % size, i) for i in range(size)])]
    ppermute x17, starting transfers between devices: 16.1 us -> 18.2 us  [take_from(): lax.ppermute(array, axis, [((i + places) % size, i) for i in range(size)])]
  transfers between devices with their start and end apart: 18 -> 18, of which waited for: 11 -> 10; matrix products, arithmetic and copies ran while one was open for 1% -> 1% of each run, Pallas kernels for 24% -> 24%
where the time goes in v14:
time: 100 us; the launch traced here: 99.8 us
  waiting for transfers between devices  53.9 us (54%)
  Pallas kernels  25.5 us (26%)
  starting transfers between devices  18.7 us (19%)
    ppermute x17, waiting for transfers between devices, take_from(): lax.ppermute(array, axis, [((i + places) % size, i) for i in range(size)])  53.9 us
    ppermute x17, starting transfers between devices, take_from(): lax.ppermute(array, axis, [((i + places) % size, i) for i in range(size)])  18.2 us
    pallas_call x1, Pallas kernels, early_matmul_call(): pl.pallas_call(functools.partial(early_matmul_kernel, width), grid=(colum...  6.62 us
    pallas_call x1, Pallas kernels, matmul_call(): pl.pallas_call(functools.partial(matmul_kernel, low, ends), grid=(ends[-1...  4.45 us
    pallas_call x1, Pallas kernels, per_device(): pl.pallas_call(lay_kernel, out_shape=jax.ShapeDtypeStruct((laid * width,...  3.99 us
    pallas_call x3, Pallas kernels, last_call(): pl.pallas_call(functools.partial(last_kernel, low), out_shape=shape, in_s...  2.41 us
    pallas_call x2, Pallas kernels, delta_call(): pl.pallas_call(functools.partial(delta_kernel, sizes, low, len(given)), o...  2.18 us
  transfers between devices with their start and end apart: 18, of which 10 were waited for; matrix products, arithmetic and copies ran while one was open for 1% of the time, Pallas kernels for 24%

profile of v14, /device:TPU:0, one launch (start us, length us, event | category | flops | bytes accessed | tf_op | source)
XLA Modules:
  0.0 99.8 jit_solution(18383548386587707980)
XLA Ops:
  1.1 2.6 %collective-permute-start.4 = (bf16[128,2048]{1,0:T(8,128)(2,1)}, bf16[128,2048]{1,0:T(8,128)(2,1)S(1)}, u32[]{:S(2)}, u32[]{:S(2)}) collective-permute-start(bf16[128,2048]{1,0:T(8,128)(2,1)} %own.1), channel_id=1, source_target_pairs={{2,0},{0,2},{3,1},{1,3},{6,4},{4,6},{7,5},{5,7},{10,8},{8,10},{11,... | collective-permute-start | bytes 1572872 | tf_op jit(solution)/shard_map/ppermute | solution.py:427
  4.5 3.6 %collective-permute-start.2 = (s32[1,8]{1,0:T(1,128)S(1)}, s32[1,8]{1,0:T(1,128)S(1)}, u32[]{:S(2)}, u32[]{:S(2)}) collective-permute-start(s32[1,8]{1,0:T(1,128)S(1)} %pad_add_fusion.refs_0_), channel_id=1, source_target_pairs={{4,0},{8,4},{12,8},{0,12},{5,1},{9,5},{13,9},{1,13},{6,2},{10,6},{... | collective-permute-start | bytes 104 | tf_op jit(solution)/shard_map/ppermute | solution.py:427
  8.1 1.0 %collective-permute-start = (s32[1,8]{1,0:T(1,128)S(1)}, s32[1,8]{1,0:T(1,128)S(1)}, u32[]{:S(2)}, u32[]{:S(2)}) collective-permute-start(s32[1,8]{1,0:T(1,128)S(1)} %pad_add_fusion.refs_0_), channel_id=1, source_target_pairs={{12,0},{0,4},{4,8},{8,12},{13,1},{1,5},{5,9},{9,13},{14,2},{2,6},{... | collective-permute-start | bytes 104 | tf_op jit(solution)/shard_map/ppermute | solution.py:427
  9.1 1.4 %early.1 = (bf16[4,128,128]{2,1,0:T(8,128)(2,1)S(1)}, bf16[128,3584]{1,0:T(8,128)(2,1)S(1)}, bf16[256,2048]{1,0:T(8,128)(2,1)S(1)}) custom-call(f32[4,128,128]{2,1,0:T(8,128)} %bitcast.8, bf16[128,3584]{1,0:T(8,128)(2,1)} %hidden.1, bf16[128,2048]{1,0:T(8,128)(2,1)} %own.1, bf16[128,2048]{1,0:T(8,128)(2,1)S(1)} %collective-permute-done.3.refs_0_), custom_call_target="tpu_custom_call" | custom-call | flops 458752 | bytes 917504 | tf_op jit(solution)/shard_map/early/pallas_call | solution.py:465
  10.5 2.0 %collective-permute-done.1.refs_2_ = s32[1,8]{1,0:T(1,128)S(1)} collective-permute-done((s32[1,8]{1,0:T(1,128)S(1)}, s32[1,8]{1,0:T(1,128)S(1)}, u32[]{:S(2)}, u32[]{:S(2)}) %collective-permute-start.1) | collective-permute-done | bytes 64 | tf_op jit(solution)/shard_map/ppermute | solution.py:427
  13.4 1.4 %pick.1 = (s32[4,12]{1,0:T(4,128)S(1)}, bf16[5,128,128]{2,1,0:T(8,128)(2,1)S(1)}, bf16[5,128,128]{2,1,0:T(8,128)(2,1)S(1)}, bf16[5,128,128]{2,1,0:T(8,128)(2,1)S(1)}, bf16[5,128,128]{2,1,0:T(8,128)(2,1)S(1)}) custom-call(s32[1,8]{1,0:T(1,128)S(1)} %pad_add_fusion.refs_0_, s32[1,8]{1,0:T(1,128)S(1)} %collective-permute-done.refs_1_, ...), custom_call_target="tpu_custom_call" | custom-call | flops 458752 | bytes 917504 | tf_op jit(solution)/shard_map/pick/pallas_call | solution.py:482
  14.9 1.2 %collective-permute-start.7 = (bf16[5,128,128]{2,1,0:T(8,128)(2,1)S(1)}, bf16[5,128,128]{2,1,0:T(8,128)(2,1)S(1)}, u32[]{:S(2)}, u32[]{:S(2)}) collective-permute-start(bf16[5,128,128]{2,1,0:T(8,128)(2,1)S(1)} %get-tuple-element.45), channel_id=1, source_target_pairs={{8,0},{12,4},{0,8},{4,12},{9,1},{13,5},{1,9},{5,13},{10,2},{14,6},... | collective-permute-start | bytes 491528 | tf_op jit(solution)/shard_map/ppermute | solution.py:427
  16.1 2.8 %collective-permute-start.8 = (bf16[5,128,128]{2,1,0:T(8,128)(2,1)S(1)}, bf16[5,128,128]{2,1,0:T(8,128)(2,1)S(1)}, u32[]{:S(2)}, u32[]{:S(2)}) collective-permute-start(bf16[5,128,128]{2,1,0:T(8,128)(2,1)S(1)} %get-tuple-element.46), channel_id=1, source_target_pairs={{4,0},{8,4},{12,8},{0,12},{5,1},{9,5},{13,9},{1,13},{6,2},{10,6},{... | collective-permute-start | bytes 491528 | tf_op jit(solution)/shard_map/ppermute | solution.py:427
  18.9 4.0 %lay.1.weight = bf16[2560,2048]{1,0:T(8,128)(2,1)S(1)} custom-call(bf16[3584,2048]{1,0:T(8,128)(2,1)} %weight.3), custom_call_target="tpu_custom_call" | custom-call | flops 26214400000 | bytes 52428800000 | tf_op jit(solution)/shard_map/lay/pallas_call | solution.py:495
  22.9 6.6 %partial.2 = (f32[512,2560]{1,0:T(8,128)S(1)}, bf16[512,2048]{1,0:T(8,128)(2,1)S(1)}) custom-call(bf16[2560,2048]{1,0:T(8,128)(2,1)S(1)} %lay.1.weight, bf16[256,2048]{1,0:T(8,128)(2,1)S(1)} %get-tuple-element.42.refs_0_, bf16[128,2048]{1,0:T(8,128)(2,1)S(1)} %collective-permute-done.4.refs_1_, bf16[128,2048]{1,0:T(8,128)(2,1)S(1)} %collective-permute-done.5.refs_2_), custom_call_target="tpu_custom_call" | custom-call | flops 1310720 | bytes 2621440 | tf_op jit(solution)/shard_map/partial/pallas_call | solution.py:141
  29.6 1.1 %delta.2 = (bf16[4,128,1536]{2,1,0:T(8,128)(2,1)S(1)}, bf16[128,1536]{1,0:T(8,128)(2,1)S(1)}, bf16[4,128,128]{2,1,0:T(8,128)(2,1)S(1)}) custom-call(s32[4,12]{1,0:T(4,128)S(1)} %get-tuple-element.41.table, f32[512,2560]{1,0:T(8,128)S(1)} %get-tuple-element.48.early, bf16[512,2048]{1,0:T(8,128)(2,1)S(1)} %get-tuple-element.49.rows, ...), custom_call_target="tpu_custom_call" | custom-call | flops 1310720 | bytes 2621440 | tf_op jit(solution)/shard_map/delta/pallas_call | solution.py:216
  30.7 3.0 %collective-permute-start.15 = (bf16[128,1536]{1,0:T(8,128)(2,1)S(1)}, bf16[128,1536]{1,0:T(8,128)(2,1)S(1)}, u32[]{:S(2)}, u32[]{:S(2)}) collective-permute-start(bf16[128,1536]{1,0:T(8,128)(2,1)S(1)} %get-tuple-element.62), channel_id=1, source_target_pairs={{12,0},{0,4},{4,8},{8,12},{13,1},{1,5},{5,9},{9,13},{14,2},{2,6},{... | collective-permute-start | bytes 1179656 | tf_op jit(solution)/shard_map/ppermute | solution.py:427
  34.6 4.5 %partial.3 = (bf16[4,128,1024]{2,1,0:T(8,128)(2,1)S(1)}, bf16[128,1024]{1,0:T(8,128)(2,1)S(1)}) custom-call(s32[4,12]{1,0:T(4,128)S(1)} %get-tuple-element.41.table, bf16[3584,2048]{1,0:T(8,128)(2,1)} %weight.3, bf16[512,2048]{1,0:T(8,128)(2,1)S(1)} %get-tuple-element.49.rows, bf16[4,128,128]{2,1,0:T(8,128)(2,1)S(1)} %get-tuple-element.50.refs_0_.held), custom_call_target="tpu_custom_call" | custom-call | flops 2147483648 | bytes 4294967296 | tf_op jit(solution)/shard_map/partial/pallas_call | solution.py:249
  39.8 4.7 %collective-permute-done.15.arrived = bf16[128,1536]{1,0:T(8,128)(2,1)S(1)} collective-permute-done((bf16[128,1536]{1,0:T(8,128)(2,1)S(1)}, bf16[128,1536]{1,0:T(8,128)(2,1)S(1)}, u32[]{:S(2)}, u32[]{:S(2)}) %collective-permute-start.15) | collective-permute-done | bytes 393248 | tf_op jit(solution)/shard_map/ppermute | solution.py:427
  44.9 1.1 %delta.3 = (bf16[4,128,1024]{2,1,0:T(8,128)(2,1)S(1)}, bf16[128,1024]{1,0:T(8,128)(2,1)S(1)}) custom-call(s32[4,12]{1,0:T(4,128)S(1)} %get-tuple-element.41.table, f32[512,2560]{1,0:T(8,128)S(1)} %get-tuple-element.48.early, bf16[512,2048]{1,0:T(8,128)(2,1)S(1)} %get-tuple-element.49.rows, bf16[4,128,128]{2,1,0:T(8,128)(2,1)S(1)} %get-tuple-element.50.refs_0_.held), custom_call_target="tpu_custom_call" | custom-call | flops 1310720 | bytes 2621440 | tf_op jit(solution)/shard_map/delta/pallas_call | solution.py:216
  46.8 5.5 %collective-permute-done.12.arrived = bf16[128,1408]{1,0:T(8,128)(2,1)S(1)} collective-permute-done((bf16[128,1408]{1,0:T(8,128)(2,1)S(1)}, bf16[128,1408]{1,0:T(8,128)(2,1)S(1)}, u32[]{:S(2)}, u32[]{:S(2)}) %collective-permute-start.12) | collective-permute-done | bytes 360480 | tf_op jit(solution)/shard_map/ppermute | solution.py:427
  52.6 13.7 %collective-permute-done.9.arrived = bf16[128,1024]{1,0:T(8,128)(2,1)S(1)} collective-permute-done((bf16[128,1024]{1,0:T(8,128)(2,1)S(1)}, bf16[128,1024]{1,0:T(8,128)(2,1)S(1)}, u32[]{:S(2)}, u32[]{:S(2)}) %collective-permute-start.9) | collective-permute-done | bytes 262176 | tf_op jit(solution)/shard_map/ppermute | solution.py:427
  66.8 1.0 collective-permute-start.17
  67.8 5.5 %collective-permute-done.13.arrived = bf16[128,1280]{1,0:T(8,128)(2,1)S(1)} collective-permute-done((bf16[128,1280]{1,0:T(8,128)(2,1)S(1)}, bf16[128,1280]{1,0:T(8,128)(2,1)S(1)}, u32[]{:S(2)}, u32[]{:S(2)}) %collective-permute-start.13) | collective-permute-done | bytes 327712 | tf_op jit(solution)/shard_map/ppermute | solution.py:427
  73.7 5.3 %collective-permute-done.10.arrived = bf16[128,1024]{1,0:T(8,128)(2,1)S(1)} collective-permute-done((bf16[128,1024]{1,0:T(8,128)(2,1)S(1)}, bf16[128,1024]{1,0:T(8,128)(2,1)S(1)}, u32[]{:S(2)}, u32[]{:S(2)}) %collective-permute-start.10) | collective-permute-done | bytes 262176 | tf_op jit(solution)/shard_map/ppermute | solution.py:427
  79.3 8.1 %collective-permute-done.17.arrived = bf16[128,1536]{1,0:T(8,128)(2,1)S(1)} collective-permute-done((bf16[128,1536]{1,0:T(8,128)(2,1)S(1)}, bf16[128,1536]{1,0:T(8,128)(2,1)S(1)}, u32[]{:S(2)}, u32[]{:S(2)}) %collective-permute-start.17) | collective-permute-done | bytes 393248 | tf_op jit(solution)/shard_map/ppermute | solution.py:427
  88.2 5.5 %collective-permute-done.14.arrived.refs_3_ = bf16[128,1152]{1,0:T(8,128)(2,1)S(1)} collective-permute-done((bf16[128,1152]{1,0:T(8,128)(2,1)S(1)}, bf16[128,1152]{1,0:T(8,128)(2,1)S(1)}, u32[]{:S(2)}, u32[]{:S(2)}) %collective-permute-start.14) | collective-permute-done | bytes 294944 | tf_op jit(solution)/shard_map/ppermute | solution.py:427
  94.5 1.7 %adam.1 = (f32[4,128,128]{2,1,0:T(8,128)}, f32[4,128,128]{2,1,0:T(8,128)}, f32[4,128,128]{2,1,0:T(8,128)}) custom-call(s32[4,12]{1,0:T(4,128)S(1)} %get-tuple-element.41.table, bf16[128,128]{1,0:T(8,128)(2,1)S(1)} %get-tuple-element.63.refs_0_, bf16[128,128]{1,0:T(8,128)(2,1)S(1)} %get-tuple-element.64.refs_1_, ...), custom_call_target="tpu_custom_call" | custom-call | flops 65536 | bytes 131072 | tf_op jit(solution)/shard_map/adam/pallas_call | solution.py:413
  96.2 2.9 %collective-permute-done.11.arrived = bf16[128,1024]{1,0:T(8,128)(2,1)S(1)} collective-permute-done((bf16[128,1024]{1,0:T(8,128)(2,1)S(1)}, bf16[128,1024]{1,0:T(8,128)(2,1)S(1)}, u32[]{:S(2)}, u32[]{:S(2)}) %collective-permute-start.11) | collective-permute-done | bytes 262176 | tf_op jit(solution)/shard_map/ppermute | solution.py:427
  (38 shorter events, 9.0 us)
Async XLA Ops:
  0.6 8.4 %collective-permute-start.3 = (bf16[128,2048]{1,0:T(8,128)(2,1)}, bf16[128,2048]{1,0:T(8,128)(2,1)S(1)}, u32[]{:S(2)}, u32[]{:S(2)}) collective-permute-start(bf16[128,2048]{1,0:T(8,128)(2,1)} %own.1), channel_id=1, source_target_pairs={{1,0},{0,1},{3,2},{2,3},{5,4},{4,5},{7,6},{6,7},{9,8},{8,9},{11,10... | collective-permute-start | bytes 1572872 | tf_op jit(solution)/shard_map/ppermute | solution.py:438
  1.1 17.8 %collective-permute-start.4 = (bf16[128,2048]{1,0:T(8,128)(2,1)}, bf16[128,2048]{1,0:T(8,128)(2,1)S(1)}, u32[]{:S(2)}, u32[]{:S(2)}) collective-permute-start(bf16[128,2048]{1,0:T(8,128)(2,1)} %own.1), channel_id=1, source_target_pairs={{2,0},{0,2},{3,1},{1,3},{6,4},{4,6},{7,5},{5,7},{10,8},{8,10},{11,... | collective-permute-start | bytes 1572872 | tf_op jit(solution)/shard_map/ppermute | solution.py:427
  4.5 6.1 %collective-permute-start.2 = (s32[1,8]{1,0:T(1,128)S(1)}, s32[1,8]{1,0:T(1,128)S(1)}, u32[]{:S(2)}, u32[]{:S(2)}) collective-permute-start(s32[1,8]{1,0:T(1,128)S(1)} %pad_add_fusion.refs_0_), channel_id=1, source_target_pairs={{4,0},{8,4},{12,8},{0,12},{5,1},{9,5},{13,9},{1,13},{6,2},{10,6},{... | collective-permute-start | bytes 104 | tf_op jit(solution)/shard_map/ppermute | solution.py:427
  8.1 4.4 %collective-permute-start.1 = (s32[1,8]{1,0:T(1,128)S(1)}, s32[1,8]{1,0:T(1,128)S(1)}, u32[]{:S(2)}, u32[]{:S(2)}) collective-permute-start(s32[1,8]{1,0:T(1,128)S(1)} %pad_add_fusion.refs_0_), channel_id=1, source_target_pairs={{8,0},{12,4},{0,8},{4,12},{9,1},{13,5},{1,9},{5,13},{10,2},{14,6},... | collective-permute-start | bytes 104 | tf_op jit(solution)/shard_map/ppermute | solution.py:427
  8.1 5.3 %collective-permute-start = (s32[1,8]{1,0:T(1,128)S(1)}, s32[1,8]{1,0:T(1,128)S(1)}, u32[]{:S(2)}, u32[]{:S(2)}) collective-permute-start(s32[1,8]{1,0:T(1,128)S(1)} %pad_add_fusion.refs_0_), channel_id=1, source_target_pairs={{12,0},{0,4},{4,8},{8,12},{13,1},{1,5},{5,9},{9,13},{14,2},{2,6},{... | collective-permute-start | bytes 104 | tf_op jit(solution)/shard_map/ppermute | solution.py:427
  14.8 14.7 %collective-permute-start.6 = (bf16[5,128,128]{2,1,0:T(8,128)(2,1)S(1)}, bf16[5,128,128]{2,1,0:T(8,128)(2,1)S(1)}, u32[]{:S(2)}, u32[]{:S(2)}) collective-permute-start(bf16[5,128,128]{2,1,0:T(8,128)(2,1)S(1)} %get-tuple-element.44), channel_id=1, source_target_pairs={{12,0},{0,4},{4,8},{8,12},{13,1},{1,5},{5,9},{9,13},{14,2},{2,6},{... | collective-permute-start | bytes 491528 | tf_op jit(solution)/shard_map/ppermute | solution.py:427
  14.9 14.7 %collective-permute-start.7 = (bf16[5,128,128]{2,1,0:T(8,128)(2,1)S(1)}, bf16[5,128,128]{2,1,0:T(8,128)(2,1)S(1)}, u32[]{:S(2)}, u32[]{:S(2)}) collective-permute-start(bf16[5,128,128]{2,1,0:T(8,128)(2,1)S(1)} %get-tuple-element.45), channel_id=1, source_target_pairs={{8,0},{12,4},{0,8},{4,12},{9,1},{13,5},{1,9},{5,13},{10,2},{14,6},... | collective-permute-start | bytes 491528 | tf_op jit(solution)/shard_map/ppermute | solution.py:427
  16.1 13.5 %collective-permute-start.8 = (bf16[5,128,128]{2,1,0:T(8,128)(2,1)S(1)}, bf16[5,128,128]{2,1,0:T(8,128)(2,1)S(1)}, u32[]{:S(2)}, u32[]{:S(2)}) collective-permute-start(bf16[5,128,128]{2,1,0:T(8,128)(2,1)S(1)} %get-tuple-element.46), channel_id=1, source_target_pairs={{4,0},{8,4},{12,8},{0,12},{5,1},{9,5},{13,9},{1,13},{6,2},{10,6},{... | collective-permute-start | bytes 491528 | tf_op jit(solution)/shard_map/ppermute | solution.py:427
  18.9 4.0 %collective-permute-start.5 = (bf16[128,2048]{1,0:T(8,128)(2,1)S(1)}, bf16[128,2048]{1,0:T(8,128)(2,1)S(1)}, u32[]{:S(2)}, u32[]{:S(2)}) collective-permute-start(bf16[128,2048]{1,0:T(8,128)(2,1)S(1)} %collective-permute-done.4.refs_1_), channel_id=1, source_target_pairs={{1,0},{0,1},{3,2},{2,3},{5,4},{4,5},{7,6},{6,7},{9,8},{8,9},{11,10... | collective-permute-start | bytes 1572872 | tf_op jit(solution)/shard_map/ppermute | solution.py:427
  30.7 13.8 %collective-permute-start.15 = (bf16[128,1536]{1,0:T(8,128)(2,1)S(1)}, bf16[128,1536]{1,0:T(8,128)(2,1)S(1)}, u32[]{:S(2)}, u32[]{:S(2)}) collective-permute-start(bf16[128,1536]{1,0:T(8,128)(2,1)S(1)} %get-tuple-element.62), channel_id=1, source_target_pairs={{12,0},{0,4},{4,8},{8,12},{13,1},{1,5},{5,9},{9,13},{14,2},{2,6},{... | collective-permute-start | bytes 1179656 | tf_op jit(solution)/shard_map/ppermute | solution.py:427
  39.1 13.2 %collective-permute-start.12 = (bf16[128,1408]{1,0:T(8,128)(2,1)S(1)}, bf16[128,1408]{1,0:T(8,128)(2,1)S(1)}, u32[]{:S(2)}, u32[]{:S(2)}) collective-permute-start(bf16[128,1408]{1,0:T(8,128)(2,1)S(1)} %attach.1), channel_id=1, source_target_pairs={{12,0},{0,4},{4,8},{8,12},{13,1},{1,5},{5,9},{9,13},{14,2},{2,6},{... | collective-permute-start | bytes 1081352 | tf_op jit(solution)/shard_map/ppermute | solution.py:427
  44.7 22.1 %collective-permute-start.16 = (bf16[128,1536]{1,0:T(8,128)(2,1)S(1)}, bf16[128,1536]{1,0:T(8,128)(2,1)S(1)}, u32[]{:S(2)}, u32[]{:S(2)}) collective-permute-start(bf16[128,1536]{1,0:T(8,128)(2,1)S(1)} %add.12), channel_id=1, source_target_pairs={{12,0},{0,4},{4,8},{8,12},{13,1},{1,5},{5,9},{9,13},{14,2},{2,6},{... | collective-permute-start | bytes 1179656 | tf_op jit(solution)/shard_map/ppermute | solution.py:427
  46.0 20.3 %collective-permute-start.9 = (bf16[128,1024]{1,0:T(8,128)(2,1)S(1)}, bf16[128,1024]{1,0:T(8,128)(2,1)S(1)}, u32[]{:S(2)}, u32[]{:S(2)}) collective-permute-start(bf16[128,1024]{1,0:T(8,128)(2,1)S(1)} %get-tuple-element.52), channel_id=1, source_target_pairs={{12,0},{0,4},{4,8},{8,12},{13,1},{1,5},{5,9},{9,13},{14,2},{2,6},{... | collective-permute-start | bytes 786440 | tf_op jit(solution)/shard_map/ppermute | solution.py:427
  52.4 21.0 %collective-permute-start.13 = (bf16[128,1280]{1,0:T(8,128)(2,1)S(1)}, bf16[128,1280]{1,0:T(8,128)(2,1)S(1)}, u32[]{:S(2)}, u32[]{:S(2)}) collective-permute-start(bf16[128,1280]{1,0:T(8,128)(2,1)S(1)} %get-tuple-element.59), channel_id=1, source_target_pairs={{12,0},{0,4},{4,8},{8,12},{13,1},{1,5},{5,9},{9,13},{14,2},{2,6},{... | collective-permute-start | bytes 983048 | tf_op jit(solution)/shard_map/ppermute | solution.py:427
  66.4 28.1 %copy-start = (f32[1,1,4,128,128]{4,3,2,1,0:T(8,128)S(1)}, f32[1,1,4,128,128]{4,3,2,1,0:T(8,128)}, u32[]{:S(2)}) copy-start(f32[1,1,4,128,128]{4,3,2,1,0:T(8,128)} %param.13) | copy-start | bytes 786436
  66.4 28.1 %copy-start.1 = (f32[1,1,4,128,128]{4,3,2,1,0:T(8,128)S(1)}, f32[1,1,4,128,128]{4,3,2,1,0:T(8,128)}, u32[]{:S(2)}) copy-start(f32[1,1,4,128,128]{4,3,2,1,0:T(8,128)} %param.14) | copy-start | bytes 786436
  66.4 28.1 %copy-start.2 = (f32[1,1,4,128,128]{4,3,2,1,0:T(8,128)S(1)}, f32[1,1,4,128,128]{4,3,2,1,0:T(8,128)}, u32[]{:S(2)}) copy-start(f32[1,1,4,128,128]{4,3,2,1,0:T(8,128)} %param.15) | copy-start | bytes 786436
  66.4 12.5 %collective-permute-start.10 = (bf16[128,1024]{1,0:T(8,128)(2,1)S(1)}, bf16[128,1024]{1,0:T(8,128)(2,1)S(1)}, u32[]{:S(2)}, u32[]{:S(2)}) collective-permute-start(bf16[128,1024]{1,0:T(8,128)(2,1)S(1)} %add.8), channel_id=1, source_target_pairs={{12,0},{0,4},{4,8},{8,12},{13,1},{1,5},{5,9},{9,13},{14,2},{2,6},{... | collective-permute-start | bytes 786440 | tf_op jit(solution)/shard_map/ppermute | solution.py:427
  66.8 20.6 %collective-permute-start.17 = (bf16[128,1536]{1,0:T(8,128)(2,1)S(1)}, bf16[128,1536]{1,0:T(8,128)(2,1)S(1)}, u32[]{:S(2)}, u32[]{:S(2)}) collective-permute-start(bf16[128,1536]{1,0:T(8,128)(2,1)S(1)} %add.13), channel_id=1, source_target_pairs={{12,0},{0,4},{4,8},{8,12},{13,1},{1,5},{5,9},{9,13},{14,2},{2,6},{... | collective-permute-start | bytes 1179656 | tf_op jit(solution)/shard_map/ppermute | solution.py:427
  73.4 20.3 %collective-permute-start.14 = (bf16[128,1152]{1,0:T(8,128)(2,1)S(1)}, bf16[128,1152]{1,0:T(8,128)(2,1)S(1)}, u32[]{:S(2)}, u32[]{:S(2)}) collective-permute-start(bf16[128,1152]{1,0:T(8,128)(2,1)S(1)} %get-tuple-element.60), channel_id=1, source_target_pairs={{12,0},{0,4},{4,8},{8,12},{13,1},{1,5},{5,9},{9,13},{14,2},{2,6},{... | collective-permute-start | bytes 884744 | tf_op jit(solution)/shard_map/ppermute | solution.py:427
  79.0 20.0 %collective-permute-start.11 = (bf16[128,1024]{1,0:T(8,128)(2,1)S(1)}, bf16[128,1024]{1,0:T(8,128)(2,1)S(1)}, u32[]{:S(2)}, u32[]{:S(2)}) collective-permute-start(bf16[128,1024]{1,0:T(8,128)(2,1)S(1)} %add.9), channel_id=1, source_target_pairs={{12,0},{0,4},{4,8},{8,12},{13,1},{1,5},{5,9},{9,13},{14,2},{2,6},{... | collective-permute-start | bytes 786440 | tf_op jit(solution)/shard_map/ppermute | solution.py:427

commit v15 on v14

--- a/solution.py
+++ b/solution.py
@@ -19,7 +19,7 @@
 PARTS = (3, 2, 2)
 RIDE = 2
 LAST = 1
-LAID = 2
+LAID = 1
 NT = (((1,), (1,)), ((), ()))
 TN = (((0,), (0,)), ((), ()))
 

time: 100 us -> 97.9 us (0.979)
  waiting for transfers between devices: 53.9 us -> 48.4 us
  starting transfers between devices: 18.7 us -> 22.7 us
    ppermute x17, waiting for transfers between devices: 53.9 us -> 48.4 us  [take_from(): lax.ppermute(array, axis, [((i + places) % size, i) for i in range(size)])]
    pallas_call x1 -> x2, Pallas kernels: 4.45 us -> 8.89 us  [matmul_call(): pl.pallas_call(functools.partial(matmul_kernel, low, ends), grid=(ends[-1...]
    ppermute x17, starting transfers between devices: 18.2 us -> 22.2 us  [take_from(): lax.ppermute(array, axis, [((i + places) % size, i) for i in range(size)])]
    pallas_call x1, Pallas kernels: 6.62 us -> 4.03 us  [early_matmul_call(): pl.pallas_call(functools.partial(early_matmul_kernel, width), grid=(colum...]
    pallas_call x1, Pallas kernels: 3.99 us -> 2.79 us  [per_device(): pl.pallas_call(lay_kernel, out_shape=jax.ShapeDtypeStruct((laid * width,...]
    pallas_call x2 -> x1, Pallas kernels: 2.18 us -> 1.3 us  [delta_call(): pl.pallas_call(functools.partial(delta_kernel, sizes, low, len(given)), o...]
  transfers between devices with their start and end apart: 18 -> 18, of which waited for: 10 -> 11; matrix products, arithmetic and copies ran while one was open for 1% -> 1% of each run, Pallas kernels for 24% -> 24%
where the time goes in v15:
time: 97.9 us; the launch traced here: 98 us
  waiting for transfers between devices  48.4 us (49%)
  Pallas kernels  25.3 us (26%)
  starting transfers between devices  22.7 us (23%)
    ppermute x17, waiting for transfers between devices, take_from(): lax.ppermute(array, axis, [((i + places) % size, i) for i in range(size)])  48.4 us
    ppermute x17, starting transfers between devices, take_from(): lax.ppermute(array, axis, [((i + places) % size, i) for i in range(size)])  22.2 us
    pallas_call x2, Pallas kernels, matmul_call(): pl.pallas_call(functools.partial(matmul_kernel, low, ends), grid=(ends[-1...  8.89 us
    pallas_call x1, Pallas kernels, early_matmul_call(): pl.pallas_call(functools.partial(early_matmul_kernel, width), grid=(colum...  4.03 us
    pallas_call x1, Pallas kernels, per_device(): pl.pallas_call(lay_kernel, out_shape=jax.ShapeDtypeStruct((laid * width,...  2.79 us
    pallas_call x3, Pallas kernels, last_call(): pl.pallas_call(functools.partial(last_kernel, low), out_shape=shape, in_s...  2.41 us
  transfers between devices with their start and end apart: 18, of which 11 were waited for; matrix products, arithmetic and copies ran while one was open for 1% of the time, Pallas kernels for 24%

profile of v15, /device:TPU:0, one launch (start us, length us, event | category | flops | bytes accessed | tf_op | source)
XLA Modules:
  0.0 98.0 jit_solution(16982273168658307299)
XLA Ops:
  1.1 2.6 %collective-permute-start.4 = (bf16[128,2048]{1,0:T(8,128)(2,1)}, bf16[128,2048]{1,0:T(8,128)(2,1)S(1)}, u32[]{:S(2)}, u32[]{:S(2)}) collective-permute-start(bf16[128,2048]{1,0:T(8,128)(2,1)} %own.1), channel_id=1, source_target_pairs={{2,0},{0,2},{3,1},{1,3},{6,4},{4,6},{7,5},{5,7},{10,8},{8,10},{11,... | collective-permute-start | bytes 1572872 | tf_op jit(solution)/shard_map/ppermute | solution.py:427
  4.5 3.6 %collective-permute-start.2 = (s32[1,8]{1,0:T(1,128)S(1)}, s32[1,8]{1,0:T(1,128)S(1)}, u32[]{:S(2)}, u32[]{:S(2)}) collective-permute-start(s32[1,8]{1,0:T(1,128)S(1)} %pad_add_fusion.refs_0_), channel_id=1, source_target_pairs={{4,0},{8,4},{12,8},{0,12},{5,1},{9,5},{13,9},{1,13},{6,2},{10,6},{... | collective-permute-start | bytes 104 | tf_op jit(solution)/shard_map/ppermute | solution.py:427
  9.1 1.4 %early.1 = (bf16[4,128,128]{2,1,0:T(8,128)(2,1)S(1)}, bf16[128,3584]{1,0:T(8,128)(2,1)S(1)}, bf16[256,2048]{1,0:T(8,128)(2,1)S(1)}) custom-call(f32[4,128,128]{2,1,0:T(8,128)} %bitcast.8, bf16[128,3584]{1,0:T(8,128)(2,1)} %hidden.1, bf16[128,2048]{1,0:T(8,128)(2,1)} %own.1, bf16[128,2048]{1,0:T(8,128)(2,1)S(1)} %collective-permute-done.3.refs_0_), custom_call_target="tpu_custom_call" | custom-call | flops 458752 | bytes 917504 | tf_op jit(solution)/shard_map/early/pallas_call | solution.py:465
  10.5 2.0 %collective-permute-done.1.refs_2_ = s32[1,8]{1,0:T(1,128)S(1)} collective-permute-done((s32[1,8]{1,0:T(1,128)S(1)}, s32[1,8]{1,0:T(1,128)S(1)}, u32[]{:S(2)}, u32[]{:S(2)}) %collective-permute-start.1) | collective-permute-done | bytes 64 | tf_op jit(solution)/shard_map/ppermute | solution.py:427
  13.4 1.4 %pick.1 = (s32[4,12]{1,0:T(4,128)S(1)}, bf16[5,128,128]{2,1,0:T(8,128)(2,1)S(1)}, bf16[5,128,128]{2,1,0:T(8,128)(2,1)S(1)}, bf16[5,128,128]{2,1,0:T(8,128)(2,1)S(1)}, bf16[5,128,128]{2,1,0:T(8,128)(2,1)S(1)}) custom-call(s32[1,8]{1,0:T(1,128)S(1)} %pad_add_fusion.refs_0_, s32[1,8]{1,0:T(1,128)S(1)} %collective-permute-done.refs_1_, ...), custom_call_target="tpu_custom_call" | custom-call | flops 458752 | bytes 917504 | tf_op jit(solution)/shard_map/pick/pallas_call | solution.py:482
  16.1 2.8 %collective-permute-start.8 = (bf16[5,128,128]{2,1,0:T(8,128)(2,1)S(1)}, bf16[5,128,128]{2,1,0:T(8,128)(2,1)S(1)}, u32[]{:S(2)}, u32[]{:S(2)}) collective-permute-start(bf16[5,128,128]{2,1,0:T(8,128)(2,1)S(1)} %get-tuple-element.46), channel_id=1, source_target_pairs={{4,0},{8,4},{12,8},{0,12},{5,1},{9,5},{13,9},{1,13},{6,2},{10,6},{... | collective-permute-start | bytes 491528 | tf_op jit(solution)/shard_map/ppermute | solution.py:427
  18.9 2.8 %lay.1.weight = bf16[1536,2048]{1,0:T(8,128)(2,1)S(1)} custom-call(bf16[3584,2048]{1,0:T(8,128)(2,1)} %weight.5), custom_call_target="tpu_custom_call" | custom-call | flops 15728640000 | bytes 31457280000 | tf_op jit(solution)/shard_map/lay/pallas_call | solution.py:495
  21.7 4.0 %partial.3 = (f32[512,1536]{1,0:T(8,128)S(1)}, bf16[512,2048]{1,0:T(8,128)(2,1)S(1)}) custom-call(bf16[1536,2048]{1,0:T(8,128)(2,1)S(1)} %lay.1.weight, bf16[256,2048]{1,0:T(8,128)(2,1)S(1)} %get-tuple-element.42.refs_0_, bf16[128,2048]{1,0:T(8,128)(2,1)S(1)} %collective-permute-done.4.refs_1_, bf16[128,2048]{1,0:T(8,128)(2,1)S(1)} %collective-permute-done.5.refs_2_), custom_call_target="tpu_custom_call" | custom-call | flops 786432 | bytes 1572864 | tf_op jit(solution)/shard_map/partial/pallas_call | solution.py:141
  25.8 2.9 %collective-permute-done.7.refs_2_ = bf16[5,128,128]{2,1,0:T(8,128)(2,1)S(1)} collective-permute-done((bf16[5,128,128]{2,1,0:T(8,128)(2,1)S(1)}, bf16[5,128,128]{2,1,0:T(8,128)(2,1)S(1)}, u32[]{:S(2)}, u32[]{:S(2)}) %collective-permute-start.7) | collective-permute-done | bytes 163872 | tf_op jit(solution)/shard_map/ppermute | solution.py:427
  28.7 1.3 %delta.1 = (bf16[4,128,1536]{2,1,0:T(8,128)(2,1)S(1)}, bf16[128,1536]{1,0:T(8,128)(2,1)S(1)}, bf16[4,128,128]{2,1,0:T(8,128)(2,1)S(1)}) custom-call(s32[4,12]{1,0:T(4,128)S(1)} %get-tuple-element.41.table, f32[512,1536]{1,0:T(8,128)S(1)} %get-tuple-element.49.early, bf16[512,2048]{1,0:T(8,128)(2,1)S(1)} %get-tuple-element.48.rows, ...), custom_call_target="tpu_custom_call" | custom-call | flops 786432 | bytes 1572864 | tf_op jit(solution)/shard_map/delta/pallas_call | solution.py:216
  30.0 3.1 %collective-permute-start.15 = (bf16[128,1536]{1,0:T(8,128)(2,1)S(1)}, bf16[128,1536]{1,0:T(8,128)(2,1)S(1)}, u32[]{:S(2)}, u32[]{:S(2)}) collective-permute-start(bf16[128,1536]{1,0:T(8,128)(2,1)S(1)} %get-tuple-element.62), channel_id=1, source_target_pairs={{12,0},{0,4},{4,8},{8,12},{13,1},{1,5},{5,9},{9,13},{14,2},{2,6},{... | collective-permute-start | bytes 1179656 | tf_op jit(solution)/shard_map/ppermute | solution.py:427
  34.0 4.5 %partial.5 = (bf16[4,128,1024]{2,1,0:T(8,128)(2,1)S(1)}, bf16[128,1024]{1,0:T(8,128)(2,1)S(1)}) custom-call(s32[4,12]{1,0:T(4,128)S(1)} %get-tuple-element.41.table, bf16[3584,2048]{1,0:T(8,128)(2,1)} %weight.5, bf16[512,2048]{1,0:T(8,128)(2,1)S(1)} %get-tuple-element.48.rows, bf16[4,128,128]{2,1,0:T(8,128)(2,1)S(1)} %get-tuple-element.50.held), custom_call_target="tpu_custom_call" | custom-call | flops 2147483648 | bytes 4294967296 | tf_op jit(solution)/shard_map/partial/pallas_call | solution.py:249
  38.6 4.1 %collective-permute-done.15.arrived = bf16[128,1536]{1,0:T(8,128)(2,1)S(1)} collective-permute-done((bf16[128,1536]{1,0:T(8,128)(2,1)S(1)}, bf16[128,1536]{1,0:T(8,128)(2,1)S(1)}, u32[]{:S(2)}, u32[]{:S(2)}) %collective-permute-start.15) | collective-permute-done | bytes 393248 | tf_op jit(solution)/shard_map/ppermute | solution.py:427
  42.8 2.5 %collective-permute-start.16 = (bf16[128,1536]{1,0:T(8,128)(2,1)S(1)}, bf16[128,1536]{1,0:T(8,128)(2,1)S(1)}, u32[]{:S(2)}, u32[]{:S(2)}) collective-permute-start(bf16[128,1536]{1,0:T(8,128)(2,1)S(1)} %add.12), channel_id=1, source_target_pairs={{12,0},{0,4},{4,8},{8,12},{13,1},{1,5},{5,9},{9,13},{14,2},{2,6},{... | collective-permute-start | bytes 1179656 | tf_op jit(solution)/shard_map/ppermute | solution.py:427
  45.4 4.4 %partial.4 = (bf16[4,128,1024]{2,1,0:T(8,128)(2,1)S(1)}, bf16[128,1024]{1,0:T(8,128)(2,1)S(1)}) custom-call(s32[4,12]{1,0:T(4,128)S(1)} %get-tuple-element.41.table, bf16[3584,2048]{1,0:T(8,128)(2,1)} %weight.5, bf16[512,2048]{1,0:T(8,128)(2,1)S(1)} %get-tuple-element.48.rows, bf16[4,128,128]{2,1,0:T(8,128)(2,1)S(1)} %get-tuple-element.50.held), custom_call_target="tpu_custom_call" | custom-call | flops 2147483648 | bytes 4294967296 | tf_op jit(solution)/shard_map/partial/pallas_call | solution.py:249
  49.9 1.8 %collective-permute-done.12.arrived = bf16[128,1408]{1,0:T(8,128)(2,1)S(1)} collective-permute-done((bf16[128,1408]{1,0:T(8,128)(2,1)S(1)}, bf16[128,1408]{1,0:T(8,128)(2,1)S(1)}, u32[]{:S(2)}, u32[]{:S(2)}) %collective-permute-start.12) | collective-permute-done | bytes 360480 | tf_op jit(solution)/shard_map/ppermute | solution.py:427
  51.8 1.2 %collective-permute-start.13 = (bf16[128,1280]{1,0:T(8,128)(2,1)S(1)}, bf16[128,1280]{1,0:T(8,128)(2,1)S(1)}, u32[]{:S(2)}, u32[]{:S(2)}) collective-permute-start(bf16[128,1280]{1,0:T(8,128)(2,1)S(1)} %get-tuple-element.59), channel_id=1, source_target_pairs={{12,0},{0,4},{4,8},{8,12},{13,1},{1,5},{5,9},{9,13},{14,2},{2,6},{... | collective-permute-start | bytes 983048 | tf_op jit(solution)/shard_map/ppermute | solution.py:427
  53.1 12.7 %collective-permute-done.9.arrived = bf16[128,1024]{1,0:T(8,128)(2,1)S(1)} collective-permute-done((bf16[128,1024]{1,0:T(8,128)(2,1)S(1)}, bf16[128,1024]{1,0:T(8,128)(2,1)S(1)}, u32[]{:S(2)}, u32[]{:S(2)}) %collective-permute-start.9) | collective-permute-done | bytes 262176 | tf_op jit(solution)/shard_map/ppermute | solution.py:427
  67.3 5.5 %collective-permute-done.13.arrived = bf16[128,1280]{1,0:T(8,128)(2,1)S(1)} collective-permute-done((bf16[128,1280]{1,0:T(8,128)(2,1)S(1)}, bf16[128,1280]{1,0:T(8,128)(2,1)S(1)}, u32[]{:S(2)}, u32[]{:S(2)}) %collective-permute-start.13) | collective-permute-done | bytes 327712 | tf_op jit(solution)/shard_map/ppermute | solution.py:427
  74.1 4.3 %collective-permute-done.10.arrived = bf16[128,1024]{1,0:T(8,128)(2,1)S(1)} collective-permute-done((bf16[128,1024]{1,0:T(8,128)(2,1)S(1)}, bf16[128,1024]{1,0:T(8,128)(2,1)S(1)}, u32[]{:S(2)}, u32[]{:S(2)}) %collective-permute-start.10) | collective-permute-done | bytes 262176 | tf_op jit(solution)/shard_map/ppermute | solution.py:427
  79.8 7.1 %collective-permute-done.17.arrived = bf16[128,1536]{1,0:T(8,128)(2,1)S(1)} collective-permute-done((bf16[128,1536]{1,0:T(8,128)(2,1)S(1)}, bf16[128,1536]{1,0:T(8,128)(2,1)S(1)}, u32[]{:S(2)}, u32[]{:S(2)}) %collective-permute-start.17) | collective-permute-done | bytes 393248 | tf_op jit(solution)/shard_map/ppermute | solution.py:427
  87.7 5.5 %collective-permute-done.14.arrived.refs_3_ = bf16[128,1152]{1,0:T(8,128)(2,1)S(1)} collective-permute-done((bf16[128,1152]{1,0:T(8,128)(2,1)S(1)}, bf16[128,1152]{1,0:T(8,128)(2,1)S(1)}, u32[]{:S(2)}, u32[]{:S(2)}) %collective-permute-start.14) | collective-permute-done | bytes 294944 | tf_op jit(solution)/shard_map/ppermute | solution.py:427
  94.0 1.7 %adam.1 = (f32[4,128,128]{2,1,0:T(8,128)}, f32[4,128,128]{2,1,0:T(8,128)}, f32[4,128,128]{2,1,0:T(8,128)}) custom-call(s32[4,12]{1,0:T(4,128)S(1)} %get-tuple-element.41.table, bf16[128,128]{1,0:T(8,128)(2,1)S(1)} %get-tuple-element.63.refs_0_, bf16[128,128]{1,0:T(8,128)(2,1)S(1)} %get-tuple-element.64.refs_1_, ...), custom_call_target="tpu_custom_call" | custom-call | flops 65536 | bytes 131072 | tf_op jit(solution)/shard_map/adam/pallas_call | solution.py:413
  95.6 1.6 %collective-permute-done.11.arrived = bf16[128,1024]{1,0:T(8,128)(2,1)S(1)} collective-permute-done((bf16[128,1024]{1,0:T(8,128)(2,1)S(1)}, bf16[128,1024]{1,0:T(8,128)(2,1)S(1)}, u32[]{:S(2)}, u32[]{:S(2)}) %collective-permute-start.11) | collective-permute-done | bytes 262176 | tf_op jit(solution)/shard_map/ppermute | solution.py:427
  (38 shorter events, 12.3 us)
Async XLA Ops:
  0.6 8.4 %collective-permute-start.3 = (bf16[128,2048]{1,0:T(8,128)(2,1)}, bf16[128,2048]{1,0:T(8,128)(2,1)S(1)}, u32[]{:S(2)}, u32[]{:S(2)}) collective-permute-start(bf16[128,2048]{1,0:T(8,128)(2,1)} %own.1), channel_id=1, source_target_pairs={{1,0},{0,1},{3,2},{2,3},{5,4},{4,5},{7,6},{6,7},{9,8},{8,9},{11,10... | collective-permute-start | bytes 1572872 | tf_op jit(solution)/shard_map/ppermute | solution.py:438
  1.1 17.8 %collective-permute-start.4 = (bf16[128,2048]{1,0:T(8,128)(2,1)}, bf16[128,2048]{1,0:T(8,128)(2,1)S(1)}, u32[]{:S(2)}, u32[]{:S(2)}) collective-permute-start(bf16[128,2048]{1,0:T(8,128)(2,1)} %own.1), channel_id=1, source_target_pairs={{2,0},{0,2},{3,1},{1,3},{6,4},{4,6},{7,5},{5,7},{10,8},{8,10},{11,... | collective-permute-start | bytes 1572872 | tf_op jit(solution)/shard_map/ppermute | solution.py:427
  4.5 6.1 %collective-permute-start.2 = (s32[1,8]{1,0:T(1,128)S(1)}, s32[1,8]{1,0:T(1,128)S(1)}, u32[]{:S(2)}, u32[]{:S(2)}) collective-permute-start(s32[1,8]{1,0:T(1,128)S(1)} %pad_add_fusion.refs_0_), channel_id=1, source_target_pairs={{4,0},{8,4},{12,8},{0,12},{5,1},{9,5},{13,9},{1,13},{6,2},{10,6},{... | collective-permute-start | bytes 104 | tf_op jit(solution)/shard_map/ppermute | solution.py:427
  8.1 4.4 %collective-permute-start.1 = (s32[1,8]{1,0:T(1,128)S(1)}, s32[1,8]{1,0:T(1,128)S(1)}, u32[]{:S(2)}, u32[]{:S(2)}) collective-permute-start(s32[1,8]{1,0:T(1,128)S(1)} %pad_add_fusion.refs_0_), channel_id=1, source_target_pairs={{8,0},{12,4},{0,8},{4,12},{9,1},{13,5},{1,9},{5,13},{10,2},{14,6},... | collective-permute-start | bytes 104 | tf_op jit(solution)/shard_map/ppermute | solution.py:427
  8.1 5.3 %collective-permute-start = (s32[1,8]{1,0:T(1,128)S(1)}, s32[1,8]{1,0:T(1,128)S(1)}, u32[]{:S(2)}, u32[]{:S(2)}) collective-permute-start(s32[1,8]{1,0:T(1,128)S(1)} %pad_add_fusion.refs_0_), channel_id=1, source_target_pairs={{12,0},{0,4},{4,8},{8,12},{13,1},{1,5},{5,9},{9,13},{14,2},{2,6},{... | collective-permute-start | bytes 104 | tf_op jit(solution)/shard_map/ppermute | solution.py:427
  14.8 11.0 %collective-permute-start.6 = (bf16[5,128,128]{2,1,0:T(8,128)(2,1)S(1)}, bf16[5,128,128]{2,1,0:T(8,128)(2,1)S(1)}, u32[]{:S(2)}, u32[]{:S(2)}) collective-permute-start(bf16[5,128,128]{2,1,0:T(8,128)(2,1)S(1)} %get-tuple-element.44), channel_id=1, source_target_pairs={{12,0},{0,4},{4,8},{8,12},{13,1},{1,5},{5,9},{9,13},{14,2},{2,6},{... | collective-permute-start | bytes 491528 | tf_op jit(solution)/shard_map/ppermute | solution.py:427
  14.9 13.8 %collective-permute-start.7 = (bf16[5,128,128]{2,1,0:T(8,128)(2,1)S(1)}, bf16[5,128,128]{2,1,0:T(8,128)(2,1)S(1)}, u32[]{:S(2)}, u32[]{:S(2)}) collective-permute-start(bf16[5,128,128]{2,1,0:T(8,128)(2,1)S(1)} %get-tuple-element.45), channel_id=1, source_target_pairs={{8,0},{12,4},{0,8},{4,12},{9,1},{13,5},{1,9},{5,13},{10,2},{14,6},... | collective-permute-start | bytes 491528 | tf_op jit(solution)/shard_map/ppermute | solution.py:427
  16.1 12.6 %collective-permute-start.8 = (bf16[5,128,128]{2,1,0:T(8,128)(2,1)S(1)}, bf16[5,128,128]{2,1,0:T(8,128)(2,1)S(1)}, u32[]{:S(2)}, u32[]{:S(2)}) collective-permute-start(bf16[5,128,128]{2,1,0:T(8,128)(2,1)S(1)} %get-tuple-element.46), channel_id=1, source_target_pairs={{4,0},{8,4},{12,8},{0,12},{5,1},{9,5},{13,9},{1,13},{6,2},{10,6},{... | collective-permute-start | bytes 491528 | tf_op jit(solution)/shard_map/ppermute | solution.py:427
  18.9 2.8 %collective-permute-start.5 = (bf16[128,2048]{1,0:T(8,128)(2,1)S(1)}, bf16[128,2048]{1,0:T(8,128)(2,1)S(1)}, u32[]{:S(2)}, u32[]{:S(2)}) collective-permute-start(bf16[128,2048]{1,0:T(8,128)(2,1)S(1)} %collective-permute-done.4.refs_1_), channel_id=1, source_target_pairs={{1,0},{0,1},{3,2},{2,3},{5,4},{4,5},{7,6},{6,7},{9,8},{8,9},{11,10... | collective-permute-start | bytes 1572872 | tf_op jit(solution)/shard_map/ppermute | solution.py:427
  30.0 12.7 %collective-permute-start.15 = (bf16[128,1536]{1,0:T(8,128)(2,1)S(1)}, bf16[128,1536]{1,0:T(8,128)(2,1)S(1)}, u32[]{:S(2)}, u32[]{:S(2)}) collective-permute-start(bf16[128,1536]{1,0:T(8,128)(2,1)S(1)} %get-tuple-element.62), channel_id=1, source_target_pairs={{12,0},{0,4},{4,8},{8,12},{13,1},{1,5},{5,9},{9,13},{14,2},{2,6},{... | collective-permute-start | bytes 1179656 | tf_op jit(solution)/shard_map/ppermute | solution.py:427
  38.5 13.2 %collective-permute-start.12 = (bf16[128,1408]{1,0:T(8,128)(2,1)S(1)}, bf16[128,1408]{1,0:T(8,128)(2,1)S(1)}, u32[]{:S(2)}, u32[]{:S(2)}) collective-permute-start(bf16[128,1408]{1,0:T(8,128)(2,1)S(1)} %attach.1), channel_id=1, source_target_pairs={{12,0},{0,4},{4,8},{8,12},{13,1},{1,5},{5,9},{9,13},{14,2},{2,6},{... | collective-permute-start | bytes 1081352 | tf_op jit(solution)/shard_map/ppermute | solution.py:427
  42.8 24.3 %collective-permute-start.16 = (bf16[128,1536]{1,0:T(8,128)(2,1)S(1)}, bf16[128,1536]{1,0:T(8,128)(2,1)S(1)}, u32[]{:S(2)}, u32[]{:S(2)}) collective-permute-start(bf16[128,1536]{1,0:T(8,128)(2,1)S(1)} %add.12), channel_id=1, source_target_pairs={{12,0},{0,4},{4,8},{8,12},{13,1},{1,5},{5,9},{9,13},{14,2},{2,6},{... | collective-permute-start | bytes 1179656 | tf_op jit(solution)/shard_map/ppermute | solution.py:427
  49.8 16.0 %collective-permute-start.9 = (bf16[128,1024]{1,0:T(8,128)(2,1)S(1)}, bf16[128,1024]{1,0:T(8,128)(2,1)S(1)}, u32[]{:S(2)}, u32[]{:S(2)}) collective-permute-start(bf16[128,1024]{1,0:T(8,128)(2,1)S(1)} %get-tuple-element.52), channel_id=1, source_target_pairs={{12,0},{0,4},{4,8},{8,12},{13,1},{1,5},{5,9},{9,13},{14,2},{2,6},{... | collective-permute-start | bytes 786440 | tf_op jit(solution)/shard_map/ppermute | solution.py:427
  51.8 21.0 %collective-permute-start.13 = (bf16[128,1280]{1,0:T(8,128)(2,1)S(1)}, bf16[128,1280]{1,0:T(8,128)(2,1)S(1)}, u32[]{:S(2)}, u32[]{:S(2)}) collective-permute-start(bf16[128,1280]{1,0:T(8,128)(2,1)S(1)} %get-tuple-element.59), channel_id=1, source_target_pairs={{12,0},{0,4},{4,8},{8,12},{13,1},{1,5},{5,9},{9,13},{14,2},{2,6},{... | collective-permute-start | bytes 983048 | tf_op jit(solution)/shard_map/ppermute | solution.py:427
  65.9 12.6 %collective-permute-start.10 = (bf16[128,1024]{1,0:T(8,128)(2,1)S(1)}, bf16[128,1024]{1,0:T(8,128)(2,1)S(1)}, u32[]{:S(2)}, u32[]{:S(2)}) collective-permute-start(bf16[128,1024]{1,0:T(8,128)(2,1)S(1)} %add.8), channel_id=1, source_target_pairs={{12,0},{0,4},{4,8},{8,12},{13,1},{1,5},{5,9},{9,13},{14,2},{2,6},{... | collective-permute-start | bytes 786440 | tf_op jit(solution)/shard_map/ppermute | solution.py:427
  67.2 19.6 %collective-permute-start.17 = (bf16[128,1536]{1,0:T(8,128)(2,1)S(1)}, bf16[128,1536]{1,0:T(8,128)(2,1)S(1)}, u32[]{:S(2)}, u32[]{:S(2)}) collective-permute-start(bf16[128,1536]{1,0:T(8,128)(2,1)S(1)} %add.13), channel_id=1, source_target_pairs={{12,0},{0,4},{4,8},{8,12},{13,1},{1,5},{5,9},{9,13},{14,2},{2,6},{... | collective-permute-start | bytes 1179656 | tf_op jit(solution)/shard_map/ppermute | solution.py:427
  72.9 20.3 %collective-permute-start.14 = (bf16[128,1152]{1,0:T(8,128)(2,1)S(1)}, bf16[128,1152]{1,0:T(8,128)(2,1)S(1)}, u32[]{:S(2)}, u32[]{:S(2)}) collective-permute-start(bf16[128,1152]{1,0:T(8,128)(2,1)S(1)} %get-tuple-element.60), channel_id=1, source_target_pairs={{12,0},{0,4},{4,8},{8,12},{13,1},{1,5},{5,9},{9,13},{14,2},{2,6},{... | collective-permute-start | bytes 884744 | tf_op jit(solution)/shard_map/ppermute | solution.py:427
  78.5 15.5 %copy-start = (f32[1,1,4,128,128]{4,3,2,1,0:T(8,128)S(1)}, f32[1,1,4,128,128]{4,3,2,1,0:T(8,128)}, u32[]{:S(2)}) copy-start(f32[1,1,4,128,128]{4,3,2,1,0:T(8,128)} %param.13) | copy-start | bytes 786436
  78.5 15.5 %copy-start.1 = (f32[1,1,4,128,128]{4,3,2,1,0:T(8,128)S(1)}, f32[1,1,4,128,128]{4,3,2,1,0:T(8,128)}, u32[]{:S(2)}) copy-start(f32[1,1,4,128,128]{4,3,2,1,0:T(8,128)} %param.14) | copy-start | bytes 786436
  78.5 15.5 %copy-start.2 = (f32[1,1,4,128,128]{4,3,2,1,0:T(8,128)S(1)}, f32[1,1,4,128,128]{4,3,2,1,0:T(8,128)}, u32[]{:S(2)}) copy-start(f32[1,1,4,128,128]{4,3,2,1,0:T(8,128)} %param.15) | copy-start | bytes 786436
  78.5 18.7 %collective-permute-start.11 = (bf16[128,1024]{1,0:T(8,128)(2,1)S(1)}, bf16[128,1024]{1,0:T(8,128)(2,1)S(1)}, u32[]{:S(2)}, u32[]{:S(2)}) collective-permute-start(bf16[128,1024]{1,0:T(8,128)(2,1)S(1)} %add.9), channel_id=1, source_target_pairs={{12,0},{0,4},{4,8},{8,12},{13,1},{1,5},{5,9},{9,13},{14,2},{2,6},{... | collective-permute-start | bytes 786440 | tf_op jit(solution)/shard_map/ppermute | solution.py:427

commit v16 on v15

--- a/solution.py
+++ b/solution.py
@@ -19,7 +19,6 @@
 PARTS = (3, 2, 2)
 RIDE = 2
 LAST = 1
-LAID = 1
 NT = (((1,), (1,)), ((), ()))
 TN = (((0,), (0,)), ((), ()))
 
@@ -180,8 +179,8 @@
             first[:, here] = result
 
 
-def held_kernel(spans, slots, block, table, *refs):
-    stored, held = refs[:-1], refs[-1]
+def begin_kernel(spans, slots, block, table, early, rows, *refs):
+    stored, (first, held, total, chunk_rows) = refs[:spans], refs[spans:]
     me = lax.axis_index("seq")
     before = rank_before(table, 0, spans, slots)
     for j in range(slots):
@@ -191,38 +190,60 @@
             def _():
                 held[j] = stored[s][slots]
 
-
-def delta_kernel(sizes, low, stores, table, early, rows, *refs):
-    given, (out, first, *more, total) = refs[:stores], refs[stores:]
-    if stores > 1:
-        (held,) = more
-        held_kernel(*sizes, table, *given, held)
-    else:
-        (held,) = given
-    total[...] = early[:, low : low + total.shape[1]]
-    add_delta(table, rows, held, total, low)
-    put_chunks(total, out, first, pl.ds(0, total.shape[1]))
-
-
-def delta_call(sizes, low, high, table, early, rows, given):
+    chunk = first.shape[0]
+    for p in range(spans):
+
+        @pl.when(chunk_at(p) == wrap(me - 1, spans))
+        def _():
+            total[...] = early[p * chunk : (p + 1) * chunk]
+            chunk_rows[...] = rows[p * chunk : (p + 1) * chunk]
+
+    add_delta(table, chunk_rows, held, total, 0)
+    first[...] = total[...].astype(first.dtype)
+
+
+def begin_call(sizes, table, early, rows, stored):
     spans, slots, block = sizes
-    tokens, columns = early.shape[0], high - low
-    shapes = [
-        jax.ShapeDtypeStruct((spans, tokens // spans, columns), rows.dtype),
-        jax.ShapeDtypeStruct((tokens // spans, columns), rows.dtype),
-    ]
-    if len(given) > 1:
-        shapes.append(jax.ShapeDtypeStruct((slots, block, block), rows.dtype))
-    return pl.pallas_call(
-        functools.partial(delta_kernel, sizes, low, len(given)),
-        out_shape=shapes,
-        in_specs=[smem()] + [vmem()] * (2 + len(given)),
-        out_specs=[vmem()] * len(shapes),
+    (tokens, columns), d_width = early.shape, rows.shape[1]
+    chunk = tokens // spans
+    return pl.pallas_call(
+        functools.partial(begin_kernel, *sizes),
+        out_shape=[
+            jax.ShapeDtypeStruct((chunk, columns), rows.dtype),
+            jax.ShapeDtypeStruct((slots, block, block), rows.dtype),
+        ],
+        in_specs=[smem()] + [vmem()] * (2 + spans),
+        out_specs=[vmem()] * 2,
+        scratch_shapes=[
+            pltpu.VMEM((chunk, columns), jnp.float32),
+            pltpu.VMEM((chunk, d_width), rows.dtype),
+        ],
+        compiler_params=params(),
+        cost_estimate=cost(chunk * columns),
+        name="begin",
+    )(table, early, rows, *stored)
+
+
+def delta_kernel(table, early, rows, held, out, total):
+    total[...] = early[...]
+    add_delta(table, rows, held, total, 0)
+    chunk = out.shape[1]
+    for p in range(out.shape[0]):
+        out[chunk_at(p)] = total[p * chunk : (p + 1) * chunk].astype(out.dtype)
+
+
+def delta_call(spans, table, early, rows, held):
+    tokens, columns = early.shape
+    return pl.pallas_call(
+        delta_kernel,
+        out_shape=jax.ShapeDtypeStruct((spans, tokens // spans, columns), rows.dtype),
+        in_specs=[smem()] + [vmem()] * 3,
+        out_specs=vmem(),
         scratch_shapes=[pltpu.VMEM((tokens, columns), jnp.float32)],
         compiler_params=params(),
         cost_estimate=cost(early.size),
         name="delta",
-    )(table, early, rows, *given)
+    )(table, early, rows, held)
 
 
 def matmul_kernel(low, ends, table, weight, rows, held, *refs):
@@ -491,7 +512,7 @@
     )(*metas, values_half, hidden_here)
     crossed = exchange(picked)
 
-    laid = ranges[LAID - 1][1]
+    laid = ranges[0][1]
     first_weight = pl.pallas_call(
         lay_kernel,
         out_shape=jax.ShapeDtypeStruct((laid * width, d_width), down_weight.dtype),
@@ -508,18 +529,13 @@
     for first in firsts:
         remote += [first] + [take_from(first, "dp", d) for d in range(1, cores)]
     early, rows = early_matmul_call(width, laid * width, first_weight, [local_rows, *remote])
-    partials, moving, held = [], [], None
-    for part, (low, high) in enumerate(ranges):
-        if part < LAID:
-            given = [held] if part else crossed
-            partial, first, *more = delta_call(
-                sizes, low * width, high * width, table, early, rows, given
-            )
-            held = more[0] if more else held
-        else:
-            partial, first = matmul_call(
-                spans, low, (high - low,), width, table, down_weight, rows, held
-            )
+    first, held = begin_call(sizes, table, early, rows, crossed)
+    moving = [take_from(first, "seq", -1)]
+    partials = [delta_call(spans, table, early, rows, held)]
+    for part, (low, high) in enumerate(ranges[1:], 1):
+        partial, first = matmul_call(
+            spans, low, (high - low,), width, table, down_weight, rows, held
+        )
         if part == RIDE:
             grads = grad_call(sizes, table, rows, crossed)
             first = attach_call(first, grads[1:])

time: 97.9 us -> 97.9 us (level)
  waiting for transfers between devices: 48.4 us -> 47.2 us
    ppermute x17, waiting for transfers between devices: 48.4 us -> 47.2 us  [take_from(): lax.ppermute(array, axis, [((i + places) % size, i) for i in range(size)])]
    pallas_call x1 -> x2, Pallas kernels: 1.3 us -> 2.13 us  [the longest x1 1.15 us: delta_call(): pl.pallas_call(delta_kernel, out_shape=jax.ShapeDtypeStruct((spans, token...]
  transfers between devices with their start and end apart: 18 -> 18, of which waited for: 11 -> 11; matrix products, arithmetic and copies ran while one was open for 1% -> 1% of each run, Pallas kernels for 24% -> 25%
where the time goes in v16:
time: 97.9 us; the launch traced here: 97.6 us
  waiting for transfers between devices  47.2 us (48%)
  Pallas kernels  26.1 us (27%)
  starting transfers between devices  22.7 us (23%)
    ppermute x17, waiting for transfers between devices, take_from(): lax.ppermute(array, axis, [((i + places) % size, i) for i in range(size)])  47.2 us
    ppermute x17, starting transfers between devices, take_from(): lax.ppermute(array, axis, [((i + places) % size, i) for i in range(size)])  22.2 us
    pallas_call x2, Pallas kernels, matmul_call(): pl.pallas_call(functools.partial(matmul_kernel, low, ends), grid=(ends[-1...  8.88 us
    pallas_call x1, Pallas kernels, early_matmul_call(): pl.pallas_call(functools.partial(early_matmul_kernel, width), grid=(colum...  4.03 us
    pallas_call x1, Pallas kernels, per_device(): pl.pallas_call(lay_kernel, out_shape=jax.ShapeDtypeStruct((laid * width,...  2.79 us
    pallas_call x3, Pallas kernels, last_call(): pl.pallas_call(functools.partial(last_kernel, low), out_shape=shape, in_s...  2.41 us
  transfers between devices with their start and end apart: 18, of which 11 were waited for; matrix products, arithmetic and copies ran while one was open for 1% of the time, Pallas kernels for 25%

profile of v16, /device:TPU:0, one launch (start us, length us, event | category | flops | bytes accessed | tf_op | source)
XLA Modules:
  0.0 97.6 jit_solution(7328347830041950533)
XLA Ops:
  1.1 2.6 %collective-permute-start.4 = (bf16[128,2048]{1,0:T(8,128)(2,1)}, bf16[128,2048]{1,0:T(8,128)(2,1)S(1)}, u32[]{:S(2)}, u32[]{:S(2)}) collective-permute-start(bf16[128,2048]{1,0:T(8,128)(2,1)} %own.1), channel_id=1, source_target_pairs={{2,0},{0,2},{3,1},{1,3},{6,4},{4,6},{7,5},{5,7},{10,8},{8,10},{11,... | collective-permute-start | bytes 1572872 | tf_op jit(solution)/shard_map/ppermute | solution.py:448
  4.5 3.6 %collective-permute-start.2 = (s32[1,8]{1,0:T(1,128)S(1)}, s32[1,8]{1,0:T(1,128)S(1)}, u32[]{:S(2)}, u32[]{:S(2)}) collective-permute-start(s32[1,8]{1,0:T(1,128)S(1)} %pad_add_fusion.refs_0_), channel_id=1, source_target_pairs={{4,0},{8,4},{12,8},{0,12},{5,1},{9,5},{13,9},{1,13},{6,2},{10,6},{... | collective-permute-start | bytes 104 | tf_op jit(solution)/shard_map/ppermute | solution.py:448
  9.1 1.4 %early.1 = (bf16[4,128,128]{2,1,0:T(8,128)(2,1)S(1)}, bf16[128,3584]{1,0:T(8,128)(2,1)S(1)}, bf16[256,2048]{1,0:T(8,128)(2,1)S(1)}) custom-call(f32[4,128,128]{2,1,0:T(8,128)} %bitcast.8, bf16[128,3584]{1,0:T(8,128)(2,1)} %hidden.1, bf16[128,2048]{1,0:T(8,128)(2,1)} %own.1, bf16[128,2048]{1,0:T(8,128)(2,1)S(1)} %collective-permute-done.3.refs_0_), custom_call_target="tpu_custom_call" | custom-call | flops 458752 | bytes 917504 | tf_op jit(solution)/shard_map/early/pallas_call | solution.py:486
  10.5 2.0 %collective-permute-done.1.refs_2_ = s32[1,8]{1,0:T(1,128)S(1)} collective-permute-done((s32[1,8]{1,0:T(1,128)S(1)}, s32[1,8]{1,0:T(1,128)S(1)}, u32[]{:S(2)}, u32[]{:S(2)}) %collective-permute-start.1) | collective-permute-done | bytes 64 | tf_op jit(solution)/shard_map/ppermute | solution.py:448
  13.4 1.4 %pick.1 = (s32[4,12]{1,0:T(4,128)S(1)}, bf16[5,128,128]{2,1,0:T(8,128)(2,1)S(1)}, bf16[5,128,128]{2,1,0:T(8,128)(2,1)S(1)}, bf16[5,128,128]{2,1,0:T(8,128)(2,1)S(1)}, bf16[5,128,128]{2,1,0:T(8,128)(2,1)S(1)}) custom-call(s32[1,8]{1,0:T(1,128)S(1)} %pad_add_fusion.refs_0_, s32[1,8]{1,0:T(1,128)S(1)} %collective-permute-done.refs_1_, ...), custom_call_target="tpu_custom_call" | custom-call | flops 458752 | bytes 917504 | tf_op jit(solution)/shard_map/pick/pallas_call | solution.py:503
  16.1 2.8 %collective-permute-start.8 = (bf16[5,128,128]{2,1,0:T(8,128)(2,1)S(1)}, bf16[5,128,128]{2,1,0:T(8,128)(2,1)S(1)}, u32[]{:S(2)}, u32[]{:S(2)}) collective-permute-start(bf16[5,128,128]{2,1,0:T(8,128)(2,1)S(1)} %get-tuple-element.45), channel_id=1, source_target_pairs={{4,0},{8,4},{12,8},{0,12},{5,1},{9,5},{13,9},{1,13},{6,2},{10,6},{... | collective-permute-start | bytes 491528 | tf_op jit(solution)/shard_map/ppermute | solution.py:448
  18.9 2.8 %lay.1.weight = bf16[1536,2048]{1,0:T(8,128)(2,1)S(1)} custom-call(bf16[3584,2048]{1,0:T(8,128)(2,1)} %weight.5), custom_call_target="tpu_custom_call" | custom-call | flops 15728640000 | bytes 31457280000 | tf_op jit(solution)/shard_map/lay/pallas_call | solution.py:516
  21.7 4.0 %partial.3 = (f32[512,1536]{1,0:T(8,128)S(1)}, bf16[512,2048]{1,0:T(8,128)(2,1)S(1)}) custom-call(bf16[1536,2048]{1,0:T(8,128)(2,1)S(1)} %lay.1.weight, bf16[256,2048]{1,0:T(8,128)(2,1)S(1)} %get-tuple-element.41.refs_0_, bf16[128,2048]{1,0:T(8,128)(2,1)S(1)} %collective-permute-done.4.refs_1_, bf16[128,2048]{1,0:T(8,128)(2,1)S(1)} %collective-permute-done.5.refs_2_), custom_call_target="tpu_custom_call" | custom-call | flops 786432 | bytes 1572864 | tf_op jit(solution)/shard_map/partial/pallas_call | solution.py:140
  25.8 2.9 %collective-permute-done.7.refs_2_ = bf16[5,128,128]{2,1,0:T(8,128)(2,1)S(1)} collective-permute-done((bf16[5,128,128]{2,1,0:T(8,128)(2,1)S(1)}, bf16[5,128,128]{2,1,0:T(8,128)(2,1)S(1)}, u32[]{:S(2)}, u32[]{:S(2)}) %collective-permute-start.7) | collective-permute-done | bytes 163872 | tf_op jit(solution)/shard_map/ppermute | solution.py:448
  29.7 3.1 %collective-permute-start.15 = (bf16[128,1536]{1,0:T(8,128)(2,1)S(1)}, bf16[128,1536]{1,0:T(8,128)(2,1)S(1)}, u32[]{:S(2)}, u32[]{:S(2)}) collective-permute-start(bf16[128,1536]{1,0:T(8,128)(2,1)S(1)} %get-tuple-element.60), channel_id=1, source_target_pairs={{12,0},{0,4},{4,8},{8,12},{13,1},{1,5},{5,9},{9,13},{14,2},{2,6},{... | collective-permute-start | bytes 1179656 | tf_op jit(solution)/shard_map/ppermute | solution.py:448
  33.7 4.4 %partial.5 = (bf16[4,128,1024]{2,1,0:T(8,128)(2,1)S(1)}, bf16[128,1024]{1,0:T(8,128)(2,1)S(1)}) custom-call(s32[4,12]{1,0:T(4,128)S(1)} %get-tuple-element.40.table, bf16[3584,2048]{1,0:T(8,128)(2,1)} %weight.5, bf16[512,2048]{1,0:T(8,128)(2,1)S(1)} %get-tuple-element.47.rows, bf16[4,128,128]{2,1,0:T(8,128)(2,1)S(1)} %get-tuple-element.49.held), custom_call_target="tpu_custom_call" | custom-call | flops 2147483648 | bytes 4294967296 | tf_op jit(solution)/shard_map/partial/pallas_call | solution.py:270
  39.4 3.0 %collective-permute-done.15.arrived = bf16[128,1536]{1,0:T(8,128)(2,1)S(1)} collective-permute-done((bf16[128,1536]{1,0:T(8,128)(2,1)S(1)}, bf16[128,1536]{1,0:T(8,128)(2,1)S(1)}, u32[]{:S(2)}, u32[]{:S(2)}) %collective-permute-start.15) | collective-permute-done | bytes 393248 | tf_op jit(solution)/shard_map/ppermute | solution.py:448
  42.5 2.5 %collective-permute-start.16 = (bf16[128,1536]{1,0:T(8,128)(2,1)S(1)}, bf16[128,1536]{1,0:T(8,128)(2,1)S(1)}, u32[]{:S(2)}, u32[]{:S(2)}) collective-permute-start(bf16[128,1536]{1,0:T(8,128)(2,1)S(1)} %add.12), channel_id=1, source_target_pairs={{12,0},{0,4},{4,8},{8,12},{13,1},{1,5},{5,9},{9,13},{14,2},{2,6},{... | collective-permute-start | bytes 1179656 | tf_op jit(solution)/shard_map/ppermute | solution.py:448
  45.0 4.4 %partial.4 = (bf16[4,128,1024]{2,1,0:T(8,128)(2,1)S(1)}, bf16[128,1024]{1,0:T(8,128)(2,1)S(1)}) custom-call(s32[4,12]{1,0:T(4,128)S(1)} %get-tuple-element.40.table, bf16[3584,2048]{1,0:T(8,128)(2,1)} %weight.5, bf16[512,2048]{1,0:T(8,128)(2,1)S(1)} %get-tuple-element.47.rows, bf16[4,128,128]{2,1,0:T(8,128)(2,1)S(1)} %get-tuple-element.49.held), custom_call_target="tpu_custom_call" | custom-call | flops 2147483648 | bytes 4294967296 | tf_op jit(solution)/shard_map/partial/pallas_call | solution.py:270
  49.6 1.8 %collective-permute-done.12.arrived = bf16[128,1408]{1,0:T(8,128)(2,1)S(1)} collective-permute-done((bf16[128,1408]{1,0:T(8,128)(2,1)S(1)}, bf16[128,1408]{1,0:T(8,128)(2,1)S(1)}, u32[]{:S(2)}, u32[]{:S(2)}) %collective-permute-start.12) | collective-permute-done | bytes 360480 | tf_op jit(solution)/shard_map/ppermute | solution.py:448
  51.5 1.2 %collective-permute-start.13 = (bf16[128,1280]{1,0:T(8,128)(2,1)S(1)}, bf16[128,1280]{1,0:T(8,128)(2,1)S(1)}, u32[]{:S(2)}, u32[]{:S(2)}) collective-permute-start(bf16[128,1280]{1,0:T(8,128)(2,1)S(1)} %get-tuple-element.58), channel_id=1, source_target_pairs={{12,0},{0,4},{4,8},{8,12},{13,1},{1,5},{5,9},{9,13},{14,2},{2,6},{... | collective-permute-start | bytes 983048 | tf_op jit(solution)/shard_map/ppermute | solution.py:448
  52.7 12.7 %collective-permute-done.9.arrived = bf16[128,1024]{1,0:T(8,128)(2,1)S(1)} collective-permute-done((bf16[128,1024]{1,0:T(8,128)(2,1)S(1)}, bf16[128,1024]{1,0:T(8,128)(2,1)S(1)}, u32[]{:S(2)}, u32[]{:S(2)}) %collective-permute-start.9) | collective-permute-done | bytes 262176 | tf_op jit(solution)/shard_map/ppermute | solution.py:448
  65.5 1.2 %collective-permute-start.10 = (bf16[128,1024]{1,0:T(8,128)(2,1)S(1)}, bf16[128,1024]{1,0:T(8,128)(2,1)S(1)}, u32[]{:S(2)}, u32[]{:S(2)}) collective-permute-start(bf16[128,1024]{1,0:T(8,128)(2,1)S(1)} %add.8), channel_id=1, source_target_pairs={{12,0},{0,4},{4,8},{8,12},{13,1},{1,5},{5,9},{9,13},{14,2},{2,6},{... | collective-permute-start | bytes 786440 | tf_op jit(solution)/shard_map/ppermute | solution.py:448
  67.0 5.5 %collective-permute-done.13.arrived = bf16[128,1280]{1,0:T(8,128)(2,1)S(1)} collective-permute-done((bf16[128,1280]{1,0:T(8,128)(2,1)S(1)}, bf16[128,1280]{1,0:T(8,128)(2,1)S(1)}, u32[]{:S(2)}, u32[]{:S(2)}) %collective-permute-start.13) | collective-permute-done | bytes 327712 | tf_op jit(solution)/shard_map/ppermute | solution.py:448
  73.8 4.3 %collective-permute-done.10.arrived = bf16[128,1024]{1,0:T(8,128)(2,1)S(1)} collective-permute-done((bf16[128,1024]{1,0:T(8,128)(2,1)S(1)}, bf16[128,1024]{1,0:T(8,128)(2,1)S(1)}, u32[]{:S(2)}, u32[]{:S(2)}) %collective-permute-start.10) | collective-permute-done | bytes 262176 | tf_op jit(solution)/shard_map/ppermute | solution.py:448
  79.5 7.1 %collective-permute-done.17.arrived = bf16[128,1536]{1,0:T(8,128)(2,1)S(1)} collective-permute-done((bf16[128,1536]{1,0:T(8,128)(2,1)S(1)}, bf16[128,1536]{1,0:T(8,128)(2,1)S(1)}, u32[]{:S(2)}, u32[]{:S(2)}) %collective-permute-start.17) | collective-permute-done | bytes 393248 | tf_op jit(solution)/shard_map/ppermute | solution.py:448
  87.4 5.5 %collective-permute-done.14.arrived.refs_3_ = bf16[128,1152]{1,0:T(8,128)(2,1)S(1)} collective-permute-done((bf16[128,1152]{1,0:T(8,128)(2,1)S(1)}, bf16[128,1152]{1,0:T(8,128)(2,1)S(1)}, u32[]{:S(2)}, u32[]{:S(2)}) %collective-permute-start.14) | collective-permute-done | bytes 294944 | tf_op jit(solution)/shard_map/ppermute | solution.py:448
  93.7 1.7 %adam.1 = (f32[4,128,128]{2,1,0:T(8,128)}, f32[4,128,128]{2,1,0:T(8,128)}, f32[4,128,128]{2,1,0:T(8,128)}) custom-call(s32[4,12]{1,0:T(4,128)S(1)} %get-tuple-element.40.table, bf16[128,128]{1,0:T(8,128)(2,1)S(1)} %get-tuple-element.61.refs_0_, bf16[128,128]{1,0:T(8,128)(2,1)S(1)} %get-tuple-element.62.refs_1_, ...), custom_call_target="tpu_custom_call" | custom-call | flops 65536 | bytes 131072 | tf_op jit(solution)/shard_map/adam/pallas_call | solution.py:434
  95.3 1.5 %collective-permute-done.11.arrived = bf16[128,1024]{1,0:T(8,128)(2,1)S(1)} collective-permute-done((bf16[128,1024]{1,0:T(8,128)(2,1)S(1)}, bf16[128,1024]{1,0:T(8,128)(2,1)S(1)}, u32[]{:S(2)}, u32[]{:S(2)}) %collective-permute-start.11) | collective-permute-done | bytes 262176 | tf_op jit(solution)/shard_map/ppermute | solution.py:448
  (39 shorter events, 13.2 us)
Async XLA Ops:
  0.6 8.4 %collective-permute-start.3 = (bf16[128,2048]{1,0:T(8,128)(2,1)}, bf16[128,2048]{1,0:T(8,128)(2,1)S(1)}, u32[]{:S(2)}, u32[]{:S(2)}) collective-permute-start(bf16[128,2048]{1,0:T(8,128)(2,1)} %own.1), channel_id=1, source_target_pairs={{1,0},{0,1},{3,2},{2,3},{5,4},{4,5},{7,6},{6,7},{9,8},{8,9},{11,10... | collective-permute-start | bytes 1572872 | tf_op jit(solution)/shard_map/ppermute | solution.py:459
  1.1 17.8 %collective-permute-start.4 = (bf16[128,2048]{1,0:T(8,128)(2,1)}, bf16[128,2048]{1,0:T(8,128)(2,1)S(1)}, u32[]{:S(2)}, u32[]{:S(2)}) collective-permute-start(bf16[128,2048]{1,0:T(8,128)(2,1)} %own.1), channel_id=1, source_target_pairs={{2,0},{0,2},{3,1},{1,3},{6,4},{4,6},{7,5},{5,7},{10,8},{8,10},{11,... | collective-permute-start | bytes 1572872 | tf_op jit(solution)/shard_map/ppermute | solution.py:448
  4.5 6.1 %collective-permute-start.2 = (s32[1,8]{1,0:T(1,128)S(1)}, s32[1,8]{1,0:T(1,128)S(1)}, u32[]{:S(2)}, u32[]{:S(2)}) collective-permute-start(s32[1,8]{1,0:T(1,128)S(1)} %pad_add_fusion.refs_0_), channel_id=1, source_target_pairs={{4,0},{8,4},{12,8},{0,12},{5,1},{9,5},{13,9},{1,13},{6,2},{10,6},{... | collective-permute-start | bytes 104 | tf_op jit(solution)/shard_map/ppermute | solution.py:448
  8.1 4.4 %collective-permute-start.1 = (s32[1,8]{1,0:T(1,128)S(1)}, s32[1,8]{1,0:T(1,128)S(1)}, u32[]{:S(2)}, u32[]{:S(2)}) collective-permute-start(s32[1,8]{1,0:T(1,128)S(1)} %pad_add_fusion.refs_0_), channel_id=1, source_target_pairs={{8,0},{12,4},{0,8},{4,12},{9,1},{13,5},{1,9},{5,13},{10,2},{14,6},... | collective-permute-start | bytes 104 | tf_op jit(solution)/shard_map/ppermute | solution.py:448
  8.1 5.3 %collective-permute-start = (s32[1,8]{1,0:T(1,128)S(1)}, s32[1,8]{1,0:T(1,128)S(1)}, u32[]{:S(2)}, u32[]{:S(2)}) collective-permute-start(s32[1,8]{1,0:T(1,128)S(1)} %pad_add_fusion.refs_0_), channel_id=1, source_target_pairs={{12,0},{0,4},{4,8},{8,12},{13,1},{1,5},{5,9},{9,13},{14,2},{2,6},{... | collective-permute-start | bytes 104 | tf_op jit(solution)/shard_map/ppermute | solution.py:448
  14.8 11.0 %collective-permute-start.6 = (bf16[5,128,128]{2,1,0:T(8,128)(2,1)S(1)}, bf16[5,128,128]{2,1,0:T(8,128)(2,1)S(1)}, u32[]{:S(2)}, u32[]{:S(2)}) collective-permute-start(bf16[5,128,128]{2,1,0:T(8,128)(2,1)S(1)} %get-tuple-element.43), channel_id=1, source_target_pairs={{12,0},{0,4},{4,8},{8,12},{13,1},{1,5},{5,9},{9,13},{14,2},{2,6},{... | collective-permute-start | bytes 491528 | tf_op jit(solution)/shard_map/ppermute | solution.py:448
  14.9 13.8 %collective-permute-start.7 = (bf16[5,128,128]{2,1,0:T(8,128)(2,1)S(1)}, bf16[5,128,128]{2,1,0:T(8,128)(2,1)S(1)}, u32[]{:S(2)}, u32[]{:S(2)}) collective-permute-start(bf16[5,128,128]{2,1,0:T(8,128)(2,1)S(1)} %get-tuple-element.44), channel_id=1, source_target_pairs={{8,0},{12,4},{0,8},{4,12},{9,1},{13,5},{1,9},{5,13},{10,2},{14,6},... | collective-permute-start | bytes 491528 | tf_op jit(solution)/shard_map/ppermute | solution.py:448
  16.1 12.6 %collective-permute-start.8 = (bf16[5,128,128]{2,1,0:T(8,128)(2,1)S(1)}, bf16[5,128,128]{2,1,0:T(8,128)(2,1)S(1)}, u32[]{:S(2)}, u32[]{:S(2)}) collective-permute-start(bf16[5,128,128]{2,1,0:T(8,128)(2,1)S(1)} %get-tuple-element.45), channel_id=1, source_target_pairs={{4,0},{8,4},{12,8},{0,12},{5,1},{9,5},{13,9},{1,13},{6,2},{10,6},{... | collective-permute-start | bytes 491528 | tf_op jit(solution)/shard_map/ppermute | solution.py:448
  18.9 2.8 %collective-permute-start.5 = (bf16[128,2048]{1,0:T(8,128)(2,1)S(1)}, bf16[128,2048]{1,0:T(8,128)(2,1)S(1)}, u32[]{:S(2)}, u32[]{:S(2)}) collective-permute-start(bf16[128,2048]{1,0:T(8,128)(2,1)S(1)} %collective-permute-done.4.refs_1_), channel_id=1, source_target_pairs={{1,0},{0,1},{3,2},{2,3},{5,4},{4,5},{7,6},{6,7},{9,8},{8,9},{11,10... | collective-permute-start | bytes 1572872 | tf_op jit(solution)/shard_map/ppermute | solution.py:448
  29.7 12.7 %collective-permute-start.15 = (bf16[128,1536]{1,0:T(8,128)(2,1)S(1)}, bf16[128,1536]{1,0:T(8,128)(2,1)S(1)}, u32[]{:S(2)}, u32[]{:S(2)}) collective-permute-start(bf16[128,1536]{1,0:T(8,128)(2,1)S(1)} %get-tuple-element.60), channel_id=1, source_target_pairs={{12,0},{0,4},{4,8},{8,12},{13,1},{1,5},{5,9},{9,13},{14,2},{2,6},{... | collective-permute-start | bytes 1179656 | tf_op jit(solution)/shard_map/ppermute | solution.py:448
  38.2 13.2 %collective-permute-start.12 = (bf16[128,1408]{1,0:T(8,128)(2,1)S(1)}, bf16[128,1408]{1,0:T(8,128)(2,1)S(1)}, u32[]{:S(2)}, u32[]{:S(2)}) collective-permute-start(bf16[128,1408]{1,0:T(8,128)(2,1)S(1)} %attach.1), channel_id=1, source_target_pairs={{12,0},{0,4},{4,8},{8,12},{13,1},{1,5},{5,9},{9,13},{14,2},{2,6},{... | collective-permute-start | bytes 1081352 | tf_op jit(solution)/shard_map/ppermute | solution.py:448
  42.5 24.3 %collective-permute-start.16 = (bf16[128,1536]{1,0:T(8,128)(2,1)S(1)}, bf16[128,1536]{1,0:T(8,128)(2,1)S(1)}, u32[]{:S(2)}, u32[]{:S(2)}) collective-permute-start(bf16[128,1536]{1,0:T(8,128)(2,1)S(1)} %add.12), channel_id=1, source_target_pairs={{12,0},{0,4},{4,8},{8,12},{13,1},{1,5},{5,9},{9,13},{14,2},{2,6},{... | collective-permute-start | bytes 1179656 | tf_op jit(solution)/shard_map/ppermute | solution.py:448
  49.5 16.0 %collective-permute-start.9 = (bf16[128,1024]{1,0:T(8,128)(2,1)S(1)}, bf16[128,1024]{1,0:T(8,128)(2,1)S(1)}, u32[]{:S(2)}, u32[]{:S(2)}) collective-permute-start(bf16[128,1024]{1,0:T(8,128)(2,1)S(1)} %get-tuple-element.51), channel_id=1, source_target_pairs={{12,0},{0,4},{4,8},{8,12},{13,1},{1,5},{5,9},{9,13},{14,2},{2,6},{... | collective-permute-start | bytes 786440 | tf_op jit(solution)/shard_map/ppermute | solution.py:448
  51.5 21.0 %collective-permute-start.13 = (bf16[128,1280]{1,0:T(8,128)(2,1)S(1)}, bf16[128,1280]{1,0:T(8,128)(2,1)S(1)}, u32[]{:S(2)}, u32[]{:S(2)}) collective-permute-start(bf16[128,1280]{1,0:T(8,128)(2,1)S(1)} %get-tuple-element.58), channel_id=1, source_target_pairs={{12,0},{0,4},{4,8},{8,12},{13,1},{1,5},{5,9},{9,13},{14,2},{2,6},{... | collective-permute-start | bytes 983048 | tf_op jit(solution)/shard_map/ppermute | solution.py:448
  65.5 12.6 %collective-permute-start.10 = (bf16[128,1024]{1,0:T(8,128)(2,1)S(1)}, bf16[128,1024]{1,0:T(8,128)(2,1)S(1)}, u32[]{:S(2)}, u32[]{:S(2)}) collective-permute-start(bf16[128,1024]{1,0:T(8,128)(2,1)S(1)} %add.8), channel_id=1, source_target_pairs={{12,0},{0,4},{4,8},{8,12},{13,1},{1,5},{5,9},{9,13},{14,2},{2,6},{... | collective-permute-start | bytes 786440 | tf_op jit(solution)/shard_map/ppermute | solution.py:448
  66.9 19.6 %collective-permute-start.17 = (bf16[128,1536]{1,0:T(8,128)(2,1)S(1)}, bf16[128,1536]{1,0:T(8,128)(2,1)S(1)}, u32[]{:S(2)}, u32[]{:S(2)}) collective-permute-start(bf16[128,1536]{1,0:T(8,128)(2,1)S(1)} %add.13), channel_id=1, source_target_pairs={{12,0},{0,4},{4,8},{8,12},{13,1},{1,5},{5,9},{9,13},{14,2},{2,6},{... | collective-permute-start | bytes 1179656 | tf_op jit(solution)/shard_map/ppermute | solution.py:448
  72.6 20.3 %collective-permute-start.14 = (bf16[128,1152]{1,0:T(8,128)(2,1)S(1)}, bf16[128,1152]{1,0:T(8,128)(2,1)S(1)}, u32[]{:S(2)}, u32[]{:S(2)}) collective-permute-start(bf16[128,1152]{1,0:T(8,128)(2,1)S(1)} %get-tuple-element.59), channel_id=1, source_target_pairs={{12,0},{0,4},{4,8},{8,12},{13,1},{1,5},{5,9},{9,13},{14,2},{2,6},{... | collective-permute-start | bytes 884744 | tf_op jit(solution)/shard_map/ppermute | solution.py:448
  78.2 15.5 %copy-start = (f32[1,1,4,128,128]{4,3,2,1,0:T(8,128)S(1)}, f32[1,1,4,128,128]{4,3,2,1,0:T(8,128)}, u32[]{:S(2)}) copy-start(f32[1,1,4,128,128]{4,3,2,1,0:T(8,128)} %param.13) | copy-start | bytes 786436
  78.2 15.5 %copy-start.1 = (f32[1,1,4,128,128]{4,3,2,1,0:T(8,128)S(1)}, f32[1,1,4,128,128]{4,3,2,1,0:T(8,128)}, u32[]{:S(2)}) copy-start(f32[1,1,4,128,128]{4,3,2,1,0:T(8,128)} %param.14) | copy-start | bytes 786436
  78.2 15.5 %copy-start.2 = (f32[1,1,4,128,128]{4,3,2,1,0:T(8,128)S(1)}, f32[1,1,4,128,128]{4,3,2,1,0:T(8,128)}, u32[]{:S(2)}) copy-start(f32[1,1,4,128,128]{4,3,2,1,0:T(8,128)} %param.15) | copy-start | bytes 786436
  78.2 18.6 %collective-permute-start.11 = (bf16[128,1024]{1,0:T(8,128)(2,1)S(1)}, bf16[128,1024]{1,0:T(8,128)(2,1)S(1)}, u32[]{:S(2)}, u32[]{:S(2)}) collective-permute-start(bf16[128,1024]{1,0:T(8,128)(2,1)S(1)} %add.9), channel_id=1, source_target_pairs={{12,0},{0,4},{4,8},{8,12},{13,1},{1,5},{5,9},{9,13},{14,2},{2,6},{... | collective-permute-start | bytes 786440 | tf_op jit(solution)/shard_map/ppermute | solution.py:448

commit v17 on v16

--- a/solution.py
+++ b/solution.py
@@ -85,14 +85,19 @@
     copies[2].wait()
 
 
+def table_kernel(slots, d_blocks, *refs):
+    metas, table = refs[:-1], refs[-1]
+    for s, meta in enumerate(metas):
+        for j in range(slots):
+            table[s, j] = lax.div(meta[0, j], d_blocks)
+            table[s, slots + j] = lax.rem(meta[0, j], d_blocks)
+            table[s, 2 * slots + j] = meta[0, slots + j]
+
+
 def pick_kernel(spans, slots, block, d_blocks, *refs):
-    metas, (values, hidden, table), outs = refs[:spans], refs[spans : spans + 3], refs[spans + 3 :]
+    metas, (values, hidden), outs, table = refs[:spans], refs[spans : spans + 2], refs[spans + 2 : -1], refs[-1]
     me = lax.axis_index("seq")
-    for s in range(spans):
-        for j in range(slots):
-            table[s, j] = lax.div(metas[s][0, j], d_blocks)
-            table[s, slots + j] = lax.rem(metas[s][0, j], d_blocks)
-            table[s, 2 * slots + j] = metas[s][0, slots + j]
+    table_kernel(slots, d_blocks, *metas, table)
     for s in range(spans):
         row = (spans - s) % spans
         before = rank_before(table, row, spans, slots)
@@ -332,14 +337,19 @@
 
 
 def last_kernel(low, partials, arrived, *refs):
-    out, total, sem = refs[-3:]
-    columns = total.shape[1]
-    result = partials[lax.axis_index("seq")].astype(jnp.float32)
-    result = result + arrived[:, :columns].astype(jnp.float32)
-    total[...] = result.astype(out.dtype)
-    copy = pltpu.make_async_copy(total, out.at[:, pl.ds(low, columns)], sem)
-    copy.start()
-    copy.wait()
+    out, total, sems = refs[-3:]
+    me, columns = lax.axis_index("seq"), total.shape[1]
+    middle, copies = columns // 256 * 128, []
+    for k, here in enumerate((slice(0, middle), slice(middle, columns))):
+        result = partials[me, :, here].astype(jnp.float32) + arrived[:, here].astype(jnp.float32)
+        total[:, here] = result.astype(out.dtype)
+        copy = pltpu.make_async_copy(
+            total.at[:, here], out.at[:, pl.ds(low + here.start, here.stop - here.start)], sems.at[k]
+        )
+        copy.start()
+        copies.append(copy)
+    for copy in copies:
+        copy.wait()
 
 
 def last_call(low, partials, arrived, out, shape):
@@ -350,7 +360,10 @@
         out_shape=shape,
         in_specs=[vmem()] * 2 + [hbm()] * len(given),
         out_specs=hbm(),
-        scratch_shapes=[pltpu.VMEM((chunk, columns), shape.dtype), pltpu.SemaphoreType.DMA],
+        scratch_shapes=[
+            pltpu.VMEM((chunk, columns), shape.dtype),
+            pltpu.SemaphoreType.DMA((2,)),
+        ],
         input_output_aliases={2: 0} if given else {},
         compiler_params=params(),
         cost_estimate=cost(partials.size),
@@ -500,12 +513,12 @@
         cost_estimate=cost(hidden_in.size),
         name="early",
     )(stay(values[0, 0]), stay(hidden_in), stay(cotangent), *local)
-    table, *picked = pl.pallas_call(
+    picked = pl.pallas_call(
         functools.partial(pick_kernel, *sizes, d_blocks),
-        out_shape=[jax.ShapeDtypeStruct((spans, 3 * slots), jnp.int32)]
-        + [jax.ShapeDtypeStruct((slots + 1, chunk, block), jnp.bfloat16)] * spans,
+        out_shape=[jax.ShapeDtypeStruct((slots + 1, chunk, block), jnp.bfloat16)] * spans,
         in_specs=[smem()] * spans + [vmem(), vmem()],
-        out_specs=[smem()] + [vmem()] * spans,
+        out_specs=[vmem()] * spans,
+        scratch_shapes=[pltpu.SMEM((spans, 3 * slots), jnp.int32)],
         compiler_params=params(),
         cost_estimate=cost(hidden_in.size),
         name="pick",
@@ -528,6 +541,17 @@
     remote = []
     for first in firsts:
         remote += [first] + [take_from(first, "dp", d) for d in range(1, cores)]
+    metas, first_weight = lax.optimization_barrier((metas, first_weight))
+    table = pl.pallas_call(
+        functools.partial(table_kernel, slots, d_blocks),
+        out_shape=jax.ShapeDtypeStruct((spans, 3 * slots), jnp.int32),
+        in_specs=[smem()] * spans,
+        out_specs=smem(),
+        compiler_params=params(),
+        cost_estimate=cost(spans * slots),
+        name="table",
+    )(*metas)
+
     early, rows = early_matmul_call(width, laid * width, first_weight, [local_rows, *remote])
     first, held = begin_call(sizes, table, early, rows, crossed)
     moving = [take_from(first, "seq", -1)]

time: 97.9 us -> 97.3 us (level)
    pallas_call x0 -> x1, Pallas kernels: none -> 1.24 us  [per_device(): pl.pallas_call(functools.partial(table_kernel, slots, d_blocks), out_shap...]
where the time goes in v17:
time: 97.3 us; the launch traced here: 97.7 us
  waiting for transfers between devices  46.6 us (48%)
  Pallas kernels  26.5 us (27%)
  starting transfers between devices  23 us (24%)
    ppermute x17, waiting for transfers between devices, take_from(): lax.ppermute(array, axis, [((i + places) % size, i) for i in range(size)])  46.6 us
    ppermute x17, starting transfers between devices, take_from(): lax.ppermute(array, axis, [((i + places) % size, i) for i in range(size)])  22.5 us
    pallas_call x2, Pallas kernels, matmul_call(): pl.pallas_call(functools.partial(matmul_kernel, low, ends), grid=(ends[-1...  9.05 us
    pallas_call x1, Pallas kernels, early_matmul_call(): pl.pallas_call(functools.partial(early_matmul_kernel, width), grid=(colum...  4.04 us
    pallas_call x1, Pallas kernels, per_device(): pl.pallas_call(lay_kernel, out_shape=jax.ShapeDtypeStruct((laid * width,...  2.79 us
    pallas_call x3, Pallas kernels, last_call(): pl.pallas_call(functools.partial(last_kernel, low), out_shape=shape, in_s...  2.32 us
  transfers between devices with their start and end apart: 18, of which 11 were waited for; matrix products, arithmetic and copies ran while one was open for 1% of the time, Pallas kernels for 25%

profile of v17, /device:TPU:0, one launch (start us, length us, event | category | flops | bytes accessed | tf_op | source)
XLA Modules:
  0.0 97.7 jit_solution(10244327313241914272)
XLA Ops:
  1.1 2.6 %collective-permute-start.4 = (bf16[128,2048]{1,0:T(8,128)(2,1)}, bf16[128,2048]{1,0:T(8,128)(2,1)S(1)}, u32[]{:S(2)}, u32[]{:S(2)}) collective-permute-start(bf16[128,2048]{1,0:T(8,128)(2,1)} %own.1), channel_id=1, source_target_pairs={{2,0},{0,2},{3,1},{1,3},{6,4},{4,6},{7,5},{5,7},{10,8},{8,10},{11,... | collective-permute-start | bytes 1572872 | tf_op jit(solution)/shard_map/ppermute | solution.py:461
  4.5 3.6 %collective-permute-start.2 = (s32[1,8]{1,0:T(1,128)S(1)}, s32[1,8]{1,0:T(1,128)S(1)}, u32[]{:S(2)}, u32[]{:S(2)}) collective-permute-start(s32[1,8]{1,0:T(1,128)S(1)} %pad_add_fusion.refs_0_), channel_id=1, source_target_pairs={{4,0},{8,4},{12,8},{0,12},{5,1},{9,5},{13,9},{1,13},{6,2},{10,6},{... | collective-permute-start | bytes 104 | tf_op jit(solution)/shard_map/ppermute | solution.py:461
  9.1 1.4 %early.1 = (bf16[4,128,128]{2,1,0:T(8,128)(2,1)S(1)}, bf16[128,3584]{1,0:T(8,128)(2,1)S(1)}, bf16[256,2048]{1,0:T(8,128)(2,1)S(1)}) custom-call(f32[4,128,128]{2,1,0:T(8,128)} %bitcast.8, bf16[128,3584]{1,0:T(8,128)(2,1)} %hidden.1, bf16[128,2048]{1,0:T(8,128)(2,1)} %own.1, bf16[128,2048]{1,0:T(8,128)(2,1)S(1)} %collective-permute-done.3.refs_0_), custom_call_target="tpu_custom_call" | custom-call | flops 458752 | bytes 917504 | tf_op jit(solution)/shard_map/early/pallas_call | solution.py:499
  10.5 2.0 %collective-permute-done.1.refs_2_ = s32[1,8]{1,0:T(1,128)S(1)} collective-permute-done((s32[1,8]{1,0:T(1,128)S(1)}, s32[1,8]{1,0:T(1,128)S(1)}, u32[]{:S(2)}, u32[]{:S(2)}) %collective-permute-start.1) | collective-permute-done | bytes 64 | tf_op jit(solution)/shard_map/ppermute | solution.py:461
  14.2 1.2 %collective-permute-start.7 = (bf16[5,128,128]{2,1,0:T(8,128)(2,1)S(1)}, bf16[5,128,128]{2,1,0:T(8,128)(2,1)S(1)}, u32[]{:S(2)}, u32[]{:S(2)}) collective-permute-start(bf16[5,128,128]{2,1,0:T(8,128)(2,1)S(1)} %get-tuple-element.52), channel_id=1, source_target_pairs={{8,0},{12,4},{0,8},{4,12},{9,1},{13,5},{1,9},{5,13},{10,2},{14,6},... | collective-permute-start | bytes 491528 | tf_op jit(solution)/shard_map/ppermute | solution.py:461
  15.4 2.8 %collective-permute-start.8 = (bf16[5,128,128]{2,1,0:T(8,128)(2,1)S(1)}, bf16[5,128,128]{2,1,0:T(8,128)(2,1)S(1)}, u32[]{:S(2)}, u32[]{:S(2)}) collective-permute-start(bf16[5,128,128]{2,1,0:T(8,128)(2,1)S(1)} %get-tuple-element.53), channel_id=1, source_target_pairs={{4,0},{8,4},{12,8},{0,12},{5,1},{9,5},{13,9},{1,13},{6,2},{10,6},{... | collective-permute-start | bytes 491528 | tf_op jit(solution)/shard_map/ppermute | solution.py:461
  18.3 2.8 %lay.1.weight = bf16[1536,2048]{1,0:T(8,128)(2,1)S(1)} custom-call(bf16[3584,2048]{1,0:T(8,128)(2,1)} %weight.5), custom_call_target="tpu_custom_call" | custom-call | flops 15728640000 | bytes 31457280000 | tf_op jit(solution)/shard_map/lay/pallas_call | solution.py:529
  21.1 1.2 %table.1 = s32[4,12]{1,0:T(4,128)S(1)} custom-call(s32[1,8]{1,0:T(1,128)S(1)} %pad_add_fusion.refs_0_, s32[1,8]{1,0:T(1,128)S(1)} %collective-permute-done.refs_1_, s32[1,8]{1,0:T(1,128)S(1)} %collective-permute-done.1.refs_2_, s32[1,8]{1,0:T(1,128)S(1)} %collective-permute-done.2.refs_3_), custom_call_target="tpu_custom_call" | custom-call | flops 16 | bytes 32 | tf_op jit(solution)/shard_map/table/pallas_call | solution.py:545
  22.3 4.0 %partial.3 = (f32[512,1536]{1,0:T(8,128)S(1)}, bf16[512,2048]{1,0:T(8,128)(2,1)S(1)}) custom-call(bf16[1536,2048]{1,0:T(8,128)(2,1)S(1)} %lay.1.weight, bf16[256,2048]{1,0:T(8,128)(2,1)S(1)} %get-tuple-element.47.refs_0_, bf16[128,2048]{1,0:T(8,128)(2,1)S(1)} %collective-permute-done.4.refs_1_, bf16[128,2048]{1,0:T(8,128)(2,1)S(1)} %collective-permute-done.5.refs_2_), custom_call_target="tpu_custom_call" | custom-call | flops 786432 | bytes 1572864 | tf_op jit(solution)/shard_map/partial/pallas_call | solution.py:145
  26.4 1.7 %collective-permute-done.7.refs_2_ = bf16[5,128,128]{2,1,0:T(8,128)(2,1)S(1)} collective-permute-done((bf16[5,128,128]{2,1,0:T(8,128)(2,1)S(1)}, bf16[5,128,128]{2,1,0:T(8,128)(2,1)S(1)}, u32[]{:S(2)}, u32[]{:S(2)}) %collective-permute-start.7) | collective-permute-done | bytes 163872 | tf_op jit(solution)/shard_map/ppermute | solution.py:461
  28.9 3.4 %collective-permute-start.15 = (bf16[128,1536]{1,0:T(8,128)(2,1)S(1)}, bf16[128,1536]{1,0:T(8,128)(2,1)S(1)}, u32[]{:S(2)}, u32[]{:S(2)}) collective-permute-start(bf16[128,1536]{1,0:T(8,128)(2,1)S(1)} %get-tuple-element.68), channel_id=1, source_target_pairs={{12,0},{0,4},{4,8},{8,12},{13,1},{1,5},{5,9},{9,13},{14,2},{2,6},{... | collective-permute-start | bytes 1179656 | tf_op jit(solution)/shard_map/ppermute | solution.py:461
  33.2 4.6 %partial.5 = (bf16[4,128,1024]{2,1,0:T(8,128)(2,1)S(1)}, bf16[128,1024]{1,0:T(8,128)(2,1)S(1)}) custom-call(s32[4,12]{1,0:T(4,128)S(1)} %table.1, bf16[3584,2048]{1,0:T(8,128)(2,1)} %weight.5, bf16[512,2048]{1,0:T(8,128)(2,1)S(1)} %get-tuple-element.55.rows, bf16[4,128,128]{2,1,0:T(8,128)(2,1)S(1)} %get-tuple-element.57.held), custom_call_target="tpu_custom_call" | custom-call | flops 2147483648 | bytes 4294967296 | tf_op jit(solution)/shard_map/partial/pallas_call | solution.py:275
  39.4 2.5 %collective-permute-done.15.arrived = bf16[128,1536]{1,0:T(8,128)(2,1)S(1)} collective-permute-done((bf16[128,1536]{1,0:T(8,128)(2,1)S(1)}, bf16[128,1536]{1,0:T(8,128)(2,1)S(1)}, u32[]{:S(2)}, u32[]{:S(2)}) %collective-permute-start.15) | collective-permute-done | bytes 393248 | tf_op jit(solution)/shard_map/ppermute | solution.py:461
  42.0 2.5 %collective-permute-start.16 = (bf16[128,1536]{1,0:T(8,128)(2,1)S(1)}, bf16[128,1536]{1,0:T(8,128)(2,1)S(1)}, u32[]{:S(2)}, u32[]{:S(2)}) collective-permute-start(bf16[128,1536]{1,0:T(8,128)(2,1)S(1)} %add.12), channel_id=1, source_target_pairs={{12,0},{0,4},{4,8},{8,12},{13,1},{1,5},{5,9},{9,13},{14,2},{2,6},{... | collective-permute-start | bytes 1179656 | tf_op jit(solution)/shard_map/ppermute | solution.py:461
  44.5 4.4 %partial.4 = (bf16[4,128,1024]{2,1,0:T(8,128)(2,1)S(1)}, bf16[128,1024]{1,0:T(8,128)(2,1)S(1)}) custom-call(s32[4,12]{1,0:T(4,128)S(1)} %table.1, bf16[3584,2048]{1,0:T(8,128)(2,1)} %weight.5, bf16[512,2048]{1,0:T(8,128)(2,1)S(1)} %get-tuple-element.55.rows, bf16[4,128,128]{2,1,0:T(8,128)(2,1)S(1)} %get-tuple-element.57.held), custom_call_target="tpu_custom_call" | custom-call | flops 2147483648 | bytes 4294967296 | tf_op jit(solution)/shard_map/partial/pallas_call | solution.py:275
  49.1 2.0 %collective-permute-done.12.arrived = bf16[128,1408]{1,0:T(8,128)(2,1)S(1)} collective-permute-done((bf16[128,1408]{1,0:T(8,128)(2,1)S(1)}, bf16[128,1408]{1,0:T(8,128)(2,1)S(1)}, u32[]{:S(2)}, u32[]{:S(2)}) %collective-permute-start.12) | collective-permute-done | bytes 360480 | tf_op jit(solution)/shard_map/ppermute | solution.py:461
  51.1 1.1 %collective-permute-start.13 = (bf16[128,1280]{1,0:T(8,128)(2,1)S(1)}, bf16[128,1280]{1,0:T(8,128)(2,1)S(1)}, u32[]{:S(2)}, u32[]{:S(2)}) collective-permute-start(bf16[128,1280]{1,0:T(8,128)(2,1)S(1)} %get-tuple-element.66), channel_id=1, source_target_pairs={{12,0},{0,4},{4,8},{8,12},{13,1},{1,5},{5,9},{9,13},{14,2},{2,6},{... | collective-permute-start | bytes 983048 | tf_op jit(solution)/shard_map/ppermute | solution.py:461
  52.2 12.8 %collective-permute-done.9.arrived = bf16[128,1024]{1,0:T(8,128)(2,1)S(1)} collective-permute-done((bf16[128,1024]{1,0:T(8,128)(2,1)S(1)}, bf16[128,1024]{1,0:T(8,128)(2,1)S(1)}, u32[]{:S(2)}, u32[]{:S(2)}) %collective-permute-start.9) | collective-permute-done | bytes 262176 | tf_op jit(solution)/shard_map/ppermute | solution.py:461
  66.5 5.6 %collective-permute-done.13.arrived = bf16[128,1280]{1,0:T(8,128)(2,1)S(1)} collective-permute-done((bf16[128,1280]{1,0:T(8,128)(2,1)S(1)}, bf16[128,1280]{1,0:T(8,128)(2,1)S(1)}, u32[]{:S(2)}, u32[]{:S(2)}) %collective-permute-start.13) | collective-permute-done | bytes 327712 | tf_op jit(solution)/shard_map/ppermute | solution.py:461
  73.3 4.4 %collective-permute-done.10.arrived = bf16[128,1024]{1,0:T(8,128)(2,1)S(1)} collective-permute-done((bf16[128,1024]{1,0:T(8,128)(2,1)S(1)}, bf16[128,1024]{1,0:T(8,128)(2,1)S(1)}, u32[]{:S(2)}, u32[]{:S(2)}) %collective-permute-start.10) | collective-permute-done | bytes 262176 | tf_op jit(solution)/shard_map/ppermute | solution.py:461
  79.0 7.2 %collective-permute-done.17.arrived = bf16[128,1536]{1,0:T(8,128)(2,1)S(1)} collective-permute-done((bf16[128,1536]{1,0:T(8,128)(2,1)S(1)}, bf16[128,1536]{1,0:T(8,128)(2,1)S(1)}, u32[]{:S(2)}, u32[]{:S(2)}) %collective-permute-start.17) | collective-permute-done | bytes 393248 | tf_op jit(solution)/shard_map/ppermute | solution.py:461
  87.0 5.5 %collective-permute-done.14.arrived.refs_3_ = bf16[128,1152]{1,0:T(8,128)(2,1)S(1)} collective-permute-done((bf16[128,1152]{1,0:T(8,128)(2,1)S(1)}, bf16[128,1152]{1,0:T(8,128)(2,1)S(1)}, u32[]{:S(2)}, u32[]{:S(2)}) %collective-permute-start.14) | collective-permute-done | bytes 294944 | tf_op jit(solution)/shard_map/ppermute | solution.py:461
  93.2 1.7 %adam.1 = (f32[4,128,128]{2,1,0:T(8,128)}, f32[4,128,128]{2,1,0:T(8,128)}, f32[4,128,128]{2,1,0:T(8,128)}) custom-call(s32[4,12]{1,0:T(4,128)S(1)} %table.1, bf16[128,128]{1,0:T(8,128)(2,1)S(1)} %get-tuple-element.69.refs_0_, bf16[128,128]{1,0:T(8,128)(2,1)S(1)} %get-tuple-element.70.refs_1_, bf16[128,128]{1,0:T(8,128)(2,1)S(1)} %get-tuple-element.71.refs_2_, ...), custom_call_target="tpu_custom_call" | custom-call | flops 65536 | bytes 131072 | tf_op jit(solution)/shard_map/adam/pallas_call | solution.py:447
  94.9 2.1 %collective-permute-done.11.arrived = bf16[128,1024]{1,0:T(8,128)(2,1)S(1)} collective-permute-done((bf16[128,1024]{1,0:T(8,128)(2,1)S(1)}, bf16[128,1024]{1,0:T(8,128)(2,1)S(1)}, u32[]{:S(2)}, u32[]{:S(2)}) %collective-permute-start.11) | collective-permute-done | bytes 262176 | tf_op jit(solution)/shard_map/ppermute | solution.py:461
  (40 shorter events, 13.7 us)
Async XLA Ops:
  0.6 8.4 %collective-permute-start.3 = (bf16[128,2048]{1,0:T(8,128)(2,1)}, bf16[128,2048]{1,0:T(8,128)(2,1)S(1)}, u32[]{:S(2)}, u32[]{:S(2)}) collective-permute-start(bf16[128,2048]{1,0:T(8,128)(2,1)} %own.1), channel_id=1, source_target_pairs={{1,0},{0,1},{3,2},{2,3},{5,4},{4,5},{7,6},{6,7},{9,8},{8,9},{11,10... | collective-permute-start | bytes 1572872 | tf_op jit(solution)/shard_map/ppermute | solution.py:472
  1.1 17.1 %collective-permute-start.4 = (bf16[128,2048]{1,0:T(8,128)(2,1)}, bf16[128,2048]{1,0:T(8,128)(2,1)S(1)}, u32[]{:S(2)}, u32[]{:S(2)}) collective-permute-start(bf16[128,2048]{1,0:T(8,128)(2,1)} %own.1), channel_id=1, source_target_pairs={{2,0},{0,2},{3,1},{1,3},{6,4},{4,6},{7,5},{5,7},{10,8},{8,10},{11,... | collective-permute-start | bytes 1572872 | tf_op jit(solution)/shard_map/ppermute | solution.py:461
  4.5 6.1 %collective-permute-start.2 = (s32[1,8]{1,0:T(1,128)S(1)}, s32[1,8]{1,0:T(1,128)S(1)}, u32[]{:S(2)}, u32[]{:S(2)}) collective-permute-start(s32[1,8]{1,0:T(1,128)S(1)} %pad_add_fusion.refs_0_), channel_id=1, source_target_pairs={{4,0},{8,4},{12,8},{0,12},{5,1},{9,5},{13,9},{1,13},{6,2},{10,6},{... | collective-permute-start | bytes 104 | tf_op jit(solution)/shard_map/ppermute | solution.py:461
  8.1 4.4 %collective-permute-start.1 = (s32[1,8]{1,0:T(1,128)S(1)}, s32[1,8]{1,0:T(1,128)S(1)}, u32[]{:S(2)}, u32[]{:S(2)}) collective-permute-start(s32[1,8]{1,0:T(1,128)S(1)} %pad_add_fusion.refs_0_), channel_id=1, source_target_pairs={{8,0},{12,4},{0,8},{4,12},{9,1},{13,5},{1,9},{5,13},{10,2},{14,6},... | collective-permute-start | bytes 104 | tf_op jit(solution)/shard_map/ppermute | solution.py:461
  8.1 5.3 %collective-permute-start = (s32[1,8]{1,0:T(1,128)S(1)}, s32[1,8]{1,0:T(1,128)S(1)}, u32[]{:S(2)}, u32[]{:S(2)}) collective-permute-start(s32[1,8]{1,0:T(1,128)S(1)} %pad_add_fusion.refs_0_), channel_id=1, source_target_pairs={{12,0},{0,4},{4,8},{8,12},{13,1},{1,5},{5,9},{9,13},{14,2},{2,6},{... | collective-permute-start | bytes 104 | tf_op jit(solution)/shard_map/ppermute | solution.py:461
  14.2 12.2 %collective-permute-start.6 = (bf16[5,128,128]{2,1,0:T(8,128)(2,1)S(1)}, bf16[5,128,128]{2,1,0:T(8,128)(2,1)S(1)}, u32[]{:S(2)}, u32[]{:S(2)}) collective-permute-start(bf16[5,128,128]{2,1,0:T(8,128)(2,1)S(1)} %get-tuple-element.51), channel_id=1, source_target_pairs={{12,0},{0,4},{4,8},{8,12},{13,1},{1,5},{5,9},{9,13},{14,2},{2,6},{... | collective-permute-start | bytes 491528 | tf_op jit(solution)/shard_map/ppermute | solution.py:461
  14.2 13.8 %collective-permute-start.7 = (bf16[5,128,128]{2,1,0:T(8,128)(2,1)S(1)}, bf16[5,128,128]{2,1,0:T(8,128)(2,1)S(1)}, u32[]{:S(2)}, u32[]{:S(2)}) collective-permute-start(bf16[5,128,128]{2,1,0:T(8,128)(2,1)S(1)} %get-tuple-element.52), channel_id=1, source_target_pairs={{8,0},{12,4},{0,8},{4,12},{9,1},{13,5},{1,9},{5,13},{10,2},{14,6},... | collective-permute-start | bytes 491528 | tf_op jit(solution)/shard_map/ppermute | solution.py:461
  15.4 12.6 %collective-permute-start.8 = (bf16[5,128,128]{2,1,0:T(8,128)(2,1)S(1)}, bf16[5,128,128]{2,1,0:T(8,128)(2,1)S(1)}, u32[]{:S(2)}, u32[]{:S(2)}) collective-permute-start(bf16[5,128,128]{2,1,0:T(8,128)(2,1)S(1)} %get-tuple-element.53), channel_id=1, source_target_pairs={{4,0},{8,4},{12,8},{0,12},{5,1},{9,5},{13,9},{1,13},{6,2},{10,6},{... | collective-permute-start | bytes 491528 | tf_op jit(solution)/shard_map/ppermute | solution.py:461
  18.3 4.1 %collective-permute-start.5 = (bf16[128,2048]{1,0:T(8,128)(2,1)S(1)}, bf16[128,2048]{1,0:T(8,128)(2,1)S(1)}, u32[]{:S(2)}, u32[]{:S(2)}) collective-permute-start(bf16[128,2048]{1,0:T(8,128)(2,1)S(1)} %collective-permute-done.4.refs_1_), channel_id=1, source_target_pairs={{1,0},{0,1},{3,2},{2,3},{5,4},{4,5},{7,6},{6,7},{9,8},{8,9},{11,10... | collective-permute-start | bytes 1572872 | tf_op jit(solution)/shard_map/ppermute | solution.py:461
  28.9 13.0 %collective-permute-start.15 = (bf16[128,1536]{1,0:T(8,128)(2,1)S(1)}, bf16[128,1536]{1,0:T(8,128)(2,1)S(1)}, u32[]{:S(2)}, u32[]{:S(2)}) collective-permute-start(bf16[128,1536]{1,0:T(8,128)(2,1)S(1)} %get-tuple-element.68), channel_id=1, source_target_pairs={{12,0},{0,4},{4,8},{8,12},{13,1},{1,5},{5,9},{9,13},{14,2},{2,6},{... | collective-permute-start | bytes 1179656 | tf_op jit(solution)/shard_map/ppermute | solution.py:461
  37.9 13.1 %collective-permute-start.12 = (bf16[128,1408]{1,0:T(8,128)(2,1)S(1)}, bf16[128,1408]{1,0:T(8,128)(2,1)S(1)}, u32[]{:S(2)}, u32[]{:S(2)}) collective-permute-start(bf16[128,1408]{1,0:T(8,128)(2,1)S(1)} %attach.1), channel_id=1, source_target_pairs={{12,0},{0,4},{4,8},{8,12},{13,1},{1,5},{5,9},{9,13},{14,2},{2,6},{... | collective-permute-start | bytes 1081352 | tf_op jit(solution)/shard_map/ppermute | solution.py:461
  42.0 24.3 %collective-permute-start.16 = (bf16[128,1536]{1,0:T(8,128)(2,1)S(1)}, bf16[128,1536]{1,0:T(8,128)(2,1)S(1)}, u32[]{:S(2)}, u32[]{:S(2)}) collective-permute-start(bf16[128,1536]{1,0:T(8,128)(2,1)S(1)} %add.12), channel_id=1, source_target_pairs={{12,0},{0,4},{4,8},{8,12},{13,1},{1,5},{5,9},{9,13},{14,2},{2,6},{... | collective-permute-start | bytes 1179656 | tf_op jit(solution)/shard_map/ppermute | solution.py:461
  49.0 16.1 %collective-permute-start.9 = (bf16[128,1024]{1,0:T(8,128)(2,1)S(1)}, bf16[128,1024]{1,0:T(8,128)(2,1)S(1)}, u32[]{:S(2)}, u32[]{:S(2)}) collective-permute-start(bf16[128,1024]{1,0:T(8,128)(2,1)S(1)} %get-tuple-element.59), channel_id=1, source_target_pairs={{12,0},{0,4},{4,8},{8,12},{13,1},{1,5},{5,9},{9,13},{14,2},{2,6},{... | collective-permute-start | bytes 786440 | tf_op jit(solution)/shard_map/ppermute | solution.py:461
  51.1 21.0 %collective-permute-start.13 = (bf16[128,1280]{1,0:T(8,128)(2,1)S(1)}, bf16[128,1280]{1,0:T(8,128)(2,1)S(1)}, u32[]{:S(2)}, u32[]{:S(2)}) collective-permute-start(bf16[128,1280]{1,0:T(8,128)(2,1)S(1)} %get-tuple-element.66), channel_id=1, source_target_pairs={{12,0},{0,4},{4,8},{8,12},{13,1},{1,5},{5,9},{9,13},{14,2},{2,6},{... | collective-permute-start | bytes 983048 | tf_op jit(solution)/shard_map/ppermute | solution.py:461
  65.1 12.6 %collective-permute-start.10 = (bf16[128,1024]{1,0:T(8,128)(2,1)S(1)}, bf16[128,1024]{1,0:T(8,128)(2,1)S(1)}, u32[]{:S(2)}, u32[]{:S(2)}) collective-permute-start(bf16[128,1024]{1,0:T(8,128)(2,1)S(1)} %add.8), channel_id=1, source_target_pairs={{12,0},{0,4},{4,8},{8,12},{13,1},{1,5},{5,9},{9,13},{14,2},{2,6},{... | collective-permute-start | bytes 786440 | tf_op jit(solution)/shard_map/ppermute | solution.py:461
  66.4 19.7 %collective-permute-start.17 = (bf16[128,1536]{1,0:T(8,128)(2,1)S(1)}, bf16[128,1536]{1,0:T(8,128)(2,1)S(1)}, u32[]{:S(2)}, u32[]{:S(2)}) collective-permute-start(bf16[128,1536]{1,0:T(8,128)(2,1)S(1)} %add.13), channel_id=1, source_target_pairs={{12,0},{0,4},{4,8},{8,12},{13,1},{1,5},{5,9},{9,13},{14,2},{2,6},{... | collective-permute-start | bytes 1179656 | tf_op jit(solution)/shard_map/ppermute | solution.py:461
  72.2 20.3 %collective-permute-start.14 = (bf16[128,1152]{1,0:T(8,128)(2,1)S(1)}, bf16[128,1152]{1,0:T(8,128)(2,1)S(1)}, u32[]{:S(2)}, u32[]{:S(2)}) collective-permute-start(bf16[128,1152]{1,0:T(8,128)(2,1)S(1)} %get-tuple-element.67), channel_id=1, source_target_pairs={{12,0},{0,4},{4,8},{8,12},{13,1},{1,5},{5,9},{9,13},{14,2},{2,6},{... | collective-permute-start | bytes 884744 | tf_op jit(solution)/shard_map/ppermute | solution.py:461
  77.8 15.4 %copy-start = (f32[1,1,4,128,128]{4,3,2,1,0:T(8,128)S(1)}, f32[1,1,4,128,128]{4,3,2,1,0:T(8,128)}, u32[]{:S(2)}) copy-start(f32[1,1,4,128,128]{4,3,2,1,0:T(8,128)} %param.13) | copy-start | bytes 786436
  77.8 15.4 %copy-start.1 = (f32[1,1,4,128,128]{4,3,2,1,0:T(8,128)S(1)}, f32[1,1,4,128,128]{4,3,2,1,0:T(8,128)}, u32[]{:S(2)}) copy-start(f32[1,1,4,128,128]{4,3,2,1,0:T(8,128)} %param.14) | copy-start | bytes 786436
  77.8 15.4 %copy-start.2 = (f32[1,1,4,128,128]{4,3,2,1,0:T(8,128)S(1)}, f32[1,1,4,128,128]{4,3,2,1,0:T(8,128)}, u32[]{:S(2)}) copy-start(f32[1,1,4,128,128]{4,3,2,1,0:T(8,128)} %param.15) | copy-start | bytes 786436
  77.8 19.2 %collective-permute-start.11 = (bf16[128,1024]{1,0:T(8,128)(2,1)S(1)}, bf16[128,1024]{1,0:T(8,128)(2,1)S(1)}, u32[]{:S(2)}, u32[]{:S(2)}) collective-permute-start(bf16[128,1024]{1,0:T(8,128)(2,1)S(1)} %add.9), channel_id=1, source_target_pairs={{12,0},{0,4},{4,8},{8,12},{13,1},{1,5},{5,9},{9,13},{14,2},{2,6},{... | collective-permute-start | bytes 786440 | tf_op jit(solution)/shard_map/ppermute | solution.py:461

commit v18 on v17

--- a/solution.py
+++ b/solution.py
@@ -185,7 +185,7 @@
 
 
 def begin_kernel(spans, slots, block, table, early, rows, *refs):
-    stored, (first, held, total, chunk_rows) = refs[:spans], refs[spans:]
+    stored, (first, held, total) = refs[:spans], refs[spans:]
     me = lax.axis_index("seq")
     before = rank_before(table, 0, spans, slots)
     for j in range(slots):
@@ -201,15 +201,14 @@
         @pl.when(chunk_at(p) == wrap(me - 1, spans))
         def _():
             total[...] = early[p * chunk : (p + 1) * chunk]
-            chunk_rows[...] = rows[p * chunk : (p + 1) * chunk]
-
-    add_delta(table, chunk_rows, held, total, 0)
+            add_delta(table, rows.at[pl.ds(p * chunk, chunk)], held, total, 0)
+
     first[...] = total[...].astype(first.dtype)
 
 
 def begin_call(sizes, table, early, rows, stored):
     spans, slots, block = sizes
-    (tokens, columns), d_width = early.shape, rows.shape[1]
+    tokens, columns = early.shape
     chunk = tokens // spans
     return pl.pallas_call(
         functools.partial(begin_kernel, *sizes),
@@ -219,10 +218,7 @@
         ],
         in_specs=[smem()] + [vmem()] * (2 + spans),
         out_specs=[vmem()] * 2,
-        scratch_shapes=[
-            pltpu.VMEM((chunk, columns), jnp.float32),
-            pltpu.VMEM((chunk, d_width), rows.dtype),
-        ],
+        scratch_shapes=[pltpu.VMEM((chunk, columns), jnp.float32)],
         compiler_params=params(),
         cost_estimate=cost(chunk * columns),
         name="begin",

time: 97.3 us -> 97 us (level)
  transfers between devices with their start and end apart: 18 -> 18, of which waited for: 11 -> 11; matrix products, arithmetic and copies ran while one was open for 1% -> 1% of each run, Pallas kernels for 25% -> 26%
where the time goes in v18:
time: 97 us; the launch traced here: 97.3 us
  waiting for transfers between devices  45.7 us (47%)
  Pallas kernels  26.6 us (27%)
  starting transfers between devices  23.3 us (24%)
    ppermute x17, waiting for transfers between devices, take_from(): lax.ppermute(array, axis, [((i + places) % size, i) for i in range(size)])  45.7 us
    ppermute x17, starting transfers between devices, take_from(): lax.ppermute(array, axis, [((i + places) % size, i) for i in range(size)])  22.8 us
    pallas_call x2, Pallas kernels, matmul_call(): pl.pallas_call(functools.partial(matmul_kernel, low, ends), grid=(ends[-1...  8.89 us
    pallas_call x1, Pallas kernels, early_matmul_call(): pl.pallas_call(functools.partial(early_matmul_kernel, width), grid=(colum...  4.04 us
    pallas_call x1, Pallas kernels, per_device(): pl.pallas_call(lay_kernel, out_shape=jax.ShapeDtypeStruct((laid * width,...  2.79 us
    pallas_call x3, Pallas kernels, last_call(): pl.pallas_call(functools.partial(last_kernel, low), out_shape=shape, in_s...  2.32 us
  transfers between devices with their start and end apart: 18, of which 11 were waited for; matrix products, arithmetic and copies ran while one was open for 1% of the time, Pallas kernels for 26%

profile of v18, /device:TPU:0, one launch (start us, length us, event | category | flops | bytes accessed | tf_op | source)
XLA Modules:
  0.0 97.3 jit_solution(16526629050444625244)
XLA Ops:
  1.1 2.6 %collective-permute-start.4 = (bf16[128,2048]{1,0:T(8,128)(2,1)}, bf16[128,2048]{1,0:T(8,128)(2,1)S(1)}, u32[]{:S(2)}, u32[]{:S(2)}) collective-permute-start(bf16[128,2048]{1,0:T(8,128)(2,1)} %own.1), channel_id=1, source_target_pairs={{2,0},{0,2},{3,1},{1,3},{6,4},{4,6},{7,5},{5,7},{10,8},{8,10},{11,... | collective-permute-start | bytes 1572872 | tf_op jit(solution)/shard_map/ppermute | solution.py:457
  4.5 3.6 %collective-permute-start.2 = (s32[1,8]{1,0:T(1,128)S(1)}, s32[1,8]{1,0:T(1,128)S(1)}, u32[]{:S(2)}, u32[]{:S(2)}) collective-permute-start(s32[1,8]{1,0:T(1,128)S(1)} %pad_add_fusion.refs_0_), channel_id=1, source_target_pairs={{4,0},{8,4},{12,8},{0,12},{5,1},{9,5},{13,9},{1,13},{6,2},{10,6},{... | collective-permute-start | bytes 104 | tf_op jit(solution)/shard_map/ppermute | solution.py:457
  9.1 1.4 %early.1 = (bf16[4,128,128]{2,1,0:T(8,128)(2,1)S(1)}, bf16[128,3584]{1,0:T(8,128)(2,1)S(1)}, bf16[256,2048]{1,0:T(8,128)(2,1)S(1)}) custom-call(f32[4,128,128]{2,1,0:T(8,128)} %bitcast.8, bf16[128,3584]{1,0:T(8,128)(2,1)} %hidden.1, bf16[128,2048]{1,0:T(8,128)(2,1)} %own.1, bf16[128,2048]{1,0:T(8,128)(2,1)S(1)} %collective-permute-done.3.refs_0_), custom_call_target="tpu_custom_call" | custom-call | flops 458752 | bytes 917504 | tf_op jit(solution)/shard_map/early/pallas_call | solution.py:495
  10.5 2.0 %collective-permute-done.1.refs_2_ = s32[1,8]{1,0:T(1,128)S(1)} collective-permute-done((s32[1,8]{1,0:T(1,128)S(1)}, s32[1,8]{1,0:T(1,128)S(1)}, u32[]{:S(2)}, u32[]{:S(2)}) %collective-permute-start.1) | collective-permute-done | bytes 64 | tf_op jit(solution)/shard_map/ppermute | solution.py:457
  14.2 1.2 %collective-permute-start.7 = (bf16[5,128,128]{2,1,0:T(8,128)(2,1)S(1)}, bf16[5,128,128]{2,1,0:T(8,128)(2,1)S(1)}, u32[]{:S(2)}, u32[]{:S(2)}) collective-permute-start(bf16[5,128,128]{2,1,0:T(8,128)(2,1)S(1)} %get-tuple-element.52), channel_id=1, source_target_pairs={{8,0},{12,4},{0,8},{4,12},{9,1},{13,5},{1,9},{5,13},{10,2},{14,6},... | collective-permute-start | bytes 491528 | tf_op jit(solution)/shard_map/ppermute | solution.py:457
  15.4 2.8 %collective-permute-start.8 = (bf16[5,128,128]{2,1,0:T(8,128)(2,1)S(1)}, bf16[5,128,128]{2,1,0:T(8,128)(2,1)S(1)}, u32[]{:S(2)}, u32[]{:S(2)}) collective-permute-start(bf16[5,128,128]{2,1,0:T(8,128)(2,1)S(1)} %get-tuple-element.53), channel_id=1, source_target_pairs={{4,0},{8,4},{12,8},{0,12},{5,1},{9,5},{13,9},{1,13},{6,2},{10,6},{... | collective-permute-start | bytes 491528 | tf_op jit(solution)/shard_map/ppermute | solution.py:457
  18.3 2.8 %lay.1.weight = bf16[1536,2048]{1,0:T(8,128)(2,1)S(1)} custom-call(bf16[3584,2048]{1,0:T(8,128)(2,1)} %weight.5), custom_call_target="tpu_custom_call" | custom-call | flops 15728640000 | bytes 31457280000 | tf_op jit(solution)/shard_map/lay/pallas_call | solution.py:525
  21.1 1.2 %table.1 = s32[4,12]{1,0:T(4,128)S(1)} custom-call(s32[1,8]{1,0:T(1,128)S(1)} %pad_add_fusion.refs_0_, s32[1,8]{1,0:T(1,128)S(1)} %collective-permute-done.refs_1_, s32[1,8]{1,0:T(1,128)S(1)} %collective-permute-done.1.refs_2_, s32[1,8]{1,0:T(1,128)S(1)} %collective-permute-done.2.refs_3_), custom_call_target="tpu_custom_call" | custom-call | flops 16 | bytes 32 | tf_op jit(solution)/shard_map/table/pallas_call | solution.py:541
  22.3 4.0 %partial.3 = (f32[512,1536]{1,0:T(8,128)S(1)}, bf16[512,2048]{1,0:T(8,128)(2,1)S(1)}) custom-call(bf16[1536,2048]{1,0:T(8,128)(2,1)S(1)} %lay.1.weight, bf16[256,2048]{1,0:T(8,128)(2,1)S(1)} %get-tuple-element.47.refs_0_, bf16[128,2048]{1,0:T(8,128)(2,1)S(1)} %collective-permute-done.4.refs_1_, bf16[128,2048]{1,0:T(8,128)(2,1)S(1)} %collective-permute-done.5.refs_2_), custom_call_target="tpu_custom_call" | custom-call | flops 786432 | bytes 1572864 | tf_op jit(solution)/shard_map/partial/pallas_call | solution.py:145
  26.4 1.7 %collective-permute-done.7.refs_2_ = bf16[5,128,128]{2,1,0:T(8,128)(2,1)S(1)} collective-permute-done((bf16[5,128,128]{2,1,0:T(8,128)(2,1)S(1)}, bf16[5,128,128]{2,1,0:T(8,128)(2,1)S(1)}, u32[]{:S(2)}, u32[]{:S(2)}) %collective-permute-start.7) | collective-permute-done | bytes 163872 | tf_op jit(solution)/shard_map/ppermute | solution.py:457
  29.0 3.1 %collective-permute-start.15 = (bf16[128,1536]{1,0:T(8,128)(2,1)S(1)}, bf16[128,1536]{1,0:T(8,128)(2,1)S(1)}, u32[]{:S(2)}, u32[]{:S(2)}) collective-permute-start(bf16[128,1536]{1,0:T(8,128)(2,1)S(1)} %get-tuple-element.68), channel_id=1, source_target_pairs={{12,0},{0,4},{4,8},{8,12},{13,1},{1,5},{5,9},{9,13},{14,2},{2,6},{... | collective-permute-start | bytes 1179656 | tf_op jit(solution)/shard_map/ppermute | solution.py:457
  33.0 4.4 %partial.5 = (bf16[4,128,1024]{2,1,0:T(8,128)(2,1)S(1)}, bf16[128,1024]{1,0:T(8,128)(2,1)S(1)}) custom-call(s32[4,12]{1,0:T(4,128)S(1)} %table.1, bf16[3584,2048]{1,0:T(8,128)(2,1)} %weight.5, bf16[512,2048]{1,0:T(8,128)(2,1)S(1)} %get-tuple-element.55.rows, bf16[4,128,128]{2,1,0:T(8,128)(2,1)S(1)} %get-tuple-element.57.held), custom_call_target="tpu_custom_call" | custom-call | flops 2147483648 | bytes 4294967296 | tf_op jit(solution)/shard_map/partial/pallas_call | solution.py:271
  38.2 1.1 %delta.1.partials = bf16[4,128,1536]{2,1,0:T(8,128)(2,1)S(1)} custom-call(s32[4,12]{1,0:T(4,128)S(1)} %table.1, f32[512,1536]{1,0:T(8,128)S(1)} %get-tuple-element.56.early, bf16[512,2048]{1,0:T(8,128)(2,1)S(1)} %get-tuple-element.55.rows, bf16[4,128,128]{2,1,0:T(8,128)(2,1)S(1)} %get-tuple-element.57.held), custom_call_target="tpu_custom_call" | custom-call | flops 786432 | bytes 1572864 | tf_op jit(solution)/shard_map/delta/pallas_call | solution.py:238
  39.4 2.2 %collective-permute-done.15.arrived = bf16[128,1536]{1,0:T(8,128)(2,1)S(1)} collective-permute-done((bf16[128,1536]{1,0:T(8,128)(2,1)S(1)}, bf16[128,1536]{1,0:T(8,128)(2,1)S(1)}, u32[]{:S(2)}, u32[]{:S(2)}) %collective-permute-start.15) | collective-permute-done | bytes 393248 | tf_op jit(solution)/shard_map/ppermute | solution.py:457
  41.6 2.5 %collective-permute-start.16 = (bf16[128,1536]{1,0:T(8,128)(2,1)S(1)}, bf16[128,1536]{1,0:T(8,128)(2,1)S(1)}, u32[]{:S(2)}, u32[]{:S(2)}) collective-permute-start(bf16[128,1536]{1,0:T(8,128)(2,1)S(1)} %add.12), channel_id=1, source_target_pairs={{12,0},{0,4},{4,8},{8,12},{13,1},{1,5},{5,9},{9,13},{14,2},{2,6},{... | collective-permute-start | bytes 1179656 | tf_op jit(solution)/shard_map/ppermute | solution.py:457
  44.2 4.4 %partial.4 = (bf16[4,128,1024]{2,1,0:T(8,128)(2,1)S(1)}, bf16[128,1024]{1,0:T(8,128)(2,1)S(1)}) custom-call(s32[4,12]{1,0:T(4,128)S(1)} %table.1, bf16[3584,2048]{1,0:T(8,128)(2,1)} %weight.5, bf16[512,2048]{1,0:T(8,128)(2,1)S(1)} %get-tuple-element.55.rows, bf16[4,128,128]{2,1,0:T(8,128)(2,1)S(1)} %get-tuple-element.57.held), custom_call_target="tpu_custom_call" | custom-call | flops 2147483648 | bytes 4294967296 | tf_op jit(solution)/shard_map/partial/pallas_call | solution.py:271
  49.0 1.6 %collective-permute-done.12.arrived = bf16[128,1408]{1,0:T(8,128)(2,1)S(1)} collective-permute-done((bf16[128,1408]{1,0:T(8,128)(2,1)S(1)}, bf16[128,1408]{1,0:T(8,128)(2,1)S(1)}, u32[]{:S(2)}, u32[]{:S(2)}) %collective-permute-start.12) | collective-permute-done | bytes 360480 | tf_op jit(solution)/shard_map/ppermute | solution.py:457
  51.9 12.8 %collective-permute-done.9.arrived = bf16[128,1024]{1,0:T(8,128)(2,1)S(1)} collective-permute-done((bf16[128,1024]{1,0:T(8,128)(2,1)S(1)}, bf16[128,1024]{1,0:T(8,128)(2,1)S(1)}, u32[]{:S(2)}, u32[]{:S(2)}) %collective-permute-start.9) | collective-permute-done | bytes 262176 | tf_op jit(solution)/shard_map/ppermute | solution.py:457
  66.3 5.5 %collective-permute-done.13.arrived = bf16[128,1280]{1,0:T(8,128)(2,1)S(1)} collective-permute-done((bf16[128,1280]{1,0:T(8,128)(2,1)S(1)}, bf16[128,1280]{1,0:T(8,128)(2,1)S(1)}, u32[]{:S(2)}, u32[]{:S(2)}) %collective-permute-start.13) | collective-permute-done | bytes 327712 | tf_op jit(solution)/shard_map/ppermute | solution.py:457
  73.0 4.4 %collective-permute-done.10.arrived = bf16[128,1024]{1,0:T(8,128)(2,1)S(1)} collective-permute-done((bf16[128,1024]{1,0:T(8,128)(2,1)S(1)}, bf16[128,1024]{1,0:T(8,128)(2,1)S(1)}, u32[]{:S(2)}, u32[]{:S(2)}) %collective-permute-start.10) | collective-permute-done | bytes 262176 | tf_op jit(solution)/shard_map/ppermute | solution.py:457
  78.6 7.2 %collective-permute-done.17.arrived = bf16[128,1536]{1,0:T(8,128)(2,1)S(1)} collective-permute-done((bf16[128,1536]{1,0:T(8,128)(2,1)S(1)}, bf16[128,1536]{1,0:T(8,128)(2,1)S(1)}, u32[]{:S(2)}, u32[]{:S(2)}) %collective-permute-start.17) | collective-permute-done | bytes 393248 | tf_op jit(solution)/shard_map/ppermute | solution.py:457
  86.6 5.5 %collective-permute-done.14.arrived.refs_3_ = bf16[128,1152]{1,0:T(8,128)(2,1)S(1)} collective-permute-done((bf16[128,1152]{1,0:T(8,128)(2,1)S(1)}, bf16[128,1152]{1,0:T(8,128)(2,1)S(1)}, u32[]{:S(2)}, u32[]{:S(2)}) %collective-permute-start.14) | collective-permute-done | bytes 294944 | tf_op jit(solution)/shard_map/ppermute | solution.py:457
  92.9 1.7 %adam.1 = (f32[4,128,128]{2,1,0:T(8,128)}, f32[4,128,128]{2,1,0:T(8,128)}, f32[4,128,128]{2,1,0:T(8,128)}) custom-call(s32[4,12]{1,0:T(4,128)S(1)} %table.1, bf16[128,128]{1,0:T(8,128)(2,1)S(1)} %get-tuple-element.69.refs_0_, bf16[128,128]{1,0:T(8,128)(2,1)S(1)} %get-tuple-element.70.refs_1_, bf16[128,128]{1,0:T(8,128)(2,1)S(1)} %get-tuple-element.71.refs_2_, ...), custom_call_target="tpu_custom_call" | custom-call | flops 65536 | bytes 131072 | tf_op jit(solution)/shard_map/adam/pallas_call | solution.py:443
  94.5 2.0 %collective-permute-done.11.arrived = bf16[128,1024]{1,0:T(8,128)(2,1)S(1)} collective-permute-done((bf16[128,1024]{1,0:T(8,128)(2,1)S(1)}, bf16[128,1024]{1,0:T(8,128)(2,1)S(1)}, u32[]{:S(2)}, u32[]{:S(2)}) %collective-permute-start.11) | collective-permute-done | bytes 262176 | tf_op jit(solution)/shard_map/ppermute | solution.py:457
  (40 shorter events, 14.6 us)
Async XLA Ops:
  0.6 8.4 %collective-permute-start.3 = (bf16[128,2048]{1,0:T(8,128)(2,1)}, bf16[128,2048]{1,0:T(8,128)(2,1)S(1)}, u32[]{:S(2)}, u32[]{:S(2)}) collective-permute-start(bf16[128,2048]{1,0:T(8,128)(2,1)} %own.1), channel_id=1, source_target_pairs={{1,0},{0,1},{3,2},{2,3},{5,4},{4,5},{7,6},{6,7},{9,8},{8,9},{11,10... | collective-permute-start | bytes 1572872 | tf_op jit(solution)/shard_map/ppermute | solution.py:468
  1.1 17.1 %collective-permute-start.4 = (bf16[128,2048]{1,0:T(8,128)(2,1)}, bf16[128,2048]{1,0:T(8,128)(2,1)S(1)}, u32[]{:S(2)}, u32[]{:S(2)}) collective-permute-start(bf16[128,2048]{1,0:T(8,128)(2,1)} %own.1), channel_id=1, source_target_pairs={{2,0},{0,2},{3,1},{1,3},{6,4},{4,6},{7,5},{5,7},{10,8},{8,10},{11,... | collective-permute-start | bytes 1572872 | tf_op jit(solution)/shard_map/ppermute | solution.py:457
  4.5 6.1 %collective-permute-start.2 = (s32[1,8]{1,0:T(1,128)S(1)}, s32[1,8]{1,0:T(1,128)S(1)}, u32[]{:S(2)}, u32[]{:S(2)}) collective-permute-start(s32[1,8]{1,0:T(1,128)S(1)} %pad_add_fusion.refs_0_), channel_id=1, source_target_pairs={{4,0},{8,4},{12,8},{0,12},{5,1},{9,5},{13,9},{1,13},{6,2},{10,6},{... | collective-permute-start | bytes 104 | tf_op jit(solution)/shard_map/ppermute | solution.py:457
  8.1 4.4 %collective-permute-start.1 = (s32[1,8]{1,0:T(1,128)S(1)}, s32[1,8]{1,0:T(1,128)S(1)}, u32[]{:S(2)}, u32[]{:S(2)}) collective-permute-start(s32[1,8]{1,0:T(1,128)S(1)} %pad_add_fusion.refs_0_), channel_id=1, source_target_pairs={{8,0},{12,4},{0,8},{4,12},{9,1},{13,5},{1,9},{5,13},{10,2},{14,6},... | collective-permute-start | bytes 104 | tf_op jit(solution)/shard_map/ppermute | solution.py:457
  8.1 5.3 %collective-permute-start = (s32[1,8]{1,0:T(1,128)S(1)}, s32[1,8]{1,0:T(1,128)S(1)}, u32[]{:S(2)}, u32[]{:S(2)}) collective-permute-start(s32[1,8]{1,0:T(1,128)S(1)} %pad_add_fusion.refs_0_), channel_id=1, source_target_pairs={{12,0},{0,4},{4,8},{8,12},{13,1},{1,5},{5,9},{9,13},{14,2},{2,6},{... | collective-permute-start | bytes 104 | tf_op jit(solution)/shard_map/ppermute | solution.py:457
  14.2 12.2 %collective-permute-start.6 = (bf16[5,128,128]{2,1,0:T(8,128)(2,1)S(1)}, bf16[5,128,128]{2,1,0:T(8,128)(2,1)S(1)}, u32[]{:S(2)}, u32[]{:S(2)}) collective-permute-start(bf16[5,128,128]{2,1,0:T(8,128)(2,1)S(1)} %get-tuple-element.51), channel_id=1, source_target_pairs={{12,0},{0,4},{4,8},{8,12},{13,1},{1,5},{5,9},{9,13},{14,2},{2,6},{... | collective-permute-start | bytes 491528 | tf_op jit(solution)/shard_map/ppermute | solution.py:457
  14.2 13.8 %collective-permute-start.7 = (bf16[5,128,128]{2,1,0:T(8,128)(2,1)S(1)}, bf16[5,128,128]{2,1,0:T(8,128)(2,1)S(1)}, u32[]{:S(2)}, u32[]{:S(2)}) collective-permute-start(bf16[5,128,128]{2,1,0:T(8,128)(2,1)S(1)} %get-tuple-element.52), channel_id=1, source_target_pairs={{8,0},{12,4},{0,8},{4,12},{9,1},{13,5},{1,9},{5,13},{10,2},{14,6},... | collective-permute-start | bytes 491528 | tf_op jit(solution)/shard_map/ppermute | solution.py:457
  15.4 12.6 %collective-permute-start.8 = (bf16[5,128,128]{2,1,0:T(8,128)(2,1)S(1)}, bf16[5,128,128]{2,1,0:T(8,128)(2,1)S(1)}, u32[]{:S(2)}, u32[]{:S(2)}) collective-permute-start(bf16[5,128,128]{2,1,0:T(8,128)(2,1)S(1)} %get-tuple-element.53), channel_id=1, source_target_pairs={{4,0},{8,4},{12,8},{0,12},{5,1},{9,5},{13,9},{1,13},{6,2},{10,6},{... | collective-permute-start | bytes 491528 | tf_op jit(solution)/shard_map/ppermute | solution.py:457
  18.3 4.1 %collective-permute-start.5 = (bf16[128,2048]{1,0:T(8,128)(2,1)S(1)}, bf16[128,2048]{1,0:T(8,128)(2,1)S(1)}, u32[]{:S(2)}, u32[]{:S(2)}) collective-permute-start(bf16[128,2048]{1,0:T(8,128)(2,1)S(1)} %collective-permute-done.4.refs_1_), channel_id=1, source_target_pairs={{1,0},{0,1},{3,2},{2,3},{5,4},{4,5},{7,6},{6,7},{9,8},{8,9},{11,10... | collective-permute-start | bytes 1572872 | tf_op jit(solution)/shard_map/ppermute | solution.py:457
  29.0 12.5 %collective-permute-start.15 = (bf16[128,1536]{1,0:T(8,128)(2,1)S(1)}, bf16[128,1536]{1,0:T(8,128)(2,1)S(1)}, u32[]{:S(2)}, u32[]{:S(2)}) collective-permute-start(bf16[128,1536]{1,0:T(8,128)(2,1)S(1)} %get-tuple-element.68), channel_id=1, source_target_pairs={{12,0},{0,4},{4,8},{8,12},{13,1},{1,5},{5,9},{9,13},{14,2},{2,6},{... | collective-permute-start | bytes 1179656 | tf_op jit(solution)/shard_map/ppermute | solution.py:457
  37.5 13.2 %collective-permute-start.12 = (bf16[128,1408]{1,0:T(8,128)(2,1)S(1)}, bf16[128,1408]{1,0:T(8,128)(2,1)S(1)}, u32[]{:S(2)}, u32[]{:S(2)}) collective-permute-start(bf16[128,1408]{1,0:T(8,128)(2,1)S(1)} %attach.1), channel_id=1, source_target_pairs={{12,0},{0,4},{4,8},{8,12},{13,1},{1,5},{5,9},{9,13},{14,2},{2,6},{... | collective-permute-start | bytes 1081352 | tf_op jit(solution)/shard_map/ppermute | solution.py:457
  41.6 24.3 %collective-permute-start.16 = (bf16[128,1536]{1,0:T(8,128)(2,1)S(1)}, bf16[128,1536]{1,0:T(8,128)(2,1)S(1)}, u32[]{:S(2)}, u32[]{:S(2)}) collective-permute-start(bf16[128,1536]{1,0:T(8,128)(2,1)S(1)} %add.12), channel_id=1, source_target_pairs={{12,0},{0,4},{4,8},{8,12},{13,1},{1,5},{5,9},{9,13},{14,2},{2,6},{... | collective-permute-start | bytes 1179656 | tf_op jit(solution)/shard_map/ppermute | solution.py:457
  48.6 16.1 %collective-permute-start.9 = (bf16[128,1024]{1,0:T(8,128)(2,1)S(1)}, bf16[128,1024]{1,0:T(8,128)(2,1)S(1)}, u32[]{:S(2)}, u32[]{:S(2)}) collective-permute-start(bf16[128,1024]{1,0:T(8,128)(2,1)S(1)} %get-tuple-element.59), channel_id=1, source_target_pairs={{12,0},{0,4},{4,8},{8,12},{13,1},{1,5},{5,9},{9,13},{14,2},{2,6},{... | collective-permute-start | bytes 786440 | tf_op jit(solution)/shard_map/ppermute | solution.py:457
  50.7 21.0 %collective-permute-start.13 = (bf16[128,1280]{1,0:T(8,128)(2,1)S(1)}, bf16[128,1280]{1,0:T(8,128)(2,1)S(1)}, u32[]{:S(2)}, u32[]{:S(2)}) collective-permute-start(bf16[128,1280]{1,0:T(8,128)(2,1)S(1)} %get-tuple-element.66), channel_id=1, source_target_pairs={{12,0},{0,4},{4,8},{8,12},{13,1},{1,5},{5,9},{9,13},{14,2},{2,6},{... | collective-permute-start | bytes 983048 | tf_op jit(solution)/shard_map/ppermute | solution.py:457
  64.8 12.6 %collective-permute-start.10 = (bf16[128,1024]{1,0:T(8,128)(2,1)S(1)}, bf16[128,1024]{1,0:T(8,128)(2,1)S(1)}, u32[]{:S(2)}, u32[]{:S(2)}) collective-permute-start(bf16[128,1024]{1,0:T(8,128)(2,1)S(1)} %add.8), channel_id=1, source_target_pairs={{12,0},{0,4},{4,8},{8,12},{13,1},{1,5},{5,9},{9,13},{14,2},{2,6},{... | collective-permute-start | bytes 786440 | tf_op jit(solution)/shard_map/ppermute | solution.py:457
  66.0 19.7 %collective-permute-start.17 = (bf16[128,1536]{1,0:T(8,128)(2,1)S(1)}, bf16[128,1536]{1,0:T(8,128)(2,1)S(1)}, u32[]{:S(2)}, u32[]{:S(2)}) collective-permute-start(bf16[128,1536]{1,0:T(8,128)(2,1)S(1)} %add.13), channel_id=1, source_target_pairs={{12,0},{0,4},{4,8},{8,12},{13,1},{1,5},{5,9},{9,13},{14,2},{2,6},{... | collective-permute-start | bytes 1179656 | tf_op jit(solution)/shard_map/ppermute | solution.py:457
  71.8 20.3 %collective-permute-start.14 = (bf16[128,1152]{1,0:T(8,128)(2,1)S(1)}, bf16[128,1152]{1,0:T(8,128)(2,1)S(1)}, u32[]{:S(2)}, u32[]{:S(2)}) collective-permute-start(bf16[128,1152]{1,0:T(8,128)(2,1)S(1)} %get-tuple-element.67), channel_id=1, source_target_pairs={{12,0},{0,4},{4,8},{8,12},{13,1},{1,5},{5,9},{9,13},{14,2},{2,6},{... | collective-permute-start | bytes 884744 | tf_op jit(solution)/shard_map/ppermute | solution.py:457
  77.4 15.4 %copy-start = (f32[1,1,4,128,128]{4,3,2,1,0:T(8,128)S(1)}, f32[1,1,4,128,128]{4,3,2,1,0:T(8,128)}, u32[]{:S(2)}) copy-start(f32[1,1,4,128,128]{4,3,2,1,0:T(8,128)} %param.13) | copy-start | bytes 786436
  77.4 15.4 %copy-start.1 = (f32[1,1,4,128,128]{4,3,2,1,0:T(8,128)S(1)}, f32[1,1,4,128,128]{4,3,2,1,0:T(8,128)}, u32[]{:S(2)}) copy-start(f32[1,1,4,128,128]{4,3,2,1,0:T(8,128)} %param.14) | copy-start | bytes 786436
  77.5 15.4 %copy-start.2 = (f32[1,1,4,128,128]{4,3,2,1,0:T(8,128)S(1)}, f32[1,1,4,128,128]{4,3,2,1,0:T(8,128)}, u32[]{:S(2)}) copy-start(f32[1,1,4,128,128]{4,3,2,1,0:T(8,128)} %param.15) | copy-start | bytes 786436
  77.5 19.1 %collective-permute-start.11 = (bf16[128,1024]{1,0:T(8,128)(2,1)S(1)}, bf16[128,1024]{1,0:T(8,128)(2,1)S(1)}, u32[]{:S(2)}, u32[]{:S(2)}) collective-permute-start(bf16[128,1024]{1,0:T(8,128)(2,1)S(1)} %add.9), channel_id=1, source_target_pairs={{12,0},{0,4},{4,8},{8,12},{13,1},{1,5},{5,9},{9,13},{14,2},{2,6},{... | collective-permute-start | bytes 786440 | tf_op jit(solution)/shard_map/ppermute | solution.py:457
